TPU v7x, 512 devices: a whole 4x8x8 slice. The times are simulated.
512 devices in a mesh: rows: 16 (over z, core), cols: 32 (over y, x).
Axes of the slice: x: 4, y: 8, z: 8, core: 2. Of those that a mesh axis runs over, the one named last changes fastest.
Arguments:
- fine_in: bfloat16 [16, 32, 312, 196], P('rows', 'cols'), may hold values from -6 to 6
- coarse_in: bfloat16 [16, 32, 624, 49], P('rows', 'cols'), may hold values from -6 to 6
- inproj_fine: bfloat16 [3, 312, 312], replicated, as said below
- outproj_fine: bfloat16 [312, 312], replicated, may hold values from -0.3125 to 0.3125
- expand_fine: bfloat16 [1248, 312], replicated, may hold values from -0.3125 to 0.3125
- depth_fine: float32 [9, 1248], replicated, may hold values from -2 to 2
- shrink_fine: bfloat16 [312, 1248], replicated, may hold values from -0.15625 to 0.15625
- inproj_coarse: bfloat16 [3, 624, 624], P(None, 'rows'), as said below
- outproj_coarse: bfloat16 [624, 624], P(None, 'rows'), may hold values from -0.25 to 0.25
- expand_coarse: bfloat16 [2496, 624], P('rows'), may hold values from -0.25 to 0.25
- depth_coarse: float32 [9, 2496], replicated, may hold values from -2 to 2
- shrink_coarse: bfloat16 [624, 2496], P(None, 'rows'), may hold values from -0.125 to 0.125
- to_fine: bfloat16 [312, 624], replicated, may hold values from -0.25 to 0.25
- to_coarse: bfloat16 [9, 624, 312], P(None, 'rows'), may hold values from -0.109375 to 0.109375
Outputs:
- fine_out: bfloat16 [16, 32, 312, 196], P('rows', 'cols')
- coarse_out: bfloat16 [16, 32, 624, 49], P('rows', 'cols')
Inputs may be any that keep to these rules, and one draw needn't show every extreme that they name: `inproj_fine`: queries, keys and values projections stacked in this order along the first dimension, output channel second. `inproj_coarse`: queries, keys and values projections stacked in this order along the first dimension, output channel second.
All inputs are finite; a program needn't handle non-finite values.
Results may differ from a plain program's by a relative error of at most 0.014.
Values may be sent and summed in bfloat16 or wider, within the bound.
No kernel may reach another device: no remote copies, remote signals or barrier semaphores. Data moves between devices by JAX's collectives and lax.ppermute only.
A program may use at most 64 MiB of HBM per device.

v0:
```python
import math

import jax
import jax.numpy as jnp
from jax import lax
from jax.sharding import PartitionSpec as P

HEADS_FINE = 8
HEADS_COARSE = 16
WIN = 7


EPSILON = 1e-05


def padded_2(shard, sides, width):
    for axis, dim in sides:
        size, length = (lax.axis_size(axis), shard.shape[dim])
        up = [(i, (i + 1) % size) for i in range(size - 1)]
        down = [(j, i) for i, j in up]
        last = lax.slice_in_dim(shard, length - width, length, axis=dim)
        first = lax.slice_in_dim(shard, 0, width, axis=dim)
        before = lax.ppermute(last, axis, up)
        after = lax.ppermute(first, axis, down)
        shard = jnp.concatenate([before, shard, after], axis=dim)
    return shard


def passed_along(block, axis, distance):
    devices = range(lax.axis_size(axis))
    route = [(i - distance, i) for i in devices if i - distance in devices]
    return lax.ppermute(block, axis, route)


def normalize(values_in):
    values = values_in.astype(jnp.float32)
    center = jnp.mean(values, axis=0, keepdims=True)
    spread = jnp.mean((values - center) ** 2, axis=0, keepdims=True)
    return ((values - center) * lax.rsqrt(spread + EPSILON)).astype(jnp.bfloat16)


def to_windows(picture, head_count):
    channels, height, breadth = picture.shape
    head_width = channels // head_count
    shaped = picture.reshape(head_count, head_width, height // WIN, WIN, breadth // WIN, WIN)
    return shaped.transpose(0, 2, 4, 3, 5, 1).reshape(
        head_count, height // WIN, breadth // WIN, WIN * WIN, head_width
    )


def from_windows(blocks, height, breadth):
    head_count, grid_rows, grid_cols, cellcount, head_width = blocks.shape
    shaped = blocks.reshape(head_count, grid_rows, grid_cols, WIN, WIN, head_width)
    return shaped.transpose(0, 5, 1, 3, 2, 4).reshape(head_count * head_width, height, breadth)


def attend(queries, key_rows, value_rows, head_count):
    channels, height, breadth = queries.shape
    scaling = 1.0 / math.sqrt(channels // head_count)
    query_win = to_windows(queries, head_count)
    key_win = to_windows(key_rows, head_count)
    value_win = to_windows(value_rows, head_count)
    scores = (
        jnp.einsum("hrcqd,hrckd->hrcqk", query_win, key_win, preferred_element_type=jnp.float32)
        * scaling
    )
    row_max = jnp.max(scores, axis=-1, keepdims=True)
    exponent = jnp.exp(scores - row_max)
    probabilities = (exponent / jnp.sum(exponent, axis=-1, keepdims=True)).astype(jnp.bfloat16)
    mixture = jnp.einsum(
        "hrcqk,hrckd->hrcqd", probabilities, value_win, preferred_element_type=jnp.float32
    ).astype(jnp.bfloat16)
    return from_windows(mixture, height, breadth)


def depthwise(padded, kernel):
    height = padded.shape[1] - 2
    breadth = padded.shape[2] - 2
    running = jnp.zeros((padded.shape[0], height, breadth), jnp.float32)
    for offset in range(9):
        row_step, col_step = divmod(offset, 3)
        sample = padded[:, row_step : row_step + height, col_step : col_step + breadth].astype(
            jnp.float32
        )
        running = running + kernel[offset][:, None, None] * sample
    return running


def local(
    fine_in,
    coarse_in,
    inproj_fine,
    outproj_fine,
    expand_fine,
    depth_fine,
    shrink_fine,
    inproj_coarse,
    outproj_coarse,
    expand_coarse,
    depth_coarse,
    shrink_coarse,
    to_fine,
    to_coarse,
):
    fine_ch = fine_in.shape[2]
    coarse_ch = coarse_in.shape[2]
    fine_cells = fine_in.shape[3]
    coarse_cells = coarse_in.shape[3]
    fine_rows = fine_cells // (2 * WIN)
    coarse_rows = coarse_cells // WIN
    fine_pic = fine_in.reshape(fine_ch, fine_rows, 2 * WIN)
    coarse_pic = coarse_in.reshape(coarse_ch, coarse_rows, WIN)
    normed = normalize(fine_pic).reshape(fine_ch, fine_cells)
    projected = jnp.einsum(
        "tnc,cs->tns", inproj_fine, normed, preferred_element_type=jnp.float32
    ).astype(jnp.bfloat16)
    attended = attend(
        projected[0].reshape(fine_pic.shape),
        projected[1].reshape(fine_pic.shape),
        projected[2].reshape(fine_pic.shape),
        HEADS_FINE,
    ).reshape(fine_ch, fine_cells)
    middle = (
        fine_pic.reshape(fine_ch, fine_cells).astype(jnp.float32)
        + jnp.dot(outproj_fine, attended, preferred_element_type=jnp.float32)
    ).astype(jnp.bfloat16)
    normed_mid = normalize(middle)
    hidden = jax.nn.gelu(
        jnp.dot(expand_fine, normed_mid, preferred_element_type=jnp.float32), approximate=False
    ).astype(jnp.bfloat16)
    padded = padded_2(hidden.reshape(-1, fine_rows, 2 * WIN), (("rows", 1), ("cols", 2)), 1)
    convolved = (
        jax.nn.gelu(depthwise(padded, depth_fine), approximate=False)
        .astype(jnp.bfloat16)
        .reshape(-1, fine_cells)
    )
    fine_res = (
        middle.astype(jnp.float32)
        + jnp.dot(shrink_fine, convolved, preferred_element_type=jnp.float32)
    ).astype(jnp.bfloat16)
    coarse_norm = normalize(coarse_pic).reshape(coarse_ch, coarse_cells)
    coarse_proj = jnp.einsum(
        "tnc,cs->tns",
        lax.all_gather(inproj_coarse, "rows", axis=1, tiled=True),
        coarse_norm,
        preferred_element_type=jnp.float32,
    ).astype(jnp.bfloat16)
    coarse_att = attend(
        coarse_proj[0].reshape(coarse_pic.shape),
        coarse_proj[1].reshape(coarse_pic.shape),
        coarse_proj[2].reshape(coarse_pic.shape),
        HEADS_COARSE,
    ).reshape(coarse_ch, coarse_cells)
    section = coarse_att
    mixture = jnp.dot(
        lax.all_gather(outproj_coarse, "rows", axis=1, tiled=True),
        section,
        preferred_element_type=jnp.float32,
    )
    coarse_mid = (coarse_pic.reshape(coarse_ch, coarse_cells).astype(jnp.float32) + mixture).astype(
        jnp.bfloat16
    )
    coarse_normed_mid = normalize(coarse_mid)
    coarse_hidden = jax.nn.gelu(
        jnp.dot(
            lax.all_gather(expand_coarse, "rows", axis=0, tiled=True),
            coarse_normed_mid,
            preferred_element_type=jnp.float32,
        ),
        approximate=False,
    ).astype(jnp.bfloat16)
    coarse_pad = padded_2(
        coarse_hidden.reshape(-1, coarse_rows, WIN), (("rows", 1), ("cols", 2)), 1
    )
    coarse_conv = (
        jax.nn.gelu(depthwise(coarse_pad, depth_coarse), approximate=False)
        .astype(jnp.bfloat16)
        .reshape(-1, coarse_cells)
    )
    section = coarse_conv
    update = jnp.dot(
        lax.all_gather(shrink_coarse, "rows", axis=1, tiled=True),
        section,
        preferred_element_type=jnp.float32,
    )
    coarse_res = (coarse_mid.astype(jnp.float32) + update).astype(jnp.bfloat16)
    upsampled = jnp.dot(to_fine, coarse_res, preferred_element_type=jnp.float32).reshape(
        fine_ch, coarse_rows, WIN
    )
    upsampled = jnp.repeat(jnp.repeat(upsampled, 2, axis=1), 2, axis=2)
    fine_grid = fine_res.reshape(fine_ch, fine_rows, 2 * WIN)
    fine_out = (
        jax.nn.relu(fine_grid.astype(jnp.float32) + upsampled)
        .astype(jnp.bfloat16)
        .reshape(fine_in.shape)
    )
    above_row = passed_along(fine_grid[:, -1:, :], "rows", 1)
    extended = jnp.concatenate([above_row, fine_grid], axis=1)
    beside = passed_along(extended[:, :, -1:], "cols", 1)
    extended = jnp.concatenate([beside, extended], axis=2)
    extended = jnp.pad(extended, ((0, 0), (0, 1), (0, 1)))
    grouped = extended.reshape(fine_ch, coarse_rows + 1, 2, WIN + 1, 2)
    samples = []
    for offset in range(9):
        row_step, col_step = divmod(offset, 3)
        sample = grouped[
            :,
            row_step // 2 : row_step // 2 + coarse_rows,
            row_step % 2,
            col_step // 2 : col_step // 2 + WIN,
            col_step % 2,
        ]
        samples.append(sample.reshape(fine_ch, coarse_cells))
    stacked = jnp.stack(samples)
    downsampled = jnp.einsum(
        "gql,glm->qm",
        lax.all_gather(to_coarse, "rows", axis=1, tiled=True),
        stacked,
        preferred_element_type=jnp.float32,
    ).astype(jnp.bfloat16)
    coarse_out = jax.nn.relu(
        coarse_res.astype(jnp.float32) + downsampled.astype(jnp.float32)
    ).astype(jnp.bfloat16)
    return (fine_out, coarse_out.reshape(coarse_in.shape))


def solution(mesh):
    return jax.shard_map(
        local,
        mesh=mesh,
        in_specs=(
            P("rows", "cols", None, None),
            P("rows", "cols", None, None),
            P(),
            P(),
            P(),
            P(),
            P(),
            P(None, "rows", None),
            P(None, "rows"),
            P("rows", None),
            P(),
            P(None, "rows"),
            P(),
            P(None, "rows", None),
        ),
        out_specs=(P("rows", "cols", None, None), P("rows", "cols", None, None)),
        check_vma=False,
    )
```

profile of v0, /device:TPU:1, one launch (start us, length us, event | category | flops | bytes accessed | tf_op | source)
XLA Modules:
  0.0 219.4 jit_solution(8207015265681015755)
XLA Ops:
  7.2 1.8 copy.65
  9.1 0.7 all-gather.12.cloned.1.call-update
  9.8 0.7 all-gather.14.cloned.1.call-update
  10.6 1.0 convert_reduce_fusion
  11.6 0.2 fusion.124
  11.8 0.5 fusion.9
  12.4 0.3 reshape_reshape_squeeze.18
  12.8 0.3 reshape_reshape_squeeze.19
  13.2 0.3 reshape_reshape_squeeze.20
  13.6 0.6 fusion.178
  14.2 0.4 convolution_multiply_fusion
  14.6 0.4 convolution_convert_fusion.1
  15.0 0.4 copy.63
  15.5 0.3 reshape_reshape.8
  15.8 0.2 copy-done.6
  16.0 0.4 fusion.183
  16.4 0.2 multiply_reduce_fusion
  16.6 2.7 %fusion.63 = bf16[1248,196]{0,1:T(8,128)(2,1)S(1)} fusion(bf16[1248,312]{0,1:T(8,128)(2,1)S(1)} %copy-done, f32[312,196]{0,1:T(8,128)S(1)} %get-tuple-element.46, f32[196]{0:T(256)S(1)} %add_rsqrt_fusion, f32[196]{0:T(256)S(1)} %broadcast_multiply_fusion), kind=kOutput, calls=%fused_computation.64 | convolution fusion | flops 168718368 | bytes 1514144 | tf_op jit(solution)/shard_map/dot_general | solution.py:129
  19.4 0.2 reshape.199
  19.6 5.5 %collective-permute-start = (bf16[1248,1,14]{0,2,1:T(8,128)(2,1)S(1)}, bf16[1248,1,14]{0,2,1:T(8,128)(2,1)S(1)}, u32[]{:S(2)}, u32[]{:S(2)}) collective-permute-start(bf16[1248,1,14]{0,2,1:T(8,128)(2,1)S(1)} %get-tuple-element.32), channel_id=1, source_target_pairs={{0,32},{32,64},{64,96},{96,128},{128,160},{160,192},{192,224},{224... | collective-permute-start | bytes 104840 | tf_op jit(solution)/shard_map/ppermute | solution.py:23
  25.1 4.7 %collective-permute-start.1 = (bf16[1248,1,14]{0,2,1:T(8,128)(2,1)S(1)}, bf16[1248,1,14]{0,2,1:T(8,128)(2,1)S(1)}, u32[]{:S(2)}, u32[]{:S(2)}) collective-permute-start(bf16[1248,1,14]{0,2,1:T(8,128)(2,1)S(1)} %get-tuple-element.31), channel_id=1, source_target_pairs={{32,0},{64,32},{96,64},{128,96},{160,128},{192,160},{224,192},{256... | collective-permute-start | bytes 104840 | tf_op jit(solution)/shard_map/ppermute | solution.py:24
  29.8 0.8 copy.81
  30.8 23.9 %all-gather = bf16[16,39,624]{2,1,0:T(8,128)(2,1)S(1)} all-gather(bf16[1,39,624]{2,1,0:T(8,128)(2,1)S(1)} %bitcast.339), channel_id=1, replica_groups=mesh['rows'=16,'cols'=32] {'rows'}, dimensions={0}, use_global_device_ids=true | all-gather | bytes 827424 | tf_op jit(solution)/shard_map/all_gather | solution.py:156
  55.1 3.4 %collective-permute-start.2 = (bf16[1248,16,1]{0,2,1:T(2,128)(2,1)S(1)}, bf16[1248,16,1]{0,2,1:T(2,128)(2,1)S(1)}, u32[]{:S(2)}, u32[]{:S(2)}) collective-permute-start(bf16[1248,16,1]{0,2,1:T(2,128)(2,1)S(1)} %get-tuple-element.29), channel_id=1, source_target_pairs={{0,1},{1,2},{2,3},{3,4},{4,5},{5,6},{6,7},{7,8},{8,9},{9,10},{10,1... | collective-permute-start | bytes 119816 | tf_op jit(solution)/shard_map/ppermute | solution.py:23
  58.4 1.3 collective-permute-start.3
  60.1 4.3 %collective-permute-done.3 = bf16[1248,16,1]{0,2,1:T(2,128)(2,1)S(1)} collective-permute-done((bf16[1248,16,1]{0,2,1:T(2,128)(2,1)S(1)}, bf16[1248,16,1]{0,2,1:T(2,128)(2,1)S(1)}, u32[]{:S(2)}, u32[]{:S(2)}) %collective-permute-start.3) | collective-permute-done | bytes 39968 | tf_op jit(solution)/shard_map/ppermute | solution.py:24
  64.4 5.7 %fusion.24 = bf16[1248,14,14]{0,2,1:T(8,128)(2,1)S(1)} fusion(bf16[1248,14,14]{0,2,1:T(8,128)(2,1)S(1)} %reshape.199, bf16[1248,16,14]{0,2,1:T(8,128)(2,1)S(1)} %constant_dynamic-update-slice_fusion, bf16[1248,16,1]{0,2,1:T(2,128)(2,1)S(1)} %collective-permute-done.3, bf16[1248,16,1]{0,2,1:T(2,128)(2,1)S(1)} %collective-permute-done.2, ...), kind=kLoop, calls=%fused_computation.29 | loop fusion | flops 28129920 | bytes 1732224 | tf_op jit(solution)/shard_map/convert_element_type | solution.py:134
  70.1 0.2 reshape.200
  70.4 1.7 fusion.16
  72.2 3.2 %collective-permute-start.8 = (bf16[312,1,14]{0,2,1:T(8,128)(2,1)S(1)}, bf16[312,1,14]{0,2,1:T(8,128)(2,1)S(1)}, u32[]{:S(2)}, u32[]{:S(2)}) collective-permute-start(bf16[312,1,14]{0,2,1:T(8,128)(2,1)S(1)} %slice.282), channel_id=1, source_target_pairs={{0,32},{32,64},{64,96},{96,128},{128,160},{160,192},{192,224},{224... | collective-permute-start | bytes 26216 | tf_op jit(solution)/shard_map/ppermute | solution.py:32
  75.3 0.8 collective-permute-done.8
  76.2 3.3 %collective-permute-start.9 = (bf16[312,15,1]{0,2,1:T(2,128)(2,1)S(1)}, bf16[312,15,1]{0,2,1:T(2,128)(2,1)S(1)}, u32[]{:S(2)}, u32[]{:S(2)}) collective-permute-start(bf16[312,15,1]{0,2,1:T(2,128)(2,1)S(1)} %slice.283), channel_id=1, source_target_pairs={{0,1},{1,2},{2,3},{3,4},{4,5},{5,6},{6,7},{7,8},{8,9},{9,10},{10,1... | collective-permute-start | bytes 28088 | tf_op jit(solution)/shard_map/ppermute | solution.py:32
  79.5 0.2 slice_reduce_fusion.17
  79.8 0.4 reshape.216
  80.4 1.5 slice_reduce_fusion
  82.3 0.8 copy-done.10
  83.1 2.8 %fusion.19 = bf16[3,624,49]{1,2,0:T(8,128)(2,1)S(1)} fusion(bf16[3,624,624]{2,0,1:T(4,128)(2,1)} %all-gather.8.cloned.1.call-done, bf16[1,1,624,49]{2,3,1,0:T(8,128)(2,1)S(1)} %copy-done.3, f32[49]{0:T(128)S(1)} %add_rsqrt_fusion.3, f32[49]{0:T(128)S(1)} %broadcast_multiply_fusion.3), kind=kOutput, calls=%fused_computation.26 | convolution fusion | flops 114690576 | bytes 2581256 | tf_op jit(solution)/shard_map/tnc,cs->tns/dot_general | solution.py:142
  85.9 0.3 reshape_reshape_squeeze.21
  86.2 0.3 reshape_reshape_squeeze.22
  86.6 0.3 reshape_reshape_squeeze.23
  86.9 0.3 fusion.172
  87.2 0.3 convolution_multiply_fusion.1
  87.5 0.3 convolution_convert_fusion.2
  87.8 0.3 copy.71
  88.1 0.2 reshape_reshape.9
  88.3 0.4 fusion.177
  88.7 0.2 multiply_reduce_fusion.1
  88.9 17.4 %all-gather.12.cloned.1.call-done = bf16[16,156,624]{2,1,0:T(8,128)(2,1)} async-done(((bf16[1,156,624]{2,1,0:T(8,128)(2,1)}), bf16[16,156,624]{2,1,0:T(8,128)(2,1)}) %all-gather.12.cloned.1.call-update) | async-done | bytes 3115024 | tf_op jit(solution)/shard_map/all_gather | solution.py:166
  106.3 4.8 %reshape.218 = bf16[2496,624]{1,0:T(8,128)(2,1)} reshape(bf16[16,156,624]{2,1,0:T(8,128)(2,1)} %all-gather.12.cloned.1.call-done) | data formatting | bytes 6230016
  111.1 3.9 %fusion.85 = bf16[2496,49]{0,1:T(8,128)(2,1)S(1)} fusion(bf16[2496,624]{1,0:T(8,128)(2,1)} %reshape.218, f32[624,49]{0,1:T(8,128)S(1)} %get-tuple-element.44, f32[49]{0:T(128)S(1)} %add_rsqrt_fusion.2, f32[49]{0:T(128)S(1)} %broadcast_multiply_fusion.2), kind=kOutput, calls=%fused_computation.102 | convolution fusion | flops 160676880 | bytes 3482312 | tf_op jit(solution)/shard_map/dot_general | solution.py:165
  115.2 2.7 %collective-permute-start.4 = (bf16[2496,1,7]{0,2,1:T(8,128)(2,1)S(1)}, bf16[2496,1,7]{0,2,1:T(8,128)(2,1)S(1)}, u32[]{:S(2)}, u32[]{:S(2)}) collective-permute-start(bf16[2496,1,7]{0,2,1:T(8,128)(2,1)S(1)} %get-tuple-element.39), channel_id=1, source_target_pairs={{0,32},{32,64},{64,96},{96,128},{128,160},{160,192},{192,224},{224... | collective-permute-start | bytes 104840 | tf_op jit(solution)/shard_map/ppermute | solution.py:23
  118.0 1.9 collective-permute-start.5
  120.0 4.2 %collective-permute-done.5 = bf16[2496,1,7]{0,2,1:T(8,128)(2,1)S(1)} collective-permute-done((bf16[2496,1,7]{0,2,1:T(8,128)(2,1)S(1)}, bf16[2496,1,7]{0,2,1:T(8,128)(2,1)S(1)}, u32[]{:S(2)}, u32[]{:S(2)}) %collective-permute-start.5) | collective-permute-done | bytes 34976 | tf_op jit(solution)/shard_map/ppermute | solution.py:24
  124.3 3.1 %collective-permute-start.6 = (bf16[2496,9,1]{0,2,1:T(2,128)(2,1)S(1)}, bf16[2496,9,1]{0,2,1:T(2,128)(2,1)S(1)}, u32[]{:S(2)}, u32[]{:S(2)}) collective-permute-start(bf16[2496,9,1]{0,2,1:T(2,128)(2,1)S(1)} %get-tuple-element.36), channel_id=1, source_target_pairs={{0,1},{1,2},{2,3},{3,4},{4,5},{5,6},{6,7},{7,8},{8,9},{9,10},{10,1... | collective-permute-start | bytes 134792 | tf_op jit(solution)/shard_map/ppermute | solution.py:23
  127.4 1.5 collective-permute-start.7
  128.9 22.3 %all-gather.14.cloned.1.call-done = bf16[16,156,624]{2,1,0:T(8,128)(2,1)} async-done(((bf16[1,156,624]{2,1,0:T(8,128)(2,1)}), bf16[16,156,624]{2,1,0:T(8,128)(2,1)}) %all-gather.14.cloned.1.call-update) | async-done | bytes 3115024 | tf_op jit(solution)/shard_map/all_gather | solution.py:182
  151.2 4.8 %reshape.220 = bf16[2496,624]{1,0:T(8,128)(2,1)} reshape(bf16[16,156,624]{2,1,0:T(8,128)(2,1)} %all-gather.14.cloned.1.call-done) | data formatting | bytes 6230016
  156.0 2.8 %fusion.88 = bf16[2496,7,7]{0,2,1:T(8,128)(2,1)S(1)} fusion(bf16[2496,7,7]{0,2,1:T(8,128)(2,1)S(1)} %reshape.205, bf16[2496,9,7]{0,2,1:T(8,128)(2,1)S(1)} %constant_dynamic-update-slice_fusion.3, bf16[2496,9,1]{0,2,1:T(2,128)(2,1)S(1)} %collective-permute-done.7, bf16[2496,9,1]{0,2,1:T(2,128)(2,1)S(1)} %collective-permute-done.6, ...), kind=kLoop, calls=%fused_computation.105 | loop fusion | flops 14064960 | bytes 1053312 | tf_op jit(solution)/shard_map/convert_element_type | solution.py:177
  159.0 2.6 %fusion.39 = bf16[624,49]{0,1:T(8,128)(2,1)S(1)} fusion(f32[624,49]{0,1:T(8,128)S(1)} %get-tuple-element.44, bf16[2496,49]{0,1:T(8,128)(2,1)S(1)} %reshape.206, bf16[2496,624]{1,0:T(8,128)(2,1)} %reshape.220), kind=kOutput, calls=%fused_computation.53 | convolution fusion | flops 152696544 | bytes 3543072 | tf_op jit(solution)/shard_map/dot_general | solution.py:181
  161.6 0.2 convolution_bitcast_fusion.4
  162.0 0.2 reshape.209
  162.2 0.7 fusion.136
  162.9 44.4 %all-gather.10.cloned.1.call-done = bf16[9,624,312]{2,0,1:T(8,128)(2,1)} async-done(((bf16[9,39,312]{2,0,1:T(8,128)(2,1)}), bf16[9,624,312]{2,0,1:T(8,128)(2,1)}) %all-gather.10.cloned.1.call-update) | async-done | bytes 3504400 | tf_op jit(solution)/shard_map/all_gather | solution.py:217
  207.3 5.6 %fusion.58 = bf16[1,1,624,49]{2,3,1,0:T(8,128)(2,1)} fusion(bf16[9,312,49]{1,2,0:T(8,128)(2,1)S(1)} %constant_dynamic-update-slice_fusion.8, bf16[9,624,312]{2,0,1:T(8,128)(2,1)} %all-gather.10.cloned.1.call-done, bf16[624,49]{0,1:T(8,128)(2,1)S(1)} %fusion.39), kind=kOutput, calls=%fused_computation.61 | convolution fusion | flops 171898272 | bytes 3901872 | tf_op jit(solution)/shard_map/gql,glm->qm/dot_general | solution.py:215
  (93 shorter events, 2.7 us)
Async XLA Ops:
  7.2 9.4 %copy-start = (bf16[1248,312]{0,1:T(8,128)(2,1)S(1)}, bf16[1248,312]{0,1:T(8,128)(2,1)}, u32[]{:S(2)}) copy-start(bf16[1248,312]{0,1:T(8,128)(2,1)} %param.18) | copy-start | bytes 2336260
  7.2 4.4 %copy-start.1 = (bf16[1,1,312,196]{2,3,1,0:T(8,128)(2,1)S(1)}, bf16[1,1,312,196]{2,3,1,0:T(8,128)(2,1)}, u32[]{:S(2)}) copy-start(bf16[1,1,312,196]{2,3,1,0:T(8,128)(2,1)} %param.14) | copy-start | bytes 366916
  7.2 4.6 %copy-start.2 = (bf16[3,312,312]{2,1,0:T(8,128)(2,1)S(1)}, bf16[3,312,312]{2,1,0:T(8,128)(2,1)}, u32[]{:S(2)}) copy-start(bf16[3,312,312]{2,1,0:T(8,128)(2,1)} %param.16) | copy-start | bytes 1752196
  7.2 75.9 %all-gather.8.cloned.1.call-start = ((), (), s32[]{:S(2)}) async-start(), calls=%async_computation | async-start | bytes 3394560 | tf_op jit(solution)/shard_map/all_gather | solution.py:144
  9.0 97.2 %all-gather.12.cloned.1.call-start = ((), (), s32[]{:S(2)}) async-start(), calls=%async_computation.2 | async-start | bytes 3481600 | tf_op jit(solution)/shard_map/all_gather | solution.py:166
  9.8 141.4 %all-gather.14.cloned.1.call-start = ((), (), s32[]{:S(2)}) async-start(), calls=%async_computation.3 | async-start | bytes 3481600 | tf_op jit(solution)/shard_map/all_gather | solution.py:182
  10.5 196.8 %all-gather.10.cloned.1.call-start = ((), (), s32[]{:S(2)}) async-start(), calls=%async_computation.1 | async-start | bytes 8146944 | tf_op jit(solution)/shard_map/all_gather | solution.py:217
  15.0 0.9 copy-start.6
  19.3 10.5 %copy-start.5 = (bf16[9,39,312]{2,1,0:T(8,128)(2,1)S(1)}, bf16[9,39,312]{2,1,0:T(8,128)(2,1)}, u32[]{:S(2)}) copy-start(bf16[9,39,312]{2,1,0:T(8,128)(2,1)} %param.27) | copy-start | bytes 657076
  19.3 11.4 %copy-start.3 = (bf16[1,1,624,49]{2,3,1,0:T(8,128)(2,1)S(1)}, bf16[1,1,624,49]{2,3,1,0:T(8,128)(2,1)}, u32[]{:S(2)}) copy-start(bf16[1,1,624,49]{2,3,1,0:T(8,128)(2,1)} %param.15) | copy-start | bytes 183460
  19.3 11.5 %copy-start.8 = (bf16[624,39]{0,1:T(8,128)(2,1)S(1)}, bf16[624,39]{0,1:T(8,128)(2,1)}, u32[]{:S(2)}) copy-start(bf16[624,39]{0,1:T(8,128)(2,1)} %param.22) | copy-start | bytes 146020
  19.6 35.1 %copy-start.9 = (f32[9,1248]{1,0:T(8,128)S(1)}, f32[9,1248]{1,0:T(8,128)}, u32[]{:S(2)}) copy-start(f32[9,1248]{1,0:T(8,128)} %param.19) | copy-start | bytes 134788
  19.6 35.2 %collective-permute-start = (bf16[1248,1,14]{0,2,1:T(8,128)(2,1)S(1)}, bf16[1248,1,14]{0,2,1:T(8,128)(2,1)S(1)}, u32[]{:S(2)}, u32[]{:S(2)}) collective-permute-start(bf16[1248,1,14]{0,2,1:T(8,128)(2,1)S(1)} %get-tuple-element.32), channel_id=1, source_target_pairs={{0,32},{32,64},{64,96},{96,128},{128,160},{160,192},{192,224},{224... | collective-permute-start | bytes 104840 | tf_op jit(solution)/shard_map/ppermute | solution.py:23
  25.1 29.8 %collective-permute-start.1 = (bf16[1248,1,14]{0,2,1:T(8,128)(2,1)S(1)}, bf16[1248,1,14]{0,2,1:T(8,128)(2,1)S(1)}, u32[]{:S(2)}, u32[]{:S(2)}) collective-permute-start(bf16[1248,1,14]{0,2,1:T(8,128)(2,1)S(1)} %get-tuple-element.31), channel_id=1, source_target_pairs={{32,0},{64,32},{96,64},{128,96},{160,128},{192,160},{224,192},{256... | collective-permute-start | bytes 104840 | tf_op jit(solution)/shard_map/ppermute | solution.py:24
  55.1 5.0 %collective-permute-start.2 = (bf16[1248,16,1]{0,2,1:T(2,128)(2,1)S(1)}, bf16[1248,16,1]{0,2,1:T(2,128)(2,1)S(1)}, u32[]{:S(2)}, u32[]{:S(2)}) collective-permute-start(bf16[1248,16,1]{0,2,1:T(2,128)(2,1)S(1)} %get-tuple-element.29), channel_id=1, source_target_pairs={{0,1},{1,2},{2,3},{3,4},{4,5},{5,6},{6,7},{7,8},{8,9},{9,10},{10,1... | collective-permute-start | bytes 119816 | tf_op jit(solution)/shard_map/ppermute | solution.py:23
  58.4 6.0 %collective-permute-start.3 = (bf16[1248,16,1]{0,2,1:T(2,128)(2,1)S(1)}, bf16[1248,16,1]{0,2,1:T(2,128)(2,1)S(1)}, u32[]{:S(2)}, u32[]{:S(2)}) collective-permute-start(bf16[1248,16,1]{0,2,1:T(2,128)(2,1)S(1)} %get-tuple-element.30), channel_id=1, source_target_pairs={{1,0},{2,1},{3,2},{4,3},{5,4},{6,5},{7,6},{8,7},{9,8},{10,9},{11,1... | collective-permute-start | bytes 119816 | tf_op jit(solution)/shard_map/ppermute | solution.py:24
  70.4 9.1 %copy-start.7 = (f32[9,2496]{1,0:T(8,128)S(1)}, f32[9,2496]{1,0:T(8,128)}, u32[]{:S(2)}) copy-start(f32[9,2496]{1,0:T(8,128)} %param.24) | copy-start | bytes 269572
  72.2 4.0 %collective-permute-start.8 = (bf16[312,1,14]{0,2,1:T(8,128)(2,1)S(1)}, bf16[312,1,14]{0,2,1:T(8,128)(2,1)S(1)}, u32[]{:S(2)}, u32[]{:S(2)}) collective-permute-start(bf16[312,1,14]{0,2,1:T(8,128)(2,1)S(1)} %slice.282), channel_id=1, source_target_pairs={{0,32},{32,64},{64,96},{96,128},{128,160},{160,192},{192,224},{224... | collective-permute-start | bytes 26216 | tf_op jit(solution)/shard_map/ppermute | solution.py:32
  76.2 4.0 %collective-permute-start.9 = (bf16[312,15,1]{0,2,1:T(2,128)(2,1)S(1)}, bf16[312,15,1]{0,2,1:T(2,128)(2,1)S(1)}, u32[]{:S(2)}, u32[]{:S(2)}) collective-permute-start(bf16[312,15,1]{0,2,1:T(2,128)(2,1)S(1)} %slice.283), channel_id=1, source_target_pairs={{0,1},{1,2},{2,3},{3,4},{4,5},{5,6},{6,7},{7,8},{8,9},{9,10},{10,1... | collective-permute-start | bytes 28088 | tf_op jit(solution)/shard_map/ppermute | solution.py:32
  82.3 0.8 copy-start.10
  111.1 6.8 %copy-start.11 = (bf16[9,312,49]{1,2,0:T(8,128)(2,1)S(1)}, bf16[9,312,49]{1,2,0:T(8,128)(2,1)}, u32[]{:S(2)}) copy-start(bf16[9,312,49]{1,2,0:T(8,128)(2,1)} %copy-done.10) | copy-start | bytes 825556
  115.2 4.7 %collective-permute-start.4 = (bf16[2496,1,7]{0,2,1:T(8,128)(2,1)S(1)}, bf16[2496,1,7]{0,2,1:T(8,128)(2,1)S(1)}, u32[]{:S(2)}, u32[]{:S(2)}) collective-permute-start(bf16[2496,1,7]{0,2,1:T(8,128)(2,1)S(1)} %get-tuple-element.39), channel_id=1, source_target_pairs={{0,32},{32,64},{64,96},{96,128},{128,160},{160,192},{192,224},{224... | collective-permute-start | bytes 104840 | tf_op jit(solution)/shard_map/ppermute | solution.py:23
  118.0 6.2 %collective-permute-start.5 = (bf16[2496,1,7]{0,2,1:T(8,128)(2,1)S(1)}, bf16[2496,1,7]{0,2,1:T(8,128)(2,1)S(1)}, u32[]{:S(2)}, u32[]{:S(2)}) collective-permute-start(bf16[2496,1,7]{0,2,1:T(8,128)(2,1)S(1)} %get-tuple-element.38), channel_id=1, source_target_pairs={{32,0},{64,32},{96,64},{128,96},{160,128},{192,160},{224,192},{256... | collective-permute-start | bytes 104840 | tf_op jit(solution)/shard_map/ppermute | solution.py:24
  124.3 31.7 %collective-permute-start.6 = (bf16[2496,9,1]{0,2,1:T(2,128)(2,1)S(1)}, bf16[2496,9,1]{0,2,1:T(2,128)(2,1)S(1)}, u32[]{:S(2)}, u32[]{:S(2)}) collective-permute-start(bf16[2496,9,1]{0,2,1:T(2,128)(2,1)S(1)} %get-tuple-element.36), channel_id=1, source_target_pairs={{0,1},{1,2},{2,3},{3,4},{4,5},{5,6},{6,7},{7,8},{8,9},{9,10},{10,1... | collective-permute-start | bytes 134792 | tf_op jit(solution)/shard_map/ppermute | solution.py:23
  127.4 28.6 %collective-permute-start.7 = (bf16[2496,9,1]{0,2,1:T(2,128)(2,1)S(1)}, bf16[2496,9,1]{0,2,1:T(2,128)(2,1)S(1)}, u32[]{:S(2)}, u32[]{:S(2)}) collective-permute-start(bf16[2496,9,1]{0,2,1:T(2,128)(2,1)S(1)} %get-tuple-element.37), channel_id=1, source_target_pairs={{1,0},{2,1},{3,2},{4,3},{5,4},{6,5},{7,6},{8,7},{9,8},{10,9},{11,1... | collective-permute-start | bytes 134792 | tf_op jit(solution)/shard_map/ppermute | solution.py:24
  158.9 2.6 %copy-start.4 = (bf16[312,624]{1,0:T(8,128)(2,1)S(1)}, bf16[312,624]{1,0:T(8,128)(2,1)}, u32[]{:S(2)}) copy-start(bf16[312,624]{1,0:T(8,128)(2,1)} %param.26) | copy-start | bytes 1168132
Sparse Core Ops, SparseCore 0:
  10.2 51.1 all-gather.7
  63.5 42.7 all-gather.11
  108.4 42.7 all-gather.13
  153.2 54.0 all-gather.9
where the time goes:
time: 220 us; the launch traced here: 219 us
  waiting for transfers between devices  95.1 us (43%)
  starting transfers between devices  30.7 us (14%)
  blocking collectives  23.9 us (11%)
  matrix products  23.1 us (10%)
  local copies, waits for them, and re-layouts  20.8 us (9%)
  between operations  14.5 us (7%)
  other arithmetic  11.3 us (5%)
    all_gather x1, waiting for transfers between devices, local(): lax.all_gather(to_coarse, 'rows', axis=1, tiled=True)  44.4 us
    all_gather x1, blocking collectives, local(): lax.all_gather(outproj_coarse, 'rows', axis=1, tiled=True)  23.9 us
    all_gather x1, waiting for transfers between devices, local(): lax.all_gather(shrink_coarse, 'rows', axis=1, tiled=True)  22.3 us
    all_gather x1, waiting for transfers between devices, local(): lax.all_gather(expand_coarse, 'rows', axis=0, tiled=True)  17.4 us
    ppermute x4, starting transfers between devices, padded_2(): before = lax.ppermute(last, axis, up)  14.7 us
    unnamed x42, local copies, waits for them, and re-layouts  13.8 us
    ppermute x4, starting transfers between devices, padded_2(): after = lax.ppermute(first, axis, down)  9.42 us
    ppermute x4, waiting for transfers between devices, padded_2(): after = lax.ppermute(first, axis, down)  8.52 us
  transfers between devices with their start and end apart: 14, of which 8 were waited for; matrix products, arithmetic and copies ran while one was open for 21% of the time, Pallas kernels for 0%

commit v1 on v0

--- a/solution.py
+++ b/solution.py
@@ -71,6 +71,34 @@
         "hrcqk,hrckd->hrcqd", probabilities, value_win, preferred_element_type=jnp.float32
     ).astype(jnp.bfloat16)
     return from_windows(mixture, height, breadth)
+
+
+def attend_whole(queries, key_rows, value_rows):
+    scores = jnp.einsum(
+        "hdq,hdk->hqk", queries, key_rows, preferred_element_type=jnp.float32
+    ) * (1.0 / math.sqrt(39))
+    row_max = jnp.max(scores, axis=-1, keepdims=True)
+    exponent = jnp.exp(scores - row_max)
+    probabilities = (exponent / jnp.sum(exponent, axis=-1, keepdims=True)).astype(jnp.bfloat16)
+    return jnp.einsum(
+        "hqk,hdk->hdq", probabilities, value_rows, preferred_element_type=jnp.float32
+    ).astype(jnp.bfloat16)
+
+
+def pack(inproj, outproj, expand, shrink, to_coarse):
+    width = inproj.shape[-1]
+    one = ((0, 0), (0, 1), (0, 0))
+    taps = jnp.pad(to_coarse, ((0, 1), (0, 1), (0, 0))).reshape(5, 2, 40, -1)
+    return jnp.concatenate(
+        [
+            jnp.pad(inproj, one).reshape(-1, width),
+            jnp.pad(outproj.T, ((0, 1), (0, 0))),
+            jnp.pad(expand, ((0, 4), (0, 0))),
+            jnp.pad(shrink.T, ((0, 4), (0, 0))),
+            taps.transpose(0, 2, 1, 3).reshape(-1, width),
+            jnp.zeros((8, width), inproj.dtype),
+        ]
+    )
 
 
 def depthwise(padded, kernel):
@@ -106,6 +134,9 @@
     coarse_ch = coarse_in.shape[2]
     fine_cells = fine_in.shape[3]
     coarse_cells = coarse_in.shape[3]
+    gathered = lax.all_gather(
+        pack(inproj_coarse, outproj_coarse, expand_coarse, shrink_coarse, to_coarse), "rows"
+    )
     fine_rows = fine_cells // (2 * WIN)
     coarse_rows = coarse_cells // WIN
     fine_pic = fine_in.reshape(fine_ch, fine_rows, 2 * WIN)
@@ -140,30 +171,20 @@
     ).astype(jnp.bfloat16)
     coarse_norm = normalize(coarse_pic).reshape(coarse_ch, coarse_cells)
     coarse_proj = jnp.einsum(
-        "tnc,cs->tns",
-        lax.all_gather(inproj_coarse, "rows", axis=1, tiled=True),
-        coarse_norm,
-        preferred_element_type=jnp.float32,
-    ).astype(jnp.bfloat16)
-    coarse_att = attend(
-        coarse_proj[0].reshape(coarse_pic.shape),
-        coarse_proj[1].reshape(coarse_pic.shape),
-        coarse_proj[2].reshape(coarse_pic.shape),
-        HEADS_COARSE,
-    ).reshape(coarse_ch, coarse_cells)
-    section = coarse_att
-    mixture = jnp.dot(
-        lax.all_gather(outproj_coarse, "rows", axis=1, tiled=True),
-        section,
-        preferred_element_type=jnp.float32,
+        "drc,cs->drs", gathered[:, :120], coarse_norm, preferred_element_type=jnp.float32
+    ).astype(jnp.bfloat16)
+    coarse_att = attend_whole(coarse_proj[:, :40], coarse_proj[:, 40:80], coarse_proj[:, 80:120])
+    mixture = jnp.einsum(
+        "drn,drs->ns", gathered[:, 120:160], coarse_att, preferred_element_type=jnp.float32
     )
     coarse_mid = (coarse_pic.reshape(coarse_ch, coarse_cells).astype(jnp.float32) + mixture).astype(
         jnp.bfloat16
     )
     coarse_normed_mid = normalize(coarse_mid)
     coarse_hidden = jax.nn.gelu(
-        jnp.dot(
-            lax.all_gather(expand_coarse, "rows", axis=0, tiled=True),
+        jnp.einsum(
+            "drc,cs->drs",
+            gathered[:, 160:320],
             coarse_normed_mid,
             preferred_element_type=jnp.float32,
         ),
@@ -172,16 +193,15 @@
     coarse_pad = padded_2(
         coarse_hidden.reshape(-1, coarse_rows, WIN), (("rows", 1), ("cols", 2)), 1
     )
+    members = gathered.shape[0]
+    kernel = jnp.pad(depth_coarse.reshape(9, members, -1), ((0, 0), (0, 0), (0, 4)))
     coarse_conv = (
-        jax.nn.gelu(depthwise(coarse_pad, depth_coarse), approximate=False)
-        .astype(jnp.bfloat16)
-        .reshape(-1, coarse_cells)
-    )
-    section = coarse_conv
-    update = jnp.dot(
-        lax.all_gather(shrink_coarse, "rows", axis=1, tiled=True),
-        section,
-        preferred_element_type=jnp.float32,
+        jax.nn.gelu(depthwise(coarse_pad, kernel.reshape(9, -1)), approximate=False)
+        .astype(jnp.bfloat16)
+        .reshape(members, -1, coarse_cells)
+    )
+    update = jnp.einsum(
+        "drn,drs->ns", gathered[:, 320:480], coarse_conv, preferred_element_type=jnp.float32
     )
     coarse_res = (coarse_mid.astype(jnp.float32) + update).astype(jnp.bfloat16)
     upsampled = jnp.dot(to_fine, coarse_res, preferred_element_type=jnp.float32).reshape(
@@ -211,13 +231,13 @@
             col_step % 2,
         ]
         samples.append(sample.reshape(fine_ch, coarse_cells))
-    stacked = jnp.stack(samples)
-    downsampled = jnp.einsum(
-        "gql,glm->qm",
-        lax.all_gather(to_coarse, "rows", axis=1, tiled=True),
-        stacked,
-        preferred_element_type=jnp.float32,
-    ).astype(jnp.bfloat16)
+    stacked = jnp.stack(samples + [jnp.zeros_like(samples[0])]).reshape(5, -1, coarse_cells)
+    taps = gathered[:, 480:680].reshape(members, 5, 40, -1)
+    downsampled = (
+        jnp.einsum("dbrc,bcs->drs", taps, stacked, preferred_element_type=jnp.float32)[:, :39]
+        .astype(jnp.bfloat16)
+        .reshape(coarse_ch, coarse_cells)
+    )
     coarse_out = jax.nn.relu(
         coarse_res.astype(jnp.float32) + downsampled.astype(jnp.float32)
     ).astype(jnp.bfloat16)

time: 220 us -> 155 us (0.70)
  the two profiles are of different devices: /device:TPU:1 before, /device:TPU:33 now
where the time goes in v1:
time: 155 us; the launch traced here: 154 us
  waiting for transfers between devices  60.9 us (39%)
  starting transfers between devices  28.9 us (19%)
  matrix products  21.7 us (14%)
  local copies, waits for them, and re-layouts  16.7 us (11%)
  between operations  14.9 us (10%)
  other arithmetic  10.8 us (7%)
    all_gather x1, waiting for transfers between devices, local(): lax.all_gather(pack(inproj_coarse, outproj_coarse, expand_coarse, shrink_...  38.8 us
    ppermute x4, waiting for transfers between devices, padded_2(): before = lax.ppermute(last, axis, up)  13.4 us
    ppermute x4, starting transfers between devices, padded_2(): after = lax.ppermute(first, axis, down)  12.9 us
    ppermute x4, starting transfers between devices, padded_2(): before = lax.ppermute(last, axis, up)  10.5 us
    convert_element_type x1, other arithmetic, local(): convolved = jax.nn.gelu(depthwise(padded, depth_fine), approximate=False)...  5.73 us
    ppermute x2, waiting for transfers between devices, passed_along(): return lax.ppermute(block, axis, route)  5.62 us
    ppermute x2, starting transfers between devices, passed_along(): return lax.ppermute(block, axis, route)  5.43 us
    dot_general x1, matrix products, local(): jnp.einsum('drc,cs->drs', gathered[:, 160:320], coarse_normed_mid, prefer...  4.44 us
  transfers between devices with their start and end apart: 11, of which 6 were waited for; matrix products, arithmetic and copies ran while one was open for 15% of the time, Pallas kernels for 0%

profile of v1, /device:TPU:33, one launch (start us, length us, event | category | flops | bytes accessed | tf_op | source)
XLA Modules:
  0.0 153.9 jit_solution(8099679514372547341)
XLA Ops:
  7.2 1.0 pad.27
  8.3 1.1 pad.31
  9.3 0.2 copy.69
  9.6 0.2 reshape.206
  10.0 0.9 copy-done.2
  11.1 0.2 fusion.106
  11.3 0.5 fusion.11
  11.9 0.3 reshape_reshape_squeeze.11
  12.3 0.3 reshape_reshape_squeeze.10
  12.7 0.3 reshape_reshape_squeeze.9
  13.1 0.6 fusion.167
  13.7 0.4 convolution_multiply_fusion
  14.1 0.5 convolution_convert_fusion.1
  14.5 0.4 copy.67
  15.0 0.3 reshape_reshape.2
  15.3 0.2 copy-done.7
  15.5 0.4 fusion.172
  15.9 0.2 multiply_reduce_fusion
  16.1 2.7 %fusion.47 = bf16[1248,196]{0,1:T(8,128)(2,1)S(1)} fusion(bf16[1248,312]{0,1:T(8,128)(2,1)S(1)} %copy-done, f32[312,196]{0,1:T(8,128)S(1)} %get-tuple-element.43, f32[196]{0:T(256)S(1)} %add_rsqrt_fusion, f32[196]{0:T(256)S(1)} %broadcast_multiply_fusion), kind=kOutput, calls=%fused_computation.60 | convolution fusion | flops 168718368 | bytes 1514144 | tf_op jit(solution)/shard_map/dot_general | solution.py:160
  18.8 0.2 reshape.202
  19.1 4.5 %collective-permute-start = (bf16[1248,1,14]{0,2,1:T(8,128)(2,1)S(1)}, bf16[1248,1,14]{0,2,1:T(8,128)(2,1)S(1)}, u32[]{:S(2)}, u32[]{:S(2)}) collective-permute-start(bf16[1248,1,14]{0,2,1:T(8,128)(2,1)S(1)} %get-tuple-element.23), channel_id=1, source_target_pairs={{0,32},{32,64},{64,96},{96,128},{128,160},{160,192},{192,224},{224... | collective-permute-start | bytes 104840 | tf_op jit(solution)/shard_map/ppermute | solution.py:23
  23.6 1.9 %collective-permute-start.1 = (bf16[1248,1,14]{0,2,1:T(8,128)(2,1)S(1)}, bf16[1248,1,14]{0,2,1:T(8,128)(2,1)S(1)}, u32[]{:S(2)}, u32[]{:S(2)}) collective-permute-start(bf16[1248,1,14]{0,2,1:T(8,128)(2,1)S(1)} %get-tuple-element.22), channel_id=1, source_target_pairs={{32,0},{64,32},{96,64},{128,96},{160,128},{192,160},{224,192},{256... | collective-permute-start | bytes 104840 | tf_op jit(solution)/shard_map/ppermute | solution.py:24
  25.7 0.1 slice_reduce_fusion.17
  25.9 3.0 %collective-permute-done.1 = bf16[1248,1,14]{0,2,1:T(8,128)(2,1)S(1)} collective-permute-done((bf16[1248,1,14]{0,2,1:T(8,128)(2,1)S(1)}, bf16[1248,1,14]{0,2,1:T(8,128)(2,1)S(1)}, u32[]{:S(2)}, u32[]{:S(2)}) %collective-permute-start.1) | collective-permute-done | bytes 34976 | tf_op jit(solution)/shard_map/ppermute | solution.py:24
  29.0 0.1 fusion.154
  29.1 4.3 %collective-permute-start.3 = (bf16[1248,16,1]{0,2,1:T(2,128)(2,1)S(1)}, bf16[1248,16,1]{0,2,1:T(2,128)(2,1)S(1)}, u32[]{:S(2)}, u32[]{:S(2)}) collective-permute-start(bf16[1248,16,1]{0,2,1:T(2,128)(2,1)S(1)} %get-tuple-element.21), channel_id=1, source_target_pairs={{1,0},{2,1},{3,2},{4,3},{5,4},{6,5},{7,6},{8,7},{9,8},{10,9},{11,1... | collective-permute-start | bytes 119816 | tf_op jit(solution)/shard_map/ppermute | solution.py:24
  33.4 1.9 %collective-permute-start.2 = (bf16[1248,16,1]{0,2,1:T(2,128)(2,1)S(1)}, bf16[1248,16,1]{0,2,1:T(2,128)(2,1)S(1)}, u32[]{:S(2)}, u32[]{:S(2)}) collective-permute-start(bf16[1248,16,1]{0,2,1:T(2,128)(2,1)S(1)} %get-tuple-element.20), channel_id=1, source_target_pairs={{0,1},{1,2},{2,3},{3,4},{4,5},{5,6},{6,7},{7,8},{8,9},{9,10},{10,1... | collective-permute-start | bytes 119816 | tf_op jit(solution)/shard_map/ppermute | solution.py:23
  35.3 0.2 fusion.131
  35.5 6.4 %collective-permute-done.2 = bf16[1248,16,1]{0,2,1:T(2,128)(2,1)S(1)} collective-permute-done((bf16[1248,16,1]{0,2,1:T(2,128)(2,1)S(1)}, bf16[1248,16,1]{0,2,1:T(2,128)(2,1)S(1)}, u32[]{:S(2)}, u32[]{:S(2)}) %collective-permute-start.2) | collective-permute-done | bytes 39968 | tf_op jit(solution)/shard_map/ppermute | solution.py:23
  41.9 5.7 %fusion.23 = bf16[1248,14,14]{0,2,1:T(8,128)(2,1)S(1)} fusion(bf16[1248,14,14]{0,2,1:T(8,128)(2,1)S(1)} %reshape.202, bf16[1248,16,14]{0,2,1:T(8,128)(2,1)S(1)} %constant_dynamic-update-slice_fusion, bf16[1248,16,1]{0,2,1:T(2,128)(2,1)S(1)} %collective-permute-done.3, bf16[1248,16,1]{0,2,1:T(2,128)(2,1)S(1)} %collective-permute-done.2, ...), kind=kLoop, calls=%fused_computation.32 | loop fusion | flops 28129920 | bytes 1732224 | tf_op jit(solution)/shard_map/convert_element_type | solution.py:165
  47.6 0.2 reshape.203
  47.9 0.5 fusion.18
  48.5 3.3 %collective-permute-start.8 = (bf16[312,1,14]{0,2,1:T(8,128)(2,1)S(1)}, bf16[312,1,14]{0,2,1:T(8,128)(2,1)S(1)}, u32[]{:S(2)}, u32[]{:S(2)}) collective-permute-start(bf16[312,1,14]{0,2,1:T(8,128)(2,1)S(1)} %slice.321), channel_id=1, source_target_pairs={{0,32},{32,64},{64,96},{96,128},{128,160},{160,192},{192,224},{224... | collective-permute-start | bytes 26216 | tf_op jit(solution)/shard_map/ppermute | solution.py:32
  51.8 0.2 reshape.207
  52.0 0.6 collective-permute-done.8
  52.7 2.1 %collective-permute-start.9 = (bf16[312,15,1]{0,2,1:T(2,128)(2,1)S(1)}, bf16[312,15,1]{0,2,1:T(2,128)(2,1)S(1)}, u32[]{:S(2)}, u32[]{:S(2)}) collective-permute-start(bf16[312,15,1]{0,2,1:T(2,128)(2,1)S(1)} %slice.322), channel_id=1, source_target_pairs={{0,1},{1,2},{2,3},{3,4},{4,5},{5,6},{6,7},{7,8},{8,9},{9,10},{10,1... | collective-permute-start | bytes 28088 | tf_op jit(solution)/shard_map/ppermute | solution.py:32
  55.5 5.0 %collective-permute-done.9 = bf16[312,15,1]{0,2,1:T(2,128)(2,1)S(1)} collective-permute-done((bf16[312,15,1]{0,2,1:T(2,128)(2,1)S(1)}, bf16[312,15,1]{0,2,1:T(2,128)(2,1)S(1)}, u32[]{:S(2)}, u32[]{:S(2)}) %collective-permute-start.9) | collective-permute-done | bytes 9392 | tf_op jit(solution)/shard_map/ppermute | solution.py:32
  60.7 1.5 slice_reduce_fusion
  62.8 0.5 reshape.216
  63.2 38.8 %all-gather.3.cloned.1.call-done = bf16[11008,624]{1,0:T(8,128)(2,1)} async-done(((bf16[688,624]{1,0:T(8,128)(2,1)}), bf16[11008,624]{1,0:T(8,128)(2,1)}) %all-gather.3.cloned.1.call-update) | async-done | bytes 13738000 | tf_op jit(solution)/shard_map/all_gather | solution.py:137
  102.0 2.8 %fusion.13 = bf16[16,120,49]{1,2,0:T(8,128)(2,1)S(1)} fusion(bf16[16,688,624]{2,1,0:T(8,128)(2,1)} %bitcast.228, bf16[1,1,624,49]{2,3,1,0:T(8,128)(2,1)S(1)} %copy-done.6, f32[49]{0:T(128)S(1)} %add_rsqrt_fusion.3, f32[49]{0:T(128)S(1)} %broadcast_multiply_fusion.3), kind=kOutput, calls=%fused_computation.20 | convolution fusion | flops 117628224 | bytes 2707304 | tf_op jit(solution)/shard_map/drc,cs->drs/dot_general | solution.py:173
  104.8 0.4 fusion.159
  105.2 0.3 convolution_multiply_fusion.1
  105.5 4.4 %slice.320 = bf16[16,200,624]{2,1,0:T(8,128)(2,1)} slice(bf16[16,688,624]{2,1,0:T(8,128)(2,1)} %bitcast.229), slice={[0:16], [480:680], [0:624]} | slice | bytes 7987200 | tf_op jit(solution)/shard_map/slice | solution.py:235
  110.0 2.0 %fusion.164 = (f32[49]{0:T(128)S(1)}, f32[624,49]{0,1:T(8,128)S(1)}) fusion(bf16[16,120,49]{1,2,0:T(8,128)(2,1)S(1)} %fusion.13, f32[16,49]{1,0:T(8,128)S(1)} %fusion.159, f32[16,49,49]{1,2,0:T(8,128)S(1)} %convolution_multiply_fusion.1, bf16[16,688,624]{2,1,0:T(8,128)(2,1)} %bitcast.230, bf16[1,1,624,49]{2,3,1,0:T(8,128)(2,1)S(1)} %copy-done.6), kind=kOutput, calls=%fused_computation.280 | convolution fusion | flops 42510832 | bytes 2168452 | tf_op jit(solution)/shard_map/drn,drs->ns/dot_general | solution.py:177
  111.9 0.2 multiply_reduce_fusion.1
  112.1 4.4 %fusion.65 = bf16[16,160,49]{1,2,0:T(8,128)(2,1)S(1)} fusion(bf16[16,688,624]{2,1,0:T(8,128)(2,1)} %bitcast.231, f32[624,49]{0,1:T(8,128)S(1)} %get-tuple-element.41, f32[49]{0:T(128)S(1)} %add_rsqrt_fusion.2, f32[49]{0:T(128)S(1)} %broadcast_multiply_fusion.2), kind=kOutput, calls=%fused_computation.83 | convolution fusion | flops 164794448 | bytes 3650376 | tf_op jit(solution)/shard_map/drc,cs->drs/dot_general | solution.py:185
  116.7 0.6 reshape.208
  117.3 1.9 %collective-permute-start.4 = (bf16[2560,1,7]{0,2,1:T(8,128)(2,1)S(1)}, bf16[2560,1,7]{0,2,1:T(8,128)(2,1)S(1)}, u32[]{:S(2)}, u32[]{:S(2)}) collective-permute-start(bf16[2560,1,7]{0,2,1:T(8,128)(2,1)S(1)} %get-tuple-element.30), channel_id=1, source_target_pairs={{0,32},{32,64},{64,96},{96,128},{128,160},{160,192},{192,224},{224... | collective-permute-start | bytes 107528 | tf_op jit(solution)/shard_map/ppermute | solution.py:23
  119.2 2.4 %collective-permute-start.5 = (bf16[2560,1,7]{0,2,1:T(8,128)(2,1)S(1)}, bf16[2560,1,7]{0,2,1:T(8,128)(2,1)S(1)}, u32[]{:S(2)}, u32[]{:S(2)}) collective-permute-start(bf16[2560,1,7]{0,2,1:T(8,128)(2,1)S(1)} %get-tuple-element.29), channel_id=1, source_target_pairs={{32,0},{64,32},{96,64},{128,96},{160,128},{192,160},{224,192},{256... | collective-permute-start | bytes 107528 | tf_op jit(solution)/shard_map/ppermute | solution.py:24
  121.6 3.4 %convolution_bitcast_fusion = bf16[16,40,49]{2,1,0:T(8,128)(2,1)S(1)} fusion(bf16[16,5,40,624]{3,2,1,0:T(8,128)(2,1)} %bitcast.221, bf16[5,624,49]{1,0,2:T(8,128)(2,1)S(1)} %reshape.216), kind=kOutput, calls=%fused_computation.21 | convolution fusion | flops 195686400 | bytes 4362080 | tf_op jit(solution)/shard_map/dbrc,bcs->drs/dot_general | solution.py:237
  125.1 0.1 fusion.157
  125.2 4.3 %collective-permute-start.7 = (bf16[2560,9,1]{0,2,1:T(2,128)(2,1)S(1)}, bf16[2560,9,1]{0,2,1:T(2,128)(2,1)S(1)}, u32[]{:S(2)}, u32[]{:S(2)}) collective-permute-start(bf16[2560,9,1]{0,2,1:T(2,128)(2,1)S(1)} %get-tuple-element.28), channel_id=1, source_target_pairs={{1,0},{2,1},{3,2},{4,3},{5,4},{6,5},{7,6},{8,7},{9,8},{10,9},{11,1... | collective-permute-start | bytes 138248 | tf_op jit(solution)/shard_map/ppermute | solution.py:24
  129.5 2.1 %collective-permute-start.6 = (bf16[2560,9,1]{0,2,1:T(2,128)(2,1)S(1)}, bf16[2560,9,1]{0,2,1:T(2,128)(2,1)S(1)}, u32[]{:S(2)}, u32[]{:S(2)}) collective-permute-start(bf16[2560,9,1]{0,2,1:T(2,128)(2,1)S(1)} %get-tuple-element.27), channel_id=1, source_target_pairs={{0,1},{1,2},{2,3},{3,4},{4,5},{5,6},{6,7},{7,8},{8,9},{9,10},{10,1... | collective-permute-start | bytes 138248 | tf_op jit(solution)/shard_map/ppermute | solution.py:23
  131.7 0.3 copy.79
  132.0 0.2 reshape.220
  132.2 7.0 %collective-permute-done.6 = bf16[2560,9,1]{0,2,1:T(2,128)(2,1)S(1)} collective-permute-done((bf16[2560,9,1]{0,2,1:T(2,128)(2,1)S(1)}, bf16[2560,9,1]{0,2,1:T(2,128)(2,1)S(1)}, u32[]{:S(2)}, u32[]{:S(2)}) %collective-permute-start.6) | collective-permute-done | bytes 46112 | tf_op jit(solution)/shard_map/ppermute | solution.py:23
  139.3 2.5 %fusion.82 = bf16[2560,7,7]{0,2,1:T(8,128)(2,1)S(1)} fusion(bf16[2560,7,7]{0,2,1:T(8,128)(2,1)S(1)} %reshape.208, bf16[2560,9,7]{0,2,1:T(8,128)(2,1)S(1)} %constant_dynamic-update-slice_fusion.7, bf16[2560,9,1]{0,2,1:T(2,128)(2,1)S(1)} %collective-permute-done.7, bf16[2560,9,1]{0,2,1:T(2,128)(2,1)S(1)} %collective-permute-done.6, ...), kind=kLoop, calls=%fused_computation.116 | loop fusion | flops 14425600 | bytes 1080320 | tf_op jit(solution)/shard_map/convert_element_type | solution.py:200
  141.8 0.5 reshape.209
  142.3 2.7 %fusion.40 = bf16[624,49]{0,1:T(8,128)(2,1)S(1)} fusion(f32[624,49]{0,1:T(8,128)S(1)} %get-tuple-element.41, bf16[16,688,624]{2,1,0:T(8,128)(2,1)} %bitcast.232, bf16[16,160,49]{1,0,2:T(8,128)(2,1)S(1)} %reshape.209), kind=kOutput, calls=%fused_computation.54 | convolution fusion | flops 156610272 | bytes 3711136 | tf_op jit(solution)/shard_map/drn,drs->ns/dot_general | solution.py:203
  145.1 0.2 convolution_bitcast_fusion.3
  145.5 0.2 reshape.212
  145.7 0.7 fusion.121
  146.4 0.7 fusion.134
  (102 shorter events, 2.6 us)
Async XLA Ops:
  7.2 8.9 %copy-start = (bf16[1248,312]{0,1:T(8,128)(2,1)S(1)}, bf16[1248,312]{0,1:T(8,128)(2,1)}, u32[]{:S(2)}) copy-start(bf16[1248,312]{0,1:T(8,128)(2,1)} %param.18) | copy-start | bytes 2336260
  7.2 2.7 %copy-start.11 = (bf16[624,39]{0,1:T(8,128)(2,1)S(1)}, bf16[624,39]{0,1:T(8,128)(2,1)}, u32[]{:S(2)}) copy-start(bf16[624,39]{0,1:T(8,128)(2,1)} %param.22) | copy-start | bytes 146020
  7.2 94.8 %all-gather.3.cloned.1.call-start = ((), (), s32[]{:S(2)}) async-start(), calls=%async_computation | async-start | bytes 14970880 | tf_op jit(solution)/shard_map/all_gather | solution.py:137
  8.2 1.6 %copy-start.8 = (bf16[156,624]{1,0:T(8,128)(2,1)S(1)}, bf16[156,624]{1,0:T(8,128)(2,1)}, u32[]{:S(2)}) copy-start(bf16[156,624]{1,0:T(8,128)(2,1)} %param.23) | copy-start | bytes 584068
  8.3 1.7 %copy-start.9 = (bf16[624,156]{0,1:T(8,128)(2,1)S(1)}, bf16[624,156]{0,1:T(8,128)(2,1)}, u32[]{:S(2)}) copy-start(bf16[624,156]{0,1:T(8,128)(2,1)} %param.25) | copy-start | bytes 584068
  9.8 1.1 copy-start.1
  9.9 1.4 copy-start.4
  10.0 0.9 copy-start.2
  14.5 0.9 copy-start.7
  18.8 6.7 %copy-start.6 = (bf16[1,1,624,49]{2,3,1,0:T(8,128)(2,1)S(1)}, bf16[1,1,624,49]{2,3,1,0:T(8,128)(2,1)}, u32[]{:S(2)}) copy-start(bf16[1,1,624,49]{2,3,1,0:T(8,128)(2,1)} %param.15) | copy-start | bytes 183460
  18.8 6.9 %copy-start.12 = (f32[9,1248]{1,0:T(8,128)S(1)}, f32[9,1248]{1,0:T(8,128)}, u32[]{:S(2)}) copy-start(f32[9,1248]{1,0:T(8,128)} %param.19) | copy-start | bytes 134788
  19.1 6.8 %collective-permute-start = (bf16[1248,1,14]{0,2,1:T(8,128)(2,1)S(1)}, bf16[1248,1,14]{0,2,1:T(8,128)(2,1)S(1)}, u32[]{:S(2)}, u32[]{:S(2)}) collective-permute-start(bf16[1248,1,14]{0,2,1:T(8,128)(2,1)S(1)} %get-tuple-element.23), channel_id=1, source_target_pairs={{0,32},{32,64},{64,96},{96,128},{128,160},{160,192},{192,224},{224... | collective-permute-start | bytes 104840 | tf_op jit(solution)/shard_map/ppermute | solution.py:23
  23.6 5.3 %collective-permute-start.1 = (bf16[1248,1,14]{0,2,1:T(8,128)(2,1)S(1)}, bf16[1248,1,14]{0,2,1:T(8,128)(2,1)S(1)}, u32[]{:S(2)}, u32[]{:S(2)}) collective-permute-start(bf16[1248,1,14]{0,2,1:T(8,128)(2,1)S(1)} %get-tuple-element.22), channel_id=1, source_target_pairs={{32,0},{64,32},{96,64},{128,96},{160,128},{192,160},{224,192},{256... | collective-permute-start | bytes 104840 | tf_op jit(solution)/shard_map/ppermute | solution.py:24
  29.1 6.4 %collective-permute-start.3 = (bf16[1248,16,1]{0,2,1:T(2,128)(2,1)S(1)}, bf16[1248,16,1]{0,2,1:T(2,128)(2,1)S(1)}, u32[]{:S(2)}, u32[]{:S(2)}) collective-permute-start(bf16[1248,16,1]{0,2,1:T(2,128)(2,1)S(1)} %get-tuple-element.21), channel_id=1, source_target_pairs={{1,0},{2,1},{3,2},{4,3},{5,4},{6,5},{7,6},{8,7},{9,8},{10,9},{11,1... | collective-permute-start | bytes 119816 | tf_op jit(solution)/shard_map/ppermute | solution.py:24
  33.4 8.5 %collective-permute-start.2 = (bf16[1248,16,1]{0,2,1:T(2,128)(2,1)S(1)}, bf16[1248,16,1]{0,2,1:T(2,128)(2,1)S(1)}, u32[]{:S(2)}, u32[]{:S(2)}) collective-permute-start(bf16[1248,16,1]{0,2,1:T(2,128)(2,1)S(1)} %get-tuple-element.20), channel_id=1, source_target_pairs={{0,1},{1,2},{2,3},{3,4},{4,5},{5,6},{6,7},{7,8},{8,9},{9,10},{10,1... | collective-permute-start | bytes 119816 | tf_op jit(solution)/shard_map/ppermute | solution.py:23
  41.9 6.0 %copy-start.3 = (bf16[312,1248]{1,0:T(8,128)(2,1)S(1)}, bf16[312,1248]{1,0:T(8,128)(2,1)}, u32[]{:S(2)}) copy-start(bf16[312,1248]{1,0:T(8,128)(2,1)} %param.20) | copy-start | bytes 2336260
  47.9 3.9 %copy-start.10 = (f32[9,2496]{1,0:T(8,128)S(1)}, f32[9,2496]{1,0:T(8,128)}, u32[]{:S(2)}) copy-start(f32[9,2496]{1,0:T(8,128)} %param.24) | copy-start | bytes 269572
  48.5 4.1 %collective-permute-start.8 = (bf16[312,1,14]{0,2,1:T(8,128)(2,1)S(1)}, bf16[312,1,14]{0,2,1:T(8,128)(2,1)S(1)}, u32[]{:S(2)}, u32[]{:S(2)}) collective-permute-start(bf16[312,1,14]{0,2,1:T(8,128)(2,1)S(1)} %slice.321), channel_id=1, source_target_pairs={{0,32},{32,64},{64,96},{96,128},{128,160},{160,192},{192,224},{224... | collective-permute-start | bytes 26216 | tf_op jit(solution)/shard_map/ppermute | solution.py:32
  52.7 7.9 %collective-permute-start.9 = (bf16[312,15,1]{0,2,1:T(2,128)(2,1)S(1)}, bf16[312,15,1]{0,2,1:T(2,128)(2,1)S(1)}, u32[]{:S(2)}, u32[]{:S(2)}) collective-permute-start(bf16[312,15,1]{0,2,1:T(2,128)(2,1)S(1)} %slice.322), channel_id=1, source_target_pairs={{0,1},{1,2},{2,3},{3,4},{4,5},{5,6},{6,7},{7,8},{8,9},{9,10},{10,1... | collective-permute-start | bytes 28088 | tf_op jit(solution)/shard_map/ppermute | solution.py:32
  117.3 7.7 %collective-permute-start.4 = (bf16[2560,1,7]{0,2,1:T(8,128)(2,1)S(1)}, bf16[2560,1,7]{0,2,1:T(8,128)(2,1)S(1)}, u32[]{:S(2)}, u32[]{:S(2)}) collective-permute-start(bf16[2560,1,7]{0,2,1:T(8,128)(2,1)S(1)} %get-tuple-element.30), channel_id=1, source_target_pairs={{0,32},{32,64},{64,96},{96,128},{128,160},{160,192},{192,224},{224... | collective-permute-start | bytes 107528 | tf_op jit(solution)/shard_map/ppermute | solution.py:23
  119.2 5.9 %collective-permute-start.5 = (bf16[2560,1,7]{0,2,1:T(8,128)(2,1)S(1)}, bf16[2560,1,7]{0,2,1:T(8,128)(2,1)S(1)}, u32[]{:S(2)}, u32[]{:S(2)}) collective-permute-start(bf16[2560,1,7]{0,2,1:T(8,128)(2,1)S(1)} %get-tuple-element.29), channel_id=1, source_target_pairs={{32,0},{64,32},{96,64},{128,96},{160,128},{192,160},{224,192},{256... | collective-permute-start | bytes 107528 | tf_op jit(solution)/shard_map/ppermute | solution.py:24
  125.2 7.0 %collective-permute-start.7 = (bf16[2560,9,1]{0,2,1:T(2,128)(2,1)S(1)}, bf16[2560,9,1]{0,2,1:T(2,128)(2,1)S(1)}, u32[]{:S(2)}, u32[]{:S(2)}) collective-permute-start(bf16[2560,9,1]{0,2,1:T(2,128)(2,1)S(1)} %get-tuple-element.28), channel_id=1, source_target_pairs={{1,0},{2,1},{3,2},{4,3},{5,4},{6,5},{7,6},{8,7},{9,8},{10,9},{11,1... | collective-permute-start | bytes 138248 | tf_op jit(solution)/shard_map/ppermute | solution.py:24
  129.5 9.8 %collective-permute-start.6 = (bf16[2560,9,1]{0,2,1:T(2,128)(2,1)S(1)}, bf16[2560,9,1]{0,2,1:T(2,128)(2,1)S(1)}, u32[]{:S(2)}, u32[]{:S(2)}) collective-permute-start(bf16[2560,9,1]{0,2,1:T(2,128)(2,1)S(1)} %get-tuple-element.27), channel_id=1, source_target_pairs={{0,1},{1,2},{2,3},{3,4},{4,5},{5,6},{6,7},{7,8},{8,9},{9,10},{10,1... | collective-permute-start | bytes 138248 | tf_op jit(solution)/shard_map/ppermute | solution.py:23
  142.3 2.7 %copy-start.5 = (bf16[312,624]{1,0:T(8,128)(2,1)S(1)}, bf16[312,624]{1,0:T(8,128)(2,1)}, u32[]{:S(2)}) copy-start(bf16[312,624]{1,0:T(8,128)(2,1)} %param.26) | copy-start | bytes 1168132
Sparse Core Ops, SparseCore 0:
  11.1 90.8 all-gather.2

commit v2 on v1

--- a/solution.py
+++ b/solution.py
@@ -3,6 +3,9 @@
 import jax
 import jax.numpy as jnp
 from jax import lax
+import numpy as np
+from jax.experimental import pallas as pl
+from jax.experimental.pallas import tpu as pltpu
 from jax.sharding import PartitionSpec as P
 
 HEADS_FINE = 8
@@ -73,32 +76,284 @@
     return from_windows(mixture, height, breadth)
 
 
-def attend_whole(queries, key_rows, value_rows):
-    scores = jnp.einsum(
-        "hdq,hdk->hqk", queries, key_rows, preferred_element_type=jnp.float32
-    ) * (1.0 / math.sqrt(39))
-    row_max = jnp.max(scores, axis=-1, keepdims=True)
-    exponent = jnp.exp(scores - row_max)
-    probabilities = (exponent / jnp.sum(exponent, axis=-1, keepdims=True)).astype(jnp.bfloat16)
-    return jnp.einsum(
-        "hqk,hdk->hdq", probabilities, value_rows, preferred_element_type=jnp.float32
-    ).astype(jnp.bfloat16)
+CELLS = WIN * WIN
+RING = WIN + 2
+HEAD_ROWS = 40
+BLOCK_ROWS = 4 * HEAD_ROWS
+TAP_ROWS = 5 * HEAD_ROWS + 8
+SHARD_ROWS = 3 * BLOCK_ROWS + TAP_ROWS
+SHARDS = 16
+KEYS = 448
+QUERIES = 96
 
 
 def pack(inproj, outproj, expand, shrink, to_coarse):
     width = inproj.shape[-1]
-    one = ((0, 0), (0, 1), (0, 0))
-    taps = jnp.pad(to_coarse, ((0, 1), (0, 1), (0, 0))).reshape(5, 2, 40, -1)
+    heads = jnp.concatenate([outproj.T[None], inproj[2:], inproj[:2]])
+    taps = jnp.pad(to_coarse, ((0, 1), (0, 1), (0, 0))).reshape(5, 2, HEAD_ROWS, -1)
     return jnp.concatenate(
         [
-            jnp.pad(inproj, one).reshape(-1, width),
-            jnp.pad(outproj.T, ((0, 1), (0, 0))),
+            jnp.pad(heads, ((0, 0), (0, 1), (0, 0))).reshape(-1, width),
             jnp.pad(expand, ((0, 4), (0, 0))),
             jnp.pad(shrink.T, ((0, 4), (0, 0))),
             taps.transpose(0, 2, 1, 3).reshape(-1, width),
             jnp.zeros((8, width), inproj.dtype),
         ]
     )
+
+
+def all_shards(mine):
+    size = lax.axis_size("rows")
+    swap = [(i, i ^ 1) for i in range(size)]
+    ring = [(i, (i + (2 if i % 2 == 0 else -2)) % size) for i in range(size)]
+    held = jnp.stack([mine, lax.ppermute(mine, "rows", swap)])
+    pairs = [held]
+    for _ in range(3):
+        held = lax.ppermute(held, "rows", ring)
+        pairs += [held, lax.ppermute(held, "rows", swap)]
+    last = lax.ppermute(held[0], "rows", ring)
+    singles = [last, lax.ppermute(last, "rows", swap)]
+    place = lax.axis_index("rows")
+    chip, core = place // 2, place % 2
+    step = 1 - 2 * core
+    owners = [2 * chip + core, 2 * chip + 1 - core]
+    for k in (1, 2, 3):
+        for sign in (-1, 1):
+            away = 2 * ((chip + sign * step * k) % (size // 2))
+            first = core if sign < 0 else 1 - core
+            owners += [away + first, away + 1 - first]
+    across = 2 * ((chip + 4) % (size // 2))
+    owners += [across + core, across + 1 - core]
+    return pairs, singles, jnp.stack(owners).astype(jnp.int32)
+
+
+def tables():
+    pick = np.zeros((QUERIES, KEYS), np.float32)
+    bias = np.full((QUERIES, KEYS), -1e30, np.float32)
+    centre = np.zeros((64, QUERIES), np.float32)
+    for row in range(RING):
+        for col in range(RING):
+            down = 1 if row == 0 else 2 if row == RING - 1 else 0
+            side = 1 if col == 0 else 2 if col == RING - 1 else 0
+            window = 3 * side + down
+            cell = (row - 1) % WIN * WIN + (col - 1) % WIN
+            query = row * RING + col
+            pick[query, window * CELLS + cell] = 1
+            bias[query, window * CELLS : (window + 1) * CELLS] = 0
+            if window == 0:
+                centre[(row - 1) * 8 + col - 1, query] = 1
+    bias[RING * RING :, :CELLS] = 0
+    repeat = np.zeros((4 * CELLS, 64), np.float32)
+    compact = np.zeros((CELLS, 64), np.float32)
+    for row in range(2 * WIN):
+        for col in range(2 * WIN):
+            repeat[row * 2 * WIN + col, row // 2 * 8 + col // 2] = 1
+    for row in range(WIN):
+        for col in range(WIN):
+            compact[row * WIN + col, row * 8 + col] = 1
+    order = np.zeros((SHARDS * HEAD_ROWS, SHARDS * 39), np.float32)
+    for shard in range(SHARDS):
+        for row in range(39):
+            order[shard * HEAD_ROWS + row, shard * 39 + row] = 1
+    half = jnp.bfloat16
+    return (
+        jnp.asarray(bias),
+        *(jnp.asarray(t).astype(half) for t in (pick, centre, repeat, compact, order)),
+    )
+
+
+def gelu(values):
+    return values * (lax.erf(values * math.sqrt(0.5)) + 1.0) * 0.5
+
+
+def norm_rows(values):
+    center = jnp.mean(values, axis=1, keepdims=True)
+    away = values - center
+    spread = jnp.mean(away * away, axis=1, keepdims=True)
+    return (away * lax.rsqrt(spread + EPSILON)).astype(jnp.bfloat16)
+
+
+def nn(left, right):
+    return lax.dot_general(
+        left, right, (((1,), (0,)), ((), ())), preferred_element_type=jnp.float32
+    )
+
+
+def nt(left, right):
+    return lax.dot_general(
+        left, right, (((1,), (1,)), ((), ())), preferred_element_type=jnp.float32
+    )
+
+
+def coarse_kernel(
+    owner_ref,
+    edge_ref,
+    *refs,
+):
+    sources, rest = refs[:9], refs[9:]
+    (
+        tiles_ref,
+        depth_ref,
+        taps_in_ref,
+        fine_ref,
+        to_fine_ref,
+        bias_ref,
+        pick_ref,
+        centre_ref,
+        repeat_ref,
+        compact_ref,
+        order_ref,
+        fine_out_ref,
+        coarse_out_ref,
+        heads_ref,
+        expand_ref,
+        shrink_ref,
+        taps_ref,
+        proj_ref,
+        hidden_ref,
+        conv_ref,
+        down_ref,
+        sems,
+    ) = rest
+    slots = []
+    for index, source in enumerate(sources):
+        if index < 7:
+            slots += [source.at[0], source.at[1]]
+        else:
+            slots += [source]
+    spans = (
+        (heads_ref, 0, BLOCK_ROWS),
+        (expand_ref, BLOCK_ROWS, BLOCK_ROWS),
+        (shrink_ref, 2 * BLOCK_ROWS, BLOCK_ROWS),
+        (taps_ref, 3 * BLOCK_ROWS, TAP_ROWS),
+    )
+    copies = []
+    for part, (target, first, count) in enumerate(spans):
+        copies.append(
+            [
+                pltpu.make_async_copy(
+                    slot.at[pl.ds(first, count)], target.at[owner_ref[place]], sems.at[part, place]
+                )
+                for place, slot in enumerate(slots)
+            ]
+        )
+        for copy in copies[-1]:
+            copy.start()
+
+    def arrive(part):
+        for copy in copies[part]:
+            copy.wait()
+
+    width = tiles_ref.shape[1]
+    tiles = tiles_ref[...]
+    normed = norm_rows(tiles.astype(jnp.float32))
+    pick = pick_ref[...]
+    arrive(0)
+    heads = heads_ref[...].reshape(SHARDS * BLOCK_ROWS, width)
+    proj_ref[...] = nt(heads, normed).reshape(SHARDS, BLOCK_ROWS, KEYS)
+    mixed = nn(pick, tiles)
+    for head in range(SHARDS):
+        values = proj_ref[head, HEAD_ROWS : 2 * HEAD_ROWS].astype(jnp.bfloat16)
+        queries = proj_ref[head, 2 * HEAD_ROWS : 3 * HEAD_ROWS].astype(jnp.bfloat16)
+        keys = proj_ref[head, 3 * HEAD_ROWS :].astype(jnp.bfloat16)
+        chosen = nt(pick, queries).astype(jnp.bfloat16)
+        scores = nn(chosen, keys) * (1.0 / math.sqrt(39)) + bias_ref[...]
+        exponent = jnp.exp(scores - jnp.max(scores, axis=1, keepdims=True))
+        total = jnp.sum(exponent, axis=1, keepdims=True)
+        probabilities = (exponent * (1.0 / total)).astype(jnp.bfloat16)
+        attended = nt(probabilities, values).astype(jnp.bfloat16)
+        mixed += nn(attended, heads_ref[head][:HEAD_ROWS])
+    middle = mixed.astype(jnp.bfloat16)
+    normed_mid = norm_rows(middle.astype(jnp.float32))
+    query = lax.broadcasted_iota(jnp.int32, (QUERIES, 128), 0)
+    column = query % RING
+    outside = (
+        ((query < RING) & (edge_ref[0] == 0))
+        | ((query >= RING * (RING - 1)) & (edge_ref[1] == 0))
+        | ((column == 0) & (edge_ref[2] == 0))
+        | ((column == RING - 1) & (edge_ref[3] == 0))
+    )
+    inside = jnp.where(outside, 0.0, 1.0)[:, :1]
+    arrive(1)
+    conv_ref[CELLS // WIN * 8 :, :] = jnp.zeros((8, conv_ref.shape[1]), jnp.float32)
+    chunk = 512
+    for first in range(0, SHARDS * BLOCK_ROWS, chunk):
+        span = pl.ds(first, chunk)
+        rows = expand_ref[...].reshape(SHARDS * BLOCK_ROWS, width)[first : first + chunk]
+        hidden = gelu(nt(normed_mid, rows)) * inside
+        hidden_ref[:, span] = hidden.astype(jnp.bfloat16).astype(jnp.float32)
+        for row in range(WIN):
+            total = jnp.zeros((8, chunk), jnp.float32)
+            for tap in range(9):
+                down, side = divmod(tap, 3)
+                window = hidden_ref[pl.ds((row + down) * RING + side, 8), span]
+                total += depth_ref[tap : tap + 1, span] * window
+            conv_ref[row * 8 : row * 8 + 8, span] = gelu(total)
+    arrive(2)
+    shrink = shrink_ref[...].reshape(SHARDS * BLOCK_ROWS, width)
+    update = nn(conv_ref[...].astype(jnp.bfloat16), shrink)
+    result = (nn(centre_ref[...], middle) + update).astype(jnp.bfloat16)
+    spread = nn(repeat_ref[...], result).astype(jnp.bfloat16)
+    upsampled = nt(spread, to_fine_ref[...])
+    fine_out_ref[...] = jnp.maximum(
+        fine_ref[...].astype(jnp.float32) + upsampled, 0.0
+    ).astype(jnp.bfloat16)
+    arrive(3)
+    samples = taps_in_ref[...]
+    for shard in range(SHARDS):
+        four = nt(taps_ref[shard], samples[: 4 * 64])
+        fifth = nt(taps_ref[shard][4 * HEAD_ROWS :], samples[4 * 64 :])
+        total = fifth[:HEAD_ROWS]
+        for block in range(4):
+            rows = slice(block * HEAD_ROWS, (block + 1) * HEAD_ROWS)
+            total += four[rows, block * 64 : (block + 1) * 64]
+        down_ref[shard * HEAD_ROWS : (shard + 1) * HEAD_ROWS, :64] = total
+    turned = down_ref[...].T.astype(jnp.bfloat16)
+    downsampled = nn(turned, order_ref[...])[:CELLS]
+    coarse_out_ref[...] = jnp.maximum(
+        nn(compact_ref[...], result) + downsampled, 0.0
+    ).astype(jnp.bfloat16)
+
+
+def coarse_tail(sources, owners, edges, tiles, depth, samples, fine_res, to_fine):
+    width = tiles.shape[1]
+    fine_cells, fine_ch = fine_res.shape
+    operands = (tiles, depth, samples, fine_res, to_fine, *tables())
+    smem, vmem, anywhere = (
+        pl.BlockSpec(memory_space=space) for space in (pltpu.SMEM, pltpu.VMEM, pl.ANY)
+    )
+    return pl.pallas_call(
+        coarse_kernel,
+        out_shape=(
+            jax.ShapeDtypeStruct((fine_cells, fine_ch), jnp.bfloat16),
+            jax.ShapeDtypeStruct((CELLS, width), jnp.bfloat16),
+        ),
+        in_specs=[smem, smem] + [anywhere] * len(sources) + [vmem] * len(operands),
+        out_specs=(vmem, vmem),
+        scratch_shapes=[
+            pltpu.VMEM((SHARDS, BLOCK_ROWS, width), jnp.bfloat16),
+            pltpu.VMEM((SHARDS, BLOCK_ROWS, width), jnp.bfloat16),
+            pltpu.VMEM((SHARDS, BLOCK_ROWS, width), jnp.bfloat16),
+            pltpu.VMEM((SHARDS, TAP_ROWS, width), jnp.bfloat16),
+            pltpu.VMEM((SHARDS, BLOCK_ROWS, KEYS), jnp.float32),
+            pltpu.VMEM((QUERIES, SHARDS * BLOCK_ROWS), jnp.float32),
+            pltpu.VMEM((64, SHARDS * BLOCK_ROWS), jnp.float32),
+            pltpu.VMEM((SHARDS * HEAD_ROWS, 128), jnp.float32),
+            pltpu.SemaphoreType.DMA((4, SHARDS)),
+        ],
+        compiler_params=pltpu.CompilerParams(vmem_limit_bytes=48 * 1024 * 1024),
+    )(owners, edges, *sources, *operands)
+
+
+def around(tile):
+    for axis in ("rows", "cols"):
+        size = lax.axis_size(axis)
+        up = [(i, i + 1) for i in range(size - 1)]
+        down = [(j, i) for i, j in up]
+        tile = jnp.concatenate(
+            [tile, lax.ppermute(tile, axis, up), lax.ppermute(tile, axis, down)]
+        )
+    return jnp.pad(tile, ((0, KEYS - tile.shape[0]), (0, 0)))
 
 
 def depthwise(padded, kernel):
@@ -134,13 +389,13 @@
     coarse_ch = coarse_in.shape[2]
     fine_cells = fine_in.shape[3]
     coarse_cells = coarse_in.shape[3]
-    gathered = lax.all_gather(
-        pack(inproj_coarse, outproj_coarse, expand_coarse, shrink_coarse, to_coarse), "rows"
-    )
+    pairs, singles, owners = all_shards(
+        pack(inproj_coarse, outproj_coarse, expand_coarse, shrink_coarse, to_coarse)
+    )
+    tiles = around(coarse_in.reshape(coarse_ch, coarse_cells).T)
     fine_rows = fine_cells // (2 * WIN)
     coarse_rows = coarse_cells // WIN
     fine_pic = fine_in.reshape(fine_ch, fine_rows, 2 * WIN)
-    coarse_pic = coarse_in.reshape(coarse_ch, coarse_rows, WIN)
     normed = normalize(fine_pic).reshape(fine_ch, fine_cells)
     projected = jnp.einsum(
         "tnc,cs->tns", inproj_fine, normed, preferred_element_type=jnp.float32
@@ -169,51 +424,7 @@
         middle.astype(jnp.float32)
         + jnp.dot(shrink_fine, convolved, preferred_element_type=jnp.float32)
     ).astype(jnp.bfloat16)
-    coarse_norm = normalize(coarse_pic).reshape(coarse_ch, coarse_cells)
-    coarse_proj = jnp.einsum(
-        "drc,cs->drs", gathered[:, :120], coarse_norm, preferred_element_type=jnp.float32
-    ).astype(jnp.bfloat16)
-    coarse_att = attend_whole(coarse_proj[:, :40], coarse_proj[:, 40:80], coarse_proj[:, 80:120])
-    mixture = jnp.einsum(
-        "drn,drs->ns", gathered[:, 120:160], coarse_att, preferred_element_type=jnp.float32
-    )
-    coarse_mid = (coarse_pic.reshape(coarse_ch, coarse_cells).astype(jnp.float32) + mixture).astype(
-        jnp.bfloat16
-    )
-    coarse_normed_mid = normalize(coarse_mid)
-    coarse_hidden = jax.nn.gelu(
-        jnp.einsum(
-            "drc,cs->drs",
-            gathered[:, 160:320],
-            coarse_normed_mid,
-            preferred_element_type=jnp.float32,
-        ),
-        approximate=False,
-    ).astype(jnp.bfloat16)
-    coarse_pad = padded_2(
-        coarse_hidden.reshape(-1, coarse_rows, WIN), (("rows", 1), ("cols", 2)), 1
-    )
-    members = gathered.shape[0]
-    kernel = jnp.pad(depth_coarse.reshape(9, members, -1), ((0, 0), (0, 0), (0, 4)))
-    coarse_conv = (
-        jax.nn.gelu(depthwise(coarse_pad, kernel.reshape(9, -1)), approximate=False)
-        .astype(jnp.bfloat16)
-        .reshape(members, -1, coarse_cells)
-    )
-    update = jnp.einsum(
-        "drn,drs->ns", gathered[:, 320:480], coarse_conv, preferred_element_type=jnp.float32
-    )
-    coarse_res = (coarse_mid.astype(jnp.float32) + update).astype(jnp.bfloat16)
-    upsampled = jnp.dot(to_fine, coarse_res, preferred_element_type=jnp.float32).reshape(
-        fine_ch, coarse_rows, WIN
-    )
-    upsampled = jnp.repeat(jnp.repeat(upsampled, 2, axis=1), 2, axis=2)
     fine_grid = fine_res.reshape(fine_ch, fine_rows, 2 * WIN)
-    fine_out = (
-        jax.nn.relu(fine_grid.astype(jnp.float32) + upsampled)
-        .astype(jnp.bfloat16)
-        .reshape(fine_in.shape)
-    )
     above_row = passed_along(fine_grid[:, -1:, :], "rows", 1)
     extended = jnp.concatenate([above_row, fine_grid], axis=1)
     beside = passed_along(extended[:, :, -1:], "cols", 1)
@@ -232,16 +443,23 @@
         ]
         samples.append(sample.reshape(fine_ch, coarse_cells))
     stacked = jnp.stack(samples + [jnp.zeros_like(samples[0])]).reshape(5, -1, coarse_cells)
-    taps = gathered[:, 480:680].reshape(members, 5, 40, -1)
-    downsampled = (
-        jnp.einsum("dbrc,bcs->drs", taps, stacked, preferred_element_type=jnp.float32)[:, :39]
-        .astype(jnp.bfloat16)
-        .reshape(coarse_ch, coarse_cells)
-    )
-    coarse_out = jax.nn.relu(
-        coarse_res.astype(jnp.float32) + downsampled.astype(jnp.float32)
-    ).astype(jnp.bfloat16)
-    return (fine_out, coarse_out.reshape(coarse_in.shape))
+    stacked = jnp.pad(stacked.transpose(0, 2, 1), ((0, 0), (0, 64 - coarse_cells), (0, 0)))
+    depth = jnp.pad(depth_coarse.reshape(9, SHARDS, -1), ((0, 0), (0, 0), (0, 4)))
+    row, col = lax.axis_index("rows"), lax.axis_index("cols")
+    edges = jnp.stack(
+        [row > 0, row < lax.axis_size("rows") - 1, col > 0, col < lax.axis_size("cols") - 1]
+    ).astype(jnp.int32)
+    fine_out, coarse_out = coarse_tail(
+        pairs + singles,
+        owners,
+        edges,
+        tiles,
+        depth.reshape(9, -1),
+        stacked.reshape(5 * 64, -1),
+        fine_res.reshape(fine_ch, fine_cells).T,
+        to_fine,
+    )
+    return (fine_out.T.reshape(fine_in.shape), coarse_out.T.reshape(coarse_in.shape))
 
 
 def solution(mesh):

time: 155 us -> 185 us (1.19)
  the two profiles are of different devices: /device:TPU:33 before, /device:TPU:96 now
where the time goes in v2:
time: 185 us; the launch traced here: 183 us
  starting transfers between devices  59.6 us (32%)
  local copies, waits for them, and re-layouts  40.2 us (22%)
  waiting for transfers between devices  36.9 us (20%)
  Pallas kernels  23.7 us (13%)
  other arithmetic  11.2 us (6%)
  matrix products  9.39 us (5%)
    pallas_call x1, Pallas kernels, coarse_tail(): pl.pallas_call(coarse_kernel, out_shape=(jax.ShapeDtypeStruct((fine_cells...  23.7 us
    ppermute x3, waiting for transfers between devices, all_shards(): held = lax.ppermute(held, 'rows', ring)  19.4 us
    ppermute x2, starting transfers between devices, padded_2(): after = lax.ppermute(first, axis, down)  14 us
    unnamed x63, local copies, waits for them, and re-layouts  11.8 us
    ppermute x2, waiting for transfers between devices, around(): lax.ppermute(tile, axis, up)  11 us
    ppermute x3, starting transfers between devices, all_shards(): held = lax.ppermute(held, 'rows', ring)  10.6 us
    concatenate x1, local copies, waits for them, and re-layouts, around(): jnp.concatenate([tile, lax.ppermute(tile, axis, up), lax.ppermute(tile, a...  7.88 us
    ppermute x3, starting transfers between devices, all_shards(): pairs += [held, lax.ppermute(held, 'rows', swap)]  7.6 us
  transfers between devices with their start and end apart: 19, of which 7 were waited for; matrix products, arithmetic and copies ran while one was open for 31% of the time, Pallas kernels for 0%

profile of v2, /device:TPU:96, one launch (start us, length us, event | category | flops | bytes accessed | tf_op | source)
XLA Modules:
  0.0 182.6 jit_solution(18323075507256286332)
XLA Ops:
  0.7 2.1 %collective-permute-start.10 = (bf16[49,624]{1,0:T(8,128)(2,1)}, bf16[49,624]{1,0:T(8,128)(2,1)}, u32[]{:S(2)}, u32[]{:S(2)}) collective-permute-start(bf16[49,624]{1,0:T(8,128)(2,1)} %bitcast.209), channel_id=1, source_target_pairs={{32,0},{64,32},{96,64},{128,96},{160,128},{192,160},{224,192},{256... | collective-permute-start | bytes 183464 | tf_op jit(solution)/shard_map/ppermute | solution.py:354
  2.7 1.0 pad.34
  4.3 0.7 constant_dynamic-update-slice_fusion.2
  5.0 0.7 pad_dynamic-update-slice_fusion.1
  5.7 0.7 pad_dynamic-update-slice_fusion
  6.5 0.7 constant_dynamic-update-slice_fusion.1
  7.2 0.6 constant_dynamic-update-slice_fusion
  7.8 2.4 %collective-permute-start = (bf16[688,624]{1,0:T(8,128)(2,1)}, bf16[688,624]{1,0:T(8,128)(2,1)}, u32[]{:S(2)}, u32[]{:S(2)}) collective-permute-start(bf16[688,624]{1,0:T(8,128)(2,1)} %constant_dynamic-update-slice_fusion), channel_id=1, source_target_pairs={{0,32},{32,0},{64,96},{96,64},{128,160},{160,128},{192,224},{224,1... | collective-permute-start | bytes 2575880 | tf_op jit(solution)/shard_map/ppermute | solution.py:109
  12.9 1.3 convolution_multiply_fusion
  14.2 1.7 pad_maximum_fusion.refs_0_
  15.9 4.3 %collective-permute-start.1 = (bf16[2,688,624]{2,1,0:T(8,128)(2,1)S(1)}, bf16[2,688,624]{2,1,0:T(8,128)(2,1)}, u32[]{:S(2)}, u32[]{:S(2)}) collective-permute-start(bf16[2,688,624]{2,1,0:T(8,128)(2,1)S(1)} %pad_maximum_fusion.refs_0_), channel_id=1, source_target_pairs={{0,64},{32,480},{64,128},{96,32},{128,192},{160,96},{192,256},{224... | collective-permute-start | bytes 5151752 | tf_op jit(solution)/shard_map/ppermute | solution.py:112
  20.2 1.9 %convolution_convert_fusion.1 = bf16[8,2,2,49,39]{3,4,2,1,0:T(8,128)(2,1)S(1)} fusion(bf16[8,2,2,49,39]{4,0,3,2,1:T(8,128)(2,1)S(1)} %bitcast.208, f32[8,2,2,49]{3,2,1,0:T(2,128)S(1)} %fusion.77, f32[8,2,2,49,49]{3,4,2,1,0:T(8,128)} %convolution_multiply_fusion), kind=kOutput, calls=%fused_computation.8 | convolution fusion | flops 6286160 | bytes 558208 | tf_op jit(solution)/shard_map/hrcqk,hrckd->hrcqd/dot_general | solution.py:73
  22.9 1.3 fusion.82
  24.4 3.2 %fusion.21 = bf16[1248,196]{0,1:T(8,128)(2,1)} fusion(bf16[1248,312]{0,1:T(8,128)(2,1)S(1)} %copy-done, f32[312,196]{0,1:T(8,128)S(1)} %get-tuple-element.32, f32[196]{0:T(256)S(1)} %add_rsqrt_fusion, f32[196]{0:T(256)S(1)} %broadcast_multiply_fusion), kind=kOutput, calls=%fused_computation.38 | convolution fusion | flops 168718368 | bytes 1514144 | tf_op jit(solution)/shard_map/dot_general | solution.py:415
  27.7 1.2 reshape.120
  28.9 11.4 %collective-permute-done.1.refs_1_ = bf16[2,688,624]{2,1,0:T(8,128)(2,1)} collective-permute-done((bf16[2,688,624]{2,1,0:T(8,128)(2,1)S(1)}, bf16[2,688,624]{2,1,0:T(8,128)(2,1)}, u32[]{:S(2)}, u32[]{:S(2)}) %collective-permute-start.1) | collective-permute-done | bytes 1717280 | tf_op jit(solution)/shard_map/ppermute | solution.py:112
  40.4 4.4 %collective-permute-start.3 = (bf16[2,688,624]{2,1,0:T(8,128)(2,1)}, bf16[2,688,624]{2,1,0:T(8,128)(2,1)}, u32[]{:S(2)}, u32[]{:S(2)}) collective-permute-start(bf16[2,688,624]{2,1,0:T(8,128)(2,1)} %collective-permute-done.1.refs_1_), channel_id=1, source_target_pairs={{0,64},{32,480},{64,128},{96,32},{128,192},{160,96},{192,256},{224... | collective-permute-start | bytes 5151752 | tf_op jit(solution)/shard_map/ppermute | solution.py:112
  44.8 8.2 %collective-permute-start.14 = (bf16[1248,1,14]{0,2,1:T(8,128)(2,1)S(1)}, bf16[1248,1,14]{0,2,1:T(8,128)(2,1)S(1)}, u32[]{:S(2)}, u32[]{:S(2)}) collective-permute-start(bf16[1248,1,14]{0,2,1:T(8,128)(2,1)S(1)} %get-tuple-element.26), channel_id=1, source_target_pairs={{32,0},{64,32},{96,64},{128,96},{160,128},{192,160},{224,192},{256... | collective-permute-start | bytes 104840 | tf_op jit(solution)/shard_map/ppermute | solution.py:27
  53.0 1.9 %collective-permute-start.13 = (bf16[1248,1,14]{0,2,1:T(8,128)(2,1)S(1)}, bf16[1248,1,14]{0,2,1:T(8,128)(2,1)S(1)}, u32[]{:S(2)}, u32[]{:S(2)}) collective-permute-start(bf16[1248,1,14]{0,2,1:T(8,128)(2,1)S(1)} %get-tuple-element.27), channel_id=1, source_target_pairs={{0,32},{32,64},{64,96},{96,128},{128,160},{160,192},{192,224},{224... | collective-permute-start | bytes 104840 | tf_op jit(solution)/shard_map/ppermute | solution.py:26
  55.0 1.4 slice_reduce_fusion.17
  56.3 2.5 %collective-permute-done.13 = bf16[1248,1,14]{0,2,1:T(8,128)(2,1)S(1)} collective-permute-done((bf16[1248,1,14]{0,2,1:T(8,128)(2,1)S(1)}, bf16[1248,1,14]{0,2,1:T(8,128)(2,1)S(1)}, u32[]{:S(2)}, u32[]{:S(2)}) %collective-permute-start.13) | collective-permute-done | bytes 34976 | tf_op jit(solution)/shard_map/ppermute | solution.py:26
  59.1 3.4 %collective-permute-start.15 = (bf16[1248,16,1]{0,2,1:T(2,128)(2,1)S(1)}, bf16[1248,16,1]{0,2,1:T(2,128)(2,1)S(1)}, u32[]{:S(2)}, u32[]{:S(2)}) collective-permute-start(bf16[1248,16,1]{0,2,1:T(2,128)(2,1)S(1)} %get-tuple-element.24), channel_id=1, source_target_pairs={{0,1},{1,2},{2,3},{3,4},{4,5},{5,6},{6,7},{7,8},{8,9},{9,10},{10,1... | collective-permute-start | bytes 119816 | tf_op jit(solution)/shard_map/ppermute | solution.py:26
  62.5 5.8 %collective-permute-start.16 = (bf16[1248,16,1]{0,2,1:T(2,128)(2,1)S(1)}, bf16[1248,16,1]{0,2,1:T(2,128)(2,1)S(1)}, u32[]{:S(2)}, u32[]{:S(2)}) collective-permute-start(bf16[1248,16,1]{0,2,1:T(2,128)(2,1)S(1)} %get-tuple-element.25), channel_id=1, source_target_pairs={{1,0},{2,1},{3,2},{4,3},{5,4},{6,5},{7,6},{8,7},{9,8},{10,9},{11,1... | collective-permute-start | bytes 119816 | tf_op jit(solution)/shard_map/ppermute | solution.py:27
  69.2 0.6 stack.94.owner_ref
  69.8 1.0 collective-permute-done.3.refs_3_
  70.8 1.9 %collective-permute-start.5 = (bf16[2,688,624]{2,1,0:T(8,128)(2,1)}, bf16[2,688,624]{2,1,0:T(8,128)(2,1)}, u32[]{:S(2)}, u32[]{:S(2)}) collective-permute-start(bf16[2,688,624]{2,1,0:T(8,128)(2,1)} %collective-permute-done.3.refs_3_), channel_id=1, source_target_pairs={{0,64},{32,480},{64,128},{96,32},{128,192},{160,96},{192,256},{224... | collective-permute-start | bytes 5151752 | tf_op jit(solution)/shard_map/ppermute | solution.py:112
  72.8 0.6 copy-done.20
  73.4 6.6 %fusion.11 = bf16[1248,14,14]{0,2,1:T(8,128)(2,1)S(1)} fusion(bf16[1248,14,14]{0,2,1:T(8,128)(2,1)S(1)} %reshape.120, bf16[1248,16,14]{0,2,1:T(8,128)(2,1)S(1)} %constant_dynamic-update-slice_fusion.3, bf16[1248,16,1]{0,2,1:T(2,128)(2,1)} %copy-done.21, bf16[1248,16,1]{0,2,1:T(2,128)(2,1)} %copy-done.20, ...), kind=kLoop, calls=%fused_computation.19 | loop fusion | flops 28129920 | bytes 1732224 | tf_op jit(solution)/shard_map/convert_element_type | solution.py:420
  80.3 0.9 copy-done.12
  81.8 1.9 %collective-permute-start.17 = (bf16[312,1,14]{0,2,1:T(8,128)(2,1)S(1)}, bf16[312,1,14]{0,2,1:T(8,128)(2,1)S(1)}, u32[]{:S(2)}, u32[]{:S(2)}) collective-permute-start(bf16[312,1,14]{0,2,1:T(8,128)(2,1)S(1)} %slice.176), channel_id=1, source_target_pairs={{0,32},{32,64},{64,96},{96,128},{128,160},{160,192},{192,224},{224... | collective-permute-start | bytes 26216 | tf_op jit(solution)/shard_map/ppermute | solution.py:35
  83.8 3.8 %collective-permute-start.2 = (bf16[2,688,624]{2,1,0:T(8,128)(2,1)}, bf16[2,688,624]{2,1,0:T(8,128)(2,1)}, u32[]{:S(2)}, u32[]{:S(2)}) collective-permute-start(bf16[2,688,624]{2,1,0:T(8,128)(2,1)} %collective-permute-done.1.refs_1_), channel_id=1, source_target_pairs={{0,32},{32,0},{64,96},{96,64},{128,160},{160,128},{192,224},{224,1... | collective-permute-start | bytes 5151752 | tf_op jit(solution)/shard_map/ppermute | solution.py:113
  87.5 1.9 %collective-permute-start.4 = (bf16[2,688,624]{2,1,0:T(8,128)(2,1)}, bf16[2,688,624]{2,1,0:T(8,128)(2,1)}, u32[]{:S(2)}, u32[]{:S(2)}) collective-permute-start(bf16[2,688,624]{2,1,0:T(8,128)(2,1)} %collective-permute-done.3.refs_3_), channel_id=1, source_target_pairs={{0,32},{32,0},{64,96},{96,64},{128,160},{160,128},{192,224},{224,1... | collective-permute-start | bytes 5151752 | tf_op jit(solution)/shard_map/ppermute | solution.py:113
  89.4 6.9 %collective-permute-done.5.refs_5_ = bf16[2,688,624]{2,1,0:T(8,128)(2,1)} collective-permute-done((bf16[2,688,624]{2,1,0:T(8,128)(2,1)}, bf16[2,688,624]{2,1,0:T(8,128)(2,1)}, u32[]{:S(2)}, u32[]{:S(2)}) %collective-permute-start.5) | collective-permute-done | bytes 1717280 | tf_op jit(solution)/shard_map/ppermute | solution.py:112
  96.4 1.2 slice_bitcast_fusion
  97.6 2.1 %collective-permute-start.7 = (bf16[688,624]{1,0:T(8,128)(2,1)S(1)}, bf16[688,624]{1,0:T(8,128)(2,1)S(1)}, u32[]{:S(2)}, u32[]{:S(2)}) collective-permute-start(bf16[688,624]{1,0:T(8,128)(2,1)S(1)} %slice_bitcast_fusion), channel_id=1, source_target_pairs={{0,64},{32,480},{64,128},{96,32},{128,192},{160,96},{192,256},{224... | collective-permute-start | bytes 2575880 | tf_op jit(solution)/shard_map/ppermute | solution.py:114
  99.7 1.9 %collective-permute-start.6 = (bf16[2,688,624]{2,1,0:T(8,128)(2,1)}, bf16[2,688,624]{2,1,0:T(8,128)(2,1)}, u32[]{:S(2)}, u32[]{:S(2)}) collective-permute-start(bf16[2,688,624]{2,1,0:T(8,128)(2,1)} %collective-permute-done.5.refs_5_), channel_id=1, source_target_pairs={{0,32},{32,0},{64,96},{96,64},{128,160},{160,128},{192,224},{224,1... | collective-permute-start | bytes 5151752 | tf_op jit(solution)/shard_map/ppermute | solution.py:113
  101.7 2.4 %collective-permute-start.9 = (bf16[49,624]{1,0:T(8,128)(2,1)S(1)}, bf16[49,624]{1,0:T(8,128)(2,1)S(1)}, u32[]{:S(2)}, u32[]{:S(2)}) collective-permute-start(bf16[49,624]{1,0:T(8,128)(2,1)S(1)} %bitcast.211), channel_id=1, source_target_pairs={{0,32},{32,64},{64,96},{96,128},{128,160},{160,192},{192,224},{224... | collective-permute-start | bytes 183464 | tf_op jit(solution)/shard_map/ppermute | solution.py:354
  104.2 5.5 %collective-permute-done.9 = bf16[49,624]{1,0:T(8,128)(2,1)S(1)} collective-permute-done((bf16[49,624]{1,0:T(8,128)(2,1)S(1)}, bf16[49,624]{1,0:T(8,128)(2,1)S(1)}, u32[]{:S(2)}, u32[]{:S(2)}) %collective-permute-start.9) | collective-permute-done | bytes 61184 | tf_op jit(solution)/shard_map/ppermute | solution.py:354
  109.6 3.4 %collective-permute-start.18 = (bf16[312,15,1]{0,2,1:T(2,128)(2,1)S(1)}, bf16[312,15,1]{0,2,1:T(2,128)(2,1)S(1)}, u32[]{:S(2)}, u32[]{:S(2)}) collective-permute-start(bf16[312,15,1]{0,2,1:T(2,128)(2,1)S(1)} %slice.177), channel_id=1, source_target_pairs={{0,1},{1,2},{2,3},{3,4},{4,5},{5,6},{6,7},{7,8},{8,9},{9,10},{10,1... | collective-permute-start | bytes 28088 | tf_op jit(solution)/shard_map/ppermute | solution.py:35
  113.0 1.6 pad_maximum_fusion.5
  114.7 4.0 %collective-permute-done.18 = bf16[312,15,1]{0,2,1:T(2,128)(2,1)S(1)} collective-permute-done((bf16[312,15,1]{0,2,1:T(2,128)(2,1)S(1)}, bf16[312,15,1]{0,2,1:T(2,128)(2,1)S(1)}, u32[]{:S(2)}, u32[]{:S(2)}) %collective-permute-start.18) | collective-permute-done | bytes 9392 | tf_op jit(solution)/shard_map/ppermute | solution.py:35
  118.7 1.9 %collective-permute-start.12 = (bf16[147,624]{1,0:T(8,128)(2,1)}, bf16[147,624]{1,0:T(8,128)(2,1)S(1)}, u32[]{:S(2)}, u32[]{:S(2)}) collective-permute-start(bf16[147,624]{1,0:T(8,128)(2,1)} %pad_maximum_fusion.5), channel_id=1, source_target_pairs={{1,0},{2,1},{3,2},{4,3},{5,4},{6,5},{7,6},{8,7},{9,8},{10,9},{11,1... | collective-permute-start | bytes 550376 | tf_op jit(solution)/shard_map/ppermute | solution.py:354
  120.8 2.1 %slice_reduce_fusion = (bf16[312,7,7]{0,2,1:T(8,128)(2,1)}, bf16[312,7,7]{0,2,1:T(8,128)(2,1)}, bf16[312,7,7]{0,2,1:T(8,128)(2,1)}, bf16[312,7,7]{0,2,1:T(8,128)...) fusion(bf16[312,8,2,8,2]{0,4,3,2,1:T(2,128)(2,1)S(1)} %reshape.123), kind=kLoop, calls=%fused_computation.115 | loop fusion | bytes 550368 | tf_op jit(solution)/shard_map/slice | solution.py:437
  122.9 1.4 stack_reshape_squeeze.35
  124.3 1.4 stack_reshape_squeeze.34
  125.7 1.4 stack_reshape_squeeze.33
  127.1 1.4 stack_reshape_squeeze.32
  128.6 0.6 stack_reshape_squeeze.31
  129.4 1.9 %collective-permute-start.8 = (bf16[688,624]{1,0:T(8,128)(2,1)S(1)}, bf16[688,624]{1,0:T(8,128)(2,1)S(1)}, u32[]{:S(2)}, u32[]{:S(2)}) collective-permute-start(bf16[688,624]{1,0:T(8,128)(2,1)S(1)} %collective-permute-done.7.refs_7_), channel_id=1, source_target_pairs={{0,32},{32,0},{64,96},{96,64},{128,160},{160,128},{192,224},{224,1... | collective-permute-start | bytes 2575880 | tf_op jit(solution)/shard_map/ppermute | solution.py:115
  131.4 0.8 constant_dynamic-update-slice_fusion.13
  132.2 0.8 constant_dynamic-update-slice_fusion.12
  132.9 0.8 constant_dynamic-update-slice_fusion.11
  133.7 0.8 constant_dynamic-update-slice_fusion.10
  134.5 3.9 %collective-permute-start.11 = (bf16[147,624]{1,0:T(8,128)(2,1)}, bf16[147,624]{1,0:T(8,128)(2,1)}, u32[]{:S(2)}, u32[]{:S(2)}) collective-permute-start(bf16[147,624]{1,0:T(8,128)(2,1)} %pad_maximum_fusion.5), channel_id=1, source_target_pairs={{0,1},{1,2},{2,3},{3,4},{4,5},{5,6},{6,7},{7,8},{8,9},{9,10},{10,1... | collective-permute-start | bytes 550376 | tf_op jit(solution)/shard_map/ppermute | solution.py:354
  138.5 0.8 constant_dynamic-update-slice_fusion.9
  139.4 1.2 reshape.124
  140.6 1.1 copy.61
  141.8 5.5 %collective-permute-done.11 = bf16[147,624]{1,0:T(8,128)(2,1)} collective-permute-done((bf16[147,624]{1,0:T(8,128)(2,1)}, bf16[147,624]{1,0:T(8,128)(2,1)}, u32[]{:S(2)}, u32[]{:S(2)}) %collective-permute-start.11) | collective-permute-done | bytes 183488 | tf_op jit(solution)/shard_map/ppermute | solution.py:354
  147.3 7.9 %concatenate.42 = bf16[441,624]{1,0:T(8,128)(2,1)} concatenate(bf16[49,624]{1,0:T(8,128)(2,1)} %bitcast.210, bf16[49,624]{1,0:T(8,128)(2,1)} %copy-done.15, bf16[49,624]{1,0:T(8,128)(2,1)} %collective-permute-done.10, bf16[147,624]{1,0:T(8,128)(2,1)} %collective-permute-done.11, bf16[147,624]{1,0:T(8,128)(2,1)} %copy-done.18), dimensions={0} | concatenate | bytes 1100736 | tf_op jit(solution)/shard_map/concatenate | solution.py:353
  155.2 1.2 pad.35.refs_9_
  156.5 1.0 copy-done.2
  157.5 0.6 copy-done.8
  158.1 0.6 copy-done.9
  158.8 23.7 %shard_map.203 = (bf16[196,312]{1,0:T(8,128)(2,1)}, bf16[49,624]{1,0:T(8,128)(2,1)}) custom-call(s32[16]{0:T(128)S(1)} %copy-done.9, s32[4]{0:T(128)S(1)} %copy-done.8, bf16[2,688,624]{2,1,0:T(8,128)(2,1)} %copy-done.10, bf16[2,688,624]{2,1,0:T(8,128)(2,1)} %collective-permute-done.1.refs_1_, bf16[2,688,624]{2,1,0:T(8,128)(2,1)} %collective-permute-done.2.refs_2_, ...), custom_call_target="tpu_custom_call" | custom-call | tf_op jit(solution)/shard_map/pallas_call | solution.py:325
  (108 shorter events, 6.7 us)
Async XLA Ops:
  0.6 23.8 %copy-start = (bf16[1248,312]{0,1:T(8,128)(2,1)S(1)}, bf16[1248,312]{0,1:T(8,128)(2,1)}, u32[]{:S(2)}) copy-start(bf16[1248,312]{0,1:T(8,128)(2,1)} %param.24) | copy-start | bytes 2336260
  0.6 3.6 %slice-start = ((bf16[3,39,624]{2,1,0:T(8,128)(2,1)}), bf16[1,39,624]{2,1,0:T(8,128)(2,1)S(1)}, s32[]{:S(2)}) async-start(bf16[3,39,624]{2,1,0:T(8,128)(2,1)} %param.27), calls=%async_computation | async-start | bytes 102400 | tf_op jit(solution)/shard_map/slice | solution.py:92
  0.7 3.6 %slice-start.1 = ((bf16[3,39,624]{2,1,0:T(8,128)(2,1)}), bf16[2,39,624]{2,1,0:T(8,128)(2,1)S(1)}, s32[]{:S(2)}) async-start(bf16[3,39,624]{2,1,0:T(8,128)(2,1)} %param.27), calls=%async_computation.1 | async-start | bytes 204800 | tf_op jit(solution)/shard_map/slice | solution.py:92
  0.7 3.6 %copy-start.22 = (bf16[624,39]{0,1:T(8,128)(2,1)S(1)}, bf16[624,39]{0,1:T(8,128)(2,1)}, u32[]{:S(2)}) copy-start(bf16[624,39]{0,1:T(8,128)(2,1)} %param.28) | copy-start | bytes 146020
  0.7 101.0 %collective-permute-start.10 = (bf16[49,624]{1,0:T(8,128)(2,1)}, bf16[49,624]{1,0:T(8,128)(2,1)}, u32[]{:S(2)}, u32[]{:S(2)}) collective-permute-start(bf16[49,624]{1,0:T(8,128)(2,1)} %bitcast.209), channel_id=1, source_target_pairs={{32,0},{64,32},{96,64},{128,96},{160,128},{192,160},{224,192},{256... | collective-permute-start | bytes 183464 | tf_op jit(solution)/shard_map/ppermute | solution.py:354
  3.7 1.3 copy-start.16
  3.7 2.0 %copy-start.17 = (bf16[624,156]{0,1:T(8,128)(2,1)S(1)}, bf16[624,156]{0,1:T(8,128)(2,1)}, u32[]{:S(2)}) copy-start(bf16[624,156]{0,1:T(8,128)(2,1)} %param.31) | copy-start | bytes 584068
  4.2 5.9 %copy-start.11 = (bf16[1,1,312,196]{2,3,1,0:T(8,128)(2,1)S(1)}, bf16[1,1,312,196]{2,3,1,0:T(8,128)(2,1)}, u32[]{:S(2)}) copy-start(bf16[1,1,312,196]{2,3,1,0:T(8,128)(2,1)} %param.20) | copy-start | bytes 366916
  4.3 6.2 %copy-start.13 = (bf16[3,312,312]{2,1,0:T(8,128)(2,1)S(1)}, bf16[3,312,312]{2,1,0:T(8,128)(2,1)}, u32[]{:S(2)}) copy-start(bf16[3,312,312]{2,1,0:T(8,128)(2,1)} %param.22) | copy-start | bytes 1752196
  7.8 6.4 %collective-permute-start = (bf16[688,624]{1,0:T(8,128)(2,1)}, bf16[688,624]{1,0:T(8,128)(2,1)}, u32[]{:S(2)}, u32[]{:S(2)}) collective-permute-start(bf16[688,624]{1,0:T(8,128)(2,1)} %constant_dynamic-update-slice_fusion), channel_id=1, source_target_pairs={{0,32},{32,0},{64,96},{96,64},{128,160},{160,128},{192,224},{224,1... | collective-permute-start | bytes 2575880 | tf_op jit(solution)/shard_map/ppermute | solution.py:109
  15.9 6.2 %copy-start.10 = (bf16[2,688,624]{2,1,0:T(8,128)(2,1)}, bf16[2,688,624]{2,1,0:T(8,128)(2,1)S(1)}, u32[]{:S(2)}) copy-start(bf16[2,688,624]{2,1,0:T(8,128)(2,1)S(1)} %pad_maximum_fusion.refs_0_) | copy-start | bytes 5151748
  15.9 24.4 %collective-permute-start.1 = (bf16[2,688,624]{2,1,0:T(8,128)(2,1)S(1)}, bf16[2,688,624]{2,1,0:T(8,128)(2,1)}, u32[]{:S(2)}, u32[]{:S(2)}) collective-permute-start(bf16[2,688,624]{2,1,0:T(8,128)(2,1)S(1)} %pad_maximum_fusion.refs_0_), channel_id=1, source_target_pairs={{0,64},{32,480},{64,128},{96,32},{128,192},{160,96},{192,256},{224... | collective-permute-start | bytes 5151752 | tf_op jit(solution)/shard_map/ppermute | solution.py:112
  40.3 28.5 %copy-start.19 = (f32[9,2496]{1,0:T(8,128)S(1)}, f32[9,2496]{1,0:T(8,128)}, u32[]{:S(2)}) copy-start(f32[9,2496]{1,0:T(8,128)} %param.30) | copy-start | bytes 269572
  40.4 30.5 %collective-permute-start.3 = (bf16[2,688,624]{2,1,0:T(8,128)(2,1)}, bf16[2,688,624]{2,1,0:T(8,128)(2,1)}, u32[]{:S(2)}, u32[]{:S(2)}) collective-permute-start(bf16[2,688,624]{2,1,0:T(8,128)(2,1)} %collective-permute-done.1.refs_1_), channel_id=1, source_target_pairs={{0,64},{32,480},{64,128},{96,32},{128,192},{160,96},{192,256},{224... | collective-permute-start | bytes 5151752 | tf_op jit(solution)/shard_map/ppermute | solution.py:112
  44.8 14.1 %collective-permute-start.14 = (bf16[1248,1,14]{0,2,1:T(8,128)(2,1)S(1)}, bf16[1248,1,14]{0,2,1:T(8,128)(2,1)S(1)}, u32[]{:S(2)}, u32[]{:S(2)}) collective-permute-start(bf16[1248,1,14]{0,2,1:T(8,128)(2,1)S(1)} %get-tuple-element.26), channel_id=1, source_target_pairs={{32,0},{64,32},{96,64},{128,96},{160,128},{192,160},{224,192},{256... | collective-permute-start | bytes 104840 | tf_op jit(solution)/shard_map/ppermute | solution.py:27
  53.0 5.8 %collective-permute-start.13 = (bf16[1248,1,14]{0,2,1:T(8,128)(2,1)S(1)}, bf16[1248,1,14]{0,2,1:T(8,128)(2,1)S(1)}, u32[]{:S(2)}, u32[]{:S(2)}) collective-permute-start(bf16[1248,1,14]{0,2,1:T(8,128)(2,1)S(1)} %get-tuple-element.27), channel_id=1, source_target_pairs={{0,32},{32,64},{64,96},{96,128},{128,160},{160,192},{192,224},{224... | collective-permute-start | bytes 104840 | tf_op jit(solution)/shard_map/ppermute | solution.py:26
  59.1 13.7 %collective-permute-start.15 = (bf16[1248,16,1]{0,2,1:T(2,128)(2,1)S(1)}, bf16[1248,16,1]{0,2,1:T(2,128)(2,1)S(1)}, u32[]{:S(2)}, u32[]{:S(2)}) collective-permute-start(bf16[1248,16,1]{0,2,1:T(2,128)(2,1)S(1)} %get-tuple-element.24), channel_id=1, source_target_pairs={{0,1},{1,2},{2,3},{3,4},{4,5},{5,6},{6,7},{7,8},{8,9},{9,10},{10,1... | collective-permute-start | bytes 119816 | tf_op jit(solution)/shard_map/ppermute | solution.py:26
  62.5 10.3 %collective-permute-start.16 = (bf16[1248,16,1]{0,2,1:T(2,128)(2,1)S(1)}, bf16[1248,16,1]{0,2,1:T(2,128)(2,1)S(1)}, u32[]{:S(2)}, u32[]{:S(2)}) collective-permute-start(bf16[1248,16,1]{0,2,1:T(2,128)(2,1)S(1)} %get-tuple-element.25), channel_id=1, source_target_pairs={{1,0},{2,1},{3,2},{4,3},{5,4},{6,5},{7,6},{8,7},{9,8},{10,9},{11,1... | collective-permute-start | bytes 119816 | tf_op jit(solution)/shard_map/ppermute | solution.py:27
  70.8 25.5 %collective-permute-start.5 = (bf16[2,688,624]{2,1,0:T(8,128)(2,1)}, bf16[2,688,624]{2,1,0:T(8,128)(2,1)}, u32[]{:S(2)}, u32[]{:S(2)}) collective-permute-start(bf16[2,688,624]{2,1,0:T(8,128)(2,1)} %collective-permute-done.3.refs_3_), channel_id=1, source_target_pairs={{0,64},{32,480},{64,128},{96,32},{128,192},{160,96},{192,256},{224... | collective-permute-start | bytes 5151752 | tf_op jit(solution)/shard_map/ppermute | solution.py:112
  72.8 0.6 copy-start.20
  72.8 0.6 copy-start.21
  80.1 1.1 copy-start.12
  81.7 20.0 %copy-start.14 = (bf16[1,1,624,49]{2,3,1,0:T(8,128)(2,1)S(1)}, bf16[1,1,624,49]{2,3,1,0:T(8,128)(2,1)}, u32[]{:S(2)}) copy-start(bf16[1,1,624,49]{2,3,1,0:T(8,128)(2,1)} %param.21) | copy-start | bytes 183460
  81.8 17.9 %collective-permute-start.17 = (bf16[312,1,14]{0,2,1:T(8,128)(2,1)S(1)}, bf16[312,1,14]{0,2,1:T(8,128)(2,1)S(1)}, u32[]{:S(2)}, u32[]{:S(2)}) collective-permute-start(bf16[312,1,14]{0,2,1:T(8,128)(2,1)S(1)} %slice.176), channel_id=1, source_target_pairs={{0,32},{32,64},{64,96},{96,128},{128,160},{160,192},{192,224},{224... | collective-permute-start | bytes 26216 | tf_op jit(solution)/shard_map/ppermute | solution.py:35
  83.8 72.7 %collective-permute-start.2 = (bf16[2,688,624]{2,1,0:T(8,128)(2,1)}, bf16[2,688,624]{2,1,0:T(8,128)(2,1)}, u32[]{:S(2)}, u32[]{:S(2)}) collective-permute-start(bf16[2,688,624]{2,1,0:T(8,128)(2,1)} %collective-permute-done.1.refs_1_), channel_id=1, source_target_pairs={{0,32},{32,0},{64,96},{96,64},{128,160},{160,128},{192,224},{224,1... | collective-permute-start | bytes 5151752 | tf_op jit(solution)/shard_map/ppermute | solution.py:113
  87.5 68.9 %collective-permute-start.4 = (bf16[2,688,624]{2,1,0:T(8,128)(2,1)}, bf16[2,688,624]{2,1,0:T(8,128)(2,1)}, u32[]{:S(2)}, u32[]{:S(2)}) collective-permute-start(bf16[2,688,624]{2,1,0:T(8,128)(2,1)} %collective-permute-done.3.refs_3_), channel_id=1, source_target_pairs={{0,32},{32,0},{64,96},{96,64},{128,160},{160,128},{192,224},{224,1... | collective-permute-start | bytes 5151752 | tf_op jit(solution)/shard_map/ppermute | solution.py:113
  97.6 31.8 %collective-permute-start.7 = (bf16[688,624]{1,0:T(8,128)(2,1)S(1)}, bf16[688,624]{1,0:T(8,128)(2,1)S(1)}, u32[]{:S(2)}, u32[]{:S(2)}) collective-permute-start(bf16[688,624]{1,0:T(8,128)(2,1)S(1)} %slice_bitcast_fusion), channel_id=1, source_target_pairs={{0,64},{32,480},{64,128},{96,32},{128,192},{160,96},{192,256},{224... | collective-permute-start | bytes 2575880 | tf_op jit(solution)/shard_map/ppermute | solution.py:114
  99.7 56.7 %collective-permute-start.6 = (bf16[2,688,624]{2,1,0:T(8,128)(2,1)}, bf16[2,688,624]{2,1,0:T(8,128)(2,1)}, u32[]{:S(2)}, u32[]{:S(2)}) collective-permute-start(bf16[2,688,624]{2,1,0:T(8,128)(2,1)} %collective-permute-done.5.refs_5_), channel_id=1, source_target_pairs={{0,32},{32,0},{64,96},{96,64},{128,160},{160,128},{192,224},{224,1... | collective-permute-start | bytes 5151752 | tf_op jit(solution)/shard_map/ppermute | solution.py:113
  101.7 7.9 %collective-permute-start.9 = (bf16[49,624]{1,0:T(8,128)(2,1)S(1)}, bf16[49,624]{1,0:T(8,128)(2,1)S(1)}, u32[]{:S(2)}, u32[]{:S(2)}) collective-permute-start(bf16[49,624]{1,0:T(8,128)(2,1)S(1)} %bitcast.211), channel_id=1, source_target_pairs={{0,32},{32,64},{64,96},{96,128},{128,160},{160,192},{192,224},{224... | collective-permute-start | bytes 183464 | tf_op jit(solution)/shard_map/ppermute | solution.py:354
  109.6 10.9 %copy-start.15 = (bf16[49,624]{1,0:T(8,128)(2,1)}, bf16[49,624]{1,0:T(8,128)(2,1)S(1)}, u32[]{:S(2)}) copy-start(bf16[49,624]{1,0:T(8,128)(2,1)S(1)} %collective-permute-done.9) | copy-start | bytes 183460
  109.6 9.0 %collective-permute-start.18 = (bf16[312,15,1]{0,2,1:T(2,128)(2,1)S(1)}, bf16[312,15,1]{0,2,1:T(2,128)(2,1)S(1)}, u32[]{:S(2)}, u32[]{:S(2)}) collective-permute-start(bf16[312,15,1]{0,2,1:T(2,128)(2,1)S(1)} %slice.177), channel_id=1, source_target_pairs={{0,1},{1,2},{2,3},{3,4},{4,5},{5,6},{6,7},{7,8},{8,9},{9,10},{10,1... | collective-permute-start | bytes 28088 | tf_op jit(solution)/shard_map/ppermute | solution.py:35
  118.7 15.9 %collective-permute-start.12 = (bf16[147,624]{1,0:T(8,128)(2,1)}, bf16[147,624]{1,0:T(8,128)(2,1)S(1)}, u32[]{:S(2)}, u32[]{:S(2)}) collective-permute-start(bf16[147,624]{1,0:T(8,128)(2,1)} %pad_maximum_fusion.5), channel_id=1, source_target_pairs={{1,0},{2,1},{3,2},{4,3},{5,4},{6,5},{7,6},{8,7},{9,8},{10,9},{11,1... | collective-permute-start | bytes 550376 | tf_op jit(solution)/shard_map/ppermute | solution.py:354
  129.4 27.1 %collective-permute-start.8 = (bf16[688,624]{1,0:T(8,128)(2,1)S(1)}, bf16[688,624]{1,0:T(8,128)(2,1)S(1)}, u32[]{:S(2)}, u32[]{:S(2)}) collective-permute-start(bf16[688,624]{1,0:T(8,128)(2,1)S(1)} %collective-permute-done.7.refs_7_), channel_id=1, source_target_pairs={{0,32},{32,0},{64,96},{96,64},{128,160},{160,128},{192,224},{224,1... | collective-permute-start | bytes 2575880 | tf_op jit(solution)/shard_map/ppermute | solution.py:115
  134.5 4.7 %copy-start.18 = (bf16[147,624]{1,0:T(8,128)(2,1)}, bf16[147,624]{1,0:T(8,128)(2,1)S(1)}, u32[]{:S(2)}) copy-start(bf16[147,624]{1,0:T(8,128)(2,1)S(1)} %collective-permute-done.12) | copy-start | bytes 550372
  134.5 12.8 %collective-permute-start.11 = (bf16[147,624]{1,0:T(8,128)(2,1)}, bf16[147,624]{1,0:T(8,128)(2,1)}, u32[]{:S(2)}, u32[]{:S(2)}) collective-permute-start(bf16[147,624]{1,0:T(8,128)(2,1)} %pad_maximum_fusion.5), channel_id=1, source_target_pairs={{0,1},{1,2},{2,3},{3,4},{4,5},{5,6},{6,7},{7,8},{8,9},{9,10},{10,1... | collective-permute-start | bytes 550376 | tf_op jit(solution)/shard_map/ppermute | solution.py:354
  141.8 14.7 %copy-start.3 = (f32[96,448]{1,0:T(8,128)S(1)}, f32[96,448]{1,0:T(8,128)}, u32[]{:S(2)}) copy-start(f32[96,448]{1,0:T(8,128)} %constant.204.clone.refs_14_) | copy-start | bytes 516100
  141.8 14.7 %copy-start.5 = (bf16[196,64]{1,0:T(8,128)(2,1)S(1)}, bf16[196,64]{1,0:T(8,128)(2,1)}, u32[]{:S(2)}) copy-start(bf16[196,64]{1,0:T(8,128)(2,1)} %constant.235.refs_17_) | copy-start | bytes 75268
  141.8 14.7 %copy-start.6 = (bf16[64,96]{1,0:T(8,128)(2,1)S(1)}, bf16[64,96]{1,0:T(8,128)(2,1)}, u32[]{:S(2)}) copy-start(bf16[64,96]{1,0:T(8,128)(2,1)} %constant.234.refs_16_) | copy-start | bytes 36868
  155.2 1.3 copy-start.1
  155.2 1.3 copy-start.4
  155.2 1.3 copy-start.7
  156.5 1.0 copy-start.2
  157.5 0.6 copy-start.8
  158.1 0.6 copy-start.9

commit v3 on v2

--- a/solution.py
+++ b/solution.py
@@ -81,23 +81,28 @@
 HEAD_ROWS = 40
 BLOCK_ROWS = 4 * HEAD_ROWS
 TAP_ROWS = 5 * HEAD_ROWS + 8
-SHARD_ROWS = 3 * BLOCK_ROWS + TAP_ROWS
 SHARDS = 16
-KEYS = 448
+TILE = 56
+KEYS = 9 * TILE + 8
 QUERIES = 96
-
-
-def pack(inproj, outproj, expand, shrink, to_coarse):
-    width = inproj.shape[-1]
+ABOVE = 200
+BESIDE = 216
+
+
+def pack_heads(inproj, outproj):
     heads = jnp.concatenate([outproj.T[None], inproj[2:], inproj[:2]])
+    return jnp.pad(heads, ((0, 0), (0, 1), (0, 0))).reshape(BLOCK_ROWS, -1)
+
+
+def pack_rest(expand, shrink, to_coarse):
+    width = expand.shape[-1]
     taps = jnp.pad(to_coarse, ((0, 1), (0, 1), (0, 0))).reshape(5, 2, HEAD_ROWS, -1)
     return jnp.concatenate(
         [
-            jnp.pad(heads, ((0, 0), (0, 1), (0, 0))).reshape(-1, width),
             jnp.pad(expand, ((0, 4), (0, 0))),
             jnp.pad(shrink.T, ((0, 4), (0, 0))),
             taps.transpose(0, 2, 1, 3).reshape(-1, width),
-            jnp.zeros((8, width), inproj.dtype),
+            jnp.zeros((8, width), expand.dtype),
         ]
     )
 
@@ -113,52 +118,52 @@
         pairs += [held, lax.ppermute(held, "rows", swap)]
     last = lax.ppermute(held[0], "rows", ring)
     singles = [last, lax.ppermute(last, "rows", swap)]
-    place = lax.axis_index("rows")
-    chip, core = place // 2, place % 2
-    step = 1 - 2 * core
-    owners = [2 * chip + core, 2 * chip + 1 - core]
-    for k in (1, 2, 3):
-        for sign in (-1, 1):
-            away = 2 * ((chip + sign * step * k) % (size // 2))
-            first = core if sign < 0 else 1 - core
-            owners += [away + first, away + 1 - first]
-    across = 2 * ((chip + 4) % (size // 2))
-    owners += [across + core, across + 1 - core]
-    return pairs, singles, jnp.stack(owners).astype(jnp.int32)
-
-
-def tables():
+    return pairs + singles
+
+
+def attention_tables():
     pick = np.zeros((QUERIES, KEYS), np.float32)
     bias = np.full((QUERIES, KEYS), -1e30, np.float32)
-    centre = np.zeros((64, QUERIES), np.float32)
     for row in range(RING):
         for col in range(RING):
             down = 1 if row == 0 else 2 if row == RING - 1 else 0
             side = 1 if col == 0 else 2 if col == RING - 1 else 0
-            window = 3 * side + down
-            cell = (row - 1) % WIN * WIN + (col - 1) % WIN
+            first = (3 * side + down) * TILE
             query = row * RING + col
-            pick[query, window * CELLS + cell] = 1
-            bias[query, window * CELLS : (window + 1) * CELLS] = 0
-            if window == 0:
-                centre[(row - 1) * 8 + col - 1, query] = 1
+            pick[query, first + (row - 1) % WIN * WIN + (col - 1) % WIN] = 1
+            bias[query, first : first + CELLS] = 0
     bias[RING * RING :, :CELLS] = 0
-    repeat = np.zeros((4 * CELLS, 64), np.float32)
+    return jnp.asarray(bias), jnp.asarray(pick).astype(jnp.bfloat16)
+
+
+def tail_tables():
+    side = 2 * WIN
+    centre = np.zeros((64, QUERIES), np.float32)
+    repeat = np.zeros((side * side, 64), np.float32)
     compact = np.zeros((CELLS, 64), np.float32)
-    for row in range(2 * WIN):
-        for col in range(2 * WIN):
-            repeat[row * 2 * WIN + col, row // 2 * 8 + col // 2] = 1
-    for row in range(WIN):
-        for col in range(WIN):
-            compact[row * WIN + col, row * 8 + col] = 1
+    sample = np.zeros((5 * 64, 512), np.float32)
     order = np.zeros((SHARDS * HEAD_ROWS, SHARDS * 39), np.float32)
+    for cell in range(CELLS):
+        row, col = divmod(cell, WIN)
+        centre[row * 8 + col, (row + 1) * RING + col + 1] = 1
+        compact[cell, row * 8 + col] = 1
+        for tap in range(9):
+            down, right = 2 * row + tap // 3 - 1, 2 * col + tap % 3 - 1
+            if right < 0:
+                source = BESIDE + down + 1
+            elif down < 0:
+                source = ABOVE + right
+            else:
+                source = down * side + right
+            sample[tap // 2 * 64 + cell, tap % 2 * 256 + source] = 1
+    for cell in range(side * side):
+        row, col = divmod(cell, side)
+        repeat[cell, row // 2 * 8 + col // 2] = 1
     for shard in range(SHARDS):
         for row in range(39):
             order[shard * HEAD_ROWS + row, shard * 39 + row] = 1
-    half = jnp.bfloat16
-    return (
-        jnp.asarray(bias),
-        *(jnp.asarray(t).astype(half) for t in (pick, centre, repeat, compact, order)),
+    return tuple(
+        jnp.asarray(t).astype(jnp.bfloat16) for t in (centre, repeat, compact, sample, order)
     )
 
 
@@ -185,73 +190,36 @@
     )
 
 
-def coarse_kernel(
-    owner_ref,
-    edge_ref,
+def attention_kernel(
+    centre_ref,
+    above_ref,
+    below_ref,
+    left_ref,
+    right_ref,
+    bias_ref,
+    pick_ref,
     *refs,
 ):
-    sources, rest = refs[:9], refs[9:]
-    (
-        tiles_ref,
-        depth_ref,
-        taps_in_ref,
-        fine_ref,
-        to_fine_ref,
-        bias_ref,
-        pick_ref,
-        centre_ref,
-        repeat_ref,
-        compact_ref,
-        order_ref,
-        fine_out_ref,
-        coarse_out_ref,
-        heads_ref,
-        expand_ref,
-        shrink_ref,
-        taps_ref,
-        proj_ref,
-        hidden_ref,
-        conv_ref,
-        down_ref,
-        sems,
-    ) = rest
-    slots = []
+    sources, (middle_ref, heads_ref, tiles_ref, proj_ref, sems) = refs[:9], refs[9:]
+    copies = []
     for index, source in enumerate(sources):
-        if index < 7:
-            slots += [source.at[0], source.at[1]]
-        else:
-            slots += [source]
-    spans = (
-        (heads_ref, 0, BLOCK_ROWS),
-        (expand_ref, BLOCK_ROWS, BLOCK_ROWS),
-        (shrink_ref, 2 * BLOCK_ROWS, BLOCK_ROWS),
-        (taps_ref, 3 * BLOCK_ROWS, TAP_ROWS),
-    )
-    copies = []
-    for part, (target, first, count) in enumerate(spans):
-        copies.append(
-            [
-                pltpu.make_async_copy(
-                    slot.at[pl.ds(first, count)], target.at[owner_ref[place]], sems.at[part, place]
-                )
-                for place, slot in enumerate(slots)
-            ]
-        )
-        for copy in copies[-1]:
-            copy.start()
-
-    def arrive(part):
-        for copy in copies[part]:
-            copy.wait()
-
-    width = tiles_ref.shape[1]
+        target = heads_ref.at[pl.ds(2 * index, 2)] if index < 7 else heads_ref.at[7 + index]
+        copies.append(pltpu.make_async_copy(source, target, sems.at[index]))
+        copies[-1].start()
+    tiles_ref[9 * TILE :, :] = jnp.zeros((KEYS - 9 * TILE, tiles_ref.shape[1]), jnp.float32)
+    first = 0
+    for piece in (centre_ref, above_ref, below_ref, left_ref, right_ref):
+        count = piece.shape[0]
+        tiles_ref[first : first + count, :] = piece[...].astype(jnp.float32)
+        first += count
     tiles = tiles_ref[...]
-    normed = norm_rows(tiles.astype(jnp.float32))
+    normed = norm_rows(tiles)
     pick = pick_ref[...]
-    arrive(0)
-    heads = heads_ref[...].reshape(SHARDS * BLOCK_ROWS, width)
+    mixed = nn(pick, tiles.astype(jnp.bfloat16))
+    for copy in copies:
+        copy.wait()
+    heads = heads_ref[...].reshape(SHARDS * BLOCK_ROWS, tiles.shape[1])
     proj_ref[...] = nt(heads, normed).reshape(SHARDS, BLOCK_ROWS, KEYS)
-    mixed = nn(pick, tiles)
     for head in range(SHARDS):
         values = proj_ref[head, HEAD_ROWS : 2 * HEAD_ROWS].astype(jnp.bfloat16)
         queries = proj_ref[head, 2 * HEAD_ROWS : 3 * HEAD_ROWS].astype(jnp.bfloat16)
@@ -263,7 +231,68 @@
         probabilities = (exponent * (1.0 / total)).astype(jnp.bfloat16)
         attended = nt(probabilities, values).astype(jnp.bfloat16)
         mixed += nn(attended, heads_ref[head][:HEAD_ROWS])
-    middle = mixed.astype(jnp.bfloat16)
+    middle_ref[...] = mixed.astype(jnp.bfloat16)
+
+
+def coarse_attention(sources, tiles):
+    width = tiles[0].shape[1]
+    operands = (*tiles, *attention_tables())
+    vmem, anywhere = (pl.BlockSpec(memory_space=space) for space in (pltpu.VMEM, pl.ANY))
+    return pl.pallas_call(
+        attention_kernel,
+        out_shape=jax.ShapeDtypeStruct((QUERIES, width), jnp.bfloat16),
+        in_specs=[vmem] * len(operands) + [anywhere] * len(sources),
+        out_specs=vmem,
+        scratch_shapes=[
+            pltpu.VMEM((SHARDS, BLOCK_ROWS, width), jnp.bfloat16),
+            pltpu.VMEM((KEYS, width), jnp.float32),
+            pltpu.VMEM((SHARDS, BLOCK_ROWS, KEYS), jnp.float32),
+            pltpu.SemaphoreType.DMA((9,)),
+        ],
+        compiler_params=pltpu.CompilerParams(vmem_limit_bytes=32 * 1024 * 1024),
+    )(*operands, *sources)
+
+
+def tail_kernel(
+    edge_ref,
+    gathered_ref,
+    middle_ref,
+    depth_ref,
+    fine_ref,
+    above_ref,
+    beside_ref,
+    to_fine_ref,
+    centre_ref,
+    repeat_ref,
+    compact_ref,
+    sample_ref,
+    order_ref,
+    fine_out_ref,
+    coarse_out_ref,
+    expand_ref,
+    shrink_ref,
+    taps_ref,
+    hidden_ref,
+    conv_ref,
+    field_ref,
+    twice_ref,
+    down_ref,
+    sems,
+):
+    spans = (
+        (expand_ref, 0, BLOCK_ROWS),
+        (shrink_ref, BLOCK_ROWS, BLOCK_ROWS),
+        (taps_ref, 2 * BLOCK_ROWS, TAP_ROWS),
+    )
+    copies = [
+        pltpu.make_async_copy(gathered_ref.at[:, pl.ds(first, count)], target, sems.at[part])
+        for part, (target, first, count) in enumerate(spans)
+    ]
+    for copy in copies:
+        copy.start()
+    width = middle_ref.shape[1]
+    channels = fine_ref.shape[1]
+    middle = middle_ref[...]
     normed_mid = norm_rows(middle.astype(jnp.float32))
     query = lax.broadcasted_iota(jnp.int32, (QUERIES, 128), 0)
     column = query % RING
@@ -274,13 +303,21 @@
         | ((column == RING - 1) & (edge_ref[3] == 0))
     )
     inside = jnp.where(outside, 0.0, 1.0)[:, :1]
-    arrive(1)
-    conv_ref[CELLS // WIN * 8 :, :] = jnp.zeros((8, conv_ref.shape[1]), jnp.float32)
+    conv_ref[8 * WIN :, :] = jnp.zeros((8, conv_ref.shape[1]), jnp.float32)
+    field_ref[...] = jnp.zeros(field_ref.shape, jnp.float32)
+    field_ref[: fine_ref.shape[0], :] = fine_ref[...].astype(jnp.float32)
+    field_ref[ABOVE : ABOVE + 16, :] = above_ref[...].astype(jnp.float32)
+    field_ref[BESIDE : BESIDE + 16, :] = beside_ref[...].astype(jnp.float32)
+    twice_ref[...] = jnp.zeros(twice_ref.shape, jnp.float32)
+    twice_ref[:256, :channels] = field_ref[...]
+    twice_ref[256:, channels:] = field_ref[...]
+    samples = nn(sample_ref[...], twice_ref[...].astype(jnp.bfloat16)).astype(jnp.bfloat16)
+    copies[0].wait()
     chunk = 512
+    expand = expand_ref[...].reshape(SHARDS * BLOCK_ROWS, width)
     for first in range(0, SHARDS * BLOCK_ROWS, chunk):
         span = pl.ds(first, chunk)
-        rows = expand_ref[...].reshape(SHARDS * BLOCK_ROWS, width)[first : first + chunk]
-        hidden = gelu(nt(normed_mid, rows)) * inside
+        hidden = gelu(nt(normed_mid, expand[first : first + chunk])) * inside
         hidden_ref[:, span] = hidden.astype(jnp.bfloat16).astype(jnp.float32)
         for row in range(WIN):
             total = jnp.zeros((8, chunk), jnp.float32)
@@ -289,7 +326,7 @@
                 window = hidden_ref[pl.ds((row + down) * RING + side, 8), span]
                 total += depth_ref[tap : tap + 1, span] * window
             conv_ref[row * 8 : row * 8 + 8, span] = gelu(total)
-    arrive(2)
+    copies[1].wait()
     shrink = shrink_ref[...].reshape(SHARDS * BLOCK_ROWS, width)
     update = nn(conv_ref[...].astype(jnp.bfloat16), shrink)
     result = (nn(centre_ref[...], middle) + update).astype(jnp.bfloat16)
@@ -298,8 +335,7 @@
     fine_out_ref[...] = jnp.maximum(
         fine_ref[...].astype(jnp.float32) + upsampled, 0.0
     ).astype(jnp.bfloat16)
-    arrive(3)
-    samples = taps_in_ref[...]
+    copies[2].wait()
     for shard in range(SHARDS):
         four = nt(taps_ref[shard], samples[: 4 * 64])
         fifth = nt(taps_ref[shard][4 * HEAD_ROWS :], samples[4 * 64 :])
@@ -315,45 +351,41 @@
     ).astype(jnp.bfloat16)
 
 
-def coarse_tail(sources, owners, edges, tiles, depth, samples, fine_res, to_fine):
-    width = tiles.shape[1]
+def coarse_tail(gathered, edges, middle, depth, fine_res, above, beside, to_fine):
+    width = middle.shape[1]
     fine_cells, fine_ch = fine_res.shape
-    operands = (tiles, depth, samples, fine_res, to_fine, *tables())
+    operands = (middle, depth, fine_res, above, beside, to_fine, *tail_tables())
     smem, vmem, anywhere = (
         pl.BlockSpec(memory_space=space) for space in (pltpu.SMEM, pltpu.VMEM, pl.ANY)
     )
     return pl.pallas_call(
-        coarse_kernel,
+        tail_kernel,
         out_shape=(
             jax.ShapeDtypeStruct((fine_cells, fine_ch), jnp.bfloat16),
             jax.ShapeDtypeStruct((CELLS, width), jnp.bfloat16),
         ),
-        in_specs=[smem, smem] + [anywhere] * len(sources) + [vmem] * len(operands),
+        in_specs=[smem, anywhere] + [vmem] * len(operands),
         out_specs=(vmem, vmem),
         scratch_shapes=[
             pltpu.VMEM((SHARDS, BLOCK_ROWS, width), jnp.bfloat16),
             pltpu.VMEM((SHARDS, BLOCK_ROWS, width), jnp.bfloat16),
-            pltpu.VMEM((SHARDS, BLOCK_ROWS, width), jnp.bfloat16),
             pltpu.VMEM((SHARDS, TAP_ROWS, width), jnp.bfloat16),
-            pltpu.VMEM((SHARDS, BLOCK_ROWS, KEYS), jnp.float32),
             pltpu.VMEM((QUERIES, SHARDS * BLOCK_ROWS), jnp.float32),
             pltpu.VMEM((64, SHARDS * BLOCK_ROWS), jnp.float32),
+            pltpu.VMEM((256, fine_ch), jnp.float32),
+            pltpu.VMEM((512, 2 * fine_ch), jnp.float32),
             pltpu.VMEM((SHARDS * HEAD_ROWS, 128), jnp.float32),
-            pltpu.SemaphoreType.DMA((4, SHARDS)),
+            pltpu.SemaphoreType.DMA((3,)),
         ],
-        compiler_params=pltpu.CompilerParams(vmem_limit_bytes=48 * 1024 * 1024),
-    )(owners, edges, *sources, *operands)
-
-
-def around(tile):
-    for axis in ("rows", "cols"):
-        size = lax.axis_size(axis)
-        up = [(i, i + 1) for i in range(size - 1)]
-        down = [(j, i) for i, j in up]
-        tile = jnp.concatenate(
-            [tile, lax.ppermute(tile, axis, up), lax.ppermute(tile, axis, down)]
-        )
-    return jnp.pad(tile, ((0, KEYS - tile.shape[0]), (0, 0)))
+        compiler_params=pltpu.CompilerParams(vmem_limit_bytes=40 * 1024 * 1024),
+    )(edges, gathered, *operands)
+
+
+def neighbours(tile, axis):
+    size = lax.axis_size(axis)
+    up = [(i, i + 1) for i in range(size - 1)]
+    down = [(j, i) for i, j in up]
+    return lax.ppermute(tile, axis, up), lax.ppermute(tile, axis, down)
 
 
 def depthwise(padded, kernel):
@@ -389,10 +421,12 @@
     coarse_ch = coarse_in.shape[2]
     fine_cells = fine_in.shape[3]
     coarse_cells = coarse_in.shape[3]
-    pairs, singles, owners = all_shards(
-        pack(inproj_coarse, outproj_coarse, expand_coarse, shrink_coarse, to_coarse)
-    )
-    tiles = around(coarse_in.reshape(coarse_ch, coarse_cells).T)
+    gathered = lax.all_gather(pack_rest(expand_coarse, shrink_coarse, to_coarse), "rows")
+    heads = all_shards(pack_heads(inproj_coarse, outproj_coarse))
+    tile = jnp.pad(coarse_in.reshape(coarse_ch, coarse_cells).T, ((0, TILE - coarse_cells), (0, 0)))
+    above, below = neighbours(tile, "rows")
+    left, right = neighbours(jnp.concatenate([tile, above, below]), "cols")
+    coarse_mid = coarse_attention(heads, (tile, above, below, left, right))
     fine_rows = fine_cells // (2 * WIN)
     coarse_rows = coarse_cells // WIN
     fine_pic = fine_in.reshape(fine_ch, fine_rows, 2 * WIN)
@@ -424,39 +458,24 @@
         middle.astype(jnp.float32)
         + jnp.dot(shrink_fine, convolved, preferred_element_type=jnp.float32)
     ).astype(jnp.bfloat16)
-    fine_grid = fine_res.reshape(fine_ch, fine_rows, 2 * WIN)
-    above_row = passed_along(fine_grid[:, -1:, :], "rows", 1)
-    extended = jnp.concatenate([above_row, fine_grid], axis=1)
-    beside = passed_along(extended[:, :, -1:], "cols", 1)
-    extended = jnp.concatenate([beside, extended], axis=2)
-    extended = jnp.pad(extended, ((0, 0), (0, 1), (0, 1)))
-    grouped = extended.reshape(fine_ch, coarse_rows + 1, 2, WIN + 1, 2)
-    samples = []
-    for offset in range(9):
-        row_step, col_step = divmod(offset, 3)
-        sample = grouped[
-            :,
-            row_step // 2 : row_step // 2 + coarse_rows,
-            row_step % 2,
-            col_step // 2 : col_step // 2 + WIN,
-            col_step % 2,
-        ]
-        samples.append(sample.reshape(fine_ch, coarse_cells))
-    stacked = jnp.stack(samples + [jnp.zeros_like(samples[0])]).reshape(5, -1, coarse_cells)
-    stacked = jnp.pad(stacked.transpose(0, 2, 1), ((0, 0), (0, 64 - coarse_cells), (0, 0)))
+    field = fine_res.T
+    above_row = passed_along(field[-2 * WIN :], "rows", 1)
+    beside = passed_along(
+        jnp.concatenate([above_row[-1:], field[2 * WIN - 1 :: 2 * WIN]]), "cols", 1
+    )
     depth = jnp.pad(depth_coarse.reshape(9, SHARDS, -1), ((0, 0), (0, 0), (0, 4)))
     row, col = lax.axis_index("rows"), lax.axis_index("cols")
     edges = jnp.stack(
         [row > 0, row < lax.axis_size("rows") - 1, col > 0, col < lax.axis_size("cols") - 1]
     ).astype(jnp.int32)
     fine_out, coarse_out = coarse_tail(
-        pairs + singles,
-        owners,
+        gathered,
         edges,
-        tiles,
+        coarse_mid,
         depth.reshape(9, -1),
-        stacked.reshape(5 * 64, -1),
-        fine_res.reshape(fine_ch, fine_cells).T,
+        field,
+        jnp.pad(above_row, ((0, 2), (0, 0))),
+        jnp.pad(beside, ((0, 1), (0, 0))),
         to_fine,
     )
     return (fine_out.T.reshape(fine_in.shape), coarse_out.T.reshape(coarse_in.shape))

time: 185 us -> 163 us (0.88)
  the two profiles are of different devices: /device:TPU:96 before, /device:TPU:94 now
where the time goes in v3:
time: 163 us; the launch traced here: 162 us
  starting transfers between devices  63.5 us (39%)
  waiting for transfers between devices  26 us (16%)
  Pallas kernels  25 us (15%)
  local copies, waits for them, and re-layouts  16.9 us (10%)
  between operations  14.8 us (9%)
  other arithmetic  8.23 us (5%)
  matrix products  7.86 us (5%)
    ppermute x3, waiting for transfers between devices, all_shards(): held = lax.ppermute(held, 'rows', ring)  17 us
    pallas_call x1, Pallas kernels, coarse_attention(): pl.pallas_call(attention_kernel, out_shape=jax.ShapeDtypeStruct((QUERIES,...  15.8 us
    ppermute x3, starting transfers between devices, all_shards(): held = lax.ppermute(held, 'rows', ring)  13.8 us
    ppermute x4, starting transfers between devices, neighbours(): return (lax.ppermute(tile, axis, up), lax.ppermute(tile, axis, down))  12.6 us
    unnamed x44, local copies, waits for them, and re-layouts  10.6 us
    pallas_call x1, Pallas kernels, coarse_tail(): pl.pallas_call(tail_kernel, out_shape=(jax.ShapeDtypeStruct((fine_cells,...  9.22 us
    ppermute x3, starting transfers between devices, all_shards(): pairs += [held, lax.ppermute(held, 'rows', swap)]  8.79 us
    ppermute x4, waiting for transfers between devices, neighbours(): return (lax.ppermute(tile, axis, up), lax.ppermute(tile, axis, down))  7.92 us
  transfers between devices with their start and end apart: 20, of which 4 were waited for; matrix products, arithmetic and copies ran while one was open for 12% of the time, Pallas kernels for 10%

profile of v3, /device:TPU:94, one launch (start us, length us, event | category | flops | bytes accessed | tf_op | source)
XLA Modules:
  0.0 162.2 jit_solution(13986701572925320515)
XLA Ops:
  7.2 1.1 pad.33
  8.3 0.2 copy.28
  8.6 0.2 reshape.99
  8.9 0.1 pad.60.clone
  8.9 1.0 fusion.43
  10.0 1.9 %collective-permute-start = (bf16[56,624]{1,0:T(8,128)(2,1)S(1)}, bf16[56,624]{1,0:T(8,128)(2,1)S(1)}, u32[]{:S(2)}, u32[]{:S(2)}) collective-permute-start(bf16[56,624]{1,0:T(8,128)(2,1)S(1)} %pad.34.centre_ref), channel_id=1, source_target_pairs={{0,32},{32,64},{64,96},{96,128},{128,160},{160,192},{192,224},{224... | collective-permute-start | bytes 209672 | tf_op jit(solution)/shard_map/ppermute | solution.py:388
  11.9 3.6 %collective-permute-start.1 = (bf16[56,624]{1,0:T(8,128)(2,1)S(1)}, bf16[56,624]{1,0:T(8,128)(2,1)S(1)}, u32[]{:S(2)}, u32[]{:S(2)}) collective-permute-start(bf16[56,624]{1,0:T(8,128)(2,1)S(1)} %pad.34.centre_ref), channel_id=1, source_target_pairs={{32,0},{64,32},{96,64},{128,96},{160,128},{192,160},{224,192},{256... | collective-permute-start | bytes 209672 | tf_op jit(solution)/shard_map/ppermute | solution.py:388
  15.6 0.1 convert_reduce_fusion
  15.7 0.2 fusion.59
  16.0 0.5 fusion.6
  16.5 0.3 reshape_reshape_squeeze.9
  16.9 0.3 reshape_reshape_squeeze.10
  17.3 0.3 reshape_reshape_squeeze.11
  17.7 0.8 copy.33
  18.5 0.6 fusion.78
  19.0 0.4 convolution_multiply_fusion
  19.4 1.5 convolution_convert_fusion.1
  20.9 0.4 copy.36
  21.3 0.3 reshape_reshape.4
  21.6 0.2 copy-done.14
  21.8 0.4 fusion.83
  22.2 0.2 multiply_reduce_fusion
  22.5 2.7 %fusion.25 = bf16[1248,196]{0,1:T(8,128)(2,1)S(1)} fusion(bf16[1248,312]{0,1:T(8,128)(2,1)S(1)} %copy-done, f32[312,196]{0,1:T(8,128)S(1)} %get-tuple-element.23, f32[196]{0:T(256)S(1)} %add_rsqrt_fusion, f32[196]{0:T(256)S(1)} %broadcast_multiply_fusion), kind=kOutput, calls=%fused_computation.44 | convolution fusion | flops 168718368 | bytes 1514144 | tf_op jit(solution)/shard_map/dot_general | solution.py:449
  25.2 0.2 reshape.108
  25.5 2.7 %collective-permute-start.13 = (bf16[1248,1,14]{0,2,1:T(8,128)(2,1)S(1)}, bf16[1248,1,14]{0,2,1:T(8,128)(2,1)S(1)}, u32[]{:S(2)}, u32[]{:S(2)}) collective-permute-start(bf16[1248,1,14]{0,2,1:T(8,128)(2,1)S(1)} %get-tuple-element.18), channel_id=1, source_target_pairs={{0,32},{32,64},{64,96},{96,128},{128,160},{160,192},{192,224},{224... | collective-permute-start | bytes 104840 | tf_op jit(solution)/shard_map/ppermute | solution.py:26
  28.1 2.9 %collective-permute-start.14 = (bf16[1248,1,14]{0,2,1:T(8,128)(2,1)S(1)}, bf16[1248,1,14]{0,2,1:T(8,128)(2,1)S(1)}, u32[]{:S(2)}, u32[]{:S(2)}) collective-permute-start(bf16[1248,1,14]{0,2,1:T(8,128)(2,1)S(1)} %get-tuple-element.17), channel_id=1, source_target_pairs={{32,0},{64,32},{96,64},{128,96},{160,128},{192,160},{224,192},{256... | collective-permute-start | bytes 104840 | tf_op jit(solution)/shard_map/ppermute | solution.py:27
  31.1 2.7 %collective-permute-start.4 = (bf16[160,624]{1,0:T(8,128)(2,1)S(1)}, bf16[160,624]{1,0:T(8,128)(2,1)S(1)}, u32[]{:S(2)}, u32[]{:S(2)}) collective-permute-start(bf16[160,624]{1,0:T(8,128)(2,1)S(1)} %bitcast.165), channel_id=1, source_target_pairs={{0,32},{32,0},{64,96},{96,64},{128,160},{160,128},{192,224},{224,1... | collective-permute-start | bytes 599048 | tf_op jit(solution)/shard_map/ppermute | solution.py:114
  33.9 1.0 collective-permute-done.4
  34.9 4.3 %collective-permute-start.5 = (bf16[2,160,624]{2,1,0:T(8,128)(2,1)S(1)}, bf16[2,160,624]{2,1,0:T(8,128)(2,1)S(1)}, u32[]{:S(2)}, u32[]{:S(2)}) collective-permute-start(bf16[2,160,624]{2,1,0:T(8,128)(2,1)S(1)} %pad_maximum_fusion.4.refs_0_), channel_id=1, source_target_pairs={{0,64},{32,480},{64,128},{96,32},{128,192},{160,96},{192,256},{224... | collective-permute-start | bytes 1198088 | tf_op jit(solution)/shard_map/ppermute | solution.py:117
  39.2 0.1 fusion.75
  39.3 4.6 %collective-permute-start.15 = (bf16[1248,16,1]{0,2,1:T(2,128)(2,1)S(1)}, bf16[1248,16,1]{0,2,1:T(2,128)(2,1)S(1)}, u32[]{:S(2)}, u32[]{:S(2)}) collective-permute-start(bf16[1248,16,1]{0,2,1:T(2,128)(2,1)S(1)} %get-tuple-element.15), channel_id=1, source_target_pairs={{0,1},{1,2},{2,3},{3,4},{4,5},{5,6},{6,7},{7,8},{8,9},{9,10},{10,1... | collective-permute-start | bytes 119816 | tf_op jit(solution)/shard_map/ppermute | solution.py:26
  44.0 1.9 %collective-permute-start.16 = (bf16[1248,16,1]{0,2,1:T(2,128)(2,1)S(1)}, bf16[1248,16,1]{0,2,1:T(2,128)(2,1)S(1)}, u32[]{:S(2)}, u32[]{:S(2)}) collective-permute-start(bf16[1248,16,1]{0,2,1:T(2,128)(2,1)S(1)} %get-tuple-element.16), channel_id=1, source_target_pairs={{1,0},{2,1},{3,2},{4,3},{5,4},{6,5},{7,6},{8,7},{9,8},{10,9},{11,1... | collective-permute-start | bytes 119816 | tf_op jit(solution)/shard_map/ppermute | solution.py:27
  45.9 0.1 slice_reduce_fusion.8
  46.0 7.5 %collective-permute-done.5.refs_1_ = bf16[2,160,624]{2,1,0:T(8,128)(2,1)S(1)} collective-permute-done((bf16[2,160,624]{2,1,0:T(8,128)(2,1)S(1)}, bf16[2,160,624]{2,1,0:T(8,128)(2,1)S(1)}, u32[]{:S(2)}, u32[]{:S(2)}) %collective-permute-start.5) | collective-permute-done | bytes 399392 | tf_op jit(solution)/shard_map/ppermute | solution.py:117
  53.5 6.6 %collective-permute-start.7 = (bf16[2,160,624]{2,1,0:T(8,128)(2,1)S(1)}, bf16[2,160,624]{2,1,0:T(8,128)(2,1)}, u32[]{:S(2)}, u32[]{:S(2)}) collective-permute-start(bf16[2,160,624]{2,1,0:T(8,128)(2,1)S(1)} %collective-permute-done.5.refs_1_), channel_id=1, source_target_pairs={{0,64},{32,480},{64,128},{96,32},{128,192},{160,96},{192,256},{224... | collective-permute-start | bytes 1198088 | tf_op jit(solution)/shard_map/ppermute | solution.py:117
  60.1 5.8 %fusion.14 = bf16[1248,14,14]{0,2,1:T(8,128)(2,1)S(1)} fusion(bf16[1248,14,14]{0,2,1:T(8,128)(2,1)S(1)} %reshape.108, bf16[1248,16,14]{0,2,1:T(8,128)(2,1)S(1)} %constant_dynamic-update-slice_fusion, bf16[1248,16,1]{0,2,1:T(2,128)(2,1)S(1)} %collective-permute-done.16, bf16[1248,16,1]{0,2,1:T(2,128)(2,1)S(1)} %collective-permute-done.15, ...), kind=kLoop, calls=%fused_computation.24 | loop fusion | flops 28129920 | bytes 1732224 | tf_op jit(solution)/shard_map/convert_element_type | solution.py:454
  65.9 1.0 reshape.109
  66.9 9.5 %collective-permute-done.7.refs_3_ = bf16[2,160,624]{2,1,0:T(8,128)(2,1)} collective-permute-done((bf16[2,160,624]{2,1,0:T(8,128)(2,1)S(1)}, bf16[2,160,624]{2,1,0:T(8,128)(2,1)}, u32[]{:S(2)}, u32[]{:S(2)}) %collective-permute-start.7) | collective-permute-done | bytes 399392 | tf_op jit(solution)/shard_map/ppermute | solution.py:117
  76.5 2.9 %collective-permute-start.9 = (bf16[2,160,624]{2,1,0:T(8,128)(2,1)}, bf16[2,160,624]{2,1,0:T(8,128)(2,1)S(1)}, u32[]{:S(2)}, u32[]{:S(2)}) collective-permute-start(bf16[2,160,624]{2,1,0:T(8,128)(2,1)} %collective-permute-done.7.refs_3_), channel_id=1, source_target_pairs={{0,64},{32,480},{64,128},{96,32},{128,192},{160,96},{192,256},{224... | collective-permute-start | bytes 1198088 | tf_op jit(solution)/shard_map/ppermute | solution.py:117
  79.4 1.8 %fusion.22.fine_ref = bf16[196,312]{1,0:T(8,128)(2,1)S(1)} fusion(f32[312,196]{0,1:T(8,128)S(1)} %get-tuple-element.23, bf16[1248,196]{0,1:T(8,128)(2,1)} %reshape.109, bf16[312,1248]{1,0:T(8,128)(2,1)} %param.27), kind=kOutput, calls=%fused_computation.41 | convolution fusion | flops 152757696 | bytes 1634880 | tf_op jit(solution)/shard_map/dot_general | solution.py:459
  81.2 1.9 %collective-permute-start.17 = (bf16[14,312]{1,0:T(8,128)(2,1)S(1)}, bf16[14,312]{1,0:T(8,128)(2,1)S(1)}, u32[]{:S(2)}, u32[]{:S(2)}) collective-permute-start(bf16[14,312]{1,0:T(8,128)(2,1)S(1)} %slice.144), channel_id=1, source_target_pairs={{0,32},{32,64},{64,96},{96,128},{128,160},{160,192},{192,224},{224... | collective-permute-start | bytes 26216 | tf_op jit(solution)/shard_map/ppermute | solution.py:35
  83.2 0.7 pad_maximum_fusion.5
  83.9 4.6 %collective-permute-start.2 = (bf16[168,624]{1,0:T(8,128)(2,1)}, bf16[168,624]{1,0:T(8,128)(2,1)S(1)}, u32[]{:S(2)}, u32[]{:S(2)}) collective-permute-start(bf16[168,624]{1,0:T(8,128)(2,1)} %pad_maximum_fusion.5), channel_id=1, source_target_pairs={{0,1},{1,2},{2,3},{3,4},{4,5},{5,6},{6,7},{7,8},{8,9},{9,10},{10,1... | collective-permute-start | bytes 629000 | tf_op jit(solution)/shard_map/ppermute | solution.py:388
  88.6 3.6 %collective-permute-start.18 = (bf16[15,312]{1,0:T(8,128)(2,1)S(1)}, bf16[15,312]{1,0:T(8,128)(2,1)S(1)}, u32[]{:S(2)}, u32[]{:S(2)}) collective-permute-start(bf16[15,312]{1,0:T(8,128)(2,1)S(1)} %pad_maximum_fusion.6), channel_id=1, source_target_pairs={{0,1},{1,2},{2,3},{3,4},{4,5},{5,6},{6,7},{7,8},{8,9},{9,10},{10,1... | collective-permute-start | bytes 28088 | tf_op jit(solution)/shard_map/ppermute | solution.py:35
  92.2 4.9 %collective-permute-start.6 = (bf16[2,160,624]{2,1,0:T(8,128)(2,1)S(1)}, bf16[2,160,624]{2,1,0:T(8,128)(2,1)}, u32[]{:S(2)}, u32[]{:S(2)}) collective-permute-start(bf16[2,160,624]{2,1,0:T(8,128)(2,1)S(1)} %collective-permute-done.5.refs_1_), channel_id=1, source_target_pairs={{0,32},{32,0},{64,96},{96,64},{128,160},{160,128},{192,224},{224,1... | collective-permute-start | bytes 1198088 | tf_op jit(solution)/shard_map/ppermute | solution.py:118
  97.1 1.9 %collective-permute-start.8 = (bf16[2,160,624]{2,1,0:T(8,128)(2,1)}, bf16[2,160,624]{2,1,0:T(8,128)(2,1)}, u32[]{:S(2)}, u32[]{:S(2)}) collective-permute-start(bf16[2,160,624]{2,1,0:T(8,128)(2,1)} %collective-permute-done.7.refs_3_), channel_id=1, source_target_pairs={{0,32},{32,0},{64,96},{96,64},{128,160},{160,128},{192,224},{224,1... | collective-permute-start | bytes 1198088 | tf_op jit(solution)/shard_map/ppermute | solution.py:118
  99.1 5.7 %collective-permute-start.11 = (bf16[160,624]{1,0:T(8,128)(2,1)S(1)}, bf16[160,624]{1,0:T(8,128)(2,1)}, u32[]{:S(2)}, u32[]{:S(2)}) collective-permute-start(bf16[160,624]{1,0:T(8,128)(2,1)S(1)} %slice_bitcast_fusion), channel_id=1, source_target_pairs={{0,64},{32,480},{64,128},{96,32},{128,192},{160,96},{192,256},{224... | collective-permute-start | bytes 599048 | tf_op jit(solution)/shard_map/ppermute | solution.py:119
  104.8 1.9 %collective-permute-start.10 = (bf16[2,160,624]{2,1,0:T(8,128)(2,1)S(1)}, bf16[2,160,624]{2,1,0:T(8,128)(2,1)}, u32[]{:S(2)}, u32[]{:S(2)}) collective-permute-start(bf16[2,160,624]{2,1,0:T(8,128)(2,1)S(1)} %collective-permute-done.9.refs_5_), channel_id=1, source_target_pairs={{0,32},{32,0},{64,96},{96,64},{128,160},{160,128},{192,224},{224,1... | collective-permute-start | bytes 1198088 | tf_op jit(solution)/shard_map/ppermute | solution.py:118
  106.7 2.5 %collective-permute-start.3 = (bf16[168,624]{1,0:T(8,128)(2,1)}, bf16[168,624]{1,0:T(8,128)(2,1)}, u32[]{:S(2)}, u32[]{:S(2)}) collective-permute-start(bf16[168,624]{1,0:T(8,128)(2,1)} %pad_maximum_fusion.5), channel_id=1, source_target_pairs={{1,0},{2,1},{3,2},{4,3},{5,4},{6,5},{7,6},{8,7},{9,8},{10,9},{11,1... | collective-permute-start | bytes 629000 | tf_op jit(solution)/shard_map/ppermute | solution.py:388
  109.2 2.3 %collective-permute-start.12 = (bf16[160,624]{1,0:T(8,128)(2,1)}, bf16[160,624]{1,0:T(8,128)(2,1)}, u32[]{:S(2)}, u32[]{:S(2)}) collective-permute-start(bf16[160,624]{1,0:T(8,128)(2,1)} %collective-permute-done.11.refs_7_), channel_id=1, source_target_pairs={{0,32},{32,0},{64,96},{96,64},{128,160},{160,128},{192,224},{224,1... | collective-permute-start | bytes 599048 | tf_op jit(solution)/shard_map/ppermute | solution.py:120
  111.5 0.2 reshape.102
  111.8 0.1 reshape.103.depth_ref
  111.9 0.1 add_convert_fusion.edge_ref
  112.1 7.9 %collective-permute-done.3.right_ref = bf16[168,624]{1,0:T(8,128)(2,1)} collective-permute-done((bf16[168,624]{1,0:T(8,128)(2,1)}, bf16[168,624]{1,0:T(8,128)(2,1)}, u32[]{:S(2)}, u32[]{:S(2)}) %collective-permute-start.3) | collective-permute-done | bytes 209696 | tf_op jit(solution)/shard_map/ppermute | solution.py:388
  120.0 0.9 copy-done.6
  120.9 0.9 copy-done.7
  121.9 0.9 copy-done.8
  122.7 15.8 %shard_map.212.middle_ref = bf16[96,624]{1,0:T(8,128)(2,1)S(1)} custom-call(bf16[56,624]{1,0:T(8,128)(2,1)S(1)} %pad.34.centre_ref, bf16[56,624]{1,0:T(8,128)(2,1)S(1)} %collective-permute-done.above_ref, bf16[56,624]{1,0:T(8,128)(2,1)S(1)} %collective-permute-done.1.below_ref, bf16[168,624]{1,0:T(8,128)(2,1)S(1)} %copy-done.6, ...), custom_call_target="tpu_custom_call" | custom-call | tf_op jit(solution)/shard_map/pallas_call | solution.py:241
  138.6 4.1 %copy-done.1 = bf16[8448,624]{1,0:T(8,128)(2,1)S(1)} copy-done((bf16[8448,624]{1,0:T(8,128)(2,1)S(1)}, bf16[8448,624]{1,0:T(8,128)(2,1)}, u32[]{:S(2)}) %copy-start.1) | copy-done | bytes 10543128
  142.7 1.0 copy-done.3
  143.7 1.0 copy-done.4
  144.7 0.8 copy-done.9
  145.5 0.7 copy-done.11
  146.2 9.2 %shard_map.213 = (bf16[196,312]{1,0:T(8,128)(2,1)}, bf16[49,624]{1,0:T(8,128)(2,1)}) custom-call(s32[4]{0:T(128)S(1)} %add_convert_fusion.edge_ref, bf16[16,528,624]{2,1,0:T(8,128)(2,1)S(1)} %bitcast.158, bf16[96,624]{1,0:T(8,128)(2,1)S(1)} %shard_map.212.middle_ref, f32[9,2560]{1,0:T(8,128)S(1)} %reshape.103.depth_ref, ...), custom_call_target="tpu_custom_call" | custom-call | tf_op jit(solution)/shard_map/pallas_call | solution.py:361
  (79 shorter events, 0.7 us)
Async XLA Ops:
  7.2 15.3 %copy-start = (bf16[1248,312]{0,1:T(8,128)(2,1)S(1)}, bf16[1248,312]{0,1:T(8,128)(2,1)}, u32[]{:S(2)}) copy-start(bf16[1248,312]{0,1:T(8,128)(2,1)} %param.25) | copy-start | bytes 2336260
  7.2 1.7 %copy-start.15 = (bf16[624,156]{0,1:T(8,128)(2,1)S(1)}, bf16[624,156]{0,1:T(8,128)(2,1)}, u32[]{:S(2)}) copy-start(bf16[624,156]{0,1:T(8,128)(2,1)} %param.32) | copy-start | bytes 584068
  7.2 1.7 %copy-start.16 = (bf16[156,624]{1,0:T(8,128)(2,1)S(1)}, bf16[156,624]{1,0:T(8,128)(2,1)}, u32[]{:S(2)}) copy-start(bf16[156,624]{1,0:T(8,128)(2,1)} %param.30) | copy-start | bytes 584068
  7.2 131.4 %all-gather.3.cloned.1.call-start = ((), (), s32[]{:S(2)}) async-start(), calls=%async_computation | async-start | bytes 11489280 | tf_op jit(solution)/shard_map/all_gather | solution.py:424
  8.8 1.2 copy-start.18
  8.8 6.8 %copy-start.12 = (bf16[1,1,312,196]{2,3,1,0:T(8,128)(2,1)S(1)}, bf16[1,1,312,196]{2,3,1,0:T(8,128)(2,1)}, u32[]{:S(2)}) copy-start(bf16[1,1,312,196]{2,3,1,0:T(8,128)(2,1)} %param.21) | copy-start | bytes 366916
  8.9 7.0 %copy-start.13 = (bf16[3,312,312]{2,1,0:T(8,128)(2,1)S(1)}, bf16[3,312,312]{2,1,0:T(8,128)(2,1)}, u32[]{:S(2)}) copy-start(bf16[3,312,312]{2,1,0:T(8,128)(2,1)} %param.23) | copy-start | bytes 1752196
  10.0 73.2 %collective-permute-start = (bf16[56,624]{1,0:T(8,128)(2,1)S(1)}, bf16[56,624]{1,0:T(8,128)(2,1)S(1)}, u32[]{:S(2)}, u32[]{:S(2)}) collective-permute-start(bf16[56,624]{1,0:T(8,128)(2,1)S(1)} %pad.34.centre_ref), channel_id=1, source_target_pairs={{0,32},{32,64},{64,96},{96,128},{128,160},{160,192},{192,224},{224... | collective-permute-start | bytes 209672 | tf_op jit(solution)/shard_map/ppermute | solution.py:388
  11.9 71.2 %collective-permute-start.1 = (bf16[56,624]{1,0:T(8,128)(2,1)S(1)}, bf16[56,624]{1,0:T(8,128)(2,1)S(1)}, u32[]{:S(2)}, u32[]{:S(2)}) collective-permute-start(bf16[56,624]{1,0:T(8,128)(2,1)S(1)} %pad.34.centre_ref), channel_id=1, source_target_pairs={{32,0},{64,32},{96,64},{128,96},{160,128},{192,160},{224,192},{256... | collective-permute-start | bytes 209672 | tf_op jit(solution)/shard_map/ppermute | solution.py:388
  20.9 0.9 copy-start.14
  25.2 5.8 %slice-start = ((bf16[3,39,624]{2,1,0:T(8,128)(2,1)}), bf16[2,39,624]{2,1,0:T(8,128)(2,1)S(1)}, s32[]{:S(2)}) async-start(bf16[3,39,624]{2,1,0:T(8,128)(2,1)} %param.28), calls=%async_computation.1 | async-start | bytes 204800 | tf_op jit(solution)/shard_map/slice | solution.py:93
  25.2 5.8 %slice-start.1 = ((bf16[3,39,624]{2,1,0:T(8,128)(2,1)}), bf16[1,39,624]{2,1,0:T(8,128)(2,1)S(1)}, s32[]{:S(2)}) async-start(bf16[3,39,624]{2,1,0:T(8,128)(2,1)} %param.28), calls=%async_computation.2 | async-start | bytes 102400 | tf_op jit(solution)/shard_map/slice | solution.py:93
  25.2 5.8 %copy-start.19 = (bf16[624,39]{0,1:T(8,128)(2,1)S(1)}, bf16[624,39]{0,1:T(8,128)(2,1)}, u32[]{:S(2)}) copy-start(bf16[624,39]{0,1:T(8,128)(2,1)} %param.29) | copy-start | bytes 146020
  25.5 8.3 %collective-permute-start.13 = (bf16[1248,1,14]{0,2,1:T(8,128)(2,1)S(1)}, bf16[1248,1,14]{0,2,1:T(8,128)(2,1)S(1)}, u32[]{:S(2)}, u32[]{:S(2)}) collective-permute-start(bf16[1248,1,14]{0,2,1:T(8,128)(2,1)S(1)} %get-tuple-element.18), channel_id=1, source_target_pairs={{0,32},{32,64},{64,96},{96,128},{128,160},{160,192},{192,224},{224... | collective-permute-start | bytes 104840 | tf_op jit(solution)/shard_map/ppermute | solution.py:26
  28.1 5.7 %collective-permute-start.14 = (bf16[1248,1,14]{0,2,1:T(8,128)(2,1)S(1)}, bf16[1248,1,14]{0,2,1:T(8,128)(2,1)S(1)}, u32[]{:S(2)}, u32[]{:S(2)}) collective-permute-start(bf16[1248,1,14]{0,2,1:T(8,128)(2,1)S(1)} %get-tuple-element.17), channel_id=1, source_target_pairs={{32,0},{64,32},{96,64},{128,96},{160,128},{192,160},{224,192},{256... | collective-permute-start | bytes 104840 | tf_op jit(solution)/shard_map/ppermute | solution.py:27
  31.1 3.7 %collective-permute-start.4 = (bf16[160,624]{1,0:T(8,128)(2,1)S(1)}, bf16[160,624]{1,0:T(8,128)(2,1)S(1)}, u32[]{:S(2)}, u32[]{:S(2)}) collective-permute-start(bf16[160,624]{1,0:T(8,128)(2,1)S(1)} %bitcast.165), channel_id=1, source_target_pairs={{0,32},{32,0},{64,96},{96,64},{128,160},{160,128},{192,224},{224,1... | collective-permute-start | bytes 599048 | tf_op jit(solution)/shard_map/ppermute | solution.py:114
  33.8 12.1 %copy-start.20 = (f32[9,1248]{1,0:T(8,128)S(1)}, f32[9,1248]{1,0:T(8,128)}, u32[]{:S(2)}) copy-start(f32[9,1248]{1,0:T(8,128)} %param.26) | copy-start | bytes 134788
  34.9 18.6 %collective-permute-start.5 = (bf16[2,160,624]{2,1,0:T(8,128)(2,1)S(1)}, bf16[2,160,624]{2,1,0:T(8,128)(2,1)S(1)}, u32[]{:S(2)}, u32[]{:S(2)}) collective-permute-start(bf16[2,160,624]{2,1,0:T(8,128)(2,1)S(1)} %pad_maximum_fusion.4.refs_0_), channel_id=1, source_target_pairs={{0,64},{32,480},{64,128},{96,32},{128,192},{160,96},{192,256},{224... | collective-permute-start | bytes 1198088 | tf_op jit(solution)/shard_map/ppermute | solution.py:117
  39.3 20.8 %collective-permute-start.15 = (bf16[1248,16,1]{0,2,1:T(2,128)(2,1)S(1)}, bf16[1248,16,1]{0,2,1:T(2,128)(2,1)S(1)}, u32[]{:S(2)}, u32[]{:S(2)}) collective-permute-start(bf16[1248,16,1]{0,2,1:T(2,128)(2,1)S(1)} %get-tuple-element.15), channel_id=1, source_target_pairs={{0,1},{1,2},{2,3},{3,4},{4,5},{5,6},{6,7},{7,8},{8,9},{9,10},{10,1... | collective-permute-start | bytes 119816 | tf_op jit(solution)/shard_map/ppermute | solution.py:26
  44.0 16.2 %collective-permute-start.16 = (bf16[1248,16,1]{0,2,1:T(2,128)(2,1)S(1)}, bf16[1248,16,1]{0,2,1:T(2,128)(2,1)S(1)}, u32[]{:S(2)}, u32[]{:S(2)}) collective-permute-start(bf16[1248,16,1]{0,2,1:T(2,128)(2,1)S(1)} %get-tuple-element.16), channel_id=1, source_target_pairs={{1,0},{2,1},{3,2},{4,3},{5,4},{6,5},{7,6},{8,7},{9,8},{10,9},{11,1... | collective-permute-start | bytes 119816 | tf_op jit(solution)/shard_map/ppermute | solution.py:27
  53.5 23.0 %collective-permute-start.7 = (bf16[2,160,624]{2,1,0:T(8,128)(2,1)S(1)}, bf16[2,160,624]{2,1,0:T(8,128)(2,1)}, u32[]{:S(2)}, u32[]{:S(2)}) collective-permute-start(bf16[2,160,624]{2,1,0:T(8,128)(2,1)S(1)} %collective-permute-done.5.refs_1_), channel_id=1, source_target_pairs={{0,64},{32,480},{64,128},{96,32},{128,192},{160,96},{192,256},{224... | collective-permute-start | bytes 1198088 | tf_op jit(solution)/shard_map/ppermute | solution.py:117
  66.9 44.6 %copy-start.17 = (f32[9,2496]{1,0:T(8,128)S(1)}, f32[9,2496]{1,0:T(8,128)}, u32[]{:S(2)}) copy-start(f32[9,2496]{1,0:T(8,128)} %param.31) | copy-start | bytes 269572
  76.5 22.6 %collective-permute-start.9 = (bf16[2,160,624]{2,1,0:T(8,128)(2,1)}, bf16[2,160,624]{2,1,0:T(8,128)(2,1)S(1)}, u32[]{:S(2)}, u32[]{:S(2)}) collective-permute-start(bf16[2,160,624]{2,1,0:T(8,128)(2,1)} %collective-permute-done.7.refs_3_), channel_id=1, source_target_pairs={{0,64},{32,480},{64,128},{96,32},{128,192},{160,96},{192,256},{224... | collective-permute-start | bytes 1198088 | tf_op jit(solution)/shard_map/ppermute | solution.py:117
  81.2 7.3 %collective-permute-start.17 = (bf16[14,312]{1,0:T(8,128)(2,1)S(1)}, bf16[14,312]{1,0:T(8,128)(2,1)S(1)}, u32[]{:S(2)}, u32[]{:S(2)}) collective-permute-start(bf16[14,312]{1,0:T(8,128)(2,1)S(1)} %slice.144), channel_id=1, source_target_pairs={{0,32},{32,64},{64,96},{96,128},{128,160},{160,192},{192,224},{224... | collective-permute-start | bytes 26216 | tf_op jit(solution)/shard_map/ppermute | solution.py:35
  83.9 22.8 %collective-permute-start.2 = (bf16[168,624]{1,0:T(8,128)(2,1)}, bf16[168,624]{1,0:T(8,128)(2,1)S(1)}, u32[]{:S(2)}, u32[]{:S(2)}) collective-permute-start(bf16[168,624]{1,0:T(8,128)(2,1)} %pad_maximum_fusion.5), channel_id=1, source_target_pairs={{0,1},{1,2},{2,3},{3,4},{4,5},{5,6},{6,7},{7,8},{8,9},{9,10},{10,1... | collective-permute-start | bytes 629000 | tf_op jit(solution)/shard_map/ppermute | solution.py:388
  88.6 16.2 %collective-permute-start.18 = (bf16[15,312]{1,0:T(8,128)(2,1)S(1)}, bf16[15,312]{1,0:T(8,128)(2,1)S(1)}, u32[]{:S(2)}, u32[]{:S(2)}) collective-permute-start(bf16[15,312]{1,0:T(8,128)(2,1)S(1)} %pad_maximum_fusion.6), channel_id=1, source_target_pairs={{0,1},{1,2},{2,3},{3,4},{4,5},{5,6},{6,7},{7,8},{8,9},{9,10},{10,1... | collective-permute-start | bytes 28088 | tf_op jit(solution)/shard_map/ppermute | solution.py:35
  92.2 27.8 %collective-permute-start.6 = (bf16[2,160,624]{2,1,0:T(8,128)(2,1)S(1)}, bf16[2,160,624]{2,1,0:T(8,128)(2,1)}, u32[]{:S(2)}, u32[]{:S(2)}) collective-permute-start(bf16[2,160,624]{2,1,0:T(8,128)(2,1)S(1)} %collective-permute-done.5.refs_1_), channel_id=1, source_target_pairs={{0,32},{32,0},{64,96},{96,64},{128,160},{160,128},{192,224},{224,1... | collective-permute-start | bytes 1198088 | tf_op jit(solution)/shard_map/ppermute | solution.py:118
  97.1 22.9 %collective-permute-start.8 = (bf16[2,160,624]{2,1,0:T(8,128)(2,1)}, bf16[2,160,624]{2,1,0:T(8,128)(2,1)}, u32[]{:S(2)}, u32[]{:S(2)}) collective-permute-start(bf16[2,160,624]{2,1,0:T(8,128)(2,1)} %collective-permute-done.7.refs_3_), channel_id=1, source_target_pairs={{0,32},{32,0},{64,96},{96,64},{128,160},{160,128},{192,224},{224,1... | collective-permute-start | bytes 1198088 | tf_op jit(solution)/shard_map/ppermute | solution.py:118
  99.1 10.1 %collective-permute-start.11 = (bf16[160,624]{1,0:T(8,128)(2,1)S(1)}, bf16[160,624]{1,0:T(8,128)(2,1)}, u32[]{:S(2)}, u32[]{:S(2)}) collective-permute-start(bf16[160,624]{1,0:T(8,128)(2,1)S(1)} %slice_bitcast_fusion), channel_id=1, source_target_pairs={{0,64},{32,480},{64,128},{96,32},{128,192},{160,96},{192,256},{224... | collective-permute-start | bytes 599048 | tf_op jit(solution)/shard_map/ppermute | solution.py:119
  104.8 15.2 %collective-permute-start.10 = (bf16[2,160,624]{2,1,0:T(8,128)(2,1)S(1)}, bf16[2,160,624]{2,1,0:T(8,128)(2,1)}, u32[]{:S(2)}, u32[]{:S(2)}) collective-permute-start(bf16[2,160,624]{2,1,0:T(8,128)(2,1)S(1)} %collective-permute-done.9.refs_5_), channel_id=1, source_target_pairs={{0,32},{32,0},{64,96},{96,64},{128,160},{160,128},{192,224},{224,1... | collective-permute-start | bytes 1198088 | tf_op jit(solution)/shard_map/ppermute | solution.py:118
  106.7 5.3 %copy-start.5 = (bf16[168,624]{1,0:T(8,128)(2,1)}, bf16[168,624]{1,0:T(8,128)(2,1)S(1)}, u32[]{:S(2)}) copy-start(bf16[168,624]{1,0:T(8,128)(2,1)S(1)} %collective-permute-done.2.left_ref) | copy-start | bytes 628996
  106.7 13.2 %collective-permute-start.3 = (bf16[168,624]{1,0:T(8,128)(2,1)}, bf16[168,624]{1,0:T(8,128)(2,1)}, u32[]{:S(2)}, u32[]{:S(2)}) collective-permute-start(bf16[168,624]{1,0:T(8,128)(2,1)} %pad_maximum_fusion.5), channel_id=1, source_target_pairs={{1,0},{2,1},{3,2},{4,3},{5,4},{6,5},{7,6},{8,7},{9,8},{10,9},{11,1... | collective-permute-start | bytes 629000 | tf_op jit(solution)/shard_map/ppermute | solution.py:388
  109.2 10.8 %collective-permute-start.12 = (bf16[160,624]{1,0:T(8,128)(2,1)}, bf16[160,624]{1,0:T(8,128)(2,1)}, u32[]{:S(2)}, u32[]{:S(2)}) collective-permute-start(bf16[160,624]{1,0:T(8,128)(2,1)} %collective-permute-done.11.refs_7_), channel_id=1, source_target_pairs={{0,32},{32,0},{64,96},{96,64},{128,160},{160,128},{192,224},{224,1... | collective-permute-start | bytes 599048 | tf_op jit(solution)/shard_map/ppermute | solution.py:120
  112.0 26.6 %copy-start.10 = (bf16[64,96]{1,0:T(8,128)(2,1)S(1)}, bf16[64,96]{1,0:T(8,128)(2,1)}, u32[]{:S(2)}) copy-start(bf16[64,96]{1,0:T(8,128)(2,1)} %constant.169.centre_ref) | copy-start | bytes 36868
  112.0 26.6 %copy-start.2 = (bf16[640,624]{1,0:T(8,128)(2,1)S(1)}, bf16[640,624]{1,0:T(8,128)(2,1)}, u32[]{:S(2)}) copy-start(bf16[640,624]{1,0:T(8,128)(2,1)} %constant.173.order_ref) | copy-start | bytes 2396164
  120.0 0.9 copy-start.6
  120.9 0.9 copy-start.7
  121.8 0.9 copy-start.8
  138.6 4.1 %copy-start.1 = (bf16[8448,624]{1,0:T(8,128)(2,1)S(1)}, bf16[8448,624]{1,0:T(8,128)(2,1)}, u32[]{:S(2)}) copy-start(bf16[8448,624]{1,0:T(8,128)(2,1)} %all-gather.3.cloned.1.call-done) | copy-start | bytes 31629316
  142.7 1.0 copy-start.3
  143.7 1.0 copy-start.4
  144.7 0.8 copy-start.9
  145.5 0.7 copy-start.11
Sparse Core Ops, SparseCore 0:
  10.2 84.6 all-gather.2

commit v4 on v3

--- a/solution.py
+++ b/solution.py
@@ -89,36 +89,19 @@
 BESIDE = 216
 
 
-def pack_heads(inproj, outproj):
+def pack(inproj, outproj, expand, shrink, to_coarse):
+    width = expand.shape[-1]
     heads = jnp.concatenate([outproj.T[None], inproj[2:], inproj[:2]])
-    return jnp.pad(heads, ((0, 0), (0, 1), (0, 0))).reshape(BLOCK_ROWS, -1)
-
-
-def pack_rest(expand, shrink, to_coarse):
-    width = expand.shape[-1]
     taps = jnp.pad(to_coarse, ((0, 1), (0, 1), (0, 0))).reshape(5, 2, HEAD_ROWS, -1)
     return jnp.concatenate(
         [
+            jnp.pad(heads, ((0, 0), (0, 1), (0, 0))).reshape(BLOCK_ROWS, -1),
             jnp.pad(expand, ((0, 4), (0, 0))),
             jnp.pad(shrink.T, ((0, 4), (0, 0))),
             taps.transpose(0, 2, 1, 3).reshape(-1, width),
             jnp.zeros((8, width), expand.dtype),
         ]
     )
-
-
-def all_shards(mine):
-    size = lax.axis_size("rows")
-    swap = [(i, i ^ 1) for i in range(size)]
-    ring = [(i, (i + (2 if i % 2 == 0 else -2)) % size) for i in range(size)]
-    held = jnp.stack([mine, lax.ppermute(mine, "rows", swap)])
-    pairs = [held]
-    for _ in range(3):
-        held = lax.ppermute(held, "rows", ring)
-        pairs += [held, lax.ppermute(held, "rows", swap)]
-    last = lax.ppermute(held[0], "rows", ring)
-    singles = [last, lax.ppermute(last, "rows", swap)]
-    return pairs + singles
 
 
 def attention_tables():
@@ -136,17 +119,11 @@
     return jnp.asarray(bias), jnp.asarray(pick).astype(jnp.bfloat16)
 
 
-def tail_tables():
+def sample_table():
     side = 2 * WIN
-    centre = np.zeros((64, QUERIES), np.float32)
-    repeat = np.zeros((side * side, 64), np.float32)
-    compact = np.zeros((CELLS, 64), np.float32)
     sample = np.zeros((5 * 64, 512), np.float32)
-    order = np.zeros((SHARDS * HEAD_ROWS, SHARDS * 39), np.float32)
     for cell in range(CELLS):
         row, col = divmod(cell, WIN)
-        centre[row * 8 + col, (row + 1) * RING + col + 1] = 1
-        compact[cell, row * 8 + col] = 1
         for tap in range(9):
             down, right = 2 * row + tap // 3 - 1, 2 * col + tap % 3 - 1
             if right < 0:
@@ -156,15 +133,22 @@
             else:
                 source = down * side + right
             sample[tap // 2 * 64 + cell, tap % 2 * 256 + source] = 1
+    return jnp.asarray(sample).astype(jnp.bfloat16)
+
+
+def cell_tables():
+    side = 2 * WIN
+    centre = np.zeros((64, QUERIES), np.float32)
+    repeat = np.zeros((side * side, 64), np.float32)
+    compact = np.zeros((CELLS, 64), np.float32)
+    for cell in range(CELLS):
+        row, col = divmod(cell, WIN)
+        centre[row * 8 + col, (row + 1) * RING + col + 1] = 1
+        compact[cell, row * 8 + col] = 1
     for cell in range(side * side):
         row, col = divmod(cell, side)
         repeat[cell, row // 2 * 8 + col // 2] = 1
-    for shard in range(SHARDS):
-        for row in range(39):
-            order[shard * HEAD_ROWS + row, shard * 39 + row] = 1
-    return tuple(
-        jnp.asarray(t).astype(jnp.bfloat16) for t in (centre, repeat, compact, sample, order)
-    )
+    return tuple(jnp.asarray(t).astype(jnp.bfloat16) for t in (centre, repeat, compact))
 
 
 def gelu(values):
@@ -190,22 +174,9 @@
     )
 
 
-def attention_kernel(
-    centre_ref,
-    above_ref,
-    below_ref,
-    left_ref,
-    right_ref,
-    bias_ref,
-    pick_ref,
-    *refs,
+def tiles_kernel(
+    centre_ref, above_ref, below_ref, left_ref, right_ref, pick_ref, normed_ref, own_ref, tiles_ref
 ):
-    sources, (middle_ref, heads_ref, tiles_ref, proj_ref, sems) = refs[:9], refs[9:]
-    copies = []
-    for index, source in enumerate(sources):
-        target = heads_ref.at[pl.ds(2 * index, 2)] if index < 7 else heads_ref.at[7 + index]
-        copies.append(pltpu.make_async_copy(source, target, sems.at[index]))
-        copies[-1].start()
     tiles_ref[9 * TILE :, :] = jnp.zeros((KEYS - 9 * TILE, tiles_ref.shape[1]), jnp.float32)
     first = 0
     for piece in (centre_ref, above_ref, below_ref, left_ref, right_ref):
@@ -213,76 +184,88 @@
         tiles_ref[first : first + count, :] = piece[...].astype(jnp.float32)
         first += count
     tiles = tiles_ref[...]
-    normed = norm_rows(tiles)
-    pick = pick_ref[...]
-    mixed = nn(pick, tiles.astype(jnp.bfloat16))
-    for copy in copies:
-        copy.wait()
-    heads = heads_ref[...].reshape(SHARDS * BLOCK_ROWS, tiles.shape[1])
-    proj_ref[...] = nt(heads, normed).reshape(SHARDS, BLOCK_ROWS, KEYS)
-    for head in range(SHARDS):
-        values = proj_ref[head, HEAD_ROWS : 2 * HEAD_ROWS].astype(jnp.bfloat16)
-        queries = proj_ref[head, 2 * HEAD_ROWS : 3 * HEAD_ROWS].astype(jnp.bfloat16)
-        keys = proj_ref[head, 3 * HEAD_ROWS :].astype(jnp.bfloat16)
-        chosen = nt(pick, queries).astype(jnp.bfloat16)
-        scores = nn(chosen, keys) * (1.0 / math.sqrt(39)) + bias_ref[...]
-        exponent = jnp.exp(scores - jnp.max(scores, axis=1, keepdims=True))
-        total = jnp.sum(exponent, axis=1, keepdims=True)
-        probabilities = (exponent * (1.0 / total)).astype(jnp.bfloat16)
-        attended = nt(probabilities, values).astype(jnp.bfloat16)
-        mixed += nn(attended, heads_ref[head][:HEAD_ROWS])
-    middle_ref[...] = mixed.astype(jnp.bfloat16)
-
-
-def coarse_attention(sources, tiles):
+    normed_ref[...] = norm_rows(tiles)
+    own_ref[...] = nn(pick_ref[...], tiles.astype(jnp.bfloat16)).astype(jnp.bfloat16)
+
+
+def normed_tiles(tiles, pick):
     width = tiles[0].shape[1]
-    operands = (*tiles, *attention_tables())
-    vmem, anywhere = (pl.BlockSpec(memory_space=space) for space in (pltpu.VMEM, pl.ANY))
+    vmem = pl.BlockSpec(memory_space=pltpu.VMEM)
     return pl.pallas_call(
-        attention_kernel,
-        out_shape=jax.ShapeDtypeStruct((QUERIES, width), jnp.bfloat16),
-        in_specs=[vmem] * len(operands) + [anywhere] * len(sources),
+        tiles_kernel,
+        out_shape=(
+            jax.ShapeDtypeStruct((KEYS, width), jnp.bfloat16),
+            jax.ShapeDtypeStruct((QUERIES, width), jnp.bfloat16),
+        ),
+        in_specs=[vmem] * 6,
+        out_specs=(vmem, vmem),
+        scratch_shapes=[pltpu.VMEM((KEYS, width), jnp.float32)],
+        compiler_params=pltpu.CompilerParams(vmem_limit_bytes=16 * 1024 * 1024),
+    )(*tiles, pick)
+
+
+def sample_kernel(fine_ref, above_ref, beside_ref, sample_ref, samples_ref, field_ref, twice_ref):
+    channels = fine_ref.shape[1]
+    field_ref[...] = jnp.zeros(field_ref.shape, jnp.float32)
+    field_ref[: fine_ref.shape[0], :] = fine_ref[...].astype(jnp.float32)
+    field_ref[ABOVE : ABOVE + 16, :] = above_ref[...].astype(jnp.float32)
+    field_ref[BESIDE : BESIDE + 16, :] = beside_ref[...].astype(jnp.float32)
+    twice_ref[...] = jnp.zeros(twice_ref.shape, jnp.float32)
+    twice_ref[:256, :channels] = field_ref[...]
+    twice_ref[256:, channels:] = field_ref[...]
+    samples_ref[...] = nn(sample_ref[...], twice_ref[...].astype(jnp.bfloat16)).astype(jnp.bfloat16)
+
+
+def tap_samples(fine_res, above, beside):
+    channels = fine_res.shape[1]
+    vmem = pl.BlockSpec(memory_space=pltpu.VMEM)
+    return pl.pallas_call(
+        sample_kernel,
+        out_shape=jax.ShapeDtypeStruct((5 * 64, 2 * channels), jnp.bfloat16),
+        in_specs=[vmem] * 4,
         out_specs=vmem,
         scratch_shapes=[
-            pltpu.VMEM((SHARDS, BLOCK_ROWS, width), jnp.bfloat16),
-            pltpu.VMEM((KEYS, width), jnp.float32),
-            pltpu.VMEM((SHARDS, BLOCK_ROWS, KEYS), jnp.float32),
-            pltpu.SemaphoreType.DMA((9,)),
+            pltpu.VMEM((256, channels), jnp.float32),
+            pltpu.VMEM((512, 2 * channels), jnp.float32),
         ],
-        compiler_params=pltpu.CompilerParams(vmem_limit_bytes=32 * 1024 * 1024),
-    )(*operands, *sources)
-
-
-def tail_kernel(
+        compiler_params=pltpu.CompilerParams(vmem_limit_bytes=16 * 1024 * 1024),
+    )(fine_res, above, beside, sample_table())
+
+
+def coarse_kernel(
     edge_ref,
     gathered_ref,
-    middle_ref,
+    normed_ref,
+    own_ref,
+    bias_ref,
+    pick_ref,
     depth_ref,
+    samples_ref,
     fine_ref,
-    above_ref,
-    beside_ref,
     to_fine_ref,
     centre_ref,
     repeat_ref,
     compact_ref,
-    sample_ref,
-    order_ref,
     fine_out_ref,
     coarse_out_ref,
+    heads_ref,
     expand_ref,
     shrink_ref,
     taps_ref,
+    proj_ref,
+    chosen_ref,
+    chance_ref,
+    attended_ref,
     hidden_ref,
     conv_ref,
-    field_ref,
-    twice_ref,
     down_ref,
     sems,
 ):
     spans = (
-        (expand_ref, 0, BLOCK_ROWS),
-        (shrink_ref, BLOCK_ROWS, BLOCK_ROWS),
-        (taps_ref, 2 * BLOCK_ROWS, TAP_ROWS),
+        (heads_ref, 0, BLOCK_ROWS),
+        (expand_ref, BLOCK_ROWS, BLOCK_ROWS),
+        (shrink_ref, 2 * BLOCK_ROWS, BLOCK_ROWS),
+        (taps_ref, 3 * BLOCK_ROWS, TAP_ROWS),
     )
     copies = [
         pltpu.make_async_copy(gathered_ref.at[:, pl.ds(first, count)], target, sems.at[part])
@@ -290,10 +273,7 @@
     ]
     for copy in copies:
         copy.start()
-    width = middle_ref.shape[1]
-    channels = fine_ref.shape[1]
-    middle = middle_ref[...]
-    normed_mid = norm_rows(middle.astype(jnp.float32))
+    width = own_ref.shape[1]
     query = lax.broadcasted_iota(jnp.int32, (QUERIES, 128), 0)
     column = query % RING
     outside = (
@@ -304,15 +284,29 @@
     )
     inside = jnp.where(outside, 0.0, 1.0)[:, :1]
     conv_ref[8 * WIN :, :] = jnp.zeros((8, conv_ref.shape[1]), jnp.float32)
-    field_ref[...] = jnp.zeros(field_ref.shape, jnp.float32)
-    field_ref[: fine_ref.shape[0], :] = fine_ref[...].astype(jnp.float32)
-    field_ref[ABOVE : ABOVE + 16, :] = above_ref[...].astype(jnp.float32)
-    field_ref[BESIDE : BESIDE + 16, :] = beside_ref[...].astype(jnp.float32)
-    twice_ref[...] = jnp.zeros(twice_ref.shape, jnp.float32)
-    twice_ref[:256, :channels] = field_ref[...]
-    twice_ref[256:, channels:] = field_ref[...]
-    samples = nn(sample_ref[...], twice_ref[...].astype(jnp.bfloat16)).astype(jnp.bfloat16)
     copies[0].wait()
+    heads = heads_ref[:, 32:BLOCK_ROWS, :].reshape(SHARDS * 128, width)
+    proj_ref[...] = nt(heads, normed_ref[...]).reshape(SHARDS, 128, KEYS)
+    pick = pick_ref[...]
+    for head in range(SHARDS):
+        queries = proj_ref[head, 48:88].astype(jnp.bfloat16)
+        chosen_ref[head] = nt(pick, queries)
+    bias = bias_ref[...]
+    for head in range(SHARDS):
+        keys = proj_ref[head, 88:128].astype(jnp.bfloat16)
+        scores = nn(chosen_ref[head].astype(jnp.bfloat16), keys) * (1.0 / math.sqrt(39)) + bias
+        exponent = jnp.exp(scores - jnp.max(scores, axis=1, keepdims=True))
+        total = jnp.sum(exponent, axis=1, keepdims=True)
+        chance_ref[head] = (exponent * (1.0 / total)).astype(jnp.bfloat16)
+    for head in range(SHARDS):
+        values = proj_ref[head, 8:48].astype(jnp.bfloat16)
+        attended_ref[head] = nt(chance_ref[head], values)
+    mixed = own_ref[...].astype(jnp.float32)
+    for head in range(SHARDS):
+        mixed += nn(attended_ref[head].astype(jnp.bfloat16), heads_ref[head][:HEAD_ROWS])
+    middle = mixed.astype(jnp.bfloat16)
+    normed_mid = norm_rows(middle.astype(jnp.float32))
+    copies[1].wait()
     chunk = 512
     expand = expand_ref[...].reshape(SHARDS * BLOCK_ROWS, width)
     for first in range(0, SHARDS * BLOCK_ROWS, chunk):
@@ -326,7 +320,7 @@
                 window = hidden_ref[pl.ds((row + down) * RING + side, 8), span]
                 total += depth_ref[tap : tap + 1, span] * window
             conv_ref[row * 8 : row * 8 + 8, span] = gelu(total)
-    copies[1].wait()
+    copies[2].wait()
     shrink = shrink_ref[...].reshape(SHARDS * BLOCK_ROWS, width)
     update = nn(conv_ref[...].astype(jnp.bfloat16), shrink)
     result = (nn(centre_ref[...], middle) + update).astype(jnp.bfloat16)
@@ -335,7 +329,8 @@
     fine_out_ref[...] = jnp.maximum(
         fine_ref[...].astype(jnp.float32) + upsampled, 0.0
     ).astype(jnp.bfloat16)
-    copies[2].wait()
+    copies[3].wait()
+    samples = samples_ref[...]
     for shard in range(SHARDS):
         four = nt(taps_ref[shard], samples[: 4 * 64])
         fifth = nt(taps_ref[shard][4 * HEAD_ROWS :], samples[4 * 64 :])
@@ -343,23 +338,22 @@
         for block in range(4):
             rows = slice(block * HEAD_ROWS, (block + 1) * HEAD_ROWS)
             total += four[rows, block * 64 : (block + 1) * 64]
-        down_ref[shard * HEAD_ROWS : (shard + 1) * HEAD_ROWS, :64] = total
-    turned = down_ref[...].T.astype(jnp.bfloat16)
-    downsampled = nn(turned, order_ref[...])[:CELLS]
+        down_ref[shard * 39 : shard * 39 + HEAD_ROWS, :64] = total
+    downsampled = down_ref[...].T[:CELLS, :width].astype(jnp.bfloat16).astype(jnp.float32)
     coarse_out_ref[...] = jnp.maximum(
         nn(compact_ref[...], result) + downsampled, 0.0
     ).astype(jnp.bfloat16)
 
 
-def coarse_tail(gathered, edges, middle, depth, fine_res, above, beside, to_fine):
-    width = middle.shape[1]
+def coarse_stream(gathered, edges, normed, own, pick, bias, depth, samples, fine_res, to_fine):
+    width = own.shape[1]
     fine_cells, fine_ch = fine_res.shape
-    operands = (middle, depth, fine_res, above, beside, to_fine, *tail_tables())
+    operands = (normed, own, bias, pick, depth, samples, fine_res, to_fine, *cell_tables())
     smem, vmem, anywhere = (
         pl.BlockSpec(memory_space=space) for space in (pltpu.SMEM, pltpu.VMEM, pl.ANY)
     )
     return pl.pallas_call(
-        tail_kernel,
+        coarse_kernel,
         out_shape=(
             jax.ShapeDtypeStruct((fine_cells, fine_ch), jnp.bfloat16),
             jax.ShapeDtypeStruct((CELLS, width), jnp.bfloat16),
@@ -369,15 +363,18 @@
         scratch_shapes=[
             pltpu.VMEM((SHARDS, BLOCK_ROWS, width), jnp.bfloat16),
             pltpu.VMEM((SHARDS, BLOCK_ROWS, width), jnp.bfloat16),
+            pltpu.VMEM((SHARDS, BLOCK_ROWS, width), jnp.bfloat16),
             pltpu.VMEM((SHARDS, TAP_ROWS, width), jnp.bfloat16),
+            pltpu.VMEM((SHARDS, 128, KEYS), jnp.float32),
+            pltpu.VMEM((SHARDS, QUERIES, HEAD_ROWS), jnp.float32),
+            pltpu.VMEM((SHARDS, QUERIES, KEYS), jnp.bfloat16),
+            pltpu.VMEM((SHARDS, QUERIES, HEAD_ROWS), jnp.float32),
             pltpu.VMEM((QUERIES, SHARDS * BLOCK_ROWS), jnp.float32),
             pltpu.VMEM((64, SHARDS * BLOCK_ROWS), jnp.float32),
-            pltpu.VMEM((256, fine_ch), jnp.float32),
-            pltpu.VMEM((512, 2 * fine_ch), jnp.float32),
             pltpu.VMEM((SHARDS * HEAD_ROWS, 128), jnp.float32),
-            pltpu.SemaphoreType.DMA((3,)),
+            pltpu.SemaphoreType.DMA((4,)),
         ],
-        compiler_params=pltpu.CompilerParams(vmem_limit_bytes=40 * 1024 * 1024),
+        compiler_params=pltpu.CompilerParams(vmem_limit_bytes=44 * 1024 * 1024),
     )(edges, gathered, *operands)
 
 
@@ -421,12 +418,14 @@
     coarse_ch = coarse_in.shape[2]
     fine_cells = fine_in.shape[3]
     coarse_cells = coarse_in.shape[3]
-    gathered = lax.all_gather(pack_rest(expand_coarse, shrink_coarse, to_coarse), "rows")
-    heads = all_shards(pack_heads(inproj_coarse, outproj_coarse))
+    gathered = lax.all_gather(
+        pack(inproj_coarse, outproj_coarse, expand_coarse, shrink_coarse, to_coarse), "rows"
+    )
     tile = jnp.pad(coarse_in.reshape(coarse_ch, coarse_cells).T, ((0, TILE - coarse_cells), (0, 0)))
     above, below = neighbours(tile, "rows")
     left, right = neighbours(jnp.concatenate([tile, above, below]), "cols")
-    coarse_mid = coarse_attention(heads, (tile, above, below, left, right))
+    bias, pick = attention_tables()
+    normed_all, own = normed_tiles((tile, above, below, left, right), pick)
     fine_rows = fine_cells // (2 * WIN)
     coarse_rows = coarse_cells // WIN
     fine_pic = fine_in.reshape(fine_ch, fine_rows, 2 * WIN)
@@ -468,14 +467,19 @@
     edges = jnp.stack(
         [row > 0, row < lax.axis_size("rows") - 1, col > 0, col < lax.axis_size("cols") - 1]
     ).astype(jnp.int32)
-    fine_out, coarse_out = coarse_tail(
+    samples = tap_samples(
+        field, jnp.pad(above_row, ((0, 2), (0, 0))), jnp.pad(beside, ((0, 1), (0, 0)))
+    )
+    fine_out, coarse_out = coarse_stream(
         gathered,
         edges,
-        coarse_mid,
+        normed_all,
+        own,
+        pick,
+        bias,
         depth.reshape(9, -1),
+        samples,
         field,
-        jnp.pad(above_row, ((0, 2), (0, 0))),
-        jnp.pad(beside, ((0, 1), (0, 0))),
         to_fine,
     )
     return (fine_out.T.reshape(fine_in.shape), coarse_out.T.reshape(coarse_in.shape))

time: 163 us -> 128 us (0.79)
  the two profiles are of different devices: /device:TPU:94 before, /device:TPU:1 now
where the time goes in v4:
time: 128 us; the launch traced here: 127 us
  waiting for transfers between devices  41.4 us (32%)
  starting transfers between devices  27.4 us (21%)
  between operations  14.6 us (11%)
  Pallas kernels  14.5 us (11%)
  local copies, waits for them, and re-layouts  13.3 us (10%)
  other arithmetic  9.07 us (7%)
  matrix products  6.71 us (5%)
    all_gather x1, waiting for transfers between devices, local(): lax.all_gather(pack(inproj_coarse, outproj_coarse, expand_coarse, shrink_...  31.9 us
    pallas_call x1, Pallas kernels, coarse_stream(): pl.pallas_call(coarse_kernel, out_shape=(jax.ShapeDtypeStruct((fine_cells...  13.5 us
    ppermute x4, starting transfers between devices, neighbours(): return (lax.ppermute(tile, axis, up), lax.ppermute(tile, axis, down))  10.4 us
    ppermute x2, waiting for transfers between devices, padded_2(): after = lax.ppermute(first, axis, down)  7.29 us
    ppermute x2, starting transfers between devices, padded_2(): before = lax.ppermute(last, axis, up)  7.07 us
    convert_element_type x1, other arithmetic, local(): convolved = jax.nn.gelu(depthwise(padded, depth_fine), approximate=False)...  6.89 us
    ppermute x2, starting transfers between devices, passed_along(): return lax.ppermute(block, axis, route)  6.72 us
    unnamed x46, local copies, waits for them, and re-layouts  6.23 us
  transfers between devices with their start and end apart: 11, of which 5 were waited for; matrix products, arithmetic and copies ran while one was open for 17% of the time, Pallas kernels for 1%

profile of v4, /device:TPU:1, one launch (start us, length us, event | category | flops | bytes accessed | tf_op | source)
XLA Modules:
  0.0 127.0 jit_solution(18433043815483514054)
XLA Ops:
  7.2 0.0 copy-start
  7.2 0.0 all-gather.3.cloned.1.call-start
  7.2 1.0 slice.96
  8.2 0.8 slice.95
  9.1 0.8 fusion.55
  10.0 0.2 copy.27
  10.2 0.2 reshape.100
  10.5 0.3 copy-done.15
  10.9 0.1 copy-done.16
  11.0 0.9 copy-done.11
  11.9 0.0 all-gather.3.cloned.1.call-update
  12.0 0.1 convert_reduce_fusion
  12.1 0.2 fusion.53
  12.3 0.5 fusion.3
  12.9 0.3 reshape_reshape_squeeze.9
  13.3 0.3 reshape_reshape_squeeze.10
  13.7 0.3 reshape_reshape_squeeze.11
  14.1 0.6 fusion.72
  14.6 0.4 convolution_multiply_fusion
  15.0 0.5 convolution_convert_fusion.1
  15.5 0.4 copy.35
  15.9 0.3 reshape_reshape.4
  16.2 0.2 copy-done.14
  16.4 0.4 fusion.77
  16.8 0.2 multiply_reduce_fusion
  17.1 2.7 %fusion.22 = bf16[1248,196]{0,1:T(8,128)(2,1)S(1)} fusion(bf16[1248,312]{0,1:T(8,128)(2,1)S(1)} %copy-done, f32[312,196]{0,1:T(8,128)S(1)} %get-tuple-element.27, f32[196]{0:T(256)S(1)} %add_rsqrt_fusion, f32[196]{0:T(256)S(1)} %broadcast_multiply_fusion), kind=kOutput, calls=%fused_computation.38 | convolution fusion | flops 168718368 | bytes 1514144 | tf_op jit(solution)/shard_map/dot_general | solution.py:448
  19.8 0.2 reshape.108
  20.0 5.5 %collective-permute-start.4 = (bf16[1248,1,14]{0,2,1:T(8,128)(2,1)S(1)}, bf16[1248,1,14]{0,2,1:T(8,128)(2,1)S(1)}, u32[]{:S(2)}, u32[]{:S(2)}) collective-permute-start(bf16[1248,1,14]{0,2,1:T(8,128)(2,1)S(1)} %get-tuple-element.22), channel_id=1, source_target_pairs={{0,32},{32,64},{64,96},{96,128},{128,160},{160,192},{192,224},{224... | collective-permute-start | bytes 104840 | tf_op jit(solution)/shard_map/ppermute | solution.py:26
  25.6 1.9 %collective-permute-start = (bf16[56,624]{1,0:T(8,128)(2,1)S(1)}, bf16[56,624]{1,0:T(8,128)(2,1)S(1)}, u32[]{:S(2)}, u32[]{:S(2)}) collective-permute-start(bf16[56,624]{1,0:T(8,128)(2,1)S(1)} %pad.35.centre_ref), channel_id=1, source_target_pairs={{0,32},{32,64},{64,96},{96,128},{128,160},{160,192},{192,224},{224... | collective-permute-start | bytes 209672 | tf_op jit(solution)/shard_map/ppermute | solution.py:385
  27.5 4.1 %collective-permute-start.1 = (bf16[56,624]{1,0:T(8,128)(2,1)S(1)}, bf16[56,624]{1,0:T(8,128)(2,1)S(1)}, u32[]{:S(2)}, u32[]{:S(2)}) collective-permute-start(bf16[56,624]{1,0:T(8,128)(2,1)S(1)} %pad.35.centre_ref), channel_id=1, source_target_pairs={{32,0},{64,32},{96,64},{128,96},{160,128},{192,160},{224,192},{256... | collective-permute-start | bytes 209672 | tf_op jit(solution)/shard_map/ppermute | solution.py:385
  31.6 1.9 %collective-permute-start.5 = (bf16[1248,1,14]{0,2,1:T(8,128)(2,1)S(1)}, bf16[1248,1,14]{0,2,1:T(8,128)(2,1)S(1)}, u32[]{:S(2)}, u32[]{:S(2)}) collective-permute-start(bf16[1248,1,14]{0,2,1:T(8,128)(2,1)S(1)} %get-tuple-element.21), channel_id=1, source_target_pairs={{32,0},{64,32},{96,64},{128,96},{160,128},{192,160},{224,192},{256... | collective-permute-start | bytes 104840 | tf_op jit(solution)/shard_map/ppermute | solution.py:27
  33.5 0.6 constant_dynamic-update-slice_fusion.5
  34.2 0.8 constant_dynamic-update-slice_fusion.4
  35.0 3.2 %collective-permute-done.5 = bf16[1248,1,14]{0,2,1:T(8,128)(2,1)S(1)} collective-permute-done((bf16[1248,1,14]{0,2,1:T(8,128)(2,1)S(1)}, bf16[1248,1,14]{0,2,1:T(8,128)(2,1)S(1)}, u32[]{:S(2)}, u32[]{:S(2)}) %collective-permute-start.5) | collective-permute-done | bytes 34976 | tf_op jit(solution)/shard_map/ppermute | solution.py:27
  38.2 0.6 constant_dynamic-update-slice_fusion.3
  38.8 1.2 fusion.69
  40.0 1.5 %collective-permute-start.6 = (bf16[1248,16,1]{0,2,1:T(2,128)(2,1)S(1)}, bf16[1248,16,1]{0,2,1:T(2,128)(2,1)S(1)}, u32[]{:S(2)}, u32[]{:S(2)}) collective-permute-start(bf16[1248,16,1]{0,2,1:T(2,128)(2,1)S(1)} %get-tuple-element.19), channel_id=1, source_target_pairs={{0,1},{1,2},{2,3},{3,4},{4,5},{5,6},{6,7},{7,8},{8,9},{9,10},{10,1... | collective-permute-start | bytes 119816 | tf_op jit(solution)/shard_map/ppermute | solution.py:26
  41.6 1.3 %collective-permute-start.7 = (bf16[1248,16,1]{0,2,1:T(2,128)(2,1)S(1)}, bf16[1248,16,1]{0,2,1:T(2,128)(2,1)S(1)}, u32[]{:S(2)}, u32[]{:S(2)}) collective-permute-start(bf16[1248,16,1]{0,2,1:T(2,128)(2,1)S(1)} %get-tuple-element.20), channel_id=1, source_target_pairs={{1,0},{2,1},{3,2},{4,3},{5,4},{6,5},{7,6},{8,7},{9,8},{10,9},{11,1... | collective-permute-start | bytes 119816 | tf_op jit(solution)/shard_map/ppermute | solution.py:27
  42.9 0.1 slice_reduce_fusion.8
  43.0 0.0 collective-permute-done.6
  43.0 4.1 %collective-permute-done.7 = bf16[1248,16,1]{0,2,1:T(2,128)(2,1)S(1)} collective-permute-done((bf16[1248,16,1]{0,2,1:T(2,128)(2,1)S(1)}, bf16[1248,16,1]{0,2,1:T(2,128)(2,1)S(1)}, u32[]{:S(2)}, u32[]{:S(2)}) %collective-permute-start.7) | collective-permute-done | bytes 39968 | tf_op jit(solution)/shard_map/ppermute | solution.py:27
  47.2 6.9 %fusion.11 = bf16[1248,14,14]{0,2,1:T(8,128)(2,1)S(1)} fusion(bf16[1248,14,14]{0,2,1:T(8,128)(2,1)S(1)} %reshape.108, bf16[1248,16,14]{0,2,1:T(8,128)(2,1)} %constant_dynamic-update-slice_fusion.3, bf16[1248,16,1]{0,2,1:T(2,128)(2,1)S(1)} %collective-permute-done.7, bf16[1248,16,1]{0,2,1:T(2,128)(2,1)S(1)} %collective-permute-done.6, ...), kind=kLoop, calls=%fused_computation.18 | loop fusion | flops 28129920 | bytes 1732224 | tf_op jit(solution)/shard_map/convert_element_type | solution.py:453
  54.1 0.2 reshape.109
  54.3 1.7 %fusion.19.fine_ref = bf16[196,312]{1,0:T(8,128)(2,1)S(1)} fusion(f32[312,196]{0,1:T(8,128)S(1)} %get-tuple-element.27, bf16[1248,196]{0,1:T(8,128)(2,1)S(1)} %reshape.109, bf16[312,1248]{1,0:T(8,128)(2,1)} %param.26), kind=kOutput, calls=%fused_computation.35 | convolution fusion | flops 152757696 | bytes 1634880 | tf_op jit(solution)/shard_map/dot_general | solution.py:458
  56.0 0.0 copy-start.3
  56.0 2.6 %collective-permute-start.8 = (bf16[14,312]{1,0:T(8,128)(2,1)S(1)}, bf16[14,312]{1,0:T(8,128)(2,1)S(1)}, u32[]{:S(2)}, u32[]{:S(2)}) collective-permute-start(bf16[14,312]{1,0:T(8,128)(2,1)S(1)} %slice.139), channel_id=1, source_target_pairs={{0,32},{32,64},{64,96},{96,128},{128,160},{160,192},{192,224},{224... | collective-permute-start | bytes 26216 | tf_op jit(solution)/shard_map/ppermute | solution.py:35
  58.6 0.7 pad_maximum_fusion.4
  59.3 3.1 %collective-permute-start.2 = (bf16[168,624]{1,0:T(8,128)(2,1)}, bf16[168,624]{1,0:T(8,128)(2,1)S(1)}, u32[]{:S(2)}, u32[]{:S(2)}) collective-permute-start(bf16[168,624]{1,0:T(8,128)(2,1)} %pad_maximum_fusion.4), channel_id=1, source_target_pairs={{0,1},{1,2},{2,3},{3,4},{4,5},{5,6},{6,7},{7,8},{8,9},{9,10},{10,1... | collective-permute-start | bytes 629000 | tf_op jit(solution)/shard_map/ppermute | solution.py:385
  62.4 1.3 %collective-permute-start.3 = (bf16[168,624]{1,0:T(8,128)(2,1)}, bf16[168,624]{1,0:T(8,128)(2,1)S(1)}, u32[]{:S(2)}, u32[]{:S(2)}) collective-permute-start(bf16[168,624]{1,0:T(8,128)(2,1)} %pad_maximum_fusion.4), channel_id=1, source_target_pairs={{1,0},{2,1},{3,2},{4,3},{5,4},{6,5},{7,6},{8,7},{9,8},{10,9},{11,1... | collective-permute-start | bytes 629000 | tf_op jit(solution)/shard_map/ppermute | solution.py:385
  63.7 0.1 slice.123
  63.8 4.2 %collective-permute-start.9 = (bf16[15,312]{1,0:T(8,128)(2,1)S(1)}, bf16[15,312]{1,0:T(8,128)(2,1)S(1)}, u32[]{:S(2)}, u32[]{:S(2)}) collective-permute-start(bf16[15,312]{1,0:T(8,128)(2,1)S(1)} %pad_maximum_fusion.5), channel_id=1, source_target_pairs={{0,1},{1,2},{2,3},{3,4},{4,5},{5,6},{6,7},{7,8},{8,9},{9,10},{10,1... | collective-permute-start | bytes 28088 | tf_op jit(solution)/shard_map/ppermute | solution.py:35
  68.0 0.1 add_convert_fusion.edge_ref
  68.1 0.2 reshape.102
  68.4 0.1 reshape.103.depth_ref
  68.5 0.1 collective-permute-done.9
  68.6 0.5 shard_map.204.samples_ref
  69.2 2.1 %collective-permute-done.3.right_ref = bf16[168,624]{1,0:T(8,128)(2,1)S(1)} collective-permute-done((bf16[168,624]{1,0:T(8,128)(2,1)}, bf16[168,624]{1,0:T(8,128)(2,1)S(1)}, u32[]{:S(2)}, u32[]{:S(2)}) %collective-permute-start.3) | collective-permute-done | bytes 209696 | tf_op jit(solution)/shard_map/ppermute | solution.py:385
  71.2 0.5 shard_map.203
  71.7 0.6 copy-done.5
  72.3 31.9 %all-gather.3.cloned.1.call-done = bf16[11008,624]{1,0:T(8,128)(2,1)} async-done(((bf16[688,624]{1,0:T(8,128)(2,1)}), bf16[11008,624]{1,0:T(8,128)(2,1)}) %all-gather.3.cloned.1.call-update) | async-done | bytes 13738000 | tf_op jit(solution)/shard_map/all_gather | solution.py:421
  104.2 0.9 copy-done.6
  105.1 0.8 copy-done.7
  105.9 0.7 copy-done.9
  106.6 13.5 %shard_map.205 = (bf16[196,312]{1,0:T(8,128)(2,1)}, bf16[49,624]{1,0:T(8,128)(2,1)}) custom-call(s32[4]{0:T(128)S(1)} %add_convert_fusion.edge_ref, bf16[16,688,624]{2,1,0:T(8,128)(2,1)} %bitcast.154, bf16[512,624]{1,0:T(8,128)(2,1)S(1)} %get-tuple-element.6.normed_ref, bf16[96,624]{1,0:T(8,128)(2,1)S(1)} %copy-done.6, f32[96,512]{1,0:T(8,128)S(1)} %copy-done.4, ...), custom_call_target="tpu_custom_call" | custom-call | tf_op jit(solution)/shard_map/pallas_call | solution.py:355
  (58 shorter events, 0.5 us)
Async XLA Ops:
  7.2 9.9 %copy-start = (bf16[1248,312]{0,1:T(8,128)(2,1)S(1)}, bf16[1248,312]{0,1:T(8,128)(2,1)}, u32[]{:S(2)}) copy-start(bf16[1248,312]{0,1:T(8,128)(2,1)} %param.24) | copy-start | bytes 2336260
  7.2 2.8 %copy-start.13 = (bf16[9,39,312]{2,1,0:T(8,128)(2,1)S(1)}, bf16[9,39,312]{2,1,0:T(8,128)(2,1)}, u32[]{:S(2)}) copy-start(bf16[9,39,312]{2,1,0:T(8,128)(2,1)} %param.33) | copy-start | bytes 657076
  7.2 97.0 %all-gather.3.cloned.1.call-start = ((), (), s32[]{:S(2)}) async-start(), calls=%async_computation | async-start | bytes 14970880 | tf_op jit(solution)/shard_map/all_gather | solution.py:421
  9.9 0.9 copy-start.15
  9.9 1.0 copy-start.16
  10.8 1.1 copy-start.10
  10.9 1.4 %copy-start.12 = (bf16[3,312,312]{2,1,0:T(8,128)(2,1)S(1)}, bf16[3,312,312]{2,1,0:T(8,128)(2,1)}, u32[]{:S(2)}) copy-start(bf16[3,312,312]{2,1,0:T(8,128)(2,1)} %param.22) | copy-start | bytes 1752196
  11.0 0.9 copy-start.11
  15.5 0.9 copy-start.14
  19.8 5.8 %copy-start.18 = (bf16[1,1,624,49]{2,3,1,0:T(8,128)(2,1)S(1)}, bf16[1,1,624,49]{2,3,1,0:T(8,128)(2,1)}, u32[]{:S(2)}) copy-start(bf16[1,1,624,49]{2,3,1,0:T(8,128)(2,1)} %param.21) | copy-start | bytes 183460
  20.0 22.9 %copy-start.19 = (f32[9,1248]{1,0:T(8,128)S(1)}, f32[9,1248]{1,0:T(8,128)}, u32[]{:S(2)}) copy-start(f32[9,1248]{1,0:T(8,128)} %param.25) | copy-start | bytes 134788
  20.0 13.5 %collective-permute-start.4 = (bf16[1248,1,14]{0,2,1:T(8,128)(2,1)S(1)}, bf16[1248,1,14]{0,2,1:T(8,128)(2,1)S(1)}, u32[]{:S(2)}, u32[]{:S(2)}) collective-permute-start(bf16[1248,1,14]{0,2,1:T(8,128)(2,1)S(1)} %get-tuple-element.22), channel_id=1, source_target_pairs={{0,32},{32,64},{64,96},{96,128},{128,160},{160,192},{192,224},{224... | collective-permute-start | bytes 104840 | tf_op jit(solution)/shard_map/ppermute | solution.py:26
  25.6 33.0 %collective-permute-start = (bf16[56,624]{1,0:T(8,128)(2,1)S(1)}, bf16[56,624]{1,0:T(8,128)(2,1)S(1)}, u32[]{:S(2)}, u32[]{:S(2)}) collective-permute-start(bf16[56,624]{1,0:T(8,128)(2,1)S(1)} %pad.35.centre_ref), channel_id=1, source_target_pairs={{0,32},{32,64},{64,96},{96,128},{128,160},{160,192},{192,224},{224... | collective-permute-start | bytes 209672 | tf_op jit(solution)/shard_map/ppermute | solution.py:385
  27.5 31.1 %collective-permute-start.1 = (bf16[56,624]{1,0:T(8,128)(2,1)S(1)}, bf16[56,624]{1,0:T(8,128)(2,1)S(1)}, u32[]{:S(2)}, u32[]{:S(2)}) collective-permute-start(bf16[56,624]{1,0:T(8,128)(2,1)S(1)} %pad.35.centre_ref), channel_id=1, source_target_pairs={{32,0},{64,32},{96,64},{128,96},{160,128},{192,160},{224,192},{256... | collective-permute-start | bytes 209672 | tf_op jit(solution)/shard_map/ppermute | solution.py:385
  31.6 6.6 %collective-permute-start.5 = (bf16[1248,1,14]{0,2,1:T(8,128)(2,1)S(1)}, bf16[1248,1,14]{0,2,1:T(8,128)(2,1)S(1)}, u32[]{:S(2)}, u32[]{:S(2)}) collective-permute-start(bf16[1248,1,14]{0,2,1:T(8,128)(2,1)S(1)} %get-tuple-element.21), channel_id=1, source_target_pairs={{32,0},{64,32},{96,64},{128,96},{160,128},{192,160},{224,192},{256... | collective-permute-start | bytes 104840 | tf_op jit(solution)/shard_map/ppermute | solution.py:27
  40.0 3.0 %collective-permute-start.6 = (bf16[1248,16,1]{0,2,1:T(2,128)(2,1)S(1)}, bf16[1248,16,1]{0,2,1:T(2,128)(2,1)S(1)}, u32[]{:S(2)}, u32[]{:S(2)}) collective-permute-start(bf16[1248,16,1]{0,2,1:T(2,128)(2,1)S(1)} %get-tuple-element.19), channel_id=1, source_target_pairs={{0,1},{1,2},{2,3},{3,4},{4,5},{5,6},{6,7},{7,8},{8,9},{9,10},{10,1... | collective-permute-start | bytes 119816 | tf_op jit(solution)/shard_map/ppermute | solution.py:26
  41.6 5.6 %collective-permute-start.7 = (bf16[1248,16,1]{0,2,1:T(2,128)(2,1)S(1)}, bf16[1248,16,1]{0,2,1:T(2,128)(2,1)S(1)}, u32[]{:S(2)}, u32[]{:S(2)}) collective-permute-start(bf16[1248,16,1]{0,2,1:T(2,128)(2,1)S(1)} %get-tuple-element.20), channel_id=1, source_target_pairs={{1,0},{2,1},{3,2},{4,3},{5,4},{6,5},{7,6},{8,7},{9,8},{10,9},{11,1... | collective-permute-start | bytes 119816 | tf_op jit(solution)/shard_map/ppermute | solution.py:27
  54.3 13.8 %copy-start.17 = (f32[9,2496]{1,0:T(8,128)S(1)}, f32[9,2496]{1,0:T(8,128)}, u32[]{:S(2)}) copy-start(f32[9,2496]{1,0:T(8,128)} %param.30) | copy-start | bytes 269572
  56.0 12.6 %copy-start.3 = (bf16[320,512]{1,0:T(8,128)(2,1)S(1)}, bf16[320,512]{1,0:T(8,128)(2,1)}, u32[]{:S(2)}) copy-start(bf16[320,512]{1,0:T(8,128)(2,1)} %constant.166.sample_ref) | copy-start | bytes 983044
  56.0 15.2 %copy-start.2 = (bf16[96,512]{1,0:T(8,128)(2,1)S(1)}, bf16[96,512]{1,0:T(8,128)(2,1)}, u32[]{:S(2)}) copy-start(bf16[96,512]{1,0:T(8,128)(2,1)} %constant.165.pick_ref) | copy-start | bytes 294916
  56.0 7.8 %collective-permute-start.8 = (bf16[14,312]{1,0:T(8,128)(2,1)S(1)}, bf16[14,312]{1,0:T(8,128)(2,1)S(1)}, u32[]{:S(2)}, u32[]{:S(2)}) collective-permute-start(bf16[14,312]{1,0:T(8,128)(2,1)S(1)} %slice.139), channel_id=1, source_target_pairs={{0,32},{32,64},{64,96},{96,128},{128,160},{160,192},{192,224},{224... | collective-permute-start | bytes 26216 | tf_op jit(solution)/shard_map/ppermute | solution.py:35
  59.3 9.8 %collective-permute-start.2 = (bf16[168,624]{1,0:T(8,128)(2,1)}, bf16[168,624]{1,0:T(8,128)(2,1)S(1)}, u32[]{:S(2)}, u32[]{:S(2)}) collective-permute-start(bf16[168,624]{1,0:T(8,128)(2,1)} %pad_maximum_fusion.4), channel_id=1, source_target_pairs={{0,1},{1,2},{2,3},{3,4},{4,5},{5,6},{6,7},{7,8},{8,9},{9,10},{10,1... | collective-permute-start | bytes 629000 | tf_op jit(solution)/shard_map/ppermute | solution.py:385
  62.4 8.8 %collective-permute-start.3 = (bf16[168,624]{1,0:T(8,128)(2,1)}, bf16[168,624]{1,0:T(8,128)(2,1)S(1)}, u32[]{:S(2)}, u32[]{:S(2)}) collective-permute-start(bf16[168,624]{1,0:T(8,128)(2,1)} %pad_maximum_fusion.4), channel_id=1, source_target_pairs={{1,0},{2,1},{3,2},{4,3},{5,4},{6,5},{7,6},{8,7},{9,8},{10,9},{11,1... | collective-permute-start | bytes 629000 | tf_op jit(solution)/shard_map/ppermute | solution.py:385
  63.8 4.8 %collective-permute-start.9 = (bf16[15,312]{1,0:T(8,128)(2,1)S(1)}, bf16[15,312]{1,0:T(8,128)(2,1)S(1)}, u32[]{:S(2)}, u32[]{:S(2)}) collective-permute-start(bf16[15,312]{1,0:T(8,128)(2,1)S(1)} %pad_maximum_fusion.5), channel_id=1, source_target_pairs={{0,1},{1,2},{2,3},{3,4},{4,5},{5,6},{6,7},{7,8},{8,9},{9,10},{10,1... | collective-permute-start | bytes 28088 | tf_op jit(solution)/shard_map/ppermute | solution.py:35
  68.3 35.9 %copy-start.1 = (bf16[312,624]{1,0:T(8,128)(2,1)S(1)}, bf16[312,624]{1,0:T(8,128)(2,1)}, u32[]{:S(2)}) copy-start(bf16[312,624]{1,0:T(8,128)(2,1)} %to_fine_ref.1) | copy-start | bytes 1168132
  68.3 35.9 %copy-start.4 = (f32[96,512]{1,0:T(8,128)S(1)}, f32[96,512]{1,0:T(8,128)}, u32[]{:S(2)}) copy-start(f32[96,512]{1,0:T(8,128)} %constant.23.clone.bias_ref) | copy-start | bytes 589828
  68.3 35.9 %copy-start.8 = (bf16[64,96]{1,0:T(8,128)(2,1)S(1)}, bf16[64,96]{1,0:T(8,128)(2,1)}, u32[]{:S(2)}) copy-start(bf16[64,96]{1,0:T(8,128)(2,1)} %constant.167.centre_ref) | copy-start | bytes 36868
  71.7 0.7 copy-start.5
  104.2 0.9 copy-start.6
  105.1 0.8 copy-start.7
  105.9 0.7 copy-start.9
Sparse Core Ops, SparseCore 0:
  12.1 92.0 all-gather.2

commit v5 on v4

v5 whole, which is shorter than its diff:
```python
import math

import jax
import jax.numpy as jnp
from jax import lax
import numpy as np
from jax.experimental import pallas as pl
from jax.experimental.pallas import tpu as pltpu
from jax.sharding import PartitionSpec as P

HEADS_FINE = 8
WIN = 7


EPSILON = 1e-05


CELLS = WIN * WIN
RING = WIN + 2
HEAD_ROWS = 40
BLOCK_ROWS = 4 * HEAD_ROWS
TAP_ROWS = 5 * HEAD_ROWS + 8
SHARDS = 16
TILE = 56
KEYS = 9 * TILE + 8
QUERIES = 96
SIDE = 2 * WIN
FIELD = SIDE + 3
FIELD_ROWS = 304
FIRST_HALF = 352
TOP, BOTTOM, LEFT, RIGHT = 200, 232, 248, 288


def pack(inproj, outproj, expand, shrink, to_coarse):
    width = expand.shape[-1]
    heads = jnp.concatenate([outproj.T[None], inproj[2:], inproj[:2]])
    taps = jnp.pad(to_coarse, ((0, 1), (0, 1), (0, 0))).reshape(5, 2, HEAD_ROWS, -1)
    return jnp.concatenate(
        [
            jnp.pad(heads, ((0, 0), (0, 1), (0, 0))).reshape(BLOCK_ROWS, -1),
            jnp.pad(expand, ((0, 4), (0, 0))),
            jnp.pad(shrink.T, ((0, 4), (0, 0))),
            taps.transpose(0, 2, 1, 3).reshape(-1, width),
            jnp.zeros((8, width), expand.dtype),
        ]
    )


def all_shards(mine):
    size = lax.axis_size("rows")
    swap = [(i, i ^ 1) for i in range(size)]
    up = [(i, (i + 2) % size) for i in range(size)]
    down = [(j, i) for i, j in up]
    rising, falling = [mine], [mine]
    for _ in range(3):
        rising.append(lax.ppermute(rising[-1], "rows", up))
        falling.append(lax.ppermute(falling[-1], "rows", down))
    near = [mine, rising[1], falling[1], rising[2], falling[2]]
    far = [rising[3], falling[3]]
    last = jnp.concatenate(
        [
            lax.ppermute(rising[3][:FIRST_HALF], "rows", up),
            lax.ppermute(falling[3][FIRST_HALF:], "rows", down),
        ]
    )
    sources = near + far + [last]
    for group in (near, far, [last]):
        sources.append(lax.ppermute(jnp.stack(group), "rows", swap))
    place = lax.axis_index("rows")
    chips = [2 * ((place // 2 + away) % (size // 2)) for away in (0, -1, 1, -2, 2, -3, 3, 4)]
    core = place % 2
    owners = [chip + core for chip in chips] + [chip + 1 - core for chip in chips]
    return sources, jnp.stack(owners).astype(jnp.int32)


def attention_tables():
    pick = np.zeros((QUERIES, KEYS), np.float32)
    bias = np.full((QUERIES, KEYS), -1e30, np.float32)
    for row in range(RING):
        for col in range(RING):
            down = 1 if row == 0 else 2 if row == RING - 1 else 0
            side = 1 if col == 0 else 2 if col == RING - 1 else 0
            first = (3 * side + down) * TILE
            query = row * RING + col
            pick[query, first + (row - 1) % WIN * WIN + (col - 1) % WIN] = 1
            bias[query, first : first + CELLS] = 0
    bias[RING * RING :, :CELLS] = 0
    return jnp.asarray(bias), jnp.asarray(pick).astype(jnp.bfloat16)


def window_table():
    cells = np.arange(SIDE * SIDE)
    window = cells // SIDE // WIN * 2 + cells % SIDE // WIN
    return jnp.asarray(np.where(window[:, None] == window[None], 0.0, -1e30).astype(np.float32))


def border_tables():
    right = np.zeros((40, 248), np.float32)
    left = np.zeros((32, 248), np.float32)

    def source(row, col):
        if row < 0:
            return TOP + (row + 2) * SIDE + col
        return row * SIDE + col if row < SIDE else BOTTOM + col

    for row in range(FIELD):
        for col in range(2):
            right[row * 2 + col, source(row - 2, SIDE - 2 + col)] = 1
        left[row, source(row - 2, 0)] = 1
    return jnp.asarray(right).astype(jnp.bfloat16), jnp.asarray(left).astype(jnp.bfloat16)


def field_tables():
    gather = np.zeros((FIELD_ROWS, 320), np.float32)
    inner = np.zeros((256, FIELD_ROWS), np.float32)
    for row in range(FIELD):
        for col in range(FIELD):
            if col < 2:
                source = LEFT + row * 2 + col
            elif col == FIELD - 1:
                source = RIGHT + row
            elif row < 2:
                source = TOP + row * SIDE + col - 2
            elif row == FIELD - 1:
                source = BOTTOM + col - 2
            else:
                source = (row - 2) * SIDE + col - 2
            gather[row * FIELD + col, source] = 1
    for row in range(15):
        for col in range(15):
            inner[row * 16 + col, (row + 1) * FIELD + col + 1] = 1
    tile = np.zeros((SIDE * SIDE, 256), np.float32)
    for row in range(SIDE):
        for col in range(SIDE):
            tile[row * SIDE + col, (row + 1) * 16 + col + 1] = 1
    sample = np.zeros((5 * 64, 512), np.float32)
    for cell in range(CELLS):
        row, col = divmod(cell, WIN)
        for tap in range(9):
            source = (2 * row + tap // 3) * 16 + 2 * col + tap % 3
            sample[tap // 2 * 64 + cell, tap % 2 * 256 + source] = 1
    return tuple(jnp.asarray(t).astype(jnp.bfloat16) for t in (gather, inner, tile, sample))


def cell_tables():
    side = 2 * WIN
    centre = np.zeros((64, QUERIES), np.float32)
    repeat = np.zeros((side * side, 64), np.float32)
    compact = np.zeros((CELLS, 64), np.float32)
    for cell in range(CELLS):
        row, col = divmod(cell, WIN)
        centre[row * 8 + col, (row + 1) * RING + col + 1] = 1
        compact[cell, row * 8 + col] = 1
    for cell in range(side * side):
        row, col = divmod(cell, side)
        repeat[cell, row // 2 * 8 + col // 2] = 1
    return tuple(jnp.asarray(t).astype(jnp.bfloat16) for t in (centre, repeat, compact))


def gelu(values):
    return values * (lax.erf(values * math.sqrt(0.5)) + 1.0) * 0.5


def norm_rows(values):
    center = jnp.mean(values, axis=1, keepdims=True)
    away = values - center
    spread = jnp.mean(away * away, axis=1, keepdims=True)
    return (away * lax.rsqrt(spread + EPSILON)).astype(jnp.bfloat16)


def nn(left, right):
    return lax.dot_general(
        left, right, (((1,), (0,)), ((), ())), preferred_element_type=jnp.float32
    )


def nt(left, right):
    return lax.dot_general(
        left, right, (((1,), (1,)), ((), ())), preferred_element_type=jnp.float32
    )


def fine_attention_kernel(
    fine_ref, inproj_ref, outproj_ref, mask_ref, tile_ref, middle_ref, down_ref, up_ref
):
    cells, channels = fine_ref.shape
    fine = fine_ref[...].astype(jnp.float32)
    normed = norm_rows(fine)
    queries, keys, values = (nt(normed, inproj_ref[i]).astype(jnp.bfloat16) for i in range(3))
    channel = lax.broadcasted_iota(jnp.int32, (cells, channels), 1)
    mask = mask_ref[...]
    nothing = jnp.zeros((cells, channels), jnp.bfloat16)
    attended = jnp.zeros((cells, channels), jnp.float32)
    for head in range(HEADS_FINE):
        mine = (channel >= head * 39) & (channel < (head + 1) * 39)
        chosen = jnp.where(mine, queries, nothing)
        scores = nt(chosen, keys) * (1.0 / math.sqrt(39)) + mask
        exponent = jnp.exp(scores - jnp.max(scores, axis=1, keepdims=True))
        total = jnp.sum(exponent, axis=1, keepdims=True)
        chance = (exponent * (1.0 / total)).astype(jnp.bfloat16)
        attended += nn(chance, jnp.where(mine, values, nothing))
    middle = fine + nt(attended.astype(jnp.bfloat16), outproj_ref[...])
    middle_ref[...] = middle.astype(jnp.bfloat16)
    for target, first, count in ((down_ref, cells - 2 * SIDE, 2 * SIDE), (up_ref, 0, SIDE)):
        target[...] = jnp.zeros(target.shape, jnp.bfloat16)
        target[:TILE, :] = tile_ref[...]
        target[TILE : TILE + count, :channels] = middle_ref[first : first + count, :]


def columns_kernel(
    tile_ref, above_ref, below_ref, middle_ref, right_ref, left_ref, to_right_ref, to_left_ref,
    field_ref,
):
    cells, channels = middle_ref.shape
    field_ref[...] = jnp.zeros(field_ref.shape, jnp.float32)
    field_ref[:cells, :] = middle_ref[...].astype(jnp.float32)
    field_ref[TOP : TOP + 2 * SIDE, :] = above_ref[TILE : TILE + 2 * SIDE, :channels].astype(
        jnp.float32
    )
    field_ref[BOTTOM : BOTTOM + SIDE, :] = below_ref[TILE : TILE + SIDE, :channels].astype(
        jnp.float32
    )
    field = field_ref[...].astype(jnp.bfloat16)
    for target, table in ((to_right_ref, right_ref), (to_left_ref, left_ref)):
        target[...] = jnp.zeros(target.shape, jnp.bfloat16)
        target[:TILE, :] = tile_ref[...]
        target[TILE : 2 * TILE, :] = above_ref[:TILE, :]
        target[2 * TILE : 3 * TILE, :] = below_ref[:TILE, :]
        count = table.shape[0]
        target[3 * TILE : 3 * TILE + count, :channels] = nn(table[...], field).astype(jnp.bfloat16)


def field_kernel(
    edge_ref,
    tile_ref,
    above_ref,
    below_ref,
    left_ref,
    right_ref,
    pick_ref,
    middle_ref,
    expand_ref,
    depth_ref,
    shrink_ref,
    gather_ref,
    inner_ref,
    cell_ref,
    sample_ref,
    normed_ref,
    own_ref,
    fine_ref,
    samples_ref,
    tiles_ref,
    pieces_ref,
    hidden_ref,
    conv_ref,
    twice_ref,
):
    cells, channels = middle_ref.shape
    tiles_ref[9 * TILE :, :] = jnp.zeros((KEYS - 9 * TILE, tiles_ref.shape[1]), jnp.float32)
    first = 0
    for piece, count in (
        (tile_ref, TILE),
        (above_ref, TILE),
        (below_ref, TILE),
        (left_ref, 3 * TILE),
        (right_ref, 3 * TILE),
    ):
        tiles_ref[first : first + count, :] = piece[:count, :].astype(jnp.float32)
        first += count
    tiles = tiles_ref[...]
    normed_ref[...] = norm_rows(tiles)
    own_ref[...] = nn(pick_ref[...], tiles.astype(jnp.bfloat16)).astype(jnp.bfloat16)

    pieces_ref[...] = jnp.zeros(pieces_ref.shape, jnp.float32)
    pieces_ref[:cells, :] = middle_ref[...].astype(jnp.float32)
    for piece, start, first, count in (
        (above_ref, TILE, TOP, 2 * SIDE),
        (below_ref, TILE, BOTTOM, SIDE),
        (left_ref, 3 * TILE, LEFT, 2 * FIELD),
        (right_ref, 3 * TILE, RIGHT, FIELD),
    ):
        pieces_ref[first : first + count, :] = piece[start : start + count, :channels].astype(
            jnp.float32
        )
    field = nn(gather_ref[...], pieces_ref[...].astype(jnp.bfloat16))
    normed_mid = norm_rows(field)
    row = lax.broadcasted_iota(jnp.int32, (FIELD_ROWS, 128), 0)
    column = row % FIELD
    outside = (
        ((row < 2 * FIELD) & (edge_ref[0] == 0))
        | ((row >= FIELD * (FIELD - 1)) & (edge_ref[1] == 0))
        | ((column < 2) & (edge_ref[2] == 0))
        | ((column == FIELD - 1) & (edge_ref[3] == 0))
    )
    inside = jnp.where(outside, 0.0, 1.0)[:, :1]
    hidden_count = hidden_ref.shape[1]
    conv_ref[15 * 16 :, :] = jnp.zeros((16, hidden_count), jnp.bfloat16)
    for first in range(0, hidden_count, 384):
        span = pl.ds(first, min(384, hidden_count - first))
        hidden = gelu(nn(normed_mid, expand_ref[:, span])) * inside
        hidden_ref[:, span] = hidden.astype(jnp.bfloat16).astype(jnp.float32)
        for out in range(15):
            total = jnp.zeros((16, span.size), jnp.float32)
            for tap in range(9):
                down, side = divmod(tap, 3)
                window = hidden_ref[pl.ds((out + down) * FIELD + side, 16), span]
                total += depth_ref[tap : tap + 1, span] * window
            conv_ref[out * 16 : out * 16 + 16, span] = gelu(total).astype(jnp.bfloat16)
    update = nt(conv_ref[...], shrink_ref[...])
    result = nn(inner_ref[...], field.astype(jnp.bfloat16)) + update
    row = lax.broadcasted_iota(jnp.int32, (256, 128), 0)
    outside = ((row < 16) & (edge_ref[0] == 0)) | ((row % 16 == 0) & (edge_ref[2] == 0))
    result = result * jnp.where(outside, 0.0, 1.0)[:, :1]
    rounded = result.astype(jnp.bfloat16)
    fine_ref[...] = nn(cell_ref[...], rounded).astype(jnp.bfloat16)
    result = rounded.astype(jnp.float32)
    twice_ref[...] = jnp.zeros(twice_ref.shape, jnp.float32)
    twice_ref[:256, :channels] = result
    twice_ref[256:, channels:] = result
    samples_ref[...] = nn(sample_ref[...], twice_ref[...].astype(jnp.bfloat16)).astype(jnp.bfloat16)


def call(kernel, shapes, operands, scratch, scalars=0, limit=32):
    smem, vmem = (pl.BlockSpec(memory_space=space) for space in (pltpu.SMEM, pltpu.VMEM))
    return pl.pallas_call(
        kernel,
        out_shape=tuple(jax.ShapeDtypeStruct(shape, jnp.bfloat16) for shape in shapes),
        in_specs=[smem] * scalars + [vmem] * (len(operands) - scalars),
        out_specs=(vmem,) * len(shapes),
        scratch_shapes=[pltpu.VMEM(shape, kind) for shape, kind in scratch],
        compiler_params=pltpu.CompilerParams(vmem_limit_bytes=limit * 1024 * 1024),
    )(*operands)


def coarse_kernel(
    edge_ref,
    owner_ref,
    *refs,
):
    sources, rest = refs[:11], refs[11:]
    coarse_body(edge_ref, owner_ref, sources, *rest)


def coarse_body(
    edge_ref,
    owner_ref,
    sources,
    normed_ref,
    own_ref,
    bias_ref,
    pick_ref,
    depth_ref,
    samples_ref,
    fine_ref,
    to_fine_ref,
    centre_ref,
    repeat_ref,
    compact_ref,
    fine_out_ref,
    coarse_out_ref,
    heads_ref,
    expand_ref,
    shrink_ref,
    taps_ref,
    proj_ref,
    chosen_ref,
    chance_ref,
    attended_ref,
    hidden_ref,
    conv_ref,
    down_ref,
    sems,
):
    spans = (
        (heads_ref, 0, BLOCK_ROWS),
        (expand_ref, BLOCK_ROWS, BLOCK_ROWS),
        (shrink_ref, 2 * BLOCK_ROWS, BLOCK_ROWS),
        (taps_ref, 3 * BLOCK_ROWS, TAP_ROWS),
    )
    slots = list(sources[:8])
    for source, count in zip(sources[8:], (5, 2, 1)):
        slots += [source.at[i] for i in range(count)]
    copies = []
    for part, (target, first, count) in enumerate(spans):
        copies.append(
            [
                pltpu.make_async_copy(
                    slot.at[pl.ds(first, count)], target.at[owner_ref[place]], sems.at[part, place]
                )
                for place, slot in enumerate(slots)
            ]
        )
        for copy in copies[-1]:
            copy.start()

    def arrive(part):
        for copy in copies[part]:
            copy.wait()

    width = own_ref.shape[1]
    query = lax.broadcasted_iota(jnp.int32, (QUERIES, 128), 0)
    column = query % RING
    outside = (
        ((query < RING) & (edge_ref[0] == 0))
        | ((query >= RING * (RING - 1)) & (edge_ref[1] == 0))
        | ((column == 0) & (edge_ref[2] == 0))
        | ((column == RING - 1) & (edge_ref[3] == 0))
    )
    inside = jnp.where(outside, 0.0, 1.0)[:, :1]
    conv_ref[8 * WIN :, :] = jnp.zeros((8, conv_ref.shape[1]), jnp.float32)
    arrive(0)
    heads = heads_ref[:, 32:BLOCK_ROWS, :].reshape(SHARDS * 128, width)
    proj_ref[...] = nt(heads, normed_ref[...]).reshape(SHARDS, 128, KEYS)
    pick = pick_ref[...]
    for head in range(SHARDS):
        queries = proj_ref[head, 48:88].astype(jnp.bfloat16)
        chosen_ref[head] = nt(pick, queries)
    bias = bias_ref[...]
    for head in range(SHARDS):
        keys = proj_ref[head, 88:128].astype(jnp.bfloat16)
        scores = nn(chosen_ref[head].astype(jnp.bfloat16), keys) * (1.0 / math.sqrt(39)) + bias
        exponent = jnp.exp(scores - jnp.max(scores, axis=1, keepdims=True))
        total = jnp.sum(exponent, axis=1, keepdims=True)
        chance_ref[head] = (exponent * (1.0 / total)).astype(jnp.bfloat16)
    for head in range(SHARDS):
        values = proj_ref[head, 8:48].astype(jnp.bfloat16)
        attended_ref[head] = nt(chance_ref[head], values)
    mixed = own_ref[...].astype(jnp.float32)
    for head in range(SHARDS):
        mixed += nn(attended_ref[head].astype(jnp.bfloat16), heads_ref[head][:HEAD_ROWS])
    middle = mixed.astype(jnp.bfloat16)
    normed_mid = norm_rows(middle.astype(jnp.float32))
    arrive(1)
    chunk = 512
    expand = expand_ref[...].reshape(SHARDS * BLOCK_ROWS, width)
    for first in range(0, SHARDS * BLOCK_ROWS, chunk):
        span = pl.ds(first, chunk)
        hidden = gelu(nt(normed_mid, expand[first : first + chunk])) * inside
        hidden_ref[:, span] = hidden.astype(jnp.bfloat16).astype(jnp.float32)
        for row in range(WIN):
            total = jnp.zeros((8, chunk), jnp.float32)
            for tap in range(9):
                down, side = divmod(tap, 3)
                window = hidden_ref[pl.ds((row + down) * RING + side, 8), span]
                total += depth_ref[tap : tap + 1, span] * window
            conv_ref[row * 8 : row * 8 + 8, span] = gelu(total)
    arrive(2)
    shrink = shrink_ref[...].reshape(SHARDS * BLOCK_ROWS, width)
    update = nn(conv_ref[...].astype(jnp.bfloat16), shrink)
    result = (nn(centre_ref[...], middle) + update).astype(jnp.bfloat16)
    spread = nn(repeat_ref[...], result).astype(jnp.bfloat16)
    upsampled = nt(spread, to_fine_ref[...])
    fine_out_ref[...] = jnp.maximum(
        fine_ref[...].astype(jnp.float32) + upsampled, 0.0
    ).astype(jnp.bfloat16)
    arrive(3)
    samples = samples_ref[...]
    for shard in range(SHARDS):
        four = nt(taps_ref[shard], samples[: 4 * 64])
        fifth = nt(taps_ref[shard][4 * HEAD_ROWS :], samples[4 * 64 :])
        total = fifth[:HEAD_ROWS]
        for block in range(4):
            rows = slice(block * HEAD_ROWS, (block + 1) * HEAD_ROWS)
            total += four[rows, block * 64 : (block + 1) * 64]
        down_ref[shard * 39 : shard * 39 + HEAD_ROWS, :64] = total
    downsampled = down_ref[...].T[:CELLS, :width].astype(jnp.bfloat16).astype(jnp.float32)
    coarse_out_ref[...] = jnp.maximum(
        nn(compact_ref[...], result) + downsampled, 0.0
    ).astype(jnp.bfloat16)


def coarse_stream(sources, edges, owners, normed, own, pick, bias, depth, samples, fine_res, to_fine):
    width = own.shape[1]
    fine_cells, fine_ch = fine_res.shape
    operands = (normed, own, bias, pick, depth, samples, fine_res, to_fine, *cell_tables())
    smem, vmem, anywhere = (
        pl.BlockSpec(memory_space=space) for space in (pltpu.SMEM, pltpu.VMEM, pl.ANY)
    )
    return pl.pallas_call(
        coarse_kernel,
        out_shape=(
            jax.ShapeDtypeStruct((fine_cells, fine_ch), jnp.bfloat16),
            jax.ShapeDtypeStruct((CELLS, width), jnp.bfloat16),
        ),
        in_specs=[smem, smem] + [anywhere] * len(sources) + [vmem] * len(operands),
        out_specs=(vmem, vmem),
        scratch_shapes=[
            pltpu.VMEM((SHARDS, BLOCK_ROWS, width), jnp.bfloat16),
            pltpu.VMEM((SHARDS, BLOCK_ROWS, width), jnp.bfloat16),
            pltpu.VMEM((SHARDS, BLOCK_ROWS, width), jnp.bfloat16),
            pltpu.VMEM((SHARDS, TAP_ROWS, width), jnp.bfloat16),
            pltpu.VMEM((SHARDS, 128, KEYS), jnp.float32),
            pltpu.VMEM((SHARDS, QUERIES, HEAD_ROWS), jnp.float32),
            pltpu.VMEM((SHARDS, QUERIES, KEYS), jnp.bfloat16),
            pltpu.VMEM((SHARDS, QUERIES, HEAD_ROWS), jnp.float32),
            pltpu.VMEM((QUERIES, SHARDS * BLOCK_ROWS), jnp.float32),
            pltpu.VMEM((64, SHARDS * BLOCK_ROWS), jnp.float32),
            pltpu.VMEM((SHARDS * HEAD_ROWS, 128), jnp.float32),
            pltpu.SemaphoreType.DMA((4, SHARDS)),
        ],
        compiler_params=pltpu.CompilerParams(vmem_limit_bytes=44 * 1024 * 1024),
    )(edges, owners, *sources, *operands)


def exchange(onward, back, axis):
    up = [(i, i + 1) for i in range(lax.axis_size(axis) - 1)]
    down = [(j, i) for i, j in up]
    return lax.ppermute(onward, axis, up), lax.ppermute(back, axis, down)


def local(
    fine_in,
    coarse_in,
    inproj_fine,
    outproj_fine,
    expand_fine,
    depth_fine,
    shrink_fine,
    inproj_coarse,
    outproj_coarse,
    expand_coarse,
    depth_coarse,
    shrink_coarse,
    to_fine,
    to_coarse,
):
    fine_ch, fine_cells = fine_in.shape[2:]
    coarse_ch, coarse_cells = coarse_in.shape[2:]
    sources, owners = all_shards(
        pack(inproj_coarse, outproj_coarse, expand_coarse, shrink_coarse, to_coarse)
    )
    tile = jnp.pad(coarse_in.reshape(coarse_ch, coarse_cells).T, ((0, TILE - coarse_cells), (0, 0)))
    fine = fine_in.reshape(fine_ch, fine_cells).T
    place = (lax.axis_index("rows"), lax.axis_index("cols"))
    edges = jnp.stack(
        [
            place[0] > 0,
            place[0] < lax.axis_size("rows") - 1,
            place[1] > 0,
            place[1] < lax.axis_size("cols") - 1,
        ]
    ).astype(jnp.int32)
    message = (TILE + 32, coarse_ch)
    middle, going_down, going_up = call(
        fine_attention_kernel,
        (fine.shape, message, message),
        (fine, inproj_fine, outproj_fine, window_table(), tile),
        (),
    )
    above, below = exchange(going_down, going_up, "rows")
    message = (3 * TILE + 40, coarse_ch)
    going_right, going_left = call(
        columns_kernel,
        (message, message),
        (tile, above, below, middle, *border_tables()),
        (((248, fine_ch), jnp.float32),),
    )
    left, right = exchange(going_right, going_left, "cols")
    bias, pick = attention_tables()
    hidden_count = expand_fine.shape[0]
    normed, own, fine_res, samples = call(
        field_kernel,
        ((KEYS, coarse_ch), (QUERIES, coarse_ch), fine.shape, (5 * 64, 2 * fine_ch)),
        (
            edges,
            tile,
            above,
            below,
            left,
            right,
            pick,
            middle,
            expand_fine.T,
            depth_fine,
            shrink_fine,
            *field_tables(),
        ),
        (
            ((KEYS, coarse_ch), jnp.float32),
            ((320, fine_ch), jnp.float32),
            ((FIELD_ROWS, hidden_count), jnp.float32),
            ((256, hidden_count), jnp.bfloat16),
            ((512, 2 * fine_ch), jnp.float32),
        ),
        scalars=1,
    )
    depth = jnp.pad(depth_coarse.reshape(9, SHARDS, -1), ((0, 0), (0, 0), (0, 4)))
    fine_out, coarse_out = coarse_stream(
        sources,
        edges,
        owners,
        normed,
        own,
        pick,
        bias,
        depth.reshape(9, -1),
        samples,
        fine_res,
        to_fine,
    )
    return (fine_out.T.reshape(fine_in.shape), coarse_out.T.reshape(coarse_in.shape))


def solution(mesh):
    return jax.shard_map(
        local,
        mesh=mesh,
        in_specs=(
            P("rows", "cols", None, None),
            P("rows", "cols", None, None),
            P(),
            P(),
            P(),
            P(),
            P(),
            P(None, "rows", None),
            P(None, "rows"),
            P("rows", None),
            P(),
            P(None, "rows"),
            P(),
            P(None, "rows", None),
        ),
        out_specs=(P("rows", "cols", None, None), P("rows", "cols", None, None)),
        check_vma=False,
    )
```

time: 128 us -> 195 us (1.52)
  the two profiles are of different devices: /device:TPU:1 before, /device:TPU:95 now
where the time goes in v5:
time: 195 us; the launch traced here: 194 us
  waiting for transfers between devices  72.7 us (37%)
  starting transfers between devices  48.7 us (25%)
  local copies, waits for them, and re-layouts  38 us (19%)
  Pallas kernels  30.5 us (16%)
  other arithmetic  2.44 us (1%)
    ppermute x3, waiting for transfers between devices, all_shards(): rising.append(lax.ppermute(rising[-1], 'rows', up))  48.1 us
    unnamed x83, local copies, waits for them, and re-layouts  27.1 us
    pallas_call x1, Pallas kernels, coarse_stream(): pl.pallas_call(coarse_kernel, out_shape=(jax.ShapeDtypeStruct((fine_cells...  19.4 us
    ppermute x3, starting transfers between devices, all_shards(): rising.append(lax.ppermute(rising[-1], 'rows', up))  12.4 us
    ppermute x4, starting transfers between devices, exchange(): return (lax.ppermute(onward, axis, up), lax.ppermute(back, axis, down))  11.2 us
    pallas_call x3, Pallas kernels, call(): pl.pallas_call(kernel, out_shape=tuple((jax.ShapeDtypeStruct(shape, jnp.b...  11.2 us
    ppermute x3, starting transfers between devices, all_shards(): falling.append(lax.ppermute(falling[-1], 'rows', down))  10.2 us
    ppermute x3, starting transfers between devices, all_shards(): sources.append(lax.ppermute(jnp.stack(group), 'rows', swap))  9.59 us
  transfers between devices with their start and end apart: 15, of which 9 were waited for; matrix products, arithmetic and copies ran while one was open for 7% of the time, Pallas kernels for 6%

profile of v5, /device:TPU:95, one launch (start us, length us, event | category | flops | bytes accessed | tf_op | source)
XLA Modules:
  0.0 193.7 jit_solution(14471408661066214636)
XLA Ops:
  0.6 0.9 slice.13
  1.5 0.8 slice.12
  2.4 0.8 fusion.4
  3.2 1.0 pad.26
  4.7 1.0 pad_dynamic-update-slice_fusion.1
  5.7 1.0 pad_dynamic-update-slice_fusion
  6.7 4.0 %collective-permute-start = (bf16[688,624]{1,0:T(8,128)(2,1)S(1)}, bf16[688,624]{1,0:T(8,128)(2,1)S(1)}, u32[]{:S(2)}, u32[]{:S(2)}) collective-permute-start(bf16[688,624]{1,0:T(8,128)(2,1)S(1)} %constant_dynamic-update-slice_fusion.refs_0_), channel_id=1, source_target_pairs={{0,64},{32,96},{64,128},{96,160},{128,192},{160,224},{192,256},{22... | collective-permute-start | bytes 2575880 | tf_op jit(solution)/shard_map/ppermute | solution.py:56
  10.7 1.9 collective-permute-start.1
  12.6 16.4 %collective-permute-done.refs_1_ = bf16[688,624]{1,0:T(8,128)(2,1)S(1)} collective-permute-done((bf16[688,624]{1,0:T(8,128)(2,1)S(1)}, bf16[688,624]{1,0:T(8,128)(2,1)S(1)}, u32[]{:S(2)}, u32[]{:S(2)}) %collective-permute-start) | collective-permute-done | bytes 858656 | tf_op jit(solution)/shard_map/ppermute | solution.py:56
  29.0 4.0 %collective-permute-start.2 = (bf16[688,624]{1,0:T(8,128)(2,1)S(1)}, bf16[688,624]{1,0:T(8,128)(2,1)S(1)}, u32[]{:S(2)}, u32[]{:S(2)}) collective-permute-start(bf16[688,624]{1,0:T(8,128)(2,1)S(1)} %collective-permute-done.refs_1_), channel_id=1, source_target_pairs={{0,64},{32,96},{64,128},{96,160},{128,192},{160,224},{192,256},{22... | collective-permute-start | bytes 2575880 | tf_op jit(solution)/shard_map/ppermute | solution.py:56
  33.6 6.2 %collective-permute-start.3 = (bf16[688,624]{1,0:T(8,128)(2,1)S(1)}, bf16[688,624]{1,0:T(8,128)(2,1)S(1)}, u32[]{:S(2)}, u32[]{:S(2)}) collective-permute-start(bf16[688,624]{1,0:T(8,128)(2,1)S(1)} %collective-permute-done.1.refs_2_), channel_id=1, source_target_pairs={{64,0},{96,32},{128,64},{160,96},{192,128},{224,160},{256,192},{28... | collective-permute-start | bytes 2575880 | tf_op jit(solution)/shard_map/ppermute | solution.py:57
  39.9 1.0 bitcast_dynamic-update-slice_fusion.4
  40.9 1.0 bitcast_dynamic-update-slice_fusion.3
  41.9 1.0 bitcast_dynamic-update-slice_fusion.2
  42.8 13.7 %collective-permute-done.2.refs_3_ = bf16[688,624]{1,0:T(8,128)(2,1)S(1)} collective-permute-done((bf16[688,624]{1,0:T(8,128)(2,1)S(1)}, bf16[688,624]{1,0:T(8,128)(2,1)S(1)}, u32[]{:S(2)}, u32[]{:S(2)}) %collective-permute-start.2) | collective-permute-done | bytes 858656 | tf_op jit(solution)/shard_map/ppermute | solution.py:56
  56.5 1.2 bitcast_dynamic-update-slice_fusion.1
  57.8 1.1 bitcast_dynamic-update-slice_fusion
  58.8 3.9 %collective-permute-start.8 = (bf16[5,688,624]{2,1,0:T(8,128)(2,1)}, bf16[5,688,624]{2,1,0:T(8,128)(2,1)}, u32[]{:S(2)}, u32[]{:S(2)}) collective-permute-start(bf16[5,688,624]{2,1,0:T(8,128)(2,1)} %bitcast_dynamic-update-slice_fusion), channel_id=1, source_target_pairs={{0,32},{32,0},{64,96},{96,64},{128,160},{160,128},{192,224},{224,1... | collective-permute-start | bytes 12879368 | tf_op jit(solution)/shard_map/ppermute | solution.py:68
  62.7 4.4 %collective-permute-start.4 = (bf16[688,624]{1,0:T(8,128)(2,1)S(1)}, bf16[688,624]{1,0:T(8,128)(2,1)S(1)}, u32[]{:S(2)}, u32[]{:S(2)}) collective-permute-start(bf16[688,624]{1,0:T(8,128)(2,1)S(1)} %collective-permute-done.2.refs_3_), channel_id=1, source_target_pairs={{0,64},{32,96},{64,128},{96,160},{128,192},{160,224},{192,256},{22... | collective-permute-start | bytes 2575880 | tf_op jit(solution)/shard_map/ppermute | solution.py:56
  67.1 2.1 %collective-permute-start.5 = (bf16[688,624]{1,0:T(8,128)(2,1)S(1)}, bf16[688,624]{1,0:T(8,128)(2,1)S(1)}, u32[]{:S(2)}, u32[]{:S(2)}) collective-permute-start(bf16[688,624]{1,0:T(8,128)(2,1)S(1)} %collective-permute-done.3.refs_4_), channel_id=1, source_target_pairs={{64,0},{96,32},{128,64},{160,96},{192,128},{224,160},{256,192},{28... | collective-permute-start | bytes 2575880 | tf_op jit(solution)/shard_map/ppermute | solution.py:57
  69.2 18.0 %collective-permute-done.4.refs_5_ = bf16[688,624]{1,0:T(8,128)(2,1)S(1)} collective-permute-done((bf16[688,624]{1,0:T(8,128)(2,1)S(1)}, bf16[688,624]{1,0:T(8,128)(2,1)S(1)}, u32[]{:S(2)}, u32[]{:S(2)}) %collective-permute-start.4) | collective-permute-done | bytes 858656 | tf_op jit(solution)/shard_map/ppermute | solution.py:56
  87.2 4.2 %collective-permute-done.5.refs_6_ = bf16[688,624]{1,0:T(8,128)(2,1)S(1)} collective-permute-done((bf16[688,624]{1,0:T(8,128)(2,1)S(1)}, bf16[688,624]{1,0:T(8,128)(2,1)S(1)}, u32[]{:S(2)}, u32[]{:S(2)}) %collective-permute-start.5) | collective-permute-done | bytes 858656 | tf_op jit(solution)/shard_map/ppermute | solution.py:57
  91.4 1.5 pad_maximum_fusion
  93.0 2.7 %collective-permute-start.9 = (bf16[2,688,624]{2,1,0:T(8,128)(2,1)}, bf16[2,688,624]{2,1,0:T(8,128)(2,1)}, u32[]{:S(2)}, u32[]{:S(2)}) collective-permute-start(bf16[2,688,624]{2,1,0:T(8,128)(2,1)} %pad_maximum_fusion), channel_id=1, source_target_pairs={{0,32},{32,0},{64,96},{96,64},{128,160},{160,128},{192,224},{224,1... | collective-permute-start | bytes 5151752 | tf_op jit(solution)/shard_map/ppermute | solution.py:68
  95.7 3.4 %collective-permute-start.6 = (bf16[352,624]{1,0:T(8,128)(2,1)S(1)}, bf16[352,624]{1,0:T(8,128)(2,1)S(1)}, u32[]{:S(2)}, u32[]{:S(2)}) collective-permute-start(bf16[352,624]{1,0:T(8,128)(2,1)S(1)} %slice.16), channel_id=1, source_target_pairs={{0,64},{32,96},{64,128},{96,160},{128,192},{160,224},{192,256},{22... | collective-permute-start | bytes 1317896 | tf_op jit(solution)/shard_map/ppermute | solution.py:62
  99.2 1.9 collective-permute-start.7
  101.1 8.5 %collective-permute-done.6 = bf16[352,624]{1,0:T(8,128)(2,1)S(1)} collective-permute-done((bf16[352,624]{1,0:T(8,128)(2,1)S(1)}, bf16[352,624]{1,0:T(8,128)(2,1)S(1)}, u32[]{:S(2)}, u32[]{:S(2)}) %collective-permute-start.6) | collective-permute-done | bytes 439328 | tf_op jit(solution)/shard_map/ppermute | solution.py:62
  109.6 0.8 constant_dynamic-update-slice_fusion.4
  110.4 1.9 collective-permute-done.7
  112.3 0.8 constant_dynamic-update-slice_fusion.3.refs_7_
  113.1 3.0 %collective-permute-start.10 = (bf16[1,688,624]{2,1,0:T(8,128)(2,1)}, bf16[1,688,624]{2,1,0:T(8,128)(2,1)}, u32[]{:S(2)}, u32[]{:S(2)}) collective-permute-start(bf16[1,688,624]{2,1,0:T(8,128)(2,1)} %bitcast.33), channel_id=1, source_target_pairs={{0,32},{32,0},{64,96},{96,64},{128,160},{160,128},{192,224},{224,1... | collective-permute-start | bytes 2575880 | tf_op jit(solution)/shard_map/ppermute | solution.py:68
  116.2 4.0 %shard_map.257 = (bf16[196,312]{1,0:T(8,128)(2,1)S(1)}, bf16[88,624]{1,0:T(8,128)(2,1)S(1)}, bf16[88,624]{1,0:T(8,128)(2,1)S(1)}) custom-call(bf16[196,312]{1,0:T(8,128)(2,1)S(1)} %bitcast.58, bf16[3,312,312]{2,1,0:T(8,128)(2,1)S(1)} %copy-done.10, bf16[312,312]{1,0:T(8,128)(2,1)S(1)} %copy-done.22, f32[196,196]{1,0:T(8,128)S(1)} %copy-done.24, ...), custom_call_target="tpu_custom_call" | custom-call | tf_op jit(solution)/shard_map/pallas_call | solution.py:326
  120.2 3.0 %collective-permute-start.11 = (bf16[88,624]{1,0:T(8,128)(2,1)S(1)}, bf16[88,624]{1,0:T(8,128)(2,1)S(1)}, u32[]{:S(2)}, u32[]{:S(2)}) collective-permute-start(bf16[88,624]{1,0:T(8,128)(2,1)S(1)} %get-tuple-element.13), channel_id=1, source_target_pairs={{0,32},{32,64},{64,96},{96,128},{128,160},{160,192},{192,224},{224... | collective-permute-start | bytes 329480 | tf_op jit(solution)/shard_map/ppermute | solution.py:509
  123.2 1.9 collective-permute-start.12
  125.2 4.1 %collective-permute-done.12.below_ref = bf16[88,624]{1,0:T(8,128)(2,1)S(1)} collective-permute-done((bf16[88,624]{1,0:T(8,128)(2,1)S(1)}, bf16[88,624]{1,0:T(8,128)(2,1)S(1)}, u32[]{:S(2)}, u32[]{:S(2)}) %collective-permute-start.12) | collective-permute-done | bytes 109856 | tf_op jit(solution)/shard_map/ppermute | solution.py:509
  129.4 1.0 shard_map.258
  130.4 4.3 %collective-permute-start.13 = (bf16[208,624]{1,0:T(8,128)(2,1)}, bf16[208,624]{1,0:T(8,128)(2,1)}, u32[]{:S(2)}, u32[]{:S(2)}) collective-permute-start(bf16[208,624]{1,0:T(8,128)(2,1)} %get-tuple-element.16), channel_id=1, source_target_pairs={{0,1},{1,2},{2,3},{3,4},{4,5},{5,6},{6,7},{7,8},{8,9},{9,10},{10,1... | collective-permute-start | bytes 778760 | tf_op jit(solution)/shard_map/ppermute | solution.py:509
  134.7 1.9 collective-permute-start.14
  136.8 1.8 reshape.36
  138.6 1.6 pad.28
  140.2 1.7 reshape.37.refs_15_
  142.6 5.3 %collective-permute-done.14.right_ref = bf16[208,624]{1,0:T(8,128)(2,1)} collective-permute-done((bf16[208,624]{1,0:T(8,128)(2,1)}, bf16[208,624]{1,0:T(8,128)(2,1)}, u32[]{:S(2)}, u32[]{:S(2)}) %collective-permute-start.14) | collective-permute-done | bytes 259616 | tf_op jit(solution)/shard_map/ppermute | solution.py:509
  147.9 0.9 copy-done.7
  148.8 1.1 copy-done.8
  149.9 1.1 copy-done.9
  151.1 0.9 copy-done.13
  152.0 0.9 copy-done.15
  152.9 0.9 copy-done.17
  153.8 0.9 copy-done.19
  154.7 1.0 copy-done.21
  155.6 0.9 copy-done.23
  156.6 0.9 copy-done.26
  157.5 0.9 copy-done.28
  158.4 0.9 copy-done.29
  159.3 6.1 %shard_map.259 = (bf16[512,624]{1,0:T(8,128)(2,1)S(1)}, bf16[96,624]{1,0:T(8,128)(2,1)S(1)}, bf16[196,312]{1,0:T(8,128)(2,1)S(1)}, bf16[320,624]{1,0:T(8,128)(2,1)S(1)}) custom-call(s32[4]{0:T(128)S(1)} %add_convert_fusion.edge_ref, bf16[56,624]{1,0:T(8,128)(2,1)S(1)} %copy-done.7, bf16[88,624]{1,0:T(8,128)(2,1)S(1)} %copy-done.15, ...), custom_call_target="tpu_custom_call" | custom-call | tf_op jit(solution)/shard_map/pallas_call | solution.py:326
  165.5 1.2 copy-done.1
  166.6 1.2 copy-done.3
  167.8 1.2 copy-done.5
  168.9 0.9 copy-done.11
  169.9 1.0 copy-done.18
  170.9 0.9 copy-done.20
  171.8 0.9 copy-done.25
  172.7 0.8 copy-done.30
  174.2 19.4 %shard_map.260 = (bf16[196,312]{1,0:T(8,128)(2,1)}, bf16[49,624]{1,0:T(8,128)(2,1)}) custom-call(s32[4]{0:T(128)S(1)} %add_convert_fusion.edge_ref, s32[16]{0:T(128)S(1)} %copy-done.35, bf16[688,624]{1,0:T(8,128)(2,1)S(1)} %constant_dynamic-update-slice_fusion.refs_0_, bf16[688,624]{1,0:T(8,128)(2,1)S(1)} %collective-permute-done.refs_1_, ...), custom_call_target="tpu_custom_call" | custom-call | tf_op jit(solution)/shard_map/pallas_call | solution.py:480
  (71 shorter events, 2.8 us)
Async XLA Ops:
  6.7 22.3 %collective-permute-start = (bf16[688,624]{1,0:T(8,128)(2,1)S(1)}, bf16[688,624]{1,0:T(8,128)(2,1)S(1)}, u32[]{:S(2)}, u32[]{:S(2)}) collective-permute-start(bf16[688,624]{1,0:T(8,128)(2,1)S(1)} %constant_dynamic-update-slice_fusion.refs_0_), channel_id=1, source_target_pairs={{0,64},{32,96},{64,128},{96,160},{128,192},{160,224},{192,256},{22... | collective-permute-start | bytes 2575880 | tf_op jit(solution)/shard_map/ppermute | solution.py:56
  10.7 23.0 %collective-permute-start.1 = (bf16[688,624]{1,0:T(8,128)(2,1)S(1)}, bf16[688,624]{1,0:T(8,128)(2,1)S(1)}, u32[]{:S(2)}, u32[]{:S(2)}) collective-permute-start(bf16[688,624]{1,0:T(8,128)(2,1)S(1)} %constant_dynamic-update-slice_fusion.refs_0_), channel_id=1, source_target_pairs={{64,0},{96,32},{128,64},{160,96},{192,128},{224,160},{256,192},{28... | collective-permute-start | bytes 2575880 | tf_op jit(solution)/shard_map/ppermute | solution.py:57
  29.0 27.5 %collective-permute-start.2 = (bf16[688,624]{1,0:T(8,128)(2,1)S(1)}, bf16[688,624]{1,0:T(8,128)(2,1)S(1)}, u32[]{:S(2)}, u32[]{:S(2)}) collective-permute-start(bf16[688,624]{1,0:T(8,128)(2,1)S(1)} %collective-permute-done.refs_1_), channel_id=1, source_target_pairs={{0,64},{32,96},{64,128},{96,160},{128,192},{160,224},{192,256},{22... | collective-permute-start | bytes 2575880 | tf_op jit(solution)/shard_map/ppermute | solution.py:56
  33.6 57.8 %copy-start = (bf16[688,624]{1,0:T(8,128)(2,1)}, bf16[688,624]{1,0:T(8,128)(2,1)S(1)}, u32[]{:S(2)}) copy-start(bf16[688,624]{1,0:T(8,128)(2,1)S(1)} %collective-permute-done.1.refs_2_) | copy-start | bytes 2575876
  33.6 24.1 %collective-permute-start.3 = (bf16[688,624]{1,0:T(8,128)(2,1)S(1)}, bf16[688,624]{1,0:T(8,128)(2,1)S(1)}, u32[]{:S(2)}, u32[]{:S(2)}) collective-permute-start(bf16[688,624]{1,0:T(8,128)(2,1)S(1)} %collective-permute-done.1.refs_2_), channel_id=1, source_target_pairs={{64,0},{96,32},{128,64},{160,96},{192,128},{224,160},{256,192},{28... | collective-permute-start | bytes 2575880 | tf_op jit(solution)/shard_map/ppermute | solution.py:57
  56.5 34.9 %copy-start.2 = (bf16[688,624]{1,0:T(8,128)(2,1)}, bf16[688,624]{1,0:T(8,128)(2,1)S(1)}, u32[]{:S(2)}) copy-start(bf16[688,624]{1,0:T(8,128)(2,1)S(1)} %collective-permute-done.2.refs_3_) | copy-start | bytes 2575876
  57.7 58.4 %copy-start.36 = (bf16[1,1,624,49]{2,3,1,0:T(8,128)(2,1)S(1)}, bf16[1,1,624,49]{2,3,1,0:T(8,128)(2,1)}, u32[]{:S(2)}) copy-start(bf16[1,1,624,49]{2,3,1,0:T(8,128)(2,1)} %param.27) | copy-start | bytes 183460
  57.7 58.4 %copy-start.10 = (bf16[3,312,312]{2,1,0:T(8,128)(2,1)S(1)}, bf16[3,312,312]{2,1,0:T(8,128)(2,1)}, u32[]{:S(2)}) copy-start(bf16[3,312,312]{2,1,0:T(8,128)(2,1)} %inproj_ref.1) | copy-start | bytes 1752196
  57.7 58.4 %copy-start.22 = (bf16[312,312]{1,0:T(8,128)(2,1)S(1)}, bf16[312,312]{1,0:T(8,128)(2,1)}, u32[]{:S(2)}) copy-start(bf16[312,312]{1,0:T(8,128)(2,1)} %outproj_ref.1) | copy-start | bytes 584068
  57.7 58.4 %copy-start.24 = (f32[196,196]{1,0:T(8,128)S(1)}, f32[196,196]{1,0:T(8,128)}, u32[]{:S(2)}) copy-start(f32[196,196]{1,0:T(8,128)} %constant.129.clone.mask_ref) | copy-start | bytes 460996
  57.7 58.4 %copy-start.27 = (bf16[1,1,312,196]{2,3,1,0:T(8,128)(2,1)S(1)}, bf16[1,1,312,196]{2,3,1,0:T(8,128)(2,1)}, u32[]{:S(2)}) copy-start(bf16[1,1,312,196]{2,3,1,0:T(8,128)(2,1)} %param.26) | copy-start | bytes 366916
  57.7 33.7 %copy-start.4 = (bf16[688,624]{1,0:T(8,128)(2,1)}, bf16[688,624]{1,0:T(8,128)(2,1)S(1)}, u32[]{:S(2)}) copy-start(bf16[688,624]{1,0:T(8,128)(2,1)S(1)} %collective-permute-done.3.refs_4_) | copy-start | bytes 2575876
  58.8 70.5 %copy-start.31 = (bf16[40,248]{1,0:T(8,128)(2,1)S(1)}, bf16[40,248]{1,0:T(8,128)(2,1)}, u32[]{:S(2)}) copy-start(bf16[40,248]{1,0:T(8,128)(2,1)} %constant.160.right_ref) | copy-start | bytes 59524
  58.8 70.5 %copy-start.32 = (bf16[32,248]{1,0:T(8,128)(2,1)S(1)}, bf16[32,248]{1,0:T(8,128)(2,1)}, u32[]{:S(2)}) copy-start(bf16[32,248]{1,0:T(8,128)(2,1)} %constant.161.left_ref) | copy-start | bytes 47620
  58.8 106.6 %collective-permute-start.8 = (bf16[5,688,624]{2,1,0:T(8,128)(2,1)}, bf16[5,688,624]{2,1,0:T(8,128)(2,1)}, u32[]{:S(2)}, u32[]{:S(2)}) collective-permute-start(bf16[5,688,624]{2,1,0:T(8,128)(2,1)} %bitcast_dynamic-update-slice_fusion), channel_id=1, source_target_pairs={{0,32},{32,0},{64,96},{96,64},{128,160},{160,128},{192,224},{224,1... | collective-permute-start | bytes 12879368 | tf_op jit(solution)/shard_map/ppermute | solution.py:68
  62.7 24.5 %collective-permute-start.4 = (bf16[688,624]{1,0:T(8,128)(2,1)S(1)}, bf16[688,624]{1,0:T(8,128)(2,1)S(1)}, u32[]{:S(2)}, u32[]{:S(2)}) collective-permute-start(bf16[688,624]{1,0:T(8,128)(2,1)S(1)} %collective-permute-done.2.refs_3_), channel_id=1, source_target_pairs={{0,64},{32,96},{64,128},{96,160},{128,192},{160,224},{192,256},{22... | collective-permute-start | bytes 2575880 | tf_op jit(solution)/shard_map/ppermute | solution.py:56
  67.1 24.3 %collective-permute-start.5 = (bf16[688,624]{1,0:T(8,128)(2,1)S(1)}, bf16[688,624]{1,0:T(8,128)(2,1)S(1)}, u32[]{:S(2)}, u32[]{:S(2)}) collective-permute-start(bf16[688,624]{1,0:T(8,128)(2,1)S(1)} %collective-permute-done.3.refs_4_), channel_id=1, source_target_pairs={{64,0},{96,32},{128,64},{160,96},{192,128},{224,160},{256,192},{28... | collective-permute-start | bytes 2575880 | tf_op jit(solution)/shard_map/ppermute | solution.py:57
  93.0 72.4 %collective-permute-start.9 = (bf16[2,688,624]{2,1,0:T(8,128)(2,1)}, bf16[2,688,624]{2,1,0:T(8,128)(2,1)}, u32[]{:S(2)}, u32[]{:S(2)}) collective-permute-start(bf16[2,688,624]{2,1,0:T(8,128)(2,1)} %pad_maximum_fusion), channel_id=1, source_target_pairs={{0,32},{32,0},{64,96},{96,64},{128,160},{160,128},{192,224},{224,1... | collective-permute-start | bytes 5151752 | tf_op jit(solution)/shard_map/ppermute | solution.py:68
  95.7 13.9 %collective-permute-start.6 = (bf16[352,624]{1,0:T(8,128)(2,1)S(1)}, bf16[352,624]{1,0:T(8,128)(2,1)S(1)}, u32[]{:S(2)}, u32[]{:S(2)}) collective-permute-start(bf16[352,624]{1,0:T(8,128)(2,1)S(1)} %slice.16), channel_id=1, source_target_pairs={{0,64},{32,96},{64,128},{96,160},{128,192},{160,224},{192,256},{22... | collective-permute-start | bytes 1317896 | tf_op jit(solution)/shard_map/ppermute | solution.py:62
  99.1 66.3 %copy-start.33 = (bf16[64,96]{1,0:T(8,128)(2,1)S(1)}, bf16[64,96]{1,0:T(8,128)(2,1)}, u32[]{:S(2)}) copy-start(bf16[64,96]{1,0:T(8,128)(2,1)} %constant.167.refs_19_) | copy-start | bytes 36868
  99.1 66.3 %copy-start.34 = (bf16[49,64]{1,0:T(8,128)(2,1)S(1)}, bf16[49,64]{1,0:T(8,128)(2,1)}, u32[]{:S(2)}) copy-start(bf16[49,64]{1,0:T(8,128)(2,1)} %constant.169.refs_21_) | copy-start | bytes 18820
  99.2 13.1 %collective-permute-start.7 = (bf16[336,624]{1,0:T(8,128)(2,1)S(1)}, bf16[336,624]{1,0:T(8,128)(2,1)S(1)}, u32[]{:S(2)}, u32[]{:S(2)}) collective-permute-start(bf16[336,624]{1,0:T(8,128)(2,1)S(1)} %slice.17), channel_id=1, source_target_pairs={{64,0},{96,32},{128,64},{160,96},{192,128},{224,160},{256,192},{28... | collective-permute-start | bytes 1257992 | tf_op jit(solution)/shard_map/ppermute | solution.py:63
  113.1 52.3 %collective-permute-start.10 = (bf16[1,688,624]{2,1,0:T(8,128)(2,1)}, bf16[1,688,624]{2,1,0:T(8,128)(2,1)}, u32[]{:S(2)}, u32[]{:S(2)}) collective-permute-start(bf16[1,688,624]{2,1,0:T(8,128)(2,1)} %bitcast.33), channel_id=1, source_target_pairs={{0,32},{32,0},{64,96},{96,64},{128,160},{160,128},{192,224},{224,1... | collective-permute-start | bytes 2575880 | tf_op jit(solution)/shard_map/ppermute | solution.py:68
  116.1 13.2 %copy-start.6 = (bf16[56,624]{1,0:T(8,128)(2,1)}, bf16[56,624]{1,0:T(8,128)(2,1)S(1)}, u32[]{:S(2)}) copy-start(bf16[56,624]{1,0:T(8,128)(2,1)S(1)} %pad.27.tile_ref) | copy-start | bytes 209668
  120.2 10.2 %copy-start.12 = (bf16[196,312]{1,0:T(8,128)(2,1)}, bf16[196,312]{1,0:T(8,128)(2,1)S(1)}, u32[]{:S(2)}) copy-start(bf16[196,312]{1,0:T(8,128)(2,1)S(1)} %get-tuple-element.15.middle_ref) | copy-start | bytes 366916
  120.2 5.0 %collective-permute-start.11 = (bf16[88,624]{1,0:T(8,128)(2,1)S(1)}, bf16[88,624]{1,0:T(8,128)(2,1)S(1)}, u32[]{:S(2)}, u32[]{:S(2)}) collective-permute-start(bf16[88,624]{1,0:T(8,128)(2,1)S(1)} %get-tuple-element.13), channel_id=1, source_target_pairs={{0,32},{32,64},{64,96},{96,128},{128,160},{160,192},{192,224},{224... | collective-permute-start | bytes 329480 | tf_op jit(solution)/shard_map/ppermute | solution.py:509
  123.2 6.1 %collective-permute-start.12 = (bf16[88,624]{1,0:T(8,128)(2,1)S(1)}, bf16[88,624]{1,0:T(8,128)(2,1)S(1)}, u32[]{:S(2)}, u32[]{:S(2)}) collective-permute-start(bf16[88,624]{1,0:T(8,128)(2,1)S(1)} %get-tuple-element.14), channel_id=1, source_target_pairs={{32,0},{64,32},{96,64},{128,96},{160,128},{192,160},{224,192},{256... | collective-permute-start | bytes 329480 | tf_op jit(solution)/shard_map/ppermute | solution.py:509
  125.2 5.2 %copy-start.14 = (bf16[88,624]{1,0:T(8,128)(2,1)}, bf16[88,624]{1,0:T(8,128)(2,1)S(1)}, u32[]{:S(2)}) copy-start(bf16[88,624]{1,0:T(8,128)(2,1)S(1)} %collective-permute-done.11.above_ref) | copy-start | bytes 329476
  129.3 5.4 %copy-start.16 = (bf16[88,624]{1,0:T(8,128)(2,1)}, bf16[88,624]{1,0:T(8,128)(2,1)S(1)}, u32[]{:S(2)}) copy-start(bf16[88,624]{1,0:T(8,128)(2,1)S(1)} %collective-permute-done.12.below_ref) | copy-start | bytes 329476
  130.4 12.3 %collective-permute-start.13 = (bf16[208,624]{1,0:T(8,128)(2,1)}, bf16[208,624]{1,0:T(8,128)(2,1)}, u32[]{:S(2)}, u32[]{:S(2)}) collective-permute-start(bf16[208,624]{1,0:T(8,128)(2,1)} %get-tuple-element.16), channel_id=1, source_target_pairs={{0,1},{1,2},{2,3},{3,4},{4,5},{5,6},{6,7},{7,8},{8,9},{9,10},{10,1... | collective-permute-start | bytes 778760 | tf_op jit(solution)/shard_map/ppermute | solution.py:509
  134.7 13.2 %collective-permute-start.14 = (bf16[208,624]{1,0:T(8,128)(2,1)}, bf16[208,624]{1,0:T(8,128)(2,1)}, u32[]{:S(2)}, u32[]{:S(2)}) collective-permute-start(bf16[208,624]{1,0:T(8,128)(2,1)} %get-tuple-element.17), channel_id=1, source_target_pairs={{1,0},{2,1},{3,2},{4,3},{5,4},{6,5},{7,6},{8,7},{9,8},{10,9},{11,1... | collective-permute-start | bytes 778760 | tf_op jit(solution)/shard_map/ppermute | solution.py:509
  147.9 0.9 copy-start.7
  148.8 1.1 copy-start.8
  149.9 1.1 copy-start.9
  151.1 0.9 copy-start.13
  152.0 0.9 copy-start.15
  152.9 0.9 copy-start.17
  153.8 0.9 copy-start.19
  154.7 1.0 copy-start.21
  155.6 0.9 copy-start.23
  156.6 0.9 copy-start.26
  157.5 0.9 copy-start.28
  158.4 0.9 copy-start.29
  165.4 1.2 copy-start.1
  166.6 1.2 copy-start.3
  167.8 1.2 copy-start.5
  168.9 0.9 copy-start.11
  169.9 1.0 copy-start.18
  170.9 0.9 copy-start.20
  171.8 0.9 copy-start.25
  172.7 0.8 copy-start.30
  173.5 0.7 copy-start.35

commit v6 on v5

--- a/solution.py
+++ b/solution.py
@@ -19,73 +19,40 @@
 RING = WIN + 2
 HEAD_ROWS = 40
 BLOCK_ROWS = 4 * HEAD_ROWS
+OUT_ROWS = 48
 TAP_ROWS = 5 * HEAD_ROWS + 8
 SHARDS = 16
 TILE = 56
-KEYS = 9 * TILE + 8
+STRIP = 64
 QUERIES = 96
 SIDE = 2 * WIN
 FIELD = SIDE + 3
 FIELD_ROWS = 304
-FIRST_HALF = 352
 TOP, BOTTOM, LEFT, RIGHT = 200, 232, 248, 288
 
 
-def pack(inproj, outproj, expand, shrink, to_coarse):
+def pack(outproj, expand, shrink, to_coarse):
     width = expand.shape[-1]
-    heads = jnp.concatenate([outproj.T[None], inproj[2:], inproj[:2]])
     taps = jnp.pad(to_coarse, ((0, 1), (0, 1), (0, 0))).reshape(5, 2, HEAD_ROWS, -1)
     return jnp.concatenate(
         [
-            jnp.pad(heads, ((0, 0), (0, 1), (0, 0))).reshape(BLOCK_ROWS, -1),
             jnp.pad(expand, ((0, 4), (0, 0))),
             jnp.pad(shrink.T, ((0, 4), (0, 0))),
+            jnp.pad(outproj.T, ((0, 1), (0, 0))),
             taps.transpose(0, 2, 1, 3).reshape(-1, width),
-            jnp.zeros((8, width), expand.dtype),
         ]
     )
 
 
-def all_shards(mine):
-    size = lax.axis_size("rows")
-    swap = [(i, i ^ 1) for i in range(size)]
-    up = [(i, (i + 2) % size) for i in range(size)]
-    down = [(j, i) for i, j in up]
-    rising, falling = [mine], [mine]
-    for _ in range(3):
-        rising.append(lax.ppermute(rising[-1], "rows", up))
-        falling.append(lax.ppermute(falling[-1], "rows", down))
-    near = [mine, rising[1], falling[1], rising[2], falling[2]]
-    far = [rising[3], falling[3]]
-    last = jnp.concatenate(
-        [
-            lax.ppermute(rising[3][:FIRST_HALF], "rows", up),
-            lax.ppermute(falling[3][FIRST_HALF:], "rows", down),
-        ]
-    )
-    sources = near + far + [last]
-    for group in (near, far, [last]):
-        sources.append(lax.ppermute(jnp.stack(group), "rows", swap))
-    place = lax.axis_index("rows")
-    chips = [2 * ((place // 2 + away) % (size // 2)) for away in (0, -1, 1, -2, 2, -3, 3, 4)]
-    core = place % 2
-    owners = [chip + core for chip in chips] + [chip + 1 - core for chip in chips]
-    return sources, jnp.stack(owners).astype(jnp.int32)
-
-
-def attention_tables():
-    pick = np.zeros((QUERIES, KEYS), np.float32)
-    bias = np.full((QUERIES, KEYS), -1e30, np.float32)
+def strip_tables():
+    spread = np.zeros((STRIP, 3 * TILE), np.float32)
+    columns = np.zeros((32, STRIP), np.float32)
     for row in range(RING):
-        for col in range(RING):
-            down = 1 if row == 0 else 2 if row == RING - 1 else 0
-            side = 1 if col == 0 else 2 if col == RING - 1 else 0
-            first = (3 * side + down) * TILE
-            query = row * RING + col
-            pick[query, first + (row - 1) % WIN * WIN + (col - 1) % WIN] = 1
-            bias[query, first : first + CELLS] = 0
-    bias[RING * RING :, :CELLS] = 0
-    return jnp.asarray(bias), jnp.asarray(pick).astype(jnp.bfloat16)
+        for col in range(WIN):
+            spread[row * WIN + col, (row + 6) // WIN * TILE + (row + 6) % WIN * WIN + col] = 1
+        columns[row, row * WIN + WIN - 1] = 1
+        columns[16 + row, row * WIN] = 1
+    return tuple(jnp.asarray(t).astype(jnp.bfloat16) for t in (spread, columns))
 
 
 def window_table():
@@ -144,6 +111,12 @@
 
 def cell_tables():
     side = 2 * WIN
+    square = np.zeros((QUERIES, QUERIES), np.float32)
+    for row in range(RING):
+        for col in range(WIN):
+            square[row * RING + col + 1, row * WIN + col] = 1
+        square[row * RING, STRIP + row] = 1
+        square[row * RING + RING - 1, STRIP + 16 + row] = 1
     centre = np.zeros((64, QUERIES), np.float32)
     repeat = np.zeros((side * side, 64), np.float32)
     compact = np.zeros((CELLS, 64), np.float32)
@@ -154,7 +127,7 @@
     for cell in range(side * side):
         row, col = divmod(cell, side)
         repeat[cell, row // 2 * 8 + col // 2] = 1
-    return tuple(jnp.asarray(t).astype(jnp.bfloat16) for t in (centre, repeat, compact))
+    return tuple(jnp.asarray(t).astype(jnp.bfloat16) for t in (square, centre, repeat, compact))
 
 
 def gelu(values):
@@ -181,7 +154,7 @@
 
 
 def fine_attention_kernel(
-    fine_ref, inproj_ref, outproj_ref, mask_ref, tile_ref, middle_ref, down_ref, up_ref
+    fine_ref, inproj_ref, outproj_ref, mask_ref, middle_ref, down_ref, up_ref
 ):
     cells, channels = fine_ref.shape
     fine = fine_ref[...].astype(jnp.float32)
@@ -203,41 +176,91 @@
     middle_ref[...] = middle.astype(jnp.bfloat16)
     for target, first, count in ((down_ref, cells - 2 * SIDE, 2 * SIDE), (up_ref, 0, SIDE)):
         target[...] = jnp.zeros(target.shape, jnp.bfloat16)
-        target[:TILE, :] = tile_ref[...]
-        target[TILE : TILE + count, :channels] = middle_ref[first : first + count, :]
+        target[:count, :] = middle_ref[first : first + count, :]
 
 
 def columns_kernel(
-    tile_ref, above_ref, below_ref, middle_ref, right_ref, left_ref, to_right_ref, to_left_ref,
+    above_ref, below_ref, middle_ref, columns_ref, right_ref, left_ref, to_right_ref, to_left_ref,
     field_ref,
 ):
     cells, channels = middle_ref.shape
     field_ref[...] = jnp.zeros(field_ref.shape, jnp.float32)
     field_ref[:cells, :] = middle_ref[...].astype(jnp.float32)
-    field_ref[TOP : TOP + 2 * SIDE, :] = above_ref[TILE : TILE + 2 * SIDE, :channels].astype(
-        jnp.float32
-    )
-    field_ref[BOTTOM : BOTTOM + SIDE, :] = below_ref[TILE : TILE + SIDE, :channels].astype(
-        jnp.float32
-    )
+    field_ref[TOP : TOP + 2 * SIDE, :] = above_ref[: 2 * SIDE, :].astype(jnp.float32)
+    field_ref[BOTTOM : BOTTOM + SIDE, :] = below_ref[:SIDE, :].astype(jnp.float32)
     field = field_ref[...].astype(jnp.bfloat16)
-    for target, table in ((to_right_ref, right_ref), (to_left_ref, left_ref)):
+    for index, (target, table) in enumerate(((to_right_ref, right_ref), (to_left_ref, left_ref))):
         target[...] = jnp.zeros(target.shape, jnp.bfloat16)
-        target[:TILE, :] = tile_ref[...]
-        target[TILE : 2 * TILE, :] = above_ref[:TILE, :]
-        target[2 * TILE : 3 * TILE, :] = below_ref[:TILE, :]
         count = table.shape[0]
-        target[3 * TILE : 3 * TILE + count, :channels] = nn(table[...], field).astype(jnp.bfloat16)
+        target[:count, :channels] = nn(table[...], field).astype(jnp.bfloat16)
+        target[48:, :] = columns_ref[16 * index : 16 * index + 16, :]
+
+
+def strip_kernel(
+    edge_ref,
+    place_ref,
+    strip_ref,
+    weights_ref,
+    spread_ref,
+    column_ref,
+    blocks_ref,
+    own_ref,
+    columns_ref,
+    normed_ref,
+    proj_ref,
+    attended_ref,
+    images_ref,
+):
+    tiles, cells, width = strip_ref.shape
+    normed_ref[...] = jnp.zeros(normed_ref.shape, jnp.float32)
+    attended_ref[...] = jnp.zeros(attended_ref.shape, jnp.float32)
+    images_ref[...] = jnp.zeros(images_ref.shape, jnp.float32)
+    for tile in range(tiles):
+        normed_ref[tile, :cells, :] = norm_rows(strip_ref[tile].astype(jnp.float32)).astype(
+            jnp.float32
+        )
+    normed = normed_ref[...].astype(jnp.bfloat16).reshape(tiles * TILE, width)
+    for part in range(3):
+        proj_ref[part] = nt(normed, weights_ref[part]).reshape(tiles, TILE, -1)
+    key = lax.broadcasted_iota(jnp.int32, (TILE, TILE), 1)
+    mask = jnp.where(key < cells, 0.0, -1e30)
+    for tile in range(tiles):
+        queries, keys, values = (proj_ref[part, tile].astype(jnp.bfloat16) for part in range(3))
+        scores = nt(queries, keys) * (1.0 / math.sqrt(39)) + mask
+        exponent = jnp.exp(scores - jnp.max(scores, axis=1, keepdims=True))
+        total = jnp.sum(exponent, axis=1, keepdims=True)
+        chance = (exponent * (1.0 / total)).astype(jnp.bfloat16)
+        attended_ref[tile + 1, :, :39] = nn(chance, values)
+    spread = spread_ref[...]
+    for tile in range(tiles):
+        near = attended_ref[tile : tile + 3].astype(jnp.bfloat16).reshape(3 * TILE, HEAD_ROWS)
+        blocks_ref[tile] = nn(spread, near).astype(jnp.bfloat16)
+    place = place_ref[0]
+    before = jnp.maximum(place - 1, 0)
+    after = jnp.minimum(place + 1, tiles - 1)
+    for index, (tile, there) in enumerate(
+        ((before, edge_ref[0]), (place, 1), (after, edge_ref[1]))
+    ):
+        image = strip_ref[tile].astype(jnp.float32)
+        images_ref[index * TILE : index * TILE + cells, :] = jnp.where(there == 1, image, 0.0)
+    own = nn(spread, images_ref[...].astype(jnp.bfloat16)).astype(jnp.bfloat16)
+    own_ref[...] = own
+    columns_ref[...] = nn(column_ref[...], own).astype(jnp.bfloat16)
+
+
+def edge_columns_kernel(blocks_ref, column_ref, right_ref, left_ref):
+    for head in range(SHARDS):
+        columns = nn(column_ref[...], blocks_ref[head]).astype(jnp.bfloat16)
+        right_ref[head] = columns[:16]
+        left_ref[head] = columns[16:]
 
 
 def field_kernel(
     edge_ref,
-    tile_ref,
     above_ref,
     below_ref,
     left_ref,
     right_ref,
-    pick_ref,
     middle_ref,
     expand_ref,
     depth_ref,
@@ -246,39 +269,21 @@
     inner_ref,
     cell_ref,
     sample_ref,
-    normed_ref,
-    own_ref,
     fine_ref,
     samples_ref,
-    tiles_ref,
     pieces_ref,
     hidden_ref,
     conv_ref,
     twice_ref,
 ):
     cells, channels = middle_ref.shape
-    tiles_ref[9 * TILE :, :] = jnp.zeros((KEYS - 9 * TILE, tiles_ref.shape[1]), jnp.float32)
-    first = 0
-    for piece, count in (
-        (tile_ref, TILE),
-        (above_ref, TILE),
-        (below_ref, TILE),
-        (left_ref, 3 * TILE),
-        (right_ref, 3 * TILE),
-    ):
-        tiles_ref[first : first + count, :] = piece[:count, :].astype(jnp.float32)
-        first += count
-    tiles = tiles_ref[...]
-    normed_ref[...] = norm_rows(tiles)
-    own_ref[...] = nn(pick_ref[...], tiles.astype(jnp.bfloat16)).astype(jnp.bfloat16)
-
     pieces_ref[...] = jnp.zeros(pieces_ref.shape, jnp.float32)
     pieces_ref[:cells, :] = middle_ref[...].astype(jnp.float32)
     for piece, start, first, count in (
-        (above_ref, TILE, TOP, 2 * SIDE),
-        (below_ref, TILE, BOTTOM, SIDE),
-        (left_ref, 3 * TILE, LEFT, 2 * FIELD),
-        (right_ref, 3 * TILE, RIGHT, FIELD),
+        (above_ref, 0, TOP, 2 * SIDE),
+        (below_ref, 0, BOTTOM, SIDE),
+        (left_ref, 0, LEFT, 2 * FIELD),
+        (right_ref, 0, RIGHT, FIELD),
     ):
         pieces_ref[first : first + count, :] = piece[start : start + count, :channels].astype(
             jnp.float32
@@ -335,69 +340,40 @@
 
 def coarse_kernel(
     edge_ref,
-    owner_ref,
-    *refs,
-):
-    sources, rest = refs[:11], refs[11:]
-    coarse_body(edge_ref, owner_ref, sources, *rest)
-
-
-def coarse_body(
-    edge_ref,
-    owner_ref,
-    sources,
-    normed_ref,
+    gathered_ref,
+    attended_ref,
     own_ref,
-    bias_ref,
-    pick_ref,
     depth_ref,
     samples_ref,
     fine_ref,
     to_fine_ref,
+    square_ref,
     centre_ref,
     repeat_ref,
     compact_ref,
     fine_out_ref,
     coarse_out_ref,
-    heads_ref,
+    out_ref,
     expand_ref,
     shrink_ref,
     taps_ref,
-    proj_ref,
-    chosen_ref,
-    chance_ref,
-    attended_ref,
     hidden_ref,
     conv_ref,
     down_ref,
     sems,
 ):
     spans = (
-        (heads_ref, 0, BLOCK_ROWS),
-        (expand_ref, BLOCK_ROWS, BLOCK_ROWS),
-        (shrink_ref, 2 * BLOCK_ROWS, BLOCK_ROWS),
-        (taps_ref, 3 * BLOCK_ROWS, TAP_ROWS),
-    )
-    slots = list(sources[:8])
-    for source, count in zip(sources[8:], (5, 2, 1)):
-        slots += [source.at[i] for i in range(count)]
-    copies = []
-    for part, (target, first, count) in enumerate(spans):
-        copies.append(
-            [
-                pltpu.make_async_copy(
-                    slot.at[pl.ds(first, count)], target.at[owner_ref[place]], sems.at[part, place]
-                )
-                for place, slot in enumerate(slots)
-            ]
-        )
-        for copy in copies[-1]:
-            copy.start()
-
-    def arrive(part):
-        for copy in copies[part]:
-            copy.wait()
-
+        (out_ref, 2 * BLOCK_ROWS, OUT_ROWS),
+        (expand_ref, 0, BLOCK_ROWS),
+        (shrink_ref, BLOCK_ROWS, BLOCK_ROWS),
+        (taps_ref, 2 * BLOCK_ROWS + 32, TAP_ROWS),
+    )
+    copies = [
+        pltpu.make_async_copy(gathered_ref.at[:, pl.ds(first, count)], target, sems.at[part])
+        for part, (target, first, count) in enumerate(spans)
+    ]
+    for copy in copies:
+        copy.start()
     width = own_ref.shape[1]
     query = lax.broadcasted_iota(jnp.int32, (QUERIES, 128), 0)
     column = query % RING
@@ -409,29 +385,13 @@
     )
     inside = jnp.where(outside, 0.0, 1.0)[:, :1]
     conv_ref[8 * WIN :, :] = jnp.zeros((8, conv_ref.shape[1]), jnp.float32)
-    arrive(0)
-    heads = heads_ref[:, 32:BLOCK_ROWS, :].reshape(SHARDS * 128, width)
-    proj_ref[...] = nt(heads, normed_ref[...]).reshape(SHARDS, 128, KEYS)
-    pick = pick_ref[...]
+    mixed = own_ref[...].astype(jnp.float32)
+    copies[0].wait()
     for head in range(SHARDS):
-        queries = proj_ref[head, 48:88].astype(jnp.bfloat16)
-        chosen_ref[head] = nt(pick, queries)
-    bias = bias_ref[...]
-    for head in range(SHARDS):
-        keys = proj_ref[head, 88:128].astype(jnp.bfloat16)
-        scores = nn(chosen_ref[head].astype(jnp.bfloat16), keys) * (1.0 / math.sqrt(39)) + bias
-        exponent = jnp.exp(scores - jnp.max(scores, axis=1, keepdims=True))
-        total = jnp.sum(exponent, axis=1, keepdims=True)
-        chance_ref[head] = (exponent * (1.0 / total)).astype(jnp.bfloat16)
-    for head in range(SHARDS):
-        values = proj_ref[head, 8:48].astype(jnp.bfloat16)
-        attended_ref[head] = nt(chance_ref[head], values)
-    mixed = own_ref[...].astype(jnp.float32)
-    for head in range(SHARDS):
-        mixed += nn(attended_ref[head].astype(jnp.bfloat16), heads_ref[head][:HEAD_ROWS])
-    middle = mixed.astype(jnp.bfloat16)
+        mixed += nn(attended_ref[head], out_ref[head][:HEAD_ROWS])
+    middle = nn(square_ref[...], mixed.astype(jnp.bfloat16)).astype(jnp.bfloat16)
     normed_mid = norm_rows(middle.astype(jnp.float32))
-    arrive(1)
+    copies[1].wait()
     chunk = 512
     expand = expand_ref[...].reshape(SHARDS * BLOCK_ROWS, width)
     for first in range(0, SHARDS * BLOCK_ROWS, chunk):
@@ -445,7 +405,7 @@
                 window = hidden_ref[pl.ds((row + down) * RING + side, 8), span]
                 total += depth_ref[tap : tap + 1, span] * window
             conv_ref[row * 8 : row * 8 + 8, span] = gelu(total)
-    arrive(2)
+    copies[2].wait()
     shrink = shrink_ref[...].reshape(SHARDS * BLOCK_ROWS, width)
     update = nn(conv_ref[...].astype(jnp.bfloat16), shrink)
     result = (nn(centre_ref[...], middle) + update).astype(jnp.bfloat16)
@@ -454,14 +414,14 @@
     fine_out_ref[...] = jnp.maximum(
         fine_ref[...].astype(jnp.float32) + upsampled, 0.0
     ).astype(jnp.bfloat16)
-    arrive(3)
+    copies[3].wait()
     samples = samples_ref[...]
     for shard in range(SHARDS):
         four = nt(taps_ref[shard], samples[: 4 * 64])
         fifth = nt(taps_ref[shard][4 * HEAD_ROWS :], samples[4 * 64 :])
-        total = fifth[:HEAD_ROWS]
+        total = fifth[8:]
         for block in range(4):
-            rows = slice(block * HEAD_ROWS, (block + 1) * HEAD_ROWS)
+            rows = slice(8 + block * HEAD_ROWS, 8 + (block + 1) * HEAD_ROWS)
             total += four[rows, block * 64 : (block + 1) * 64]
         down_ref[shard * 39 : shard * 39 + HEAD_ROWS, :64] = total
     downsampled = down_ref[...].T[:CELLS, :width].astype(jnp.bfloat16).astype(jnp.float32)
@@ -470,10 +430,10 @@
     ).astype(jnp.bfloat16)
 
 
-def coarse_stream(sources, edges, owners, normed, own, pick, bias, depth, samples, fine_res, to_fine):
+def coarse_stream(gathered, edges, attended, own, depth, samples, fine_res, to_fine):
     width = own.shape[1]
     fine_cells, fine_ch = fine_res.shape
-    operands = (normed, own, bias, pick, depth, samples, fine_res, to_fine, *cell_tables())
+    operands = (attended, own, depth, samples, fine_res, to_fine, *cell_tables())
     smem, vmem, anywhere = (
         pl.BlockSpec(memory_space=space) for space in (pltpu.SMEM, pltpu.VMEM, pl.ANY)
     )
@@ -483,24 +443,20 @@
             jax.ShapeDtypeStruct((fine_cells, fine_ch), jnp.bfloat16),
             jax.ShapeDtypeStruct((CELLS, width), jnp.bfloat16),
         ),
-        in_specs=[smem, smem] + [anywhere] * len(sources) + [vmem] * len(operands),
+        in_specs=[smem, anywhere] + [vmem] * len(operands),
         out_specs=(vmem, vmem),
         scratch_shapes=[
-            pltpu.VMEM((SHARDS, BLOCK_ROWS, width), jnp.bfloat16),
+            pltpu.VMEM((SHARDS, OUT_ROWS, width), jnp.bfloat16),
             pltpu.VMEM((SHARDS, BLOCK_ROWS, width), jnp.bfloat16),
             pltpu.VMEM((SHARDS, BLOCK_ROWS, width), jnp.bfloat16),
             pltpu.VMEM((SHARDS, TAP_ROWS, width), jnp.bfloat16),
-            pltpu.VMEM((SHARDS, 128, KEYS), jnp.float32),
-            pltpu.VMEM((SHARDS, QUERIES, HEAD_ROWS), jnp.float32),
-            pltpu.VMEM((SHARDS, QUERIES, KEYS), jnp.bfloat16),
-            pltpu.VMEM((SHARDS, QUERIES, HEAD_ROWS), jnp.float32),
             pltpu.VMEM((QUERIES, SHARDS * BLOCK_ROWS), jnp.float32),
             pltpu.VMEM((64, SHARDS * BLOCK_ROWS), jnp.float32),
             pltpu.VMEM((SHARDS * HEAD_ROWS, 128), jnp.float32),
-            pltpu.SemaphoreType.DMA((4, SHARDS)),
+            pltpu.SemaphoreType.DMA((4,)),
         ],
-        compiler_params=pltpu.CompilerParams(vmem_limit_bytes=44 * 1024 * 1024),
-    )(edges, owners, *sources, *operands)
+        compiler_params=pltpu.CompilerParams(vmem_limit_bytes=32 * 1024 * 1024),
+    )(edges, gathered, *operands)
 
 
 def exchange(onward, back, axis):
@@ -527,10 +483,8 @@
 ):
     fine_ch, fine_cells = fine_in.shape[2:]
     coarse_ch, coarse_cells = coarse_in.shape[2:]
-    sources, owners = all_shards(
-        pack(inproj_coarse, outproj_coarse, expand_coarse, shrink_coarse, to_coarse)
-    )
-    tile = jnp.pad(coarse_in.reshape(coarse_ch, coarse_cells).T, ((0, TILE - coarse_cells), (0, 0)))
+    gathered = lax.all_gather(pack(outproj_coarse, expand_coarse, shrink_coarse, to_coarse), "rows")
+    strip = lax.all_gather(coarse_in.reshape(coarse_ch, coarse_cells).T, "rows")
     fine = fine_in.reshape(fine_ch, fine_cells).T
     place = (lax.axis_index("rows"), lax.axis_index("cols"))
     edges = jnp.stack(
@@ -541,35 +495,46 @@
             place[1] < lax.axis_size("cols") - 1,
         ]
     ).astype(jnp.int32)
-    message = (TILE + 32, coarse_ch)
     middle, going_down, going_up = call(
         fine_attention_kernel,
-        (fine.shape, message, message),
-        (fine, inproj_fine, outproj_fine, window_table(), tile),
+        (fine.shape, (32, fine_ch), (16, fine_ch)),
+        (fine, inproj_fine, outproj_fine, window_table()),
         (),
     )
     above, below = exchange(going_down, going_up, "rows")
-    message = (3 * TILE + 40, coarse_ch)
+    spread, column = strip_tables()
+    blocks, own, columns = call(
+        strip_kernel,
+        ((SHARDS, STRIP, HEAD_ROWS), (STRIP, coarse_ch), (32, coarse_ch)),
+        (edges, place[0].reshape(1).astype(jnp.int32), strip, inproj_coarse, spread, column),
+        (
+            ((SHARDS, TILE, coarse_ch), jnp.float32),
+            ((3, SHARDS, TILE, 39), jnp.float32),
+            ((SHARDS + 2, TILE, HEAD_ROWS), jnp.float32),
+            ((3 * TILE, coarse_ch), jnp.float32),
+        ),
+        scalars=2,
+    )
+    blocks = lax.all_to_all(blocks, "rows", 0, 0, tiled=True)
     going_right, going_left = call(
         columns_kernel,
-        (message, message),
-        (tile, above, below, middle, *border_tables()),
+        ((64, coarse_ch), (64, coarse_ch)),
+        (above, below, middle, columns, *border_tables()),
         (((248, fine_ch), jnp.float32),),
     )
     left, right = exchange(going_right, going_left, "cols")
-    bias, pick = attention_tables()
+    edge = (SHARDS, 16, HEAD_ROWS)
+    near = exchange(*call(edge_columns_kernel, (edge, edge), (blocks, column), ()), "cols")
     hidden_count = expand_fine.shape[0]
-    normed, own, fine_res, samples = call(
+    fine_res, samples = call(
         field_kernel,
-        ((KEYS, coarse_ch), (QUERIES, coarse_ch), fine.shape, (5 * 64, 2 * fine_ch)),
+        (fine.shape, (5 * 64, 2 * fine_ch)),
         (
             edges,
-            tile,
             above,
             below,
             left,
             right,
-            pick,
             middle,
             expand_fine.T,
             depth_fine,
@@ -577,7 +542,6 @@
             *field_tables(),
         ),
         (
-            ((KEYS, coarse_ch), jnp.float32),
             ((320, fine_ch), jnp.float32),
             ((FIELD_ROWS, hidden_count), jnp.float32),
             ((256, hidden_count), jnp.bfloat16),
@@ -587,13 +551,10 @@
     )
     depth = jnp.pad(depth_coarse.reshape(9, SHARDS, -1), ((0, 0), (0, 0), (0, 4)))
     fine_out, coarse_out = coarse_stream(
-        sources,
+        gathered,
         edges,
-        owners,
-        normed,
-        own,
-        pick,
-        bias,
+        jnp.concatenate([blocks, *near], axis=1),
+        jnp.concatenate([own, left[48:], right[48:]]),
         depth.reshape(9, -1),
         samples,
         fine_res,

time: 195 us -> 123 us (0.63)
  the two profiles are of different devices: /device:TPU:95 before, /device:TPU:31 now
where the time goes in v6:
time: 123 us; the launch traced here: 122 us
  blocking collectives  29.8 us (24%)
  starting transfers between devices  26.8 us (22%)
  Pallas kernels  26.4 us (21%)
  local copies, waits for them, and re-layouts  18.2 us (15%)
  between operations  14.5 us (12%)
  waiting for transfers between devices  4.84 us (4%)
    all_gather x1, blocking collectives, local(): strip = lax.all_gather(coarse_in.reshape(coarse_ch, coarse_cells).T, 'rows')  29.8 us
    ppermute x6, starting transfers between devices, exchange(): return (lax.ppermute(onward, axis, up), lax.ppermute(back, axis, down))  23.3 us
    pallas_call x5, Pallas kernels, call(): pl.pallas_call(kernel, out_shape=tuple((jax.ShapeDtypeStruct(shape, jnp.b...  16.9 us
    unnamed x68, local copies, waits for them, and re-layouts  16 us
    pallas_call x1, Pallas kernels, coarse_stream(): pl.pallas_call(coarse_kernel, out_shape=(jax.ShapeDtypeStruct((fine_cells...  9.57 us
    ppermute x6, waiting for transfers between devices, exchange(): return (lax.ppermute(onward, axis, up), lax.ppermute(back, axis, down))  4.8 us
    all_to_all x1, starting transfers between devices, local(): blocks = lax.all_to_all(blocks, 'rows', 0, 0, tiled=True)  3.45 us
  transfers between devices with their start and end apart: 8, of which 2 were waited for; matrix products, arithmetic and copies ran while one was open for 1% of the time, Pallas kernels for 14%

profile of v6, /device:TPU:31, one launch (start us, length us, event | category | flops | bytes accessed | tf_op | source)
XLA Modules:
  0.0 121.7 jit_solution(5216452754981710421)
XLA Ops:
  7.2 0.0 all-gather.5.cloned.1.call-start
  7.2 1.1 pad.22
  8.3 0.2 copy.36
  8.6 0.0 copy-start.31
  8.6 0.2 reshape.32
  8.9 0.0 copy-start.12
  8.9 0.0 copy-start.21
  8.9 0.0 copy-start.22
  8.9 0.9 fusion.6
  9.9 0.0 all-gather.5.cloned.1.call-update
  9.9 0.1 add_convert_fusion.edge_ref
  10.0 0.0 copy-start.8
  10.0 0.0 copy-start.13
  10.0 29.8 %all-gather.2.strip_ref = bf16[16,49,624]{2,1,0:T(8,128)(2,1)S(1)} all-gather(bf16[1,49,624]{2,1,0:T(8,128)(2,1)S(1)} %bitcast.35), channel_id=3, replica_groups=mesh['rows'=16,'cols'=32] {'rows'}, dimensions={0}, use_global_device_ids=true | all-gather | bytes 1039584 | tf_op jit(solution)/shard_map/all_gather | solution.py:487
  39.8 0.0 copy-start.24
  39.8 0.0 copy-start.26
  39.8 7.1 %shard_map.266 = (bf16[16,64,40]{2,1,0:T(8,128)(2,1)S(1)}, bf16[64,624]{1,0:T(8,128)(2,1)S(1)}, bf16[32,624]{1,0:T(8,128)(2,1)S(1)}) custom-call(s32[4]{0:T(128)S(1)} %add_convert_fusion.edge_ref, s32[1]{0:T(128)} %bitcast.9.place_ref, bf16[16,49,624]{2,1,0:T(8,128)(2,1)S(1)} %all-gather.2.strip_ref, bf16[3,39,624]{2,1,0:T(8,128)(2,1)S(1)} %copy-done.12, ...), custom_call_target="tpu_custom_call" | custom-call | tf_op jit(solution)/shard_map/pallas_call | solution.py:331
  46.9 0.0 copy-start.30
  46.9 0.2 copy.37
  47.1 0.8 reshape.45
  47.9 3.4 %all-to-all-start = ((bf16[16,2,1280]{2,1,0:T(2,128)(2,1)}), bf16[16,2,1280]{2,1,0:T(2,128)(2,1)S(1)}, u32[]{:S(2)}, u32[]{:S(2)}) async-start(bf16[16,2,1280]{2,1,0:T(2,128)(2,1)} %reshape.45), calls=%async_computation | async-start | bytes 163840 | tf_op jit(solution)/shard_map/all_to_all | solution.py:518
  51.4 4.0 %shard_map.268 = (bf16[196,312]{1,0:T(8,128)(2,1)S(1)}, bf16[32,312]{1,0:T(8,128)(2,1)S(1)}, bf16[16,312]{1,0:T(8,128)(2,1)S(1)}) custom-call(bf16[196,312]{1,0:T(8,128)(2,1)S(1)} %bitcast.30, bf16[3,312,312]{2,1,0:T(8,128)(2,1)S(1)} %copy-done.3, bf16[312,312]{1,0:T(8,128)(2,1)S(1)} %copy-done.6, f32[196,196]{1,0:T(8,128)S(1)} %copy-done.8), custom_call_target="tpu_custom_call" | custom-call | tf_op jit(solution)/shard_map/pallas_call | solution.py:331
  55.4 0.0 copy-start.1
  55.4 0.0 copy-start.2
  55.4 0.0 copy-start.5
  55.4 3.7 %collective-permute-start.2 = (bf16[32,312]{1,0:T(8,128)(2,1)S(1)}, bf16[32,312]{1,0:T(8,128)(2,1)S(1)}, u32[]{:S(2)}, u32[]{:S(2)}) collective-permute-start(bf16[32,312]{1,0:T(8,128)(2,1)S(1)} %get-tuple-element.20), channel_id=1, source_target_pairs={{0,32},{32,64},{64,96},{96,128},{128,160},{160,192},{192,224},{224... | collective-permute-start | bytes 59912 | tf_op jit(solution)/shard_map/ppermute | solution.py:465
  59.1 1.9 %collective-permute-start.3 = (bf16[16,312]{1,0:T(8,128)(2,1)S(1)}, bf16[16,312]{1,0:T(8,128)(2,1)S(1)}, u32[]{:S(2)}, u32[]{:S(2)}) collective-permute-start(bf16[16,312]{1,0:T(8,128)(2,1)S(1)} %get-tuple-element.21), channel_id=1, source_target_pairs={{32,0},{64,32},{96,64},{128,96},{160,128},{192,160},{224,192},{256... | collective-permute-start | bytes 29960 | tf_op jit(solution)/shard_map/ppermute | solution.py:465
  61.0 3.7 %collective-permute-done.3.below_ref = bf16[16,312]{1,0:T(8,128)(2,1)S(1)} collective-permute-done((bf16[16,312]{1,0:T(8,128)(2,1)S(1)}, bf16[16,312]{1,0:T(8,128)(2,1)S(1)}, u32[]{:S(2)}, u32[]{:S(2)}) %collective-permute-start.3) | collective-permute-done | bytes 10016 | tf_op jit(solution)/shard_map/ppermute | solution.py:465
  64.8 0.0 collective-permute-done.2.above_ref
  64.8 0.2 shard_map.269
  65.0 0.4 copy-done.19
  65.4 2.4 %collective-permute-start.5 = (bf16[64,624]{1,0:T(8,128)(2,1)S(1)}, bf16[64,624]{1,0:T(8,128)(2,1)S(1)}, u32[]{:S(2)}, u32[]{:S(2)}) collective-permute-start(bf16[64,624]{1,0:T(8,128)(2,1)S(1)} %get-tuple-element.25), channel_id=1, source_target_pairs={{1,0},{2,1},{3,2},{4,3},{5,4},{6,5},{7,6},{8,7},{9,8},{10,9},{11,1... | collective-permute-start | bytes 239624 | tf_op jit(solution)/shard_map/ppermute | solution.py:465
  67.8 6.2 %collective-permute-start.4 = (bf16[64,624]{1,0:T(8,128)(2,1)S(1)}, bf16[64,624]{1,0:T(8,128)(2,1)S(1)}, u32[]{:S(2)}, u32[]{:S(2)}) collective-permute-start(bf16[64,624]{1,0:T(8,128)(2,1)S(1)} %get-tuple-element.24), channel_id=1, source_target_pairs={{0,1},{1,2},{2,3},{3,4},{4,5},{5,6},{6,7},{7,8},{8,9},{9,10},{10,1... | collective-permute-start | bytes 239624 | tf_op jit(solution)/shard_map/ppermute | solution.py:465
  74.0 0.2 reshape.36
  74.2 0.1 reshape.37.depth_ref
  74.3 0.0 collective-permute-done.5.right_ref
  74.4 1.1 collective-permute-done.4.left_ref
  75.4 0.2 reshape.46
  75.6 0.5 copy-done.14
  76.1 0.2 copy.39.blocks_ref
  76.2 0.2 shard_map.267
  76.4 1.9 %collective-permute-start.1 = (bf16[16,16,40]{2,1,0:T(8,128)(2,1)S(1)}, bf16[16,16,40]{2,1,0:T(8,128)(2,1)S(1)}, u32[]{:S(2)}, u32[]{:S(2)}) collective-permute-start(bf16[16,16,40]{2,1,0:T(8,128)(2,1)S(1)} %get-tuple-element.18), channel_id=1, source_target_pairs={{1,0},{2,1},{3,2},{4,3},{5,4},{6,5},{7,6},{8,7},{9,8},{10,9},{11,1... | collective-permute-start | bytes 61448 | tf_op jit(solution)/shard_map/ppermute | solution.py:465
  78.4 7.2 %collective-permute-start = (bf16[16,16,40]{2,1,0:T(8,128)(2,1)S(1)}, bf16[16,16,40]{2,1,0:T(8,128)(2,1)S(1)}, u32[]{:S(2)}, u32[]{:S(2)}) collective-permute-start(bf16[16,16,40]{2,1,0:T(8,128)(2,1)S(1)} %get-tuple-element.17), channel_id=1, source_target_pairs={{0,1},{1,2},{2,3},{3,4},{4,5},{5,6},{6,7},{7,8},{8,9},{9,10},{10,1... | collective-permute-start | bytes 61448 | tf_op jit(solution)/shard_map/ppermute | solution.py:465
  85.6 0.0 copy-start.7
  85.7 1.0 copy-done.7
  86.6 0.9 copy-done.9
  87.6 0.9 copy-done.15
  88.4 0.9 copy-done.16
  89.3 0.9 copy-done.17
  90.2 0.7 copy-done.20
  90.9 5.4 %shard_map.270 = (bf16[196,312]{1,0:T(8,128)(2,1)S(1)}, bf16[320,624]{1,0:T(8,128)(2,1)S(1)}) custom-call(s32[4]{0:T(128)S(1)} %add_convert_fusion.edge_ref, bf16[32,312]{1,0:T(8,128)(2,1)S(1)} %collective-permute-done.2.above_ref, bf16[16,312]{1,0:T(8,128)(2,1)S(1)} %copy-done.20, bf16[64,624]{1,0:T(8,128)(2,1)S(1)} %copy-done.15, ...), custom_call_target="tpu_custom_call" | custom-call | tf_op jit(solution)/shard_map/pallas_call | solution.py:331
  96.3 0.0 copy-start.10
  96.3 0.7 copy-done.10
  97.0 0.0 collective-permute-done.1
  97.0 0.0 collective-permute-done
  97.0 0.1 pad_maximum_fusion.attended_ref
  97.1 0.0 all-gather.5.cloned.1.call-done
  97.1 4.2 %copy-done = bf16[8960,624]{1,0:T(8,128)(2,1)S(1)} copy-done((bf16[8960,624]{1,0:T(8,128)(2,1)S(1)}, bf16[8960,624]{1,0:T(8,128)(2,1)}, u32[]{:S(2)}) %copy-start) | copy-done | bytes 11182104
  101.4 0.9 copy-done.11
  102.3 0.8 copy-done.18
  103.1 0.7 copy-done.23
  103.8 0.7 copy-done.25
  104.6 0.7 copy-done.27
  105.3 9.6 %shard_map.271 = (bf16[196,312]{1,0:T(8,128)(2,1)}, bf16[49,624]{1,0:T(8,128)(2,1)}) custom-call(s32[4]{0:T(128)S(1)} %add_convert_fusion.edge_ref, bf16[16,560,624]{2,1,0:T(8,128)(2,1)S(1)} %bitcast.28, bf16[16,96,40]{2,1,0:T(8,128)(2,1)S(1)} %pad_maximum_fusion.attended_ref, bf16[96,624]{1,0:T(8,128)(2,1)S(1)} %pad_maximum_fusion.1.own_ref, ...), custom_call_target="tpu_custom_call" | custom-call | tf_op jit(solution)/shard_map/pallas_call | solution.py:440
  (42 shorter events, 0.1 us)
Async XLA Ops:
  7.2 1.7 %copy-start.32 = (bf16[624,39]{0,1:T(8,128)(2,1)S(1)}, bf16[624,39]{0,1:T(8,128)(2,1)}, u32[]{:S(2)}) copy-start(bf16[624,39]{0,1:T(8,128)(2,1)} %param.35) | copy-start | bytes 146020
  7.2 1.7 %copy-start.28 = (bf16[624,156]{0,1:T(8,128)(2,1)S(1)}, bf16[624,156]{0,1:T(8,128)(2,1)}, u32[]{:S(2)}) copy-start(bf16[624,156]{0,1:T(8,128)(2,1)} %param.38) | copy-start | bytes 584068
  7.2 1.7 %copy-start.29 = (bf16[156,624]{1,0:T(8,128)(2,1)S(1)}, bf16[156,624]{1,0:T(8,128)(2,1)}, u32[]{:S(2)}) copy-start(bf16[156,624]{1,0:T(8,128)(2,1)} %param.36) | copy-start | bytes 584068
  7.2 89.9 %all-gather.5.cloned.1.call-start = ((), (), s32[]{:S(2)}) async-start(), calls=%async_computation.1 | async-start | bytes 12185600 | tf_op jit(solution)/shard_map/all_gather | solution.py:486
  8.6 1.4 %copy-start.31 = (bf16[1,1,624,49]{2,3,1,0:T(8,128)(2,1)S(1)}, bf16[1,1,624,49]{2,3,1,0:T(8,128)(2,1)}, u32[]{:S(2)}) copy-start(bf16[1,1,624,49]{2,3,1,0:T(8,128)(2,1)} %param.28) | copy-start | bytes 183460
  8.9 30.9 %copy-start.12 = (bf16[3,39,624]{2,1,0:T(8,128)(2,1)S(1)}, bf16[3,39,624]{2,1,0:T(8,128)(2,1)}, u32[]{:S(2)}) copy-start(bf16[3,39,624]{2,1,0:T(8,128)(2,1)} %weights_ref.1) | copy-start | bytes 438052
  8.9 30.9 %copy-start.21 = (bf16[32,64]{1,0:T(8,128)(2,1)S(1)}, bf16[32,64]{1,0:T(8,128)(2,1)}, u32[]{:S(2)}) copy-start(bf16[32,64]{1,0:T(8,128)(2,1)} %constant.76.column_ref) | copy-start | bytes 12292
  8.9 30.9 %copy-start.22 = (bf16[64,168]{1,0:T(8,128)(2,1)S(1)}, bf16[64,168]{1,0:T(8,128)(2,1)}, u32[]{:S(2)}) copy-start(bf16[64,168]{1,0:T(8,128)(2,1)} %constant.75.spread_ref) | copy-start | bytes 64516
  10.0 41.3 %copy-start.3 = (bf16[3,312,312]{2,1,0:T(8,128)(2,1)S(1)}, bf16[3,312,312]{2,1,0:T(8,128)(2,1)}, u32[]{:S(2)}) copy-start(bf16[3,312,312]{2,1,0:T(8,128)(2,1)} %inproj_ref.1) | copy-start | bytes 1752196
  10.0 41.3 %copy-start.6 = (bf16[312,312]{1,0:T(8,128)(2,1)S(1)}, bf16[312,312]{1,0:T(8,128)(2,1)}, u32[]{:S(2)}) copy-start(bf16[312,312]{1,0:T(8,128)(2,1)} %outproj_ref.1) | copy-start | bytes 584068
  10.0 41.4 %copy-start.8 = (f32[196,196]{1,0:T(8,128)S(1)}, f32[196,196]{1,0:T(8,128)}, u32[]{:S(2)}) copy-start(f32[196,196]{1,0:T(8,128)} %constant.45.clone.mask_ref) | copy-start | bytes 460996
  10.0 41.4 %copy-start.13 = (bf16[1,1,312,196]{2,3,1,0:T(8,128)(2,1)S(1)}, bf16[1,1,312,196]{2,3,1,0:T(8,128)(2,1)}, u32[]{:S(2)}) copy-start(bf16[1,1,312,196]{2,3,1,0:T(8,128)(2,1)} %param.27) | copy-start | bytes 366916
  39.8 24.9 %copy-start.24 = (bf16[40,248]{1,0:T(8,128)(2,1)S(1)}, bf16[40,248]{1,0:T(8,128)(2,1)}, u32[]{:S(2)}) copy-start(bf16[40,248]{1,0:T(8,128)(2,1)} %constant.77.right_ref) | copy-start | bytes 59524
  39.8 24.9 %copy-start.26 = (bf16[32,248]{1,0:T(8,128)(2,1)S(1)}, bf16[32,248]{1,0:T(8,128)(2,1)}, u32[]{:S(2)}) copy-start(bf16[32,248]{1,0:T(8,128)(2,1)} %constant.78.left_ref) | copy-start | bytes 47620
  46.9 27.1 %copy-start.30 = (f32[9,2496]{1,0:T(8,128)S(1)}, f32[9,2496]{1,0:T(8,128)}, u32[]{:S(2)}) copy-start(f32[9,2496]{1,0:T(8,128)} %param.37) | copy-start | bytes 269572
  47.9 27.6 %all-to-all-start = ((bf16[16,2,1280]{2,1,0:T(2,128)(2,1)}), bf16[16,2,1280]{2,1,0:T(2,128)(2,1)S(1)}, u32[]{:S(2)}, u32[]{:S(2)}) async-start(bf16[16,2,1280]{2,1,0:T(2,128)(2,1)} %reshape.45), calls=%async_computation | async-start | bytes 163840 | tf_op jit(solution)/shard_map/all_to_all | solution.py:518
  55.4 30.2 %copy-start.1 = (bf16[1248,312]{0,1:T(8,128)(2,1)S(1)}, bf16[1248,312]{0,1:T(8,128)(2,1)}, u32[]{:S(2)}) copy-start(bf16[1248,312]{0,1:T(8,128)(2,1)} %param.31) | copy-start | bytes 2336260
  55.4 30.2 %copy-start.2 = (bf16[312,1248]{1,0:T(8,128)(2,1)S(1)}, bf16[312,1248]{1,0:T(8,128)(2,1)}, u32[]{:S(2)}) copy-start(bf16[312,1248]{1,0:T(8,128)(2,1)} %shrink_ref.1) | copy-start | bytes 2336260
  55.4 30.2 %copy-start.5 = (bf16[320,512]{1,0:T(8,128)(2,1)S(1)}, bf16[320,512]{1,0:T(8,128)(2,1)}, u32[]{:S(2)}) copy-start(bf16[320,512]{1,0:T(8,128)(2,1)} %constant.82.sample_ref) | copy-start | bytes 983044
  55.4 9.3 %collective-permute-start.2 = (bf16[32,312]{1,0:T(8,128)(2,1)S(1)}, bf16[32,312]{1,0:T(8,128)(2,1)S(1)}, u32[]{:S(2)}, u32[]{:S(2)}) collective-permute-start(bf16[32,312]{1,0:T(8,128)(2,1)S(1)} %get-tuple-element.20), channel_id=1, source_target_pairs={{0,32},{32,64},{64,96},{96,128},{128,160},{160,192},{192,224},{224... | collective-permute-start | bytes 59912 | tf_op jit(solution)/shard_map/ppermute | solution.py:465
  59.1 5.6 %collective-permute-start.3 = (bf16[16,312]{1,0:T(8,128)(2,1)S(1)}, bf16[16,312]{1,0:T(8,128)(2,1)S(1)}, u32[]{:S(2)}, u32[]{:S(2)}) collective-permute-start(bf16[16,312]{1,0:T(8,128)(2,1)S(1)} %get-tuple-element.21), channel_id=1, source_target_pairs={{32,0},{64,32},{96,64},{128,96},{160,128},{192,160},{224,192},{256... | collective-permute-start | bytes 29960 | tf_op jit(solution)/shard_map/ppermute | solution.py:465
  64.8 0.6 copy-start.19
  65.4 9.0 %collective-permute-start.5 = (bf16[64,624]{1,0:T(8,128)(2,1)S(1)}, bf16[64,624]{1,0:T(8,128)(2,1)S(1)}, u32[]{:S(2)}, u32[]{:S(2)}) collective-permute-start(bf16[64,624]{1,0:T(8,128)(2,1)S(1)} %get-tuple-element.25), channel_id=1, source_target_pairs={{1,0},{2,1},{3,2},{4,3},{5,4},{6,5},{7,6},{8,7},{9,8},{10,9},{11,1... | collective-permute-start | bytes 239624 | tf_op jit(solution)/shard_map/ppermute | solution.py:465
  67.8 7.6 %collective-permute-start.4 = (bf16[64,624]{1,0:T(8,128)(2,1)S(1)}, bf16[64,624]{1,0:T(8,128)(2,1)S(1)}, u32[]{:S(2)}, u32[]{:S(2)}) collective-permute-start(bf16[64,624]{1,0:T(8,128)(2,1)S(1)} %get-tuple-element.24), channel_id=1, source_target_pairs={{0,1},{1,2},{2,3},{3,4},{4,5},{5,6},{6,7},{7,8},{8,9},{9,10},{10,1... | collective-permute-start | bytes 239624 | tf_op jit(solution)/shard_map/ppermute | solution.py:465
  75.4 0.6 copy-start.14
  76.4 20.6 %collective-permute-start.1 = (bf16[16,16,40]{2,1,0:T(8,128)(2,1)S(1)}, bf16[16,16,40]{2,1,0:T(8,128)(2,1)S(1)}, u32[]{:S(2)}, u32[]{:S(2)}) collective-permute-start(bf16[16,16,40]{2,1,0:T(8,128)(2,1)S(1)} %get-tuple-element.18), channel_id=1, source_target_pairs={{1,0},{2,1},{3,2},{4,3},{5,4},{6,5},{7,6},{8,7},{9,8},{10,9},{11,1... | collective-permute-start | bytes 61448 | tf_op jit(solution)/shard_map/ppermute | solution.py:465
  78.4 18.6 %collective-permute-start = (bf16[16,16,40]{2,1,0:T(8,128)(2,1)S(1)}, bf16[16,16,40]{2,1,0:T(8,128)(2,1)S(1)}, u32[]{:S(2)}, u32[]{:S(2)}) collective-permute-start(bf16[16,16,40]{2,1,0:T(8,128)(2,1)S(1)} %get-tuple-element.17), channel_id=1, source_target_pairs={{0,1},{1,2},{2,3},{3,4},{4,5},{5,6},{6,7},{7,8},{8,9},{9,10},{10,1... | collective-permute-start | bytes 61448 | tf_op jit(solution)/shard_map/ppermute | solution.py:465
  85.6 1.0 copy-start.7
  86.6 0.9 copy-start.9
  87.6 0.9 copy-start.15
  88.4 0.9 copy-start.16
  89.3 0.9 copy-start.17
  90.2 0.7 copy-start.20
  90.9 6.2 %copy-start.4 = (bf16[312,624]{1,0:T(8,128)(2,1)S(1)}, bf16[312,624]{1,0:T(8,128)(2,1)}, u32[]{:S(2)}) copy-start(bf16[312,624]{1,0:T(8,128)(2,1)} %to_fine_ref.1) | copy-start | bytes 1168132
  96.3 0.7 copy-start.10
  97.1 4.3 %copy-start = (bf16[8960,624]{1,0:T(8,128)(2,1)S(1)}, bf16[8960,624]{1,0:T(8,128)(2,1)}, u32[]{:S(2)}) copy-start(bf16[8960,624]{1,0:T(8,128)(2,1)} %all-gather.5.cloned.1.call-done) | copy-start | bytes 33546244
  101.4 0.9 copy-start.11
  102.3 0.8 copy-start.18
  103.1 0.7 copy-start.23
  103.8 0.7 copy-start.25
  104.6 0.7 copy-start.27
Sparse Core Ops, SparseCore 0:
  10.2 81.0 all-gather.4

commit v7 on v6

--- a/solution.py
+++ b/solution.py
@@ -20,7 +20,8 @@
 HEAD_ROWS = 40
 BLOCK_ROWS = 4 * HEAD_ROWS
 OUT_ROWS = 48
-TAP_ROWS = 5 * HEAD_ROWS + 8
+TAP_ROWS = 192
+HALF = HEAD_ROWS // 2
 SHARDS = 16
 TILE = 56
 STRIP = 64
@@ -33,13 +34,16 @@
 
 def pack(outproj, expand, shrink, to_coarse):
     width = expand.shape[-1]
-    taps = jnp.pad(to_coarse, ((0, 1), (0, 1), (0, 0))).reshape(5, 2, HEAD_ROWS, -1)
+    taps = jnp.pad(to_coarse, ((0, 0), (0, 1), (0, 0)))
+    pairs = taps[:8].reshape(4, 2, HEAD_ROWS, -1).transpose(0, 2, 1, 3).reshape(-1, width)
     return jnp.concatenate(
         [
             jnp.pad(expand, ((0, 4), (0, 0))),
             jnp.pad(shrink.T, ((0, 4), (0, 0))),
             jnp.pad(outproj.T, ((0, 1), (0, 0))),
-            taps.transpose(0, 2, 1, 3).reshape(-1, width),
+            pairs,
+            jnp.concatenate([taps[8, :HALF], taps[8, HALF:]], axis=1),
+            jnp.zeros((4, width), expand.dtype),
         ]
     )
 
@@ -100,12 +104,13 @@
     for row in range(SIDE):
         for col in range(SIDE):
             tile[row * SIDE + col, (row + 1) * 16 + col + 1] = 1
-    sample = np.zeros((5 * 64, 512), np.float32)
+    sample = np.zeros((6 * 64, 512), np.float32)
     for cell in range(CELLS):
         row, col = divmod(cell, WIN)
         for tap in range(9):
             source = (2 * row + tap // 3) * 16 + 2 * col + tap % 3
             sample[tap // 2 * 64 + cell, tap % 2 * 256 + source] = 1
+        sample[5 * 64 + cell, 256 + source] = 1
     return tuple(jnp.asarray(t).astype(jnp.bfloat16) for t in (gather, inner, tile, sample))
 
 
@@ -208,6 +213,7 @@
     columns_ref,
     normed_ref,
     proj_ref,
+    scores_ref,
     attended_ref,
     images_ref,
 ):
@@ -222,15 +228,18 @@
     normed = normed_ref[...].astype(jnp.bfloat16).reshape(tiles * TILE, width)
     for part in range(3):
         proj_ref[part] = nt(normed, weights_ref[part]).reshape(tiles, TILE, -1)
-    key = lax.broadcasted_iota(jnp.int32, (TILE, TILE), 1)
-    mask = jnp.where(key < cells, 0.0, -1e30)
     for tile in range(tiles):
-        queries, keys, values = (proj_ref[part, tile].astype(jnp.bfloat16) for part in range(3))
-        scores = nt(queries, keys) * (1.0 / math.sqrt(39)) + mask
-        exponent = jnp.exp(scores - jnp.max(scores, axis=1, keepdims=True))
-        total = jnp.sum(exponent, axis=1, keepdims=True)
-        chance = (exponent * (1.0 / total)).astype(jnp.bfloat16)
-        attended_ref[tile + 1, :, :39] = nn(chance, values)
+        queries, keys = (proj_ref[part, tile].astype(jnp.bfloat16) for part in range(2))
+        scores_ref[tile] = nt(queries, keys)
+    key = lax.broadcasted_iota(jnp.int32, (tiles * TILE, TILE), 1)
+    scores = scores_ref[...].reshape(tiles * TILE, TILE) * (1.0 / math.sqrt(39))
+    scores += jnp.where(key < cells, 0.0, -1e30)
+    exponent = jnp.exp(scores - jnp.max(scores, axis=1, keepdims=True))
+    total = jnp.sum(exponent, axis=1, keepdims=True)
+    scores_ref[...] = (exponent * (1.0 / total)).reshape(tiles, TILE, TILE)
+    for tile in range(tiles):
+        values = proj_ref[2, tile].astype(jnp.bfloat16)
+        attended_ref[tile + 1, :, :39] = nn(scores_ref[tile].astype(jnp.bfloat16), values)
     spread = spread_ref[...]
     for tile in range(tiles):
         near = attended_ref[tile : tile + 3].astype(jnp.bfloat16).reshape(3 * TILE, HEAD_ROWS)
@@ -253,6 +262,19 @@
         columns = nn(column_ref[...], blocks_ref[head]).astype(jnp.bfloat16)
         right_ref[head] = columns[:16]
         left_ref[head] = columns[16:]
+
+
+def attended_kernel(blocks_ref, left_ref, right_ref, flat_ref, parts_ref):
+    parts_ref[:, :STRIP, :] = blocks_ref[...]
+    parts_ref[:, STRIP : STRIP + 16, :] = left_ref[...]
+    parts_ref[:, STRIP + 16 :, :] = right_ref[...]
+    channel = lax.broadcasted_iota(jnp.int32, (HEAD_ROWS, SHARDS * OUT_ROWS), 0)
+    lane = lax.broadcasted_iota(jnp.int32, (HEAD_ROWS, SHARDS * OUT_ROWS), 1)
+    flat = jnp.zeros(flat_ref.shape, jnp.float32)
+    for head in range(SHARDS):
+        move = jnp.where(lane == channel + head * OUT_ROWS, 1.0, 0.0).astype(jnp.bfloat16)
+        flat += nn(parts_ref[head], move)
+    flat_ref[...] = flat.astype(jnp.bfloat16)
 
 
 def field_kernel(
@@ -326,21 +348,60 @@
     samples_ref[...] = nn(sample_ref[...], twice_ref[...].astype(jnp.bfloat16)).astype(jnp.bfloat16)
 
 
-def call(kernel, shapes, operands, scratch, scalars=0, limit=32):
-    smem, vmem = (pl.BlockSpec(memory_space=space) for space in (pltpu.SMEM, pltpu.VMEM))
+def call(kernel, shapes, operands, scratch, scalars=0, staged=False, limit=32):
+    smem, vmem, anywhere = (
+        pl.BlockSpec(memory_space=space) for space in (pltpu.SMEM, pltpu.VMEM, pl.ANY)
+    )
+    arrays = operands[scalars:]
+    count = len(arrays)
+    scratch_shapes = [pltpu.VMEM(shape, kind) for shape, kind in scratch]
+    if staged:
+        scratch_shapes += [pltpu.VMEM(array.shape, array.dtype) for array in arrays]
+        scratch_shapes.append(pltpu.SemaphoreType.DMA((count,)))
+
+    def fetching(*refs):
+        given, rest, landed, sems = (
+            refs[: scalars + count],
+            refs[scalars + count : -1 - count],
+            refs[-1 - count : -1],
+            refs[-1],
+        )
+        copies = [
+            pltpu.make_async_copy(source, target, sems.at[index])
+            for index, (source, target) in enumerate(zip(given[scalars:], landed))
+        ]
+        for copy in copies:
+            copy.start()
+        for copy in copies:
+            copy.wait()
+        kernel(*given[:scalars], *landed, *rest)
+
     return pl.pallas_call(
-        kernel,
+        fetching if staged else kernel,
         out_shape=tuple(jax.ShapeDtypeStruct(shape, jnp.bfloat16) for shape in shapes),
-        in_specs=[smem] * scalars + [vmem] * (len(operands) - scalars),
+        in_specs=[smem] * scalars + [anywhere if staged else vmem] * count,
         out_specs=(vmem,) * len(shapes),
-        scratch_shapes=[pltpu.VMEM(shape, kind) for shape, kind in scratch],
+        scratch_shapes=scratch_shapes,
         compiler_params=pltpu.CompilerParams(vmem_limit_bytes=limit * 1024 * 1024),
     )(*operands)
 
 
-def coarse_kernel(
+def coarse_kernel(edge_ref, gathered_ref, *refs):
+    count = 10
+    operands, outputs, landed = refs[:count], refs[count : count + 2], refs[-count - 1 : -1]
+    small = [
+        pltpu.make_async_copy(source, target, refs[-1].at[index])
+        for index, (source, target) in enumerate(zip(operands, landed))
+    ]
+    for copy in small:
+        copy.start()
+    coarse_body(edge_ref, gathered_ref, small, *landed, *outputs, *refs[count + 2 : -count - 1])
+
+
+def coarse_body(
     edge_ref,
     gathered_ref,
+    small,
     attended_ref,
     own_ref,
     depth_ref,
@@ -374,6 +435,8 @@
     ]
     for copy in copies:
         copy.start()
+    for copy in small:
+        copy.wait()
     width = own_ref.shape[1]
     query = lax.broadcasted_iota(jnp.int32, (QUERIES, 128), 0)
     column = query % RING
@@ -387,8 +450,7 @@
     conv_ref[8 * WIN :, :] = jnp.zeros((8, conv_ref.shape[1]), jnp.float32)
     mixed = own_ref[...].astype(jnp.float32)
     copies[0].wait()
-    for head in range(SHARDS):
-        mixed += nn(attended_ref[head], out_ref[head][:HEAD_ROWS])
+    mixed += nn(attended_ref[...], out_ref[...].reshape(SHARDS * OUT_ROWS, width))
     middle = nn(square_ref[...], mixed.astype(jnp.bfloat16)).astype(jnp.bfloat16)
     normed_mid = norm_rows(middle.astype(jnp.float32))
     copies[1].wait()
@@ -418,12 +480,15 @@
     samples = samples_ref[...]
     for shard in range(SHARDS):
         four = nt(taps_ref[shard], samples[: 4 * 64])
-        fifth = nt(taps_ref[shard][4 * HEAD_ROWS :], samples[4 * 64 :])
-        total = fifth[8:]
-        for block in range(4):
+        ninth = nt(taps_ref[shard][4 * HEAD_ROWS :], samples[4 * 64 :])
+        total = four[8 : 8 + HEAD_ROWS, :64]
+        for block in range(1, 4):
             rows = slice(8 + block * HEAD_ROWS, 8 + (block + 1) * HEAD_ROWS)
             total += four[rows, block * 64 : (block + 1) * 64]
-        down_ref[shard * 39 : shard * 39 + HEAD_ROWS, :64] = total
+        first = shard * 39
+        down_ref[first : first + HEAD_ROWS, :64] = total
+        down_ref[first : first + HALF, :64] += ninth[8 : 8 + HALF, :64]
+        down_ref[first + HALF : first + HEAD_ROWS, :64] += ninth[8 : 8 + HALF, 64:]
     downsampled = down_ref[...].T[:CELLS, :width].astype(jnp.bfloat16).astype(jnp.float32)
     coarse_out_ref[...] = jnp.maximum(
         nn(compact_ref[...], result) + downsampled, 0.0
@@ -443,7 +508,7 @@
             jax.ShapeDtypeStruct((fine_cells, fine_ch), jnp.bfloat16),
             jax.ShapeDtypeStruct((CELLS, width), jnp.bfloat16),
         ),
-        in_specs=[smem, anywhere] + [vmem] * len(operands),
+        in_specs=[smem, anywhere] + [anywhere] * len(operands),
         out_specs=(vmem, vmem),
         scratch_shapes=[
             pltpu.VMEM((SHARDS, OUT_ROWS, width), jnp.bfloat16),
@@ -454,8 +519,10 @@
             pltpu.VMEM((64, SHARDS * BLOCK_ROWS), jnp.float32),
             pltpu.VMEM((SHARDS * HEAD_ROWS, 128), jnp.float32),
             pltpu.SemaphoreType.DMA((4,)),
+            *(pltpu.VMEM(operand.shape, operand.dtype) for operand in operands),
+            pltpu.SemaphoreType.DMA((len(operands),)),
         ],
-        compiler_params=pltpu.CompilerParams(vmem_limit_bytes=32 * 1024 * 1024),
+        compiler_params=pltpu.CompilerParams(vmem_limit_bytes=40 * 1024 * 1024),
     )(edges, gathered, *operands)
 
 
@@ -510,6 +577,7 @@
         (
             ((SHARDS, TILE, coarse_ch), jnp.float32),
             ((3, SHARDS, TILE, 39), jnp.float32),
+            ((SHARDS, TILE, TILE), jnp.float32),
             ((SHARDS + 2, TILE, HEAD_ROWS), jnp.float32),
             ((3 * TILE, coarse_ch), jnp.float32),
         ),
@@ -528,7 +596,7 @@
     hidden_count = expand_fine.shape[0]
     fine_res, samples = call(
         field_kernel,
-        (fine.shape, (5 * 64, 2 * fine_ch)),
+        (fine.shape, (6 * 64, 2 * fine_ch)),
         (
             edges,
             above,
@@ -548,12 +616,19 @@
             ((512, 2 * fine_ch), jnp.float32),
         ),
         scalars=1,
+        staged=True,
+    )
+    (attended,) = call(
+        attended_kernel,
+        ((QUERIES, SHARDS * OUT_ROWS),),
+        (blocks, *near),
+        (((SHARDS, QUERIES, HEAD_ROWS), jnp.bfloat16),),
     )
     depth = jnp.pad(depth_coarse.reshape(9, SHARDS, -1), ((0, 0), (0, 0), (0, 4)))
     fine_out, coarse_out = coarse_stream(
         gathered,
         edges,
-        jnp.concatenate([blocks, *near], axis=1),
+        attended,
         jnp.concatenate([own, left[48:], right[48:]]),
         depth.reshape(9, -1),
         samples,

time: 123 us -> 139 us (1.13)
  the two profiles are of different devices: /device:TPU:31 before, /device:TPU:33 now
where the time goes in v7:
time: 139 us; the launch traced here: 137 us
  local copies, waits for them, and re-layouts  33.9 us (24%)
  blocking collectives  29.8 us (21%)
  Pallas kernels  26.2 us (19%)
  starting transfers between devices  23.9 us (17%)
  between operations  14.4 us (10%)
  waiting for transfers between devices  9.04 us (7%)
    all_gather x1, blocking collectives, local(): strip = lax.all_gather(coarse_in.reshape(coarse_ch, coarse_cells).T, 'rows')  29.8 us
    unnamed x56, local copies, waits for them, and re-layouts  22.5 us
    ppermute x6, starting transfers between devices, exchange(): return (lax.ppermute(onward, axis, up), lax.ppermute(back, axis, down))  20.4 us
    pallas_call x6, Pallas kernels, call(): pl.pallas_call(fetching if staged else kernel, out_shape=tuple((jax.Shape...  15.3 us
    pallas_call x1, Pallas kernels, coarse_stream(): pl.pallas_call(coarse_kernel, out_shape=(jax.ShapeDtypeStruct((fine_cells...  10.9 us
    ppermute x6, waiting for transfers between devices, exchange(): return (lax.ppermute(onward, axis, up), lax.ppermute(back, axis, down))  9 us
    concatenate x1, local copies, waits for them, and re-layouts, pack(): jnp.concatenate([jnp.pad(expand, ((0, 4), (0, 0))), jnp.pad(shrink.T, ((0...  4.75 us
    all_to_all x1, starting transfers between devices, local(): blocks = lax.all_to_all(blocks, 'rows', 0, 0, tiled=True)  3.44 us
  transfers between devices with their start and end apart: 8, of which 2 were waited for; matrix products, arithmetic and copies ran while one was open for 2% of the time, Pallas kernels for 11%

profile of v7, /device:TPU:33, one launch (start us, length us, event | category | flops | bytes accessed | tf_op | source)
XLA Modules:
  0.0 137.3 jit_solution(5512308829161071926)
XLA Ops:
  7.2 0.0 copy-start.20
  7.2 0.0 copy-start.7
  7.2 0.0 all-gather.5.cloned.1.call-start
  7.3 1.1 pad_slice_fusion.1
  8.4 0.8 slice_bitcast_fusion
  9.2 1.0 pad.19
  10.2 1.0 pad.20
  11.1 0.8 pad.21
  11.9 0.2 copy.30
  12.1 0.2 reshape.32
  12.3 0.1 pad_maximum_fusion.1
  12.4 4.7 %concatenate.10 = bf16[544,624]{1,0:T(8,128)(2,1)} concatenate(bf16[160,624]{1,0:T(8,128)(2,1)S(1)} %pad.19, bf16[160,624]{1,0:T(8,128)(2,1)S(1)} %pad.20, bf16[40,624]{1,0:T(8,128)(2,1)S(1)} %pad.21, bf16[160,624]{1,0:T(8,128)(2,1)S(1)} %reshape.32, bf16[20,624]{1,0:T(8,128)(2,1)S(1)} %pad_maximum_fusion.1, bf16[4,624]{1,0:T(4,128)(2,1)S(1)} %broadcast_in_dim.3), dimensions={0} | concatenate | bytes 1357824 | tf_op jit(solution)/shard_map/concatenate | solution.py:39
  17.2 0.0 all-gather.5.cloned.1.call-update
  17.2 0.1 add_convert_fusion.edge_ref.refs_0_
  17.3 29.8 %all-gather.2.strip_ref = bf16[16,49,624]{2,1,0:T(8,128)(2,1)S(1)} all-gather(bf16[1,49,624]{2,1,0:T(8,128)(2,1)} %bitcast.39), channel_id=3, replica_groups=mesh['rows'=16,'cols'=32] {'rows'}, dimensions={0}, use_global_device_ids=true | all-gather | bytes 1039584 | tf_op jit(solution)/shard_map/all_gather | solution.py:554
  47.0 0.9 copy-done.10
  48.0 0.7 copy-done.19
  48.7 0.8 copy-done.21
  49.4 3.1 %shard_map.266 = (bf16[16,64,40]{2,1,0:T(8,128)(2,1)S(1)}, bf16[64,624]{1,0:T(8,128)(2,1)S(1)}, bf16[32,624]{1,0:T(8,128)(2,1)S(1)}) custom-call(s32[4]{0:T(128)S(1)} %add_convert_fusion.edge_ref.refs_0_, s32[1]{0:T(128)} %bitcast.11.place_ref, bf16[16,49,624]{2,1,0:T(8,128)(2,1)S(1)} %all-gather.2.strip_ref, bf16[3,39,624]{2,1,0:T(8,128)(2,1)S(1)} %copy-done.10, ...), custom_call_target="tpu_custom_call" | custom-call | tf_op jit(solution)/shard_map/pallas_call | solution.py:379
  52.6 0.2 copy.31
  52.7 0.8 reshape.45
  53.5 3.4 %all-to-all-start = ((bf16[16,2,1280]{2,1,0:T(2,128)(2,1)}), bf16[16,2,1280]{2,1,0:T(2,128)(2,1)S(1)}, u32[]{:S(2)}, u32[]{:S(2)}) async-start(bf16[16,2,1280]{2,1,0:T(2,128)(2,1)} %reshape.45), calls=%async_computation | async-start | bytes 163840 | tf_op jit(solution)/shard_map/all_to_all | solution.py:586
  57.0 1.1 copy-done.3
  58.1 1.0 copy-done.6
  59.0 0.9 copy-done.8
  60.0 0.9 copy-done.11
  60.9 4.0 %shard_map.269 = (bf16[196,312]{1,0:T(8,128)(2,1)S(1)}, bf16[32,312]{1,0:T(8,128)(2,1)S(1)}, bf16[16,312]{1,0:T(8,128)(2,1)S(1)}) custom-call(bf16[196,312]{1,0:T(8,128)(2,1)S(1)} %bitcast.34, bf16[3,312,312]{2,1,0:T(8,128)(2,1)S(1)} %copy-done.3, bf16[312,312]{1,0:T(8,128)(2,1)S(1)} %copy-done.6, f32[196,196]{1,0:T(8,128)S(1)} %copy-done.8), custom_call_target="tpu_custom_call" | custom-call | tf_op jit(solution)/shard_map/pallas_call | solution.py:379
  64.9 3.5 %collective-permute-start.2 = (bf16[32,312]{1,0:T(8,128)(2,1)S(1)}, bf16[32,312]{1,0:T(8,128)(2,1)S(1)}, u32[]{:S(2)}, u32[]{:S(2)}) collective-permute-start(bf16[32,312]{1,0:T(8,128)(2,1)S(1)} %get-tuple-element.20), channel_id=1, source_target_pairs={{0,32},{32,64},{64,96},{96,128},{128,160},{160,192},{192,224},{224... | collective-permute-start | bytes 59912 | tf_op jit(solution)/shard_map/ppermute | solution.py:532
  68.5 1.9 %collective-permute-start.3 = (bf16[16,312]{1,0:T(8,128)(2,1)S(1)}, bf16[16,312]{1,0:T(8,128)(2,1)S(1)}, u32[]{:S(2)}, u32[]{:S(2)}) collective-permute-start(bf16[16,312]{1,0:T(8,128)(2,1)S(1)} %get-tuple-element.21), channel_id=1, source_target_pairs={{32,0},{64,32},{96,64},{128,96},{160,128},{192,160},{224,192},{256... | collective-permute-start | bytes 29960 | tf_op jit(solution)/shard_map/ppermute | solution.py:532
  70.4 3.7 %collective-permute-done.3.below_ref.refs_2_ = bf16[16,312]{1,0:T(8,128)(2,1)S(1)} collective-permute-done((bf16[16,312]{1,0:T(8,128)(2,1)S(1)}, bf16[16,312]{1,0:T(8,128)(2,1)S(1)}, u32[]{:S(2)}, u32[]{:S(2)}) %collective-permute-start.3) | collective-permute-done | bytes 10016 | tf_op jit(solution)/shard_map/ppermute | solution.py:532
  74.1 0.7 copy-done.23
  74.9 0.7 copy-done.25
  75.6 0.2 shard_map.270
  75.8 4.3 %collective-permute-start.5 = (bf16[64,624]{1,0:T(8,128)(2,1)S(1)}, bf16[64,624]{1,0:T(8,128)(2,1)S(1)}, u32[]{:S(2)}, u32[]{:S(2)}) collective-permute-start(bf16[64,624]{1,0:T(8,128)(2,1)S(1)} %get-tuple-element.25), channel_id=1, source_target_pairs={{1,0},{2,1},{3,2},{4,3},{5,4},{6,5},{7,6},{8,7},{9,8},{10,9},{11,1... | collective-permute-start | bytes 239624 | tf_op jit(solution)/shard_map/ppermute | solution.py:532
  80.0 1.9 %collective-permute-start.4 = (bf16[64,624]{1,0:T(8,128)(2,1)S(1)}, bf16[64,624]{1,0:T(8,128)(2,1)S(1)}, u32[]{:S(2)}, u32[]{:S(2)}) collective-permute-start(bf16[64,624]{1,0:T(8,128)(2,1)S(1)} %get-tuple-element.24), channel_id=1, source_target_pairs={{0,1},{1,2},{2,3},{3,4},{4,5},{5,6},{6,7},{7,8},{8,9},{9,10},{10,1... | collective-permute-start | bytes 239624 | tf_op jit(solution)/shard_map/ppermute | solution.py:532
  82.0 1.1 reshape.36
  83.1 0.1 reshape.37.refs_2_
  83.3 0.0 collective-permute-done.5.refs_4_
  83.3 5.3 %collective-permute-done.4.refs_3_ = bf16[64,624]{1,0:T(8,128)(2,1)S(1)} collective-permute-done((bf16[64,624]{1,0:T(8,128)(2,1)S(1)}, bf16[64,624]{1,0:T(8,128)(2,1)S(1)}, u32[]{:S(2)}, u32[]{:S(2)}) %collective-permute-start.4) | collective-permute-done | bytes 79904 | tf_op jit(solution)/shard_map/ppermute | solution.py:532
  88.6 0.2 reshape.46
  88.7 0.5 copy-done.14
  89.2 0.2 copy.33.blocks_ref
  89.4 0.2 shard_map.267
  89.6 1.9 %collective-permute-start = (bf16[16,16,40]{2,1,0:T(8,128)(2,1)S(1)}, bf16[16,16,40]{2,1,0:T(8,128)(2,1)S(1)}, u32[]{:S(2)}, u32[]{:S(2)}) collective-permute-start(bf16[16,16,40]{2,1,0:T(8,128)(2,1)S(1)} %get-tuple-element.17), channel_id=1, source_target_pairs={{0,1},{1,2},{2,3},{3,4},{4,5},{5,6},{6,7},{7,8},{8,9},{9,10},{10,1... | collective-permute-start | bytes 61448 | tf_op jit(solution)/shard_map/ppermute | solution.py:532
  91.5 6.9 %collective-permute-start.1 = (bf16[16,16,40]{2,1,0:T(8,128)(2,1)S(1)}, bf16[16,16,40]{2,1,0:T(8,128)(2,1)S(1)}, u32[]{:S(2)}, u32[]{:S(2)}) collective-permute-start(bf16[16,16,40]{2,1,0:T(8,128)(2,1)S(1)} %get-tuple-element.18), channel_id=1, source_target_pairs={{1,0},{2,1},{3,2},{4,3},{5,4},{6,5},{7,6},{8,7},{9,8},{10,9},{11,1... | collective-permute-start | bytes 61448 | tf_op jit(solution)/shard_map/ppermute | solution.py:532
  98.4 0.0 copy-start.5
  98.4 1.0 copy-done.5
  99.4 0.9 copy-done.9
  100.3 0.9 copy-done.15
  101.2 0.9 copy-done.16
  102.1 0.9 copy-done.17
  103.0 7.2 %shard_map.271 = (bf16[196,312]{1,0:T(8,128)(2,1)S(1)}, bf16[384,624]{1,0:T(8,128)(2,1)S(1)}) custom-call(s32[4]{0:T(128)S(1)} %add_convert_fusion.edge_ref.refs_0_, bf16[32,312]{1,0:T(8,128)(2,1)S(1)} %collective-permute-done.2.above_ref.refs_1_, bf16[16,312]{1,0:T(8,128)(2,1)S(1)} %collective-permute-done.3.below_ref.refs_2_, ...), custom_call_target="tpu_custom_call" | custom-call | tf_op jit(solution)/shard_map/pallas_call | solution.py:379
  110.2 0.0 copy-start.12
  110.2 0.7 copy-done.12
  110.9 0.0 collective-permute-done.left_ref
  110.9 0.5 shard_map.268.refs_0_
  111.4 0.0 all-gather.5.cloned.1.call-done
  111.5 4.2 %copy-done = bf16[8704,624]{1,0:T(8,128)(2,1)S(1)} copy-done((bf16[8704,624]{1,0:T(8,128)(2,1)S(1)}, bf16[8704,624]{1,0:T(8,128)(2,1)}, u32[]{:S(2)}) %copy-start) | copy-done | bytes 10862616
  115.6 0.9 copy-done.13
  116.5 0.8 copy-done.18
  117.4 0.7 copy-done.22
  118.1 0.7 copy-done.24
  118.8 0.7 copy-done.26
  119.5 10.9 %shard_map.272 = (bf16[196,312]{1,0:T(8,128)(2,1)}, bf16[49,624]{1,0:T(8,128)(2,1)}) custom-call(s32[4]{0:T(128)S(1)} %add_convert_fusion.edge_ref.refs_0_, bf16[16,544,624]{2,1,0:T(8,128)(2,1)S(1)} %bitcast.32, bf16[96,768]{1,0:T(8,128)(2,1)S(1)} %shard_map.268.refs_0_, bf16[96,624]{1,0:T(8,128)(2,1)S(1)} %pad_maximum_fusion.refs_1_, ...), custom_call_target="tpu_custom_call" | custom-call | tf_op jit(solution)/shard_map/pallas_call | solution.py:505
  (36 shorter events, 0.1 us)
Async XLA Ops:
  7.2 82.2 %copy-start.20 = (bf16[32,64]{1,0:T(8,128)(2,1)S(1)}, bf16[32,64]{1,0:T(8,128)(2,1)}, u32[]{:S(2)}) copy-start(bf16[32,64]{1,0:T(8,128)(2,1)} %constant.77.column_ref) | copy-start | bytes 12292
  7.2 91.2 %copy-start.7 = (bf16[304,320]{1,0:T(8,128)(2,1)S(1)}, bf16[304,320]{1,0:T(8,128)(2,1)}, u32[]{:S(2)}) copy-start(bf16[304,320]{1,0:T(8,128)(2,1)} %constant.80.refs_9_) | copy-start | bytes 583684
  7.2 91.2 %copy-start.1 = (bf16[1248,312]{0,1:T(8,128)(2,1)S(1)}, bf16[1248,312]{0,1:T(8,128)(2,1)}, u32[]{:S(2)}) copy-start(bf16[1248,312]{0,1:T(8,128)(2,1)} %param.31) | copy-start | bytes 2336260
  7.2 91.2 %copy-start.2 = (bf16[312,1248]{1,0:T(8,128)(2,1)S(1)}, bf16[312,1248]{1,0:T(8,128)(2,1)}, u32[]{:S(2)}) copy-start(bf16[312,1248]{1,0:T(8,128)(2,1)} %refs_8_.1) | copy-start | bytes 2336260
  7.2 104.2 %copy-start.4 = (bf16[312,624]{1,0:T(8,128)(2,1)S(1)}, bf16[312,624]{1,0:T(8,128)(2,1)}, u32[]{:S(2)}) copy-start(bf16[312,624]{1,0:T(8,128)(2,1)} %refs_5_.1) | copy-start | bytes 1168132
  7.2 104.2 %all-gather.5.cloned.1.call-start = ((), (), s32[]{:S(2)}) async-start(), calls=%async_computation.1 | async-start | bytes 11837440 | tf_op jit(solution)/shard_map/all_gather | solution.py:553
  47.0 0.9 copy-start.10
  48.0 0.7 copy-start.19
  48.6 0.8 copy-start.21
  53.5 35.0 %all-to-all-start = ((bf16[16,2,1280]{2,1,0:T(2,128)(2,1)}), bf16[16,2,1280]{2,1,0:T(2,128)(2,1)S(1)}, u32[]{:S(2)}, u32[]{:S(2)}) async-start(bf16[16,2,1280]{2,1,0:T(2,128)(2,1)} %reshape.45), calls=%async_computation | async-start | bytes 163840 | tf_op jit(solution)/shard_map/all_to_all | solution.py:586
  57.0 1.1 copy-start.3
  58.1 1.0 copy-start.6
  59.0 0.9 copy-start.8
  60.0 0.9 copy-start.11
  64.9 9.2 %collective-permute-start.2 = (bf16[32,312]{1,0:T(8,128)(2,1)S(1)}, bf16[32,312]{1,0:T(8,128)(2,1)S(1)}, u32[]{:S(2)}, u32[]{:S(2)}) collective-permute-start(bf16[32,312]{1,0:T(8,128)(2,1)S(1)} %get-tuple-element.20), channel_id=1, source_target_pairs={{0,32},{32,64},{64,96},{96,128},{128,160},{160,192},{192,224},{224... | collective-permute-start | bytes 59912 | tf_op jit(solution)/shard_map/ppermute | solution.py:532
  68.5 5.6 %collective-permute-start.3 = (bf16[16,312]{1,0:T(8,128)(2,1)S(1)}, bf16[16,312]{1,0:T(8,128)(2,1)S(1)}, u32[]{:S(2)}, u32[]{:S(2)}) collective-permute-start(bf16[16,312]{1,0:T(8,128)(2,1)S(1)} %get-tuple-element.21), channel_id=1, source_target_pairs={{32,0},{64,32},{96,64},{128,96},{160,128},{192,160},{224,192},{256... | collective-permute-start | bytes 29960 | tf_op jit(solution)/shard_map/ppermute | solution.py:532
  74.1 0.7 copy-start.23
  74.9 0.7 copy-start.25
  75.8 7.5 %collective-permute-start.5 = (bf16[64,624]{1,0:T(8,128)(2,1)S(1)}, bf16[64,624]{1,0:T(8,128)(2,1)S(1)}, u32[]{:S(2)}, u32[]{:S(2)}) collective-permute-start(bf16[64,624]{1,0:T(8,128)(2,1)S(1)} %get-tuple-element.25), channel_id=1, source_target_pairs={{1,0},{2,1},{3,2},{4,3},{5,4},{6,5},{7,6},{8,7},{9,8},{10,9},{11,1... | collective-permute-start | bytes 239624 | tf_op jit(solution)/shard_map/ppermute | solution.py:532
  80.0 8.5 %collective-permute-start.4 = (bf16[64,624]{1,0:T(8,128)(2,1)S(1)}, bf16[64,624]{1,0:T(8,128)(2,1)S(1)}, u32[]{:S(2)}, u32[]{:S(2)}) collective-permute-start(bf16[64,624]{1,0:T(8,128)(2,1)S(1)} %get-tuple-element.24), channel_id=1, source_target_pairs={{0,1},{1,2},{2,3},{3,4},{4,5},{5,6},{6,7},{7,8},{8,9},{9,10},{10,1... | collective-permute-start | bytes 239624 | tf_op jit(solution)/shard_map/ppermute | solution.py:532
  88.6 0.6 copy-start.14
  89.6 21.3 %collective-permute-start = (bf16[16,16,40]{2,1,0:T(8,128)(2,1)S(1)}, bf16[16,16,40]{2,1,0:T(8,128)(2,1)S(1)}, u32[]{:S(2)}, u32[]{:S(2)}) collective-permute-start(bf16[16,16,40]{2,1,0:T(8,128)(2,1)S(1)} %get-tuple-element.17), channel_id=1, source_target_pairs={{0,1},{1,2},{2,3},{3,4},{4,5},{5,6},{6,7},{7,8},{8,9},{9,10},{10,1... | collective-permute-start | bytes 61448 | tf_op jit(solution)/shard_map/ppermute | solution.py:532
  91.5 19.4 %collective-permute-start.1 = (bf16[16,16,40]{2,1,0:T(8,128)(2,1)S(1)}, bf16[16,16,40]{2,1,0:T(8,128)(2,1)S(1)}, u32[]{:S(2)}, u32[]{:S(2)}) collective-permute-start(bf16[16,16,40]{2,1,0:T(8,128)(2,1)S(1)} %get-tuple-element.18), channel_id=1, source_target_pairs={{1,0},{2,1},{3,2},{4,3},{5,4},{6,5},{7,6},{8,7},{9,8},{10,9},{11,1... | collective-permute-start | bytes 61448 | tf_op jit(solution)/shard_map/ppermute | solution.py:532
  98.4 1.0 copy-start.5
  99.4 0.9 copy-start.9
  100.3 0.9 copy-start.15
  101.2 0.9 copy-start.16
  102.1 0.9 copy-start.17
  110.2 0.7 copy-start.12
  111.5 4.2 %copy-start = (bf16[8704,624]{1,0:T(8,128)(2,1)S(1)}, bf16[8704,624]{1,0:T(8,128)(2,1)}, u32[]{:S(2)}) copy-start(bf16[8704,624]{1,0:T(8,128)(2,1)} %all-gather.5.cloned.1.call-done) | copy-start | bytes 32587780
  115.6 0.9 copy-start.13
  116.5 0.8 copy-start.18
  117.3 0.7 copy-start.22
  118.1 0.7 copy-start.24
  118.8 0.7 copy-start.26
Sparse Core Ops, SparseCore 0:
  17.3 79.5 all-gather.4

commit v8 on v7

--- a/solution.py
+++ b/solution.py
@@ -20,8 +20,7 @@
 HEAD_ROWS = 40
 BLOCK_ROWS = 4 * HEAD_ROWS
 OUT_ROWS = 48
-TAP_ROWS = 192
-HALF = HEAD_ROWS // 2
+TAP_ROWS = 5 * HEAD_ROWS + 8
 SHARDS = 16
 TILE = 56
 STRIP = 64
@@ -34,16 +33,13 @@
 
 def pack(outproj, expand, shrink, to_coarse):
     width = expand.shape[-1]
-    taps = jnp.pad(to_coarse, ((0, 0), (0, 1), (0, 0)))
-    pairs = taps[:8].reshape(4, 2, HEAD_ROWS, -1).transpose(0, 2, 1, 3).reshape(-1, width)
+    taps = jnp.pad(to_coarse, ((0, 1), (0, 1), (0, 0))).reshape(5, 2, HEAD_ROWS, -1)
     return jnp.concatenate(
         [
             jnp.pad(expand, ((0, 4), (0, 0))),
             jnp.pad(shrink.T, ((0, 4), (0, 0))),
             jnp.pad(outproj.T, ((0, 1), (0, 0))),
-            pairs,
-            jnp.concatenate([taps[8, :HALF], taps[8, HALF:]], axis=1),
-            jnp.zeros((4, width), expand.dtype),
+            taps.transpose(0, 2, 1, 3).reshape(-1, width),
         ]
     )
 
@@ -104,13 +100,12 @@
     for row in range(SIDE):
         for col in range(SIDE):
             tile[row * SIDE + col, (row + 1) * 16 + col + 1] = 1
-    sample = np.zeros((6 * 64, 512), np.float32)
+    sample = np.zeros((5 * 64, 512), np.float32)
     for cell in range(CELLS):
         row, col = divmod(cell, WIN)
         for tap in range(9):
             source = (2 * row + tap // 3) * 16 + 2 * col + tap % 3
             sample[tap // 2 * 64 + cell, tap % 2 * 256 + source] = 1
-        sample[5 * 64 + cell, 256 + source] = 1
     return tuple(jnp.asarray(t).astype(jnp.bfloat16) for t in (gather, inner, tile, sample))
 
 
@@ -348,38 +343,36 @@
     samples_ref[...] = nn(sample_ref[...], twice_ref[...].astype(jnp.bfloat16)).astype(jnp.bfloat16)
 
 
-def call(kernel, shapes, operands, scratch, scalars=0, staged=False, limit=32):
-    smem, vmem, anywhere = (
-        pl.BlockSpec(memory_space=space) for space in (pltpu.SMEM, pltpu.VMEM, pl.ANY)
-    )
-    arrays = operands[scalars:]
-    count = len(arrays)
+def call(kernel, shapes, operands, scratch, scalars=0, fetch=(), limit=32):
+    smem, vmem, hbm = (
+        pl.BlockSpec(memory_space=space) for space in (pltpu.SMEM, pltpu.VMEM, pltpu.HBM)
+    )
+    count = len(operands)
     scratch_shapes = [pltpu.VMEM(shape, kind) for shape, kind in scratch]
-    if staged:
-        scratch_shapes += [pltpu.VMEM(array.shape, array.dtype) for array in arrays]
-        scratch_shapes.append(pltpu.SemaphoreType.DMA((count,)))
+    scratch_shapes += [pltpu.VMEM(operands[i].shape, operands[i].dtype) for i in fetch]
+    scratch_shapes.append(pltpu.SemaphoreType.DMA((max(len(fetch), 1),)))
 
     def fetching(*refs):
-        given, rest, landed, sems = (
-            refs[: scalars + count],
-            refs[scalars + count : -1 - count],
-            refs[-1 - count : -1],
-            refs[-1],
-        )
+        given, rest, sems = list(refs[:count]), refs[count:-1], refs[-1]
+        own, landed = rest[: len(rest) - len(fetch)], rest[len(rest) - len(fetch) :]
         copies = [
-            pltpu.make_async_copy(source, target, sems.at[index])
-            for index, (source, target) in enumerate(zip(given[scalars:], landed))
+            pltpu.make_async_copy(given[place], target, sems.at[index])
+            for index, (place, target) in enumerate(zip(fetch, landed))
         ]
         for copy in copies:
             copy.start()
+        for place, target in zip(fetch, landed):
+            given[place] = target
         for copy in copies:
             copy.wait()
-        kernel(*given[:scalars], *landed, *rest)
+        kernel(*given, *own)
 
     return pl.pallas_call(
-        fetching if staged else kernel,
+        fetching,
         out_shape=tuple(jax.ShapeDtypeStruct(shape, jnp.bfloat16) for shape in shapes),
-        in_specs=[smem] * scalars + [anywhere if staged else vmem] * count,
+        in_specs=[
+            smem if place < scalars else hbm if place in fetch else vmem for place in range(count)
+        ],
         out_specs=(vmem,) * len(shapes),
         scratch_shapes=scratch_shapes,
         compiler_params=pltpu.CompilerParams(vmem_limit_bytes=limit * 1024 * 1024),
@@ -387,15 +380,18 @@
 
 
 def coarse_kernel(edge_ref, gathered_ref, *refs):
-    count = 10
-    operands, outputs, landed = refs[:count], refs[count : count + 2], refs[-count - 1 : -1]
+    count = 6
+    direct, operands = refs[:4], refs[4 : 4 + count]
+    outputs, landed = refs[4 + count : 6 + count], refs[-count - 1 : -1]
     small = [
         pltpu.make_async_copy(source, target, refs[-1].at[index])
         for index, (source, target) in enumerate(zip(operands, landed))
     ]
     for copy in small:
         copy.start()
-    coarse_body(edge_ref, gathered_ref, small, *landed, *outputs, *refs[count + 2 : -count - 1])
+    coarse_body(
+        edge_ref, gathered_ref, small, *direct, *landed, *outputs, *refs[6 + count : -count - 1]
+    )
 
 
 def coarse_body(
@@ -404,9 +400,9 @@
     small,
     attended_ref,
     own_ref,
-    depth_ref,
     samples_ref,
     fine_ref,
+    depth_ref,
     to_fine_ref,
     square_ref,
     centre_ref,
@@ -480,15 +476,12 @@
     samples = samples_ref[...]
     for shard in range(SHARDS):
         four = nt(taps_ref[shard], samples[: 4 * 64])
-        ninth = nt(taps_ref[shard][4 * HEAD_ROWS :], samples[4 * 64 :])
-        total = four[8 : 8 + HEAD_ROWS, :64]
-        for block in range(1, 4):
+        fifth = nt(taps_ref[shard][4 * HEAD_ROWS :], samples[4 * 64 :])
+        total = fifth[8:]
+        for block in range(4):
             rows = slice(8 + block * HEAD_ROWS, 8 + (block + 1) * HEAD_ROWS)
             total += four[rows, block * 64 : (block + 1) * 64]
-        first = shard * 39
-        down_ref[first : first + HEAD_ROWS, :64] = total
-        down_ref[first : first + HALF, :64] += ninth[8 : 8 + HALF, :64]
-        down_ref[first + HALF : first + HEAD_ROWS, :64] += ninth[8 : 8 + HALF, 64:]
+        down_ref[shard * 39 : shard * 39 + HEAD_ROWS, :64] = total
     downsampled = down_ref[...].T[:CELLS, :width].astype(jnp.bfloat16).astype(jnp.float32)
     coarse_out_ref[...] = jnp.maximum(
         nn(compact_ref[...], result) + downsampled, 0.0
@@ -498,9 +491,9 @@
 def coarse_stream(gathered, edges, attended, own, depth, samples, fine_res, to_fine):
     width = own.shape[1]
     fine_cells, fine_ch = fine_res.shape
-    operands = (attended, own, depth, samples, fine_res, to_fine, *cell_tables())
-    smem, vmem, anywhere = (
-        pl.BlockSpec(memory_space=space) for space in (pltpu.SMEM, pltpu.VMEM, pl.ANY)
+    operands = (attended, own, samples, fine_res, depth, to_fine, *cell_tables())
+    smem, vmem, hbm = (
+        pl.BlockSpec(memory_space=space) for space in (pltpu.SMEM, pltpu.VMEM, pltpu.HBM)
     )
     return pl.pallas_call(
         coarse_kernel,
@@ -508,7 +501,7 @@
             jax.ShapeDtypeStruct((fine_cells, fine_ch), jnp.bfloat16),
             jax.ShapeDtypeStruct((CELLS, width), jnp.bfloat16),
         ),
-        in_specs=[smem, anywhere] + [anywhere] * len(operands),
+        in_specs=[smem, hbm] + [vmem] * 4 + [hbm] * (len(operands) - 4),
         out_specs=(vmem, vmem),
         scratch_shapes=[
             pltpu.VMEM((SHARDS, OUT_ROWS, width), jnp.bfloat16),
@@ -519,8 +512,8 @@
             pltpu.VMEM((64, SHARDS * BLOCK_ROWS), jnp.float32),
             pltpu.VMEM((SHARDS * HEAD_ROWS, 128), jnp.float32),
             pltpu.SemaphoreType.DMA((4,)),
-            *(pltpu.VMEM(operand.shape, operand.dtype) for operand in operands),
-            pltpu.SemaphoreType.DMA((len(operands),)),
+            *(pltpu.VMEM(operand.shape, operand.dtype) for operand in operands[4:]),
+            pltpu.SemaphoreType.DMA((len(operands) - 4,)),
         ],
         compiler_params=pltpu.CompilerParams(vmem_limit_bytes=40 * 1024 * 1024),
     )(edges, gathered, *operands)
@@ -567,6 +560,7 @@
         (fine.shape, (32, fine_ch), (16, fine_ch)),
         (fine, inproj_fine, outproj_fine, window_table()),
         (),
+        fetch=(0, 1, 2, 3),
     )
     above, below = exchange(going_down, going_up, "rows")
     spread, column = strip_tables()
@@ -582,6 +576,7 @@
             ((3 * TILE, coarse_ch), jnp.float32),
         ),
         scalars=2,
+        fetch=(3, 4, 5),
     )
     blocks = lax.all_to_all(blocks, "rows", 0, 0, tiled=True)
     going_right, going_left = call(
@@ -589,14 +584,15 @@
         ((64, coarse_ch), (64, coarse_ch)),
         (above, below, middle, columns, *border_tables()),
         (((248, fine_ch), jnp.float32),),
+        fetch=(4, 5),
     )
     left, right = exchange(going_right, going_left, "cols")
     edge = (SHARDS, 16, HEAD_ROWS)
-    near = exchange(*call(edge_columns_kernel, (edge, edge), (blocks, column), ()), "cols")
+    near = exchange(*call(edge_columns_kernel, (edge, edge), (blocks, column), (), fetch=(1,)), "cols")
     hidden_count = expand_fine.shape[0]
     fine_res, samples = call(
         field_kernel,
-        (fine.shape, (6 * 64, 2 * fine_ch)),
+        (fine.shape, (5 * 64, 2 * fine_ch)),
         (
             edges,
             above,
@@ -616,7 +612,7 @@
             ((512, 2 * fine_ch), jnp.float32),
         ),
         scalars=1,
-        staged=True,
+        fetch=tuple(range(6, 13)),
     )
     (attended,) = call(
         attended_kernel,

time: 139 us -> 124 us (0.89)
  local copies, waits for them, and re-layouts: 33.9 us -> 18.1 us
    unnamed x56 -> x68, local copies, waits for them, and re-layouts: 22.5 us -> 15.8 us
    concatenate x1 -> x0, local copies, waits for them, and re-layouts: 4.75 us -> none  [pack(): jnp.concatenate([jnp.pad(expand, ((0, 4), (0, 0))), jnp.pad(shrink.T, ((0...]
    pad x3 -> x1, local copies, waits for them, and re-layouts: 2.72 us -> 1.11 us  [pack(): jnp.pad(to_coarse, ((0, 1), (0, 1), (0, 0))).reshape(5, 2, HEAD_ROWS, -1)]
  transfers between devices with their start and end apart: 8 -> 8, of which waited for: 2 -> 2; matrix products, arithmetic and copies ran while one was open for 2% -> 1% of each run, Pallas kernels for 11% -> 13%
where the time goes in v8:
time: 124 us; the launch traced here: 123 us
  blocking collectives  29.8 us (24%)
  Pallas kernels  25.7 us (21%)
  starting transfers between devices  24 us (19%)
  local copies, waits for them, and re-layouts  18.1 us (15%)
  between operations  14.5 us (12%)
  waiting for transfers between devices  9.95 us (8%)
    all_gather x1, blocking collectives, local(): strip = lax.all_gather(coarse_in.reshape(coarse_ch, coarse_cells).T, 'rows')  29.8 us
    ppermute x6, starting transfers between devices, exchange(): return (lax.ppermute(onward, axis, up), lax.ppermute(back, axis, down))  20.6 us
    pallas_call x6, Pallas kernels, call(): pl.pallas_call(fetching, out_shape=tuple((jax.ShapeDtypeStruct(shape, jnp...  16.1 us
    unnamed x68, local copies, waits for them, and re-layouts  15.8 us
    ppermute x6, waiting for transfers between devices, exchange(): return (lax.ppermute(onward, axis, up), lax.ppermute(back, axis, down))  9.91 us
    pallas_call x1, Pallas kernels, coarse_stream(): pl.pallas_call(coarse_kernel, out_shape=(jax.ShapeDtypeStruct((fine_cells...  9.62 us
    all_to_all x1, starting transfers between devices, local(): blocks = lax.all_to_all(blocks, 'rows', 0, 0, tiled=True)  3.44 us
  transfers between devices with their start and end apart: 8, of which 2 were waited for; matrix products, arithmetic and copies ran while one was open for 1% of the time, Pallas kernels for 13%

profile of v8, /device:TPU:33, one launch (start us, length us, event | category | flops | bytes accessed | tf_op | source)
XLA Modules:
  0.0 123.2 jit_solution(13212329735527797056)
XLA Ops:
  7.2 0.0 all-gather.5.cloned.1.call-start
  7.2 1.1 pad.22
  8.3 0.2 copy.30
  8.6 0.0 copy-start.31
  8.6 0.2 reshape.32
  8.9 0.0 copy-start.10
  8.9 0.0 copy-start.21
  8.9 0.0 copy-start.22
  8.9 0.9 fusion.6
  9.9 0.0 all-gather.5.cloned.1.call-update
  9.9 0.1 add_convert_fusion.refs_0_.edge_ref
  10.0 0.0 copy-start.8
  10.0 0.0 copy-start.11
  10.0 29.8 %all-gather.2.refs_2_ = bf16[16,49,624]{2,1,0:T(8,128)(2,1)S(1)} all-gather(bf16[1,49,624]{2,1,0:T(8,128)(2,1)S(1)} %bitcast.35), channel_id=3, replica_groups=mesh['rows'=16,'cols'=32] {'rows'}, dimensions={0}, use_global_device_ids=true | all-gather | bytes 1039584 | tf_op jit(solution)/shard_map/all_gather | solution.py:547
  39.8 0.0 copy-start.24
  39.8 0.0 copy-start.26
  39.9 3.4 %shard_map.266 = (bf16[16,64,40]{2,1,0:T(8,128)(2,1)S(1)}, bf16[64,624]{1,0:T(8,128)(2,1)S(1)}, bf16[32,624]{1,0:T(8,128)(2,1)S(1)}) custom-call(s32[4]{0:T(128)S(1)} %add_convert_fusion.refs_0_.edge_ref, s32[1]{0:T(128)} %bitcast.9.refs_1_, bf16[16,49,624]{2,1,0:T(8,128)(2,1)S(1)} %all-gather.2.refs_2_, bf16[3,39,624]{2,1,0:T(8,128)(2,1)S(1)} %copy-done.10, ...), custom_call_target="tpu_custom_call" | custom-call | tf_op jit(solution)/shard_map/pallas_call | solution.py:370
  43.3 0.0 copy-start.30
  43.3 0.2 copy.31
  43.5 0.8 reshape.45
  44.3 3.4 %all-to-all-start = ((bf16[16,2,1280]{2,1,0:T(2,128)(2,1)}), bf16[16,2,1280]{2,1,0:T(2,128)(2,1)S(1)}, u32[]{:S(2)}, u32[]{:S(2)}) async-start(bf16[16,2,1280]{2,1,0:T(2,128)(2,1)} %reshape.45), calls=%async_computation | async-start | bytes 163840 | tf_op jit(solution)/shard_map/all_to_all | solution.py:581
  47.7 5.1 %shard_map.269 = (bf16[196,312]{1,0:T(8,128)(2,1)S(1)}, bf16[32,312]{1,0:T(8,128)(2,1)S(1)}, bf16[16,312]{1,0:T(8,128)(2,1)S(1)}) custom-call(bf16[196,312]{1,0:T(8,128)(2,1)S(1)} %bitcast.30, bf16[3,312,312]{2,1,0:T(8,128)(2,1)S(1)} %copy-done.3, bf16[312,312]{1,0:T(8,128)(2,1)S(1)} %copy-done.6, f32[196,196]{1,0:T(8,128)S(1)} %copy-done.8), custom_call_target="tpu_custom_call" | custom-call | tf_op jit(solution)/shard_map/pallas_call | solution.py:370
  52.9 0.0 copy-start.1
  52.9 0.0 copy-start.2
  52.9 0.0 copy-start.5
  52.9 3.7 %collective-permute-start.2 = (bf16[32,312]{1,0:T(8,128)(2,1)S(1)}, bf16[32,312]{1,0:T(8,128)(2,1)S(1)}, u32[]{:S(2)}, u32[]{:S(2)}) collective-permute-start(bf16[32,312]{1,0:T(8,128)(2,1)S(1)} %get-tuple-element.20), channel_id=1, source_target_pairs={{0,32},{32,64},{64,96},{96,128},{128,160},{160,192},{192,224},{224... | collective-permute-start | bytes 59912 | tf_op jit(solution)/shard_map/ppermute | solution.py:525
  56.6 1.9 %collective-permute-start.3 = (bf16[16,312]{1,0:T(8,128)(2,1)S(1)}, bf16[16,312]{1,0:T(8,128)(2,1)S(1)}, u32[]{:S(2)}, u32[]{:S(2)}) collective-permute-start(bf16[16,312]{1,0:T(8,128)(2,1)S(1)} %get-tuple-element.21), channel_id=1, source_target_pairs={{32,0},{64,32},{96,64},{128,96},{160,128},{192,160},{224,192},{256... | collective-permute-start | bytes 29960 | tf_op jit(solution)/shard_map/ppermute | solution.py:525
  58.5 3.7 %collective-permute-done.3.refs_1_.refs_2_ = bf16[16,312]{1,0:T(8,128)(2,1)S(1)} collective-permute-done((bf16[16,312]{1,0:T(8,128)(2,1)S(1)}, bf16[16,312]{1,0:T(8,128)(2,1)S(1)}, u32[]{:S(2)}, u32[]{:S(2)}) %collective-permute-start.3) | collective-permute-done | bytes 10016 | tf_op jit(solution)/shard_map/ppermute | solution.py:525
  62.3 0.0 collective-permute-done.2.refs_0_.refs_1_
  62.3 0.3 shard_map.270
  62.6 0.3 copy-done.19
  62.9 4.3 %collective-permute-start.5 = (bf16[64,624]{1,0:T(8,128)(2,1)S(1)}, bf16[64,624]{1,0:T(8,128)(2,1)S(1)}, u32[]{:S(2)}, u32[]{:S(2)}) collective-permute-start(bf16[64,624]{1,0:T(8,128)(2,1)S(1)} %get-tuple-element.25), channel_id=1, source_target_pairs={{1,0},{2,1},{3,2},{4,3},{5,4},{6,5},{7,6},{8,7},{9,8},{10,9},{11,1... | collective-permute-start | bytes 239624 | tf_op jit(solution)/shard_map/ppermute | solution.py:525
  67.1 1.9 %collective-permute-start.4 = (bf16[64,624]{1,0:T(8,128)(2,1)S(1)}, bf16[64,624]{1,0:T(8,128)(2,1)S(1)}, u32[]{:S(2)}, u32[]{:S(2)}) collective-permute-start(bf16[64,624]{1,0:T(8,128)(2,1)S(1)} %get-tuple-element.24), channel_id=1, source_target_pairs={{0,1},{1,2},{2,3},{3,4},{4,5},{5,6},{6,7},{7,8},{8,9},{9,10},{10,1... | collective-permute-start | bytes 239624 | tf_op jit(solution)/shard_map/ppermute | solution.py:525
  69.1 0.2 reshape.36
  69.3 0.1 reshape.37.refs_4_
  69.4 0.0 collective-permute-done.5.refs_4_
  69.4 6.2 %collective-permute-done.4.refs_3_ = bf16[64,624]{1,0:T(8,128)(2,1)S(1)} collective-permute-done((bf16[64,624]{1,0:T(8,128)(2,1)S(1)}, bf16[64,624]{1,0:T(8,128)(2,1)S(1)}, u32[]{:S(2)}, u32[]{:S(2)}) %collective-permute-start.4) | collective-permute-done | bytes 79904 | tf_op jit(solution)/shard_map/ppermute | solution.py:525
  75.6 0.2 reshape.46
  75.8 0.5 copy-done.14
  76.3 0.2 copy.33.refs_0_
  76.4 0.2 shard_map.267
  76.7 1.9 %collective-permute-start = (bf16[16,16,40]{2,1,0:T(8,128)(2,1)S(1)}, bf16[16,16,40]{2,1,0:T(8,128)(2,1)S(1)}, u32[]{:S(2)}, u32[]{:S(2)}) collective-permute-start(bf16[16,16,40]{2,1,0:T(8,128)(2,1)S(1)} %get-tuple-element.17), channel_id=1, source_target_pairs={{0,1},{1,2},{2,3},{3,4},{4,5},{5,6},{6,7},{7,8},{8,9},{9,10},{10,1... | collective-permute-start | bytes 61448 | tf_op jit(solution)/shard_map/ppermute | solution.py:525
  78.6 6.9 %collective-permute-start.1 = (bf16[16,16,40]{2,1,0:T(8,128)(2,1)S(1)}, bf16[16,16,40]{2,1,0:T(8,128)(2,1)S(1)}, u32[]{:S(2)}, u32[]{:S(2)}) collective-permute-start(bf16[16,16,40]{2,1,0:T(8,128)(2,1)S(1)} %get-tuple-element.18), channel_id=1, source_target_pairs={{1,0},{2,1},{3,2},{4,3},{5,4},{6,5},{7,6},{8,7},{9,8},{10,9},{11,1... | collective-permute-start | bytes 61448 | tf_op jit(solution)/shard_map/ppermute | solution.py:525
  85.5 0.0 copy-start.7
  85.5 0.9 copy-done.7
  86.5 0.9 copy-done.9
  87.4 0.9 copy-done.15
  88.3 0.9 copy-done.16
  89.2 0.9 copy-done.17
  90.1 0.7 copy-done.20
  90.8 6.5 %shard_map.271 = (bf16[196,312]{1,0:T(8,128)(2,1)S(1)}, bf16[320,624]{1,0:T(8,128)(2,1)S(1)}) custom-call(s32[4]{0:T(128)S(1)} %add_convert_fusion.refs_0_.edge_ref, bf16[32,312]{1,0:T(8,128)(2,1)S(1)} %collective-permute-done.2.refs_0_.refs_1_, bf16[16,312]{1,0:T(8,128)(2,1)S(1)} %copy-done.20, bf16[64,624]{1,0:T(8,128)(2,1)S(1)} %copy-done.15, ...), custom_call_target="tpu_custom_call" | custom-call | tf_op jit(solution)/shard_map/pallas_call | solution.py:370
  97.3 0.0 copy-start.12
  97.3 0.7 copy-done.12
  98.0 0.0 collective-permute-done.refs_1_
  98.0 0.0 collective-permute-done.1.refs_2_
  98.0 0.5 shard_map.268.refs_0_
  98.5 0.0 all-gather.5.cloned.1.call-done
  98.6 4.2 %copy-done = bf16[8960,624]{1,0:T(8,128)(2,1)S(1)} copy-done((bf16[8960,624]{1,0:T(8,128)(2,1)S(1)}, bf16[8960,624]{1,0:T(8,128)(2,1)}, u32[]{:S(2)}) %copy-start) | copy-done | bytes 11182104
  102.8 0.9 copy-done.13
  103.7 0.8 copy-done.18
  104.5 0.7 copy-done.23
  105.3 0.7 copy-done.25
  106.0 0.7 copy-done.27
  106.7 9.6 %shard_map.272 = (bf16[196,312]{1,0:T(8,128)(2,1)}, bf16[49,624]{1,0:T(8,128)(2,1)}) custom-call(s32[4]{0:T(128)S(1)} %add_convert_fusion.refs_0_.edge_ref, bf16[16,560,624]{2,1,0:T(8,128)(2,1)S(1)} %bitcast.28, bf16[96,768]{1,0:T(8,128)(2,1)S(1)} %shard_map.268.refs_0_, bf16[96,624]{1,0:T(8,128)(2,1)S(1)} %pad_maximum_fusion.refs_1_, ...), custom_call_target="tpu_custom_call" | custom-call | tf_op jit(solution)/shard_map/pallas_call | solution.py:498
  (42 shorter events, 0.1 us)
Async XLA Ops:
  7.2 1.7 %copy-start.32 = (bf16[624,39]{0,1:T(8,128)(2,1)S(1)}, bf16[624,39]{0,1:T(8,128)(2,1)}, u32[]{:S(2)}) copy-start(bf16[624,39]{0,1:T(8,128)(2,1)} %param.35) | copy-start | bytes 146020
  7.2 1.7 %copy-start.28 = (bf16[624,156]{0,1:T(8,128)(2,1)S(1)}, bf16[624,156]{0,1:T(8,128)(2,1)}, u32[]{:S(2)}) copy-start(bf16[624,156]{0,1:T(8,128)(2,1)} %param.38) | copy-start | bytes 584068
  7.2 1.7 %copy-start.29 = (bf16[156,624]{1,0:T(8,128)(2,1)S(1)}, bf16[156,624]{1,0:T(8,128)(2,1)}, u32[]{:S(2)}) copy-start(bf16[156,624]{1,0:T(8,128)(2,1)} %param.36) | copy-start | bytes 584068
  7.2 91.3 %all-gather.5.cloned.1.call-start = ((), (), s32[]{:S(2)}) async-start(), calls=%async_computation.1 | async-start | bytes 12185600 | tf_op jit(solution)/shard_map/all_gather | solution.py:546
  8.6 1.4 %copy-start.31 = (bf16[1,1,624,49]{2,3,1,0:T(8,128)(2,1)S(1)}, bf16[1,1,624,49]{2,3,1,0:T(8,128)(2,1)}, u32[]{:S(2)}) copy-start(bf16[1,1,624,49]{2,3,1,0:T(8,128)(2,1)} %param.28) | copy-start | bytes 183460
  8.9 30.9 %copy-start.10 = (bf16[3,39,624]{2,1,0:T(8,128)(2,1)S(1)}, bf16[3,39,624]{2,1,0:T(8,128)(2,1)}, u32[]{:S(2)}) copy-start(bf16[3,39,624]{2,1,0:T(8,128)(2,1)} %refs_3_.2) | copy-start | bytes 438052
  8.9 30.9 %copy-start.21 = (bf16[32,64]{1,0:T(8,128)(2,1)S(1)}, bf16[32,64]{1,0:T(8,128)(2,1)}, u32[]{:S(2)}) copy-start(bf16[32,64]{1,0:T(8,128)(2,1)} %constant.76.refs_5_.refs_1_) | copy-start | bytes 12292
  8.9 30.9 %copy-start.22 = (bf16[64,168]{1,0:T(8,128)(2,1)S(1)}, bf16[64,168]{1,0:T(8,128)(2,1)}, u32[]{:S(2)}) copy-start(bf16[64,168]{1,0:T(8,128)(2,1)} %constant.75.refs_4_) | copy-start | bytes 64516
  10.0 37.7 %copy-start.3 = (bf16[3,312,312]{2,1,0:T(8,128)(2,1)S(1)}, bf16[3,312,312]{2,1,0:T(8,128)(2,1)}, u32[]{:S(2)}) copy-start(bf16[3,312,312]{2,1,0:T(8,128)(2,1)} %refs_1_.1) | copy-start | bytes 1752196
  10.0 37.7 %copy-start.6 = (bf16[312,312]{1,0:T(8,128)(2,1)S(1)}, bf16[312,312]{1,0:T(8,128)(2,1)}, u32[]{:S(2)}) copy-start(bf16[312,312]{1,0:T(8,128)(2,1)} %refs_2_.1) | copy-start | bytes 584068
  10.0 37.7 %copy-start.8 = (f32[196,196]{1,0:T(8,128)S(1)}, f32[196,196]{1,0:T(8,128)}, u32[]{:S(2)}) copy-start(f32[196,196]{1,0:T(8,128)} %constant.45.clone.refs_3_) | copy-start | bytes 460996
  10.0 37.7 %copy-start.11 = (bf16[1,1,312,196]{2,3,1,0:T(8,128)(2,1)S(1)}, bf16[1,1,312,196]{2,3,1,0:T(8,128)(2,1)}, u32[]{:S(2)}) copy-start(bf16[1,1,312,196]{2,3,1,0:T(8,128)(2,1)} %param.27) | copy-start | bytes 366916
  39.8 22.4 %copy-start.24 = (bf16[40,248]{1,0:T(8,128)(2,1)S(1)}, bf16[40,248]{1,0:T(8,128)(2,1)}, u32[]{:S(2)}) copy-start(bf16[40,248]{1,0:T(8,128)(2,1)} %constant.77.refs_4_) | copy-start | bytes 59524
  39.8 22.4 %copy-start.26 = (bf16[32,248]{1,0:T(8,128)(2,1)S(1)}, bf16[32,248]{1,0:T(8,128)(2,1)}, u32[]{:S(2)}) copy-start(bf16[32,248]{1,0:T(8,128)(2,1)} %constant.78.refs_5_) | copy-start | bytes 47620
  43.3 25.8 %copy-start.30 = (f32[9,2496]{1,0:T(8,128)S(1)}, f32[9,2496]{1,0:T(8,128)}, u32[]{:S(2)}) copy-start(f32[9,2496]{1,0:T(8,128)} %param.37) | copy-start | bytes 269572
  44.3 31.4 %all-to-all-start = ((bf16[16,2,1280]{2,1,0:T(2,128)(2,1)}), bf16[16,2,1280]{2,1,0:T(2,128)(2,1)S(1)}, u32[]{:S(2)}, u32[]{:S(2)}) async-start(bf16[16,2,1280]{2,1,0:T(2,128)(2,1)} %reshape.45), calls=%async_computation | async-start | bytes 163840 | tf_op jit(solution)/shard_map/all_to_all | solution.py:581
  52.9 32.6 %copy-start.1 = (bf16[1248,312]{0,1:T(8,128)(2,1)S(1)}, bf16[1248,312]{0,1:T(8,128)(2,1)}, u32[]{:S(2)}) copy-start(bf16[1248,312]{0,1:T(8,128)(2,1)} %param.31) | copy-start | bytes 2336260
  52.9 32.6 %copy-start.2 = (bf16[312,1248]{1,0:T(8,128)(2,1)S(1)}, bf16[312,1248]{1,0:T(8,128)(2,1)}, u32[]{:S(2)}) copy-start(bf16[312,1248]{1,0:T(8,128)(2,1)} %refs_8_.1) | copy-start | bytes 2336260
  52.9 32.6 %copy-start.5 = (bf16[320,512]{1,0:T(8,128)(2,1)S(1)}, bf16[320,512]{1,0:T(8,128)(2,1)}, u32[]{:S(2)}) copy-start(bf16[320,512]{1,0:T(8,128)(2,1)} %constant.82.refs_12_) | copy-start | bytes 983044
  52.9 9.3 %collective-permute-start.2 = (bf16[32,312]{1,0:T(8,128)(2,1)S(1)}, bf16[32,312]{1,0:T(8,128)(2,1)S(1)}, u32[]{:S(2)}, u32[]{:S(2)}) collective-permute-start(bf16[32,312]{1,0:T(8,128)(2,1)S(1)} %get-tuple-element.20), channel_id=1, source_target_pairs={{0,32},{32,64},{64,96},{96,128},{128,160},{160,192},{192,224},{224... | collective-permute-start | bytes 59912 | tf_op jit(solution)/shard_map/ppermute | solution.py:525
  56.6 5.6 %collective-permute-start.3 = (bf16[16,312]{1,0:T(8,128)(2,1)S(1)}, bf16[16,312]{1,0:T(8,128)(2,1)S(1)}, u32[]{:S(2)}, u32[]{:S(2)}) collective-permute-start(bf16[16,312]{1,0:T(8,128)(2,1)S(1)} %get-tuple-element.21), channel_id=1, source_target_pairs={{32,0},{64,32},{96,64},{128,96},{160,128},{192,160},{224,192},{256... | collective-permute-start | bytes 29960 | tf_op jit(solution)/shard_map/ppermute | solution.py:525
  62.3 0.6 copy-start.19
  62.9 6.6 %collective-permute-start.5 = (bf16[64,624]{1,0:T(8,128)(2,1)S(1)}, bf16[64,624]{1,0:T(8,128)(2,1)S(1)}, u32[]{:S(2)}, u32[]{:S(2)}) collective-permute-start(bf16[64,624]{1,0:T(8,128)(2,1)S(1)} %get-tuple-element.25), channel_id=1, source_target_pairs={{1,0},{2,1},{3,2},{4,3},{5,4},{6,5},{7,6},{8,7},{9,8},{10,9},{11,1... | collective-permute-start | bytes 239624 | tf_op jit(solution)/shard_map/ppermute | solution.py:525
  67.1 8.5 %collective-permute-start.4 = (bf16[64,624]{1,0:T(8,128)(2,1)S(1)}, bf16[64,624]{1,0:T(8,128)(2,1)S(1)}, u32[]{:S(2)}, u32[]{:S(2)}) collective-permute-start(bf16[64,624]{1,0:T(8,128)(2,1)S(1)} %get-tuple-element.24), channel_id=1, source_target_pairs={{0,1},{1,2},{2,3},{3,4},{4,5},{5,6},{6,7},{7,8},{8,9},{9,10},{10,1... | collective-permute-start | bytes 239624 | tf_op jit(solution)/shard_map/ppermute | solution.py:525
  75.6 0.6 copy-start.14
  76.7 21.3 %collective-permute-start = (bf16[16,16,40]{2,1,0:T(8,128)(2,1)S(1)}, bf16[16,16,40]{2,1,0:T(8,128)(2,1)S(1)}, u32[]{:S(2)}, u32[]{:S(2)}) collective-permute-start(bf16[16,16,40]{2,1,0:T(8,128)(2,1)S(1)} %get-tuple-element.17), channel_id=1, source_target_pairs={{0,1},{1,2},{2,3},{3,4},{4,5},{5,6},{6,7},{7,8},{8,9},{9,10},{10,1... | collective-permute-start | bytes 61448 | tf_op jit(solution)/shard_map/ppermute | solution.py:525
  78.6 19.4 %collective-permute-start.1 = (bf16[16,16,40]{2,1,0:T(8,128)(2,1)S(1)}, bf16[16,16,40]{2,1,0:T(8,128)(2,1)S(1)}, u32[]{:S(2)}, u32[]{:S(2)}) collective-permute-start(bf16[16,16,40]{2,1,0:T(8,128)(2,1)S(1)} %get-tuple-element.18), channel_id=1, source_target_pairs={{1,0},{2,1},{3,2},{4,3},{5,4},{6,5},{7,6},{8,7},{9,8},{10,9},{11,1... | collective-permute-start | bytes 61448 | tf_op jit(solution)/shard_map/ppermute | solution.py:525
  85.5 0.9 copy-start.7
  86.5 0.9 copy-start.9
  87.4 0.9 copy-start.15
  88.3 0.9 copy-start.16
  89.2 0.9 copy-start.17
  90.1 0.7 copy-start.20
  90.8 7.8 %copy-start.4 = (bf16[312,624]{1,0:T(8,128)(2,1)S(1)}, bf16[312,624]{1,0:T(8,128)(2,1)}, u32[]{:S(2)}) copy-start(bf16[312,624]{1,0:T(8,128)(2,1)} %refs_5_.1) | copy-start | bytes 1168132
  97.3 0.7 copy-start.12
  98.6 4.3 %copy-start = (bf16[8960,624]{1,0:T(8,128)(2,1)S(1)}, bf16[8960,624]{1,0:T(8,128)(2,1)}, u32[]{:S(2)}) copy-start(bf16[8960,624]{1,0:T(8,128)(2,1)} %all-gather.5.cloned.1.call-done) | copy-start | bytes 33546244
  102.8 0.9 copy-start.13
  103.7 0.8 copy-start.18
  104.5 0.7 copy-start.23
  105.3 0.7 copy-start.25
  106.0 0.7 copy-start.27
Sparse Core Ops, SparseCore 0:
  10.2 81.0 all-gather.4

commit v9 on v8

--- a/solution.py
+++ b/solution.py
@@ -367,6 +367,10 @@
             copy.wait()
         kernel(*given, *own)
 
+    operands = [
+        pltpu.with_memory_space_constraint(array, pltpu.HBM) if place in fetch else array
+        for place, array in enumerate(operands)
+    ]
     return pl.pallas_call(
         fetching,
         out_shape=tuple(jax.ShapeDtypeStruct(shape, jnp.bfloat16) for shape in shapes),
@@ -491,7 +495,9 @@
 def coarse_stream(gathered, edges, attended, own, depth, samples, fine_res, to_fine):
     width = own.shape[1]
     fine_cells, fine_ch = fine_res.shape
-    operands = (attended, own, samples, fine_res, depth, to_fine, *cell_tables())
+    fixed = (gathered, depth, to_fine, *cell_tables())
+    gathered, *fixed = (pltpu.with_memory_space_constraint(array, pltpu.HBM) for array in fixed)
+    operands = (attended, own, samples, fine_res, *fixed)
     smem, vmem, hbm = (
         pl.BlockSpec(memory_space=space) for space in (pltpu.SMEM, pltpu.VMEM, pltpu.HBM)
     )

time: 124 us -> 113 us (0.911)
  local copies, waits for them, and re-layouts: 18.1 us -> 3.91 us
  Pallas kernels: 25.7 us -> 30.5 us
    unnamed x68 -> x12, local copies, waits for them, and re-layouts: 15.8 us -> 0.98 us
    pallas_call x6, Pallas kernels: 16.1 us -> 19.1 us  [call(): pl.pallas_call(fetching, out_shape=tuple((jax.ShapeDtypeStruct(shape, jnp...]
    pallas_call x1, Pallas kernels: 9.62 us -> 11.4 us  [coarse_stream(): pl.pallas_call(coarse_kernel, out_shape=(jax.ShapeDtypeStruct((fine_cells...]
  transfers between devices with their start and end apart: 8 -> 8, of which waited for: 2 -> 2; matrix products, arithmetic and copies ran while one was open for 1% -> 2% of each run, Pallas kernels for 13% -> 17%
where the time goes in v9:
time: 113 us
  Pallas kernels  30.5 us (27%)
  blocking collectives  29.7 us (26%)
  starting transfers between devices  24 us (21%)
  between operations  14.3 us (13%)
  waiting for transfers between devices  9.31 us (8%)
  local copies, waits for them, and re-layouts  3.91 us (3%)
    all_gather x1, blocking collectives, local(): strip = lax.all_gather(coarse_in.reshape(coarse_ch, coarse_cells).T, 'rows')  29.7 us
    ppermute x6, starting transfers between devices, exchange(): return (lax.ppermute(onward, axis, up), lax.ppermute(back, axis, down))  20.5 us
    pallas_call x6, Pallas kernels, call(): pl.pallas_call(fetching, out_shape=tuple((jax.ShapeDtypeStruct(shape, jnp...  19.1 us
    pallas_call x1, Pallas kernels, coarse_stream(): pl.pallas_call(coarse_kernel, out_shape=(jax.ShapeDtypeStruct((fine_cells...  11.4 us
    ppermute x6, waiting for transfers between devices, exchange(): return (lax.ppermute(onward, axis, up), lax.ppermute(back, axis, down))  9.27 us
    all_to_all x1, starting transfers between devices, local(): blocks = lax.all_to_all(blocks, 'rows', 0, 0, tiled=True)  3.45 us
  transfers between devices with their start and end apart: 8, of which 2 were waited for; matrix products, arithmetic and copies ran while one was open for 2% of the time, Pallas kernels for 17%

profile of v9, /device:TPU:33, one launch (start us, length us, event | category | flops | bytes accessed | tf_op | source)
XLA Modules:
  0.0 112.7 jit_solution(8458881641033016140)
XLA Ops:
  7.2 0.0 copy-start.4
  7.2 0.0 copy-start
  7.2 0.0 copy-start.1
  7.2 0.0 all-gather.5.cloned.1.call-start
  7.2 1.1 pad.22
  8.3 0.2 copy.30
  8.6 0.0 copy-start.3
  8.6 0.2 reshape.32
  8.8 0.0 copy-done.4
  8.9 0.0 copy-done
  8.9 0.0 copy-done.1
  8.9 0.9 fusion.6
  9.8 0.0 all-gather.5.cloned.1.call-update
  9.8 0.1 add_convert_fusion.refs_0_.edge_ref
  9.9 0.0 copy-done.3
  9.9 29.7 %all-gather.2.refs_2_ = bf16[16,49,624]{2,1,0:T(8,128)(2,1)S(1)} all-gather(bf16[1,49,624]{2,1,0:T(8,128)(2,1)S(1)} %bitcast.35), channel_id=3, replica_groups=mesh['rows'=16,'cols'=32] {'rows'}, dimensions={0}, use_global_device_ids=true | all-gather | bytes 1039584 | tf_op jit(solution)/shard_map/all_gather | solution.py:553
  39.6 4.1 %shard_map.266 = (bf16[16,64,40]{2,1,0:T(8,128)(2,1)S(1)}, bf16[64,624]{1,0:T(8,128)(2,1)S(1)}, bf16[32,624]{1,0:T(8,128)(2,1)S(1)}) custom-call(s32[4]{0:T(128)S(1)} %add_convert_fusion.refs_0_.edge_ref, s32[1]{0:T(128)} %bitcast.9.refs_1_, bf16[16,49,624]{2,1,0:T(8,128)(2,1)S(1)} %all-gather.2.refs_2_, bf16[3,39,624]{2,1,0:T(8,128)(2,1)} %refs_3_.2, ...), custom_call_target="tpu_custom_call" | custom-call | tf_op jit(solution)/shard_map/pallas_call | solution.py:374
  43.7 0.0 copy-start.2
  43.7 0.2 copy.31
  43.9 0.8 reshape.45
  44.7 3.4 %all-to-all-start = ((bf16[16,2,1280]{2,1,0:T(2,128)(2,1)}), bf16[16,2,1280]{2,1,0:T(2,128)(2,1)S(1)}, u32[]{:S(2)}, u32[]{:S(2)}) async-start(bf16[16,2,1280]{2,1,0:T(2,128)(2,1)} %reshape.45), calls=%async_computation | async-start | bytes 163840 | tf_op jit(solution)/shard_map/all_to_all | solution.py:587
  48.1 5.4 %shard_map.269 = (bf16[196,312]{1,0:T(8,128)(2,1)S(1)}, bf16[32,312]{1,0:T(8,128)(2,1)S(1)}, bf16[16,312]{1,0:T(8,128)(2,1)S(1)}) custom-call(bf16[196,312]{1,0:T(8,128)(2,1)} %bitcast.34, bf16[3,312,312]{2,1,0:T(8,128)(2,1)} %refs_1_.1, bf16[312,312]{1,0:T(8,128)(2,1)} %refs_2_.1, f32[196,196]{1,0:T(8,128)} %constant.45.clone.refs_3_), custom_call_target="tpu_custom_call" | custom-call | tf_op jit(solution)/shard_map/pallas_call | solution.py:374
  53.5 3.6 %collective-permute-start.2 = (bf16[32,312]{1,0:T(8,128)(2,1)S(1)}, bf16[32,312]{1,0:T(8,128)(2,1)S(1)}, u32[]{:S(2)}, u32[]{:S(2)}) collective-permute-start(bf16[32,312]{1,0:T(8,128)(2,1)S(1)} %get-tuple-element.20), channel_id=1, source_target_pairs={{0,32},{32,64},{64,96},{96,128},{128,160},{160,192},{192,224},{224... | collective-permute-start | bytes 59912 | tf_op jit(solution)/shard_map/ppermute | solution.py:531
  57.1 1.9 %collective-permute-start.3 = (bf16[16,312]{1,0:T(8,128)(2,1)S(1)}, bf16[16,312]{1,0:T(8,128)(2,1)S(1)}, u32[]{:S(2)}, u32[]{:S(2)}) collective-permute-start(bf16[16,312]{1,0:T(8,128)(2,1)S(1)} %get-tuple-element.21), channel_id=1, source_target_pairs={{32,0},{64,32},{96,64},{128,96},{160,128},{192,160},{224,192},{256... | collective-permute-start | bytes 29960 | tf_op jit(solution)/shard_map/ppermute | solution.py:531
  59.0 3.7 %collective-permute-done.3.refs_1_.refs_2_ = bf16[16,312]{1,0:T(8,128)(2,1)S(1)} collective-permute-done((bf16[16,312]{1,0:T(8,128)(2,1)S(1)}, bf16[16,312]{1,0:T(8,128)(2,1)S(1)}, u32[]{:S(2)}, u32[]{:S(2)}) %collective-permute-start.3) | collective-permute-done | bytes 10016 | tf_op jit(solution)/shard_map/ppermute | solution.py:531
  62.7 0.0 collective-permute-done.2.refs_0_.refs_1_
  62.7 1.0 shard_map.270
  63.7 4.3 %collective-permute-start.5 = (bf16[64,624]{1,0:T(8,128)(2,1)S(1)}, bf16[64,624]{1,0:T(8,128)(2,1)S(1)}, u32[]{:S(2)}, u32[]{:S(2)}) collective-permute-start(bf16[64,624]{1,0:T(8,128)(2,1)S(1)} %get-tuple-element.25), channel_id=1, source_target_pairs={{1,0},{2,1},{3,2},{4,3},{5,4},{6,5},{7,6},{8,7},{9,8},{10,9},{11,1... | collective-permute-start | bytes 239624 | tf_op jit(solution)/shard_map/ppermute | solution.py:531
  68.0 1.9 %collective-permute-start.4 = (bf16[64,624]{1,0:T(8,128)(2,1)S(1)}, bf16[64,624]{1,0:T(8,128)(2,1)S(1)}, u32[]{:S(2)}, u32[]{:S(2)}) collective-permute-start(bf16[64,624]{1,0:T(8,128)(2,1)S(1)} %get-tuple-element.24), channel_id=1, source_target_pairs={{0,1},{1,2},{2,3},{3,4},{4,5},{5,6},{6,7},{7,8},{8,9},{9,10},{10,1... | collective-permute-start | bytes 239624 | tf_op jit(solution)/shard_map/ppermute | solution.py:531
  70.0 0.0 copy-done.2
  70.0 0.2 reshape.36
  70.2 0.8 reshape.37.refs_4_
  71.0 0.0 collective-permute-done.5.refs_4_
  71.0 5.5 %collective-permute-done.4.refs_3_ = bf16[64,624]{1,0:T(8,128)(2,1)S(1)} collective-permute-done((bf16[64,624]{1,0:T(8,128)(2,1)S(1)}, bf16[64,624]{1,0:T(8,128)(2,1)S(1)}, u32[]{:S(2)}, u32[]{:S(2)}) %collective-permute-start.4) | collective-permute-done | bytes 79904 | tf_op jit(solution)/shard_map/ppermute | solution.py:531
  76.5 0.0 all-to-all-done
  76.5 0.2 reshape.46
  76.7 0.2 copy.33.refs_0_
  76.9 0.9 shard_map.267
  77.8 1.9 %collective-permute-start = (bf16[16,16,40]{2,1,0:T(8,128)(2,1)S(1)}, bf16[16,16,40]{2,1,0:T(8,128)(2,1)S(1)}, u32[]{:S(2)}, u32[]{:S(2)}) collective-permute-start(bf16[16,16,40]{2,1,0:T(8,128)(2,1)S(1)} %get-tuple-element.17), channel_id=1, source_target_pairs={{0,1},{1,2},{2,3},{3,4},{4,5},{5,6},{6,7},{7,8},{8,9},{9,10},{10,1... | collective-permute-start | bytes 61448 | tf_op jit(solution)/shard_map/ppermute | solution.py:531
  79.7 6.9 %collective-permute-start.1 = (bf16[16,16,40]{2,1,0:T(8,128)(2,1)S(1)}, bf16[16,16,40]{2,1,0:T(8,128)(2,1)S(1)}, u32[]{:S(2)}, u32[]{:S(2)}) collective-permute-start(bf16[16,16,40]{2,1,0:T(8,128)(2,1)S(1)} %get-tuple-element.18), channel_id=1, source_target_pairs={{1,0},{2,1},{3,2},{4,3},{5,4},{6,5},{7,6},{8,7},{9,8},{10,9},{11,1... | collective-permute-start | bytes 61448 | tf_op jit(solution)/shard_map/ppermute | solution.py:531
  86.6 7.2 %shard_map.271 = (bf16[196,312]{1,0:T(8,128)(2,1)S(1)}, bf16[320,624]{1,0:T(8,128)(2,1)S(1)}) custom-call(s32[4]{0:T(128)S(1)} %add_convert_fusion.refs_0_.edge_ref, bf16[32,312]{1,0:T(8,128)(2,1)S(1)} %collective-permute-done.2.refs_0_.refs_1_, bf16[16,312]{1,0:T(8,128)(2,1)S(1)} %collective-permute-done.3.refs_1_.refs_2_, ...), custom_call_target="tpu_custom_call" | custom-call | tf_op jit(solution)/shard_map/pallas_call | solution.py:374
  93.8 0.0 collective-permute-done.refs_1_
  93.8 0.0 collective-permute-done.1.refs_2_
  93.8 0.5 shard_map.268.refs_0_
  94.4 0.0 all-gather.5.cloned.1.call-done
  94.4 11.4 %shard_map.272 = (bf16[196,312]{1,0:T(8,128)(2,1)}, bf16[49,624]{1,0:T(8,128)(2,1)}) custom-call(s32[4]{0:T(128)S(1)} %add_convert_fusion.refs_0_.edge_ref, bf16[16,560,624]{2,1,0:T(8,128)(2,1)} %bitcast.28, bf16[96,768]{1,0:T(8,128)(2,1)S(1)} %shard_map.268.refs_0_, bf16[96,624]{1,0:T(8,128)(2,1)S(1)} %pad_maximum_fusion.refs_1_, ...), custom_call_target="tpu_custom_call" | custom-call | tf_op jit(solution)/shard_map/pallas_call | solution.py:504
  (4 shorter events, 0.0 us)
Async XLA Ops:
  7.2 1.7 %copy-start.4 = (bf16[624,39]{0,1:T(8,128)(2,1)S(1)}, bf16[624,39]{0,1:T(8,128)(2,1)}, u32[]{:S(2)}) copy-start(bf16[624,39]{0,1:T(8,128)(2,1)} %param.35) | copy-start | bytes 146020
  7.2 1.7 %copy-start = (bf16[624,156]{0,1:T(8,128)(2,1)S(1)}, bf16[624,156]{0,1:T(8,128)(2,1)}, u32[]{:S(2)}) copy-start(bf16[624,156]{0,1:T(8,128)(2,1)} %param.38) | copy-start | bytes 584068
  7.2 1.7 %copy-start.1 = (bf16[156,624]{1,0:T(8,128)(2,1)S(1)}, bf16[156,624]{1,0:T(8,128)(2,1)}, u32[]{:S(2)}) copy-start(bf16[156,624]{1,0:T(8,128)(2,1)} %param.36) | copy-start | bytes 584068
  7.2 87.2 %all-gather.5.cloned.1.call-start = ((), (), s32[]{:S(2)}) async-start(), calls=%async_computation.1 | async-start | bytes 12185600 | tf_op jit(solution)/shard_map/all_gather | solution.py:552
  8.6 1.3 %copy-start.3 = (bf16[1,1,624,49]{2,3,1,0:T(8,128)(2,1)S(1)}, bf16[1,1,624,49]{2,3,1,0:T(8,128)(2,1)}, u32[]{:S(2)}) copy-start(bf16[1,1,624,49]{2,3,1,0:T(8,128)(2,1)} %param.28) | copy-start | bytes 183460
  43.7 26.2 %copy-start.2 = (f32[9,2496]{1,0:T(8,128)S(1)}, f32[9,2496]{1,0:T(8,128)}, u32[]{:S(2)}) copy-start(f32[9,2496]{1,0:T(8,128)} %param.37) | copy-start | bytes 269572
  44.7 31.9 %all-to-all-start = ((bf16[16,2,1280]{2,1,0:T(2,128)(2,1)}), bf16[16,2,1280]{2,1,0:T(2,128)(2,1)S(1)}, u32[]{:S(2)}, u32[]{:S(2)}) async-start(bf16[16,2,1280]{2,1,0:T(2,128)(2,1)} %reshape.45), calls=%async_computation | async-start | bytes 163840 | tf_op jit(solution)/shard_map/all_to_all | solution.py:587
  53.5 9.2 %collective-permute-start.2 = (bf16[32,312]{1,0:T(8,128)(2,1)S(1)}, bf16[32,312]{1,0:T(8,128)(2,1)S(1)}, u32[]{:S(2)}, u32[]{:S(2)}) collective-permute-start(bf16[32,312]{1,0:T(8,128)(2,1)S(1)} %get-tuple-element.20), channel_id=1, source_target_pairs={{0,32},{32,64},{64,96},{96,128},{128,160},{160,192},{192,224},{224... | collective-permute-start | bytes 59912 | tf_op jit(solution)/shard_map/ppermute | solution.py:531
  57.1 5.7 %collective-permute-start.3 = (bf16[16,312]{1,0:T(8,128)(2,1)S(1)}, bf16[16,312]{1,0:T(8,128)(2,1)S(1)}, u32[]{:S(2)}, u32[]{:S(2)}) collective-permute-start(bf16[16,312]{1,0:T(8,128)(2,1)S(1)} %get-tuple-element.21), channel_id=1, source_target_pairs={{32,0},{64,32},{96,64},{128,96},{160,128},{192,160},{224,192},{256... | collective-permute-start | bytes 29960 | tf_op jit(solution)/shard_map/ppermute | solution.py:531
  63.7 7.3 %collective-permute-start.5 = (bf16[64,624]{1,0:T(8,128)(2,1)S(1)}, bf16[64,624]{1,0:T(8,128)(2,1)S(1)}, u32[]{:S(2)}, u32[]{:S(2)}) collective-permute-start(bf16[64,624]{1,0:T(8,128)(2,1)S(1)} %get-tuple-element.25), channel_id=1, source_target_pairs={{1,0},{2,1},{3,2},{4,3},{5,4},{6,5},{7,6},{8,7},{9,8},{10,9},{11,1... | collective-permute-start | bytes 239624 | tf_op jit(solution)/shard_map/ppermute | solution.py:531
  68.0 8.5 %collective-permute-start.4 = (bf16[64,624]{1,0:T(8,128)(2,1)S(1)}, bf16[64,624]{1,0:T(8,128)(2,1)S(1)}, u32[]{:S(2)}, u32[]{:S(2)}) collective-permute-start(bf16[64,624]{1,0:T(8,128)(2,1)S(1)} %get-tuple-element.24), channel_id=1, source_target_pairs={{0,1},{1,2},{2,3},{3,4},{4,5},{5,6},{6,7},{7,8},{8,9},{9,10},{10,1... | collective-permute-start | bytes 239624 | tf_op jit(solution)/shard_map/ppermute | solution.py:531
  77.8 16.0 %collective-permute-start = (bf16[16,16,40]{2,1,0:T(8,128)(2,1)S(1)}, bf16[16,16,40]{2,1,0:T(8,128)(2,1)S(1)}, u32[]{:S(2)}, u32[]{:S(2)}) collective-permute-start(bf16[16,16,40]{2,1,0:T(8,128)(2,1)S(1)} %get-tuple-element.17), channel_id=1, source_target_pairs={{0,1},{1,2},{2,3},{3,4},{4,5},{5,6},{6,7},{7,8},{8,9},{9,10},{10,1... | collective-permute-start | bytes 61448 | tf_op jit(solution)/shard_map/ppermute | solution.py:531
  79.7 14.1 %collective-permute-start.1 = (bf16[16,16,40]{2,1,0:T(8,128)(2,1)S(1)}, bf16[16,16,40]{2,1,0:T(8,128)(2,1)S(1)}, u32[]{:S(2)}, u32[]{:S(2)}) collective-permute-start(bf16[16,16,40]{2,1,0:T(8,128)(2,1)S(1)} %get-tuple-element.18), channel_id=1, source_target_pairs={{1,0},{2,1},{3,2},{4,3},{5,4},{6,5},{7,6},{8,7},{9,8},{10,9},{11,1... | collective-permute-start | bytes 61448 | tf_op jit(solution)/shard_map/ppermute | solution.py:531
Sparse Core Ops, SparseCore 0:
  10.2 81.0 all-gather.4

commit v10 on v9

--- a/solution.py
+++ b/solution.py
@@ -20,7 +20,9 @@
 HEAD_ROWS = 40
 BLOCK_ROWS = 4 * HEAD_ROWS
 OUT_ROWS = 48
-TAP_ROWS = 5 * HEAD_ROWS + 8
+TAP_ROWS = 192
+HALF = HEAD_ROWS // 2
+SHARD_ROWS = 544
 SHARDS = 16
 TILE = 56
 STRIP = 64
@@ -31,17 +33,21 @@
 TOP, BOTTOM, LEFT, RIGHT = 200, 232, 248, 288
 
 
-def pack(outproj, expand, shrink, to_coarse):
-    width = expand.shape[-1]
-    taps = jnp.pad(to_coarse, ((0, 1), (0, 1), (0, 0))).reshape(5, 2, HEAD_ROWS, -1)
-    return jnp.concatenate(
-        [
-            jnp.pad(expand, ((0, 4), (0, 0))),
-            jnp.pad(shrink.T, ((0, 4), (0, 0))),
-            jnp.pad(outproj.T, ((0, 1), (0, 0))),
-            taps.transpose(0, 2, 1, 3).reshape(-1, width),
-        ]
-    )
+def pack_kernel(outproj_ref, expand_ref, shrink_ref, taps_ref, packed_ref, rows_ref):
+    rows_ref[...] = jnp.zeros(rows_ref.shape, jnp.float32)
+    half = taps_ref.shape[2]
+    for first, piece in ((0, expand_ref), (BLOCK_ROWS, shrink_ref), (2 * BLOCK_ROWS, outproj_ref)):
+        rows_ref[first : first + piece.shape[0], :] = piece[...].astype(jnp.float32)
+    first = 2 * BLOCK_ROWS + HEAD_ROWS
+    for tap in range(8):
+        start = first + tap // 2 * HEAD_ROWS
+        lanes = slice(tap % 2 * half, (tap % 2 + 1) * half)
+        rows_ref[start : start + 39, lanes] = taps_ref[tap].astype(jnp.float32)
+    start = first + 4 * HEAD_ROWS
+    ninth = taps_ref[8].astype(jnp.float32)
+    rows_ref[start : start + HALF, :half] = ninth[:HALF]
+    rows_ref[start : start + 19, half:] = ninth[HALF:]
+    packed_ref[...] = rows_ref[...].astype(jnp.bfloat16)
 
 
 def strip_tables():
@@ -100,12 +106,13 @@
     for row in range(SIDE):
         for col in range(SIDE):
             tile[row * SIDE + col, (row + 1) * 16 + col + 1] = 1
-    sample = np.zeros((5 * 64, 512), np.float32)
+    sample = np.zeros((6 * 64, 512), np.float32)
     for cell in range(CELLS):
         row, col = divmod(cell, WIN)
         for tap in range(9):
             source = (2 * row + tap // 3) * 16 + 2 * col + tap % 3
             sample[tap // 2 * 64 + cell, tap % 2 * 256 + source] = 1
+        sample[5 * 64 + cell, 256 + source] = 1
     return tuple(jnp.asarray(t).astype(jnp.bfloat16) for t in (gather, inner, tile, sample))
 
 
@@ -180,8 +187,8 @@
 
 
 def columns_kernel(
-    above_ref, below_ref, middle_ref, columns_ref, right_ref, left_ref, to_right_ref, to_left_ref,
-    field_ref,
+    above_ref, below_ref, middle_ref, columns_ref, blocks_ref, right_ref, left_ref, column_ref,
+    to_right_ref, to_left_ref, flat_ref, field_ref,
 ):
     cells, channels = middle_ref.shape
     field_ref[...] = jnp.zeros(field_ref.shape, jnp.float32)
@@ -189,11 +196,23 @@
     field_ref[TOP : TOP + 2 * SIDE, :] = above_ref[: 2 * SIDE, :].astype(jnp.float32)
     field_ref[BOTTOM : BOTTOM + SIDE, :] = below_ref[:SIDE, :].astype(jnp.float32)
     field = field_ref[...].astype(jnp.bfloat16)
+    width = columns_ref.shape[1]
+    channel = lax.broadcasted_iota(jnp.int32, (HEAD_ROWS, SHARDS * OUT_ROWS), 0)
+    lane = lax.broadcasted_iota(jnp.int32, (HEAD_ROWS, SHARDS * OUT_ROWS), 1)
+    flat = jnp.zeros(flat_ref.shape, jnp.float32)
+    for head in range(SHARDS):
+        move = jnp.where(lane == channel + head * OUT_ROWS, 1.0, 0.0).astype(jnp.bfloat16)
+        flat += nn(blocks_ref[head], move)
+    flat = flat.astype(jnp.bfloat16)
+    flat_ref[...] = flat
+    edges = nn(column_ref[...], flat).astype(jnp.bfloat16)
     for index, (target, table) in enumerate(((to_right_ref, right_ref), (to_left_ref, left_ref))):
         target[...] = jnp.zeros(target.shape, jnp.bfloat16)
         count = table.shape[0]
+        rows = slice(16 * index, 16 * index + 16)
         target[:count, :channels] = nn(table[...], field).astype(jnp.bfloat16)
-        target[48:, :] = columns_ref[16 * index : 16 * index + 16, :]
+        target[48:64, :width] = columns_ref[rows, :]
+        target[64:, :] = edges[rows]
 
 
 def strip_kernel(
@@ -252,26 +271,6 @@
     columns_ref[...] = nn(column_ref[...], own).astype(jnp.bfloat16)
 
 
-def edge_columns_kernel(blocks_ref, column_ref, right_ref, left_ref):
-    for head in range(SHARDS):
-        columns = nn(column_ref[...], blocks_ref[head]).astype(jnp.bfloat16)
-        right_ref[head] = columns[:16]
-        left_ref[head] = columns[16:]
-
-
-def attended_kernel(blocks_ref, left_ref, right_ref, flat_ref, parts_ref):
-    parts_ref[:, :STRIP, :] = blocks_ref[...]
-    parts_ref[:, STRIP : STRIP + 16, :] = left_ref[...]
-    parts_ref[:, STRIP + 16 :, :] = right_ref[...]
-    channel = lax.broadcasted_iota(jnp.int32, (HEAD_ROWS, SHARDS * OUT_ROWS), 0)
-    lane = lax.broadcasted_iota(jnp.int32, (HEAD_ROWS, SHARDS * OUT_ROWS), 1)
-    flat = jnp.zeros(flat_ref.shape, jnp.float32)
-    for head in range(SHARDS):
-        move = jnp.where(lane == channel + head * OUT_ROWS, 1.0, 0.0).astype(jnp.bfloat16)
-        flat += nn(parts_ref[head], move)
-    flat_ref[...] = flat.astype(jnp.bfloat16)
-
-
 def field_kernel(
     edge_ref,
     above_ref,
@@ -385,8 +384,8 @@
 
 def coarse_kernel(edge_ref, gathered_ref, *refs):
     count = 6
-    direct, operands = refs[:4], refs[4 : 4 + count]
-    outputs, landed = refs[4 + count : 6 + count], refs[-count - 1 : -1]
+    direct, operands = refs[:6], refs[6 : 6 + count]
+    outputs, landed = refs[6 + count : 8 + count], refs[-count - 1 : -1]
     small = [
         pltpu.make_async_copy(source, target, refs[-1].at[index])
         for index, (source, target) in enumerate(zip(operands, landed))
@@ -394,7 +393,7 @@
     for copy in small:
         copy.start()
     coarse_body(
-        edge_ref, gathered_ref, small, *direct, *landed, *outputs, *refs[6 + count : -count - 1]
+        edge_ref, gathered_ref, small, *direct, *landed, *outputs, *refs[8 + count : -count - 1]
     )
 
 
@@ -402,8 +401,10 @@
     edge_ref,
     gathered_ref,
     small,
-    attended_ref,
+    flat_ref,
     own_ref,
+    left_ref,
+    right_ref,
     samples_ref,
     fine_ref,
     depth_ref,
@@ -421,6 +422,7 @@
     hidden_ref,
     conv_ref,
     down_ref,
+    mixed_ref,
     sems,
 ):
     spans = (
@@ -429,12 +431,13 @@
         (shrink_ref, BLOCK_ROWS, BLOCK_ROWS),
         (taps_ref, 2 * BLOCK_ROWS + 32, TAP_ROWS),
     )
+    order = (0, 1, 3, 2)
     copies = [
         pltpu.make_async_copy(gathered_ref.at[:, pl.ds(first, count)], target, sems.at[part])
         for part, (target, first, count) in enumerate(spans)
     ]
-    for copy in copies:
-        copy.start()
+    for part in order:
+        copies[part].start()
     for copy in small:
         copy.wait()
     width = own_ref.shape[1]
@@ -448,15 +451,40 @@
     )
     inside = jnp.where(outside, 0.0, 1.0)[:, :1]
     conv_ref[8 * WIN :, :] = jnp.zeros((8, conv_ref.shape[1]), jnp.float32)
-    mixed = own_ref[...].astype(jnp.float32)
+    pieces = ((slice(0, STRIP), flat_ref[...], own_ref[...]),) + tuple(
+        (slice(first, first + 16), side[64:80, :], side[48:64, :width])
+        for first, side in ((STRIP, left_ref), (STRIP + 16, right_ref))
+    )
     copies[0].wait()
-    mixed += nn(attended_ref[...], out_ref[...].reshape(SHARDS * OUT_ROWS, width))
+    out = out_ref[...].reshape(SHARDS * OUT_ROWS, width)
+    for rows, attended, image in pieces:
+        mixed_ref[rows, :] = image.astype(jnp.float32) + nn(attended, out)
+    mixed = mixed_ref[...]
     middle = nn(square_ref[...], mixed.astype(jnp.bfloat16)).astype(jnp.bfloat16)
     normed_mid = norm_rows(middle.astype(jnp.float32))
     copies[1].wait()
     chunk = 512
     expand = expand_ref[...].reshape(SHARDS * BLOCK_ROWS, width)
+
+    def downsample(shard):
+        samples = samples_ref[...]
+        four = nt(taps_ref[shard], samples[: 4 * 64])
+        ninth = nt(taps_ref[shard][4 * HEAD_ROWS :], samples[4 * 64 :])
+        total = four[8 : 8 + HEAD_ROWS, :64]
+        for block in range(1, 4):
+            rows = slice(8 + block * HEAD_ROWS, 8 + (block + 1) * HEAD_ROWS)
+            total += four[rows, block * 64 : (block + 1) * 64]
+        first = shard * 39
+        down_ref[first : first + HEAD_ROWS, :64] = total
+        down_ref[first : first + HALF, :64] += ninth[8 : 8 + HALF, :64]
+        down_ref[first + HALF : first + HEAD_ROWS, :64] += ninth[8 : 8 + HALF, 64:]
+
+    shares = {2: range(0, 6), 3: range(6, 11), 4: range(11, SHARDS)}
     for first in range(0, SHARDS * BLOCK_ROWS, chunk):
+        if first == 2 * chunk:
+            copies[3].wait()
+        for shard in shares.get(first // chunk, ()):
+            downsample(shard)
         span = pl.ds(first, chunk)
         hidden = gelu(nt(normed_mid, expand[first : first + chunk])) * inside
         hidden_ref[:, span] = hidden.astype(jnp.bfloat16).astype(jnp.float32)
@@ -476,28 +504,18 @@
     fine_out_ref[...] = jnp.maximum(
         fine_ref[...].astype(jnp.float32) + upsampled, 0.0
     ).astype(jnp.bfloat16)
-    copies[3].wait()
-    samples = samples_ref[...]
-    for shard in range(SHARDS):
-        four = nt(taps_ref[shard], samples[: 4 * 64])
-        fifth = nt(taps_ref[shard][4 * HEAD_ROWS :], samples[4 * 64 :])
-        total = fifth[8:]
-        for block in range(4):
-            rows = slice(8 + block * HEAD_ROWS, 8 + (block + 1) * HEAD_ROWS)
-            total += four[rows, block * 64 : (block + 1) * 64]
-        down_ref[shard * 39 : shard * 39 + HEAD_ROWS, :64] = total
     downsampled = down_ref[...].T[:CELLS, :width].astype(jnp.bfloat16).astype(jnp.float32)
     coarse_out_ref[...] = jnp.maximum(
         nn(compact_ref[...], result) + downsampled, 0.0
     ).astype(jnp.bfloat16)
 
 
-def coarse_stream(gathered, edges, attended, own, depth, samples, fine_res, to_fine):
+def coarse_stream(gathered, edges, flat, own, left, right, depth, samples, fine_res, to_fine):
     width = own.shape[1]
     fine_cells, fine_ch = fine_res.shape
     fixed = (gathered, depth, to_fine, *cell_tables())
     gathered, *fixed = (pltpu.with_memory_space_constraint(array, pltpu.HBM) for array in fixed)
-    operands = (attended, own, samples, fine_res, *fixed)
+    operands = (flat, own, left, right, samples, fine_res, *fixed)
     smem, vmem, hbm = (
         pl.BlockSpec(memory_space=space) for space in (pltpu.SMEM, pltpu.VMEM, pltpu.HBM)
     )
@@ -507,7 +525,7 @@
             jax.ShapeDtypeStruct((fine_cells, fine_ch), jnp.bfloat16),
             jax.ShapeDtypeStruct((CELLS, width), jnp.bfloat16),
         ),
-        in_specs=[smem, hbm] + [vmem] * 4 + [hbm] * (len(operands) - 4),
+        in_specs=[smem, hbm] + [vmem] * 6 + [hbm] * (len(operands) - 6),
         out_specs=(vmem, vmem),
         scratch_shapes=[
             pltpu.VMEM((SHARDS, OUT_ROWS, width), jnp.bfloat16),
@@ -517,9 +535,10 @@
             pltpu.VMEM((QUERIES, SHARDS * BLOCK_ROWS), jnp.float32),
             pltpu.VMEM((64, SHARDS * BLOCK_ROWS), jnp.float32),
             pltpu.VMEM((SHARDS * HEAD_ROWS, 128), jnp.float32),
+            pltpu.VMEM((QUERIES, width), jnp.float32),
             pltpu.SemaphoreType.DMA((4,)),
-            *(pltpu.VMEM(operand.shape, operand.dtype) for operand in operands[4:]),
-            pltpu.SemaphoreType.DMA((len(operands) - 4,)),
+            *(pltpu.VMEM(operand.shape, operand.dtype) for operand in operands[6:]),
+            pltpu.SemaphoreType.DMA((len(operands) - 6,)),
         ],
         compiler_params=pltpu.CompilerParams(vmem_limit_bytes=40 * 1024 * 1024),
     )(edges, gathered, *operands)
@@ -549,7 +568,15 @@
 ):
     fine_ch, fine_cells = fine_in.shape[2:]
     coarse_ch, coarse_cells = coarse_in.shape[2:]
-    gathered = lax.all_gather(pack(outproj_coarse, expand_coarse, shrink_coarse, to_coarse), "rows")
+    packed = (SHARD_ROWS, coarse_ch)
+    (mine,) = call(
+        pack_kernel,
+        (packed,),
+        (outproj_coarse.T, expand_coarse, shrink_coarse.T, to_coarse),
+        ((packed, jnp.float32),),
+        fetch=(0, 1, 2, 3),
+    )
+    gathered = lax.all_gather(mine, "rows")
     strip = lax.all_gather(coarse_in.reshape(coarse_ch, coarse_cells).T, "rows")
     fine = fine_in.reshape(fine_ch, fine_cells).T
     place = (lax.axis_index("rows"), lax.axis_index("cols"))
@@ -585,20 +612,19 @@
         fetch=(3, 4, 5),
     )
     blocks = lax.all_to_all(blocks, "rows", 0, 0, tiled=True)
-    going_right, going_left = call(
+    message = (80, SHARDS * OUT_ROWS)
+    going_right, going_left, flat = call(
         columns_kernel,
-        ((64, coarse_ch), (64, coarse_ch)),
-        (above, below, middle, columns, *border_tables()),
+        (message, message, (STRIP, SHARDS * OUT_ROWS)),
+        (above, below, middle, columns, blocks, *border_tables(), column),
         (((248, fine_ch), jnp.float32),),
-        fetch=(4, 5),
+        fetch=(5, 6, 7),
     )
     left, right = exchange(going_right, going_left, "cols")
-    edge = (SHARDS, 16, HEAD_ROWS)
-    near = exchange(*call(edge_columns_kernel, (edge, edge), (blocks, column), (), fetch=(1,)), "cols")
     hidden_count = expand_fine.shape[0]
     fine_res, samples = call(
         field_kernel,
-        (fine.shape, (5 * 64, 2 * fine_ch)),
+        (fine.shape, (6 * 64, 2 * fine_ch)),
         (
             edges,
             above,
@@ -620,18 +646,14 @@
         scalars=1,
         fetch=tuple(range(6, 13)),
     )
-    (attended,) = call(
-        attended_kernel,
-        ((QUERIES, SHARDS * OUT_ROWS),),
-        (blocks, *near),
-        (((SHARDS, QUERIES, HEAD_ROWS), jnp.bfloat16),),
-    )
     depth = jnp.pad(depth_coarse.reshape(9, SHARDS, -1), ((0, 0), (0, 0), (0, 4)))
     fine_out, coarse_out = coarse_stream(
         gathered,
         edges,
-        attended,
-        jnp.concatenate([own, left[48:], right[48:]]),
+        flat,
+        own,
+        left,
+        right,
         depth.reshape(9, -1),
         samples,
         fine_res,

time: 113 us -> 110 us (0.973)
  the two profiles are of different devices: /device:TPU:33 before, /device:TPU:1 now
where the time goes in v10:
time: 110 us
  Pallas kernels  32.4 us (29%)
  blocking collectives  30.2 us (27%)
  waiting for transfers between devices  15.8 us (14%)
  between operations  14.2 us (13%)
  starting transfers between devices  13.9 us (13%)
  local copies, waits for them, and re-layouts  3.22 us (3%)
    all_gather x1, blocking collectives, local(): strip = lax.all_gather(coarse_in.reshape(coarse_ch, coarse_cells).T, 'rows')  30.2 us
    pallas_call x5, Pallas kernels, call(): pl.pallas_call(fetching, out_shape=tuple((jax.ShapeDtypeStruct(shape, jnp...  20.4 us
    pallas_call x1, Pallas kernels, coarse_stream(): pl.pallas_call(coarse_kernel, out_shape=(jax.ShapeDtypeStruct((fine_cells...  12 us
    ppermute x4, starting transfers between devices, exchange(): return (lax.ppermute(onward, axis, up), lax.ppermute(back, axis, down))  10.5 us
    all_gather x1, waiting for transfers between devices, local(): gathered = lax.all_gather(mine, 'rows')  9.79 us
    ppermute x4, waiting for transfers between devices, exchange(): return (lax.ppermute(onward, axis, up), lax.ppermute(back, axis, down))  5.96 us
    all_to_all x1, starting transfers between devices, local(): blocks = lax.all_to_all(blocks, 'rows', 0, 0, tiled=True)  3.45 us
  transfers between devices with their start and end apart: 6, of which 3 were waited for; matrix products, arithmetic and copies ran while one was open for 3% of the time, Pallas kernels for 17%

profile of v10, /device:TPU:1, one launch (start us, length us, event | category | flops | bytes accessed | tf_op | source)
XLA Modules:
  0.0 109.8 jit_solution(3506535419096275343)
XLA Ops:
  7.2 0.0 all-gather.5.cloned.1.call-start
  7.2 2.2 %shard_map.266 = bf16[544,624]{1,0:T(8,128)(2,1)} custom-call(bf16[39,624]{1,0:T(8,128)(2,1)} %bitcast.32, bf16[156,624]{1,0:T(8,128)(2,1)} %refs_1_.2, bf16[156,624]{1,0:T(8,128)(2,1)} %bitcast.29, bf16[9,39,312]{2,1,0:T(8,128)(2,1)} %refs_3_.3), custom_call_target="tpu_custom_call" | custom-call | tf_op jit(solution)/shard_map/pallas_call | solution.py:373
  9.5 0.0 all-gather.5.cloned.1.call-update
  9.5 0.1 add_convert_fusion.refs_0_.edge_ref
  9.6 30.2 %all-gather.2.refs_2_ = bf16[16,49,624]{2,1,0:T(8,128)(2,1)S(1)} all-gather(bf16[1,49,624]{2,1,0:T(8,128)(2,1)} %bitcast.31), channel_id=3, replica_groups=mesh['rows'=16,'cols'=32] {'rows'}, dimensions={0}, use_global_device_ids=true | all-gather | bytes 1039584 | tf_op jit(solution)/shard_map/all_gather | solution.py:580
  39.8 4.1 %shard_map.268 = (bf16[16,64,40]{2,1,0:T(8,128)(2,1)S(1)}, bf16[64,624]{1,0:T(8,128)(2,1)S(1)}, bf16[32,624]{1,0:T(8,128)(2,1)S(1)}) custom-call(s32[4]{0:T(128)S(1)} %add_convert_fusion.refs_0_.edge_ref, s32[1]{0:T(128)} %bitcast.9.refs_1_, bf16[16,49,624]{2,1,0:T(8,128)(2,1)S(1)} %all-gather.2.refs_2_, bf16[3,39,624]{2,1,0:T(8,128)(2,1)} %refs_3_.4, ...), custom_call_target="tpu_custom_call" | custom-call | tf_op jit(solution)/shard_map/pallas_call | solution.py:373
  43.9 0.2 copy.29
  44.0 0.8 reshape.37
  44.8 3.5 %all-to-all-start = ((bf16[16,2,1280]{2,1,0:T(2,128)(2,1)}), bf16[16,2,1280]{2,1,0:T(2,128)(2,1)S(1)}, u32[]{:S(2)}, u32[]{:S(2)}) async-start(bf16[16,2,1280]{2,1,0:T(2,128)(2,1)} %reshape.37), calls=%async_computation | async-start | bytes 163840 | tf_op jit(solution)/shard_map/all_to_all | solution.py:614
  48.3 5.4 %shard_map.267 = (bf16[196,312]{1,0:T(8,128)(2,1)S(1)}, bf16[32,312]{1,0:T(8,128)(2,1)S(1)}, bf16[16,312]{1,0:T(8,128)(2,1)S(1)}) custom-call(bf16[196,312]{1,0:T(8,128)(2,1)} %bitcast.30, bf16[3,312,312]{2,1,0:T(8,128)(2,1)} %refs_1_.3, bf16[312,312]{1,0:T(8,128)(2,1)} %refs_2_.1, f32[196,196]{1,0:T(8,128)} %constant.43.clone.refs_3_), custom_call_target="tpu_custom_call" | custom-call | tf_op jit(solution)/shard_map/pallas_call | solution.py:373
  53.7 3.5 %collective-permute-start = (bf16[32,312]{1,0:T(8,128)(2,1)S(1)}, bf16[32,312]{1,0:T(8,128)(2,1)S(1)}, u32[]{:S(2)}, u32[]{:S(2)}) collective-permute-start(bf16[32,312]{1,0:T(8,128)(2,1)S(1)} %get-tuple-element.15), channel_id=1, source_target_pairs={{0,32},{32,64},{64,96},{96,128},{128,160},{160,192},{192,224},{224... | collective-permute-start | bytes 59912 | tf_op jit(solution)/shard_map/ppermute | solution.py:550
  57.2 1.9 %collective-permute-start.1 = (bf16[16,312]{1,0:T(8,128)(2,1)S(1)}, bf16[16,312]{1,0:T(8,128)(2,1)S(1)}, u32[]{:S(2)}, u32[]{:S(2)}) collective-permute-start(bf16[16,312]{1,0:T(8,128)(2,1)S(1)} %get-tuple-element.16), channel_id=1, source_target_pairs={{32,0},{64,32},{96,64},{128,96},{160,128},{192,160},{224,192},{256... | collective-permute-start | bytes 29960 | tf_op jit(solution)/shard_map/ppermute | solution.py:550
  59.2 0.0 all-to-all-done
  59.2 0.2 reshape.38
  59.3 0.2 copy.30.refs_4_
  59.5 3.4 %collective-permute-done.1.refs_1_.refs_2_ = bf16[16,312]{1,0:T(8,128)(2,1)S(1)} collective-permute-done((bf16[16,312]{1,0:T(8,128)(2,1)S(1)}, bf16[16,312]{1,0:T(8,128)(2,1)S(1)}, u32[]{:S(2)}, u32[]{:S(2)}) %collective-permute-start.1) | collective-permute-done | bytes 10016 | tf_op jit(solution)/shard_map/ppermute | solution.py:550
  62.9 0.0 collective-permute-done.refs_0_.refs_1_
  62.9 1.3 %shard_map.269 = (bf16[80,768]{1,0:T(8,128)(2,1)S(1)}, bf16[80,768]{1,0:T(8,128)(2,1)S(1)}, bf16[64,768]{1,0:T(8,128)(2,1)S(1)}) custom-call(bf16[32,312]{1,0:T(8,128)(2,1)S(1)} %collective-permute-done.refs_0_.refs_1_, bf16[16,312]{1,0:T(8,128)(2,1)S(1)} %collective-permute-done.1.refs_1_.refs_2_, bf16[196,312]{1,0:T(8,128)(2,1)S(1)} %get-tuple-element.17.refs_2_.refs_5_, ...), custom_call_target="tpu_custom_call" | custom-call | tf_op jit(solution)/shard_map/pallas_call | solution.py:373
  64.2 3.6 %collective-permute-start.2 = (bf16[80,768]{1,0:T(8,128)(2,1)S(1)}, bf16[80,768]{1,0:T(8,128)(2,1)S(1)}, u32[]{:S(2)}, u32[]{:S(2)}) collective-permute-start(bf16[80,768]{1,0:T(8,128)(2,1)S(1)} %get-tuple-element.22), channel_id=1, source_target_pairs={{0,1},{1,2},{2,3},{3,4},{4,5},{5,6},{6,7},{7,8},{8,9},{9,10},{10,1... | collective-permute-start | bytes 368648 | tf_op jit(solution)/shard_map/ppermute | solution.py:550
  67.8 1.5 %collective-permute-start.3 = (bf16[80,768]{1,0:T(8,128)(2,1)S(1)}, bf16[80,768]{1,0:T(8,128)(2,1)S(1)}, u32[]{:S(2)}, u32[]{:S(2)}) collective-permute-start(bf16[80,768]{1,0:T(8,128)(2,1)S(1)} %get-tuple-element.23), channel_id=1, source_target_pairs={{1,0},{2,1},{3,2},{4,3},{5,4},{6,5},{7,6},{8,7},{9,8},{10,9},{11,1... | collective-permute-start | bytes 368648 | tf_op jit(solution)/shard_map/ppermute | solution.py:550
  69.3 1.1 %reshape.28 = f32[9,16,156]{2,1,0:T(8,128)S(1)} reshape(f32[9,2496]{1,0:T(8,128)} %param.37) | data formatting | bytes 179712 | tf_op jit(solution)/shard_map/reshape | solution.py:649
  70.4 0.8 reshape.29.refs_6_
  71.2 0.0 collective-permute-done.2.refs_3_.refs_2_
  71.2 2.6 %collective-permute-done.3.refs_4_.refs_3_ = bf16[80,768]{1,0:T(8,128)(2,1)S(1)} collective-permute-done((bf16[80,768]{1,0:T(8,128)(2,1)S(1)}, bf16[80,768]{1,0:T(8,128)(2,1)S(1)}, u32[]{:S(2)}, u32[]{:S(2)}) %collective-permute-start.3) | collective-permute-done | bytes 122912 | tf_op jit(solution)/shard_map/ppermute | solution.py:550
  73.8 7.3 %shard_map.270 = (bf16[196,312]{1,0:T(8,128)(2,1)S(1)}, bf16[384,624]{1,0:T(8,128)(2,1)S(1)}) custom-call(s32[4]{0:T(128)S(1)} %add_convert_fusion.refs_0_.edge_ref, bf16[32,312]{1,0:T(8,128)(2,1)S(1)} %collective-permute-done.refs_0_.refs_1_, bf16[16,312]{1,0:T(8,128)(2,1)S(1)} %collective-permute-done.1.refs_1_.refs_2_, ...), custom_call_target="tpu_custom_call" | custom-call | tf_op jit(solution)/shard_map/pallas_call | solution.py:373
  81.1 9.8 %all-gather.5.cloned.1.call-done = bf16[8704,624]{1,0:T(8,128)(2,1)} async-done(((bf16[544,624]{1,0:T(8,128)(2,1)}), bf16[8704,624]{1,0:T(8,128)(2,1)}) %all-gather.5.cloned.1.call-update) | async-done | bytes 10862608 | tf_op jit(solution)/shard_map/all_gather | solution.py:579
  90.9 12.0 %shard_map.271 = (bf16[196,312]{1,0:T(8,128)(2,1)}, bf16[49,624]{1,0:T(8,128)(2,1)}) custom-call(s32[4]{0:T(128)S(1)} %add_convert_fusion.refs_0_.edge_ref, bf16[16,544,624]{2,1,0:T(8,128)(2,1)} %bitcast.25, bf16[64,768]{1,0:T(8,128)(2,1)S(1)} %get-tuple-element.20.refs_0_, bf16[64,624]{1,0:T(8,128)(2,1)S(1)} %get-tuple-element.21.refs_1_, ...), custom_call_target="tpu_custom_call" | custom-call | tf_op jit(solution)/shard_map/pallas_call | solution.py:522
  (1 shorter events, 0.0 us)
Async XLA Ops:
  7.2 83.7 %all-gather.5.cloned.1.call-start = ((), (), s32[]{:S(2)}) async-start(), calls=%async_computation.1 | async-start | bytes 11837440 | tf_op jit(solution)/shard_map/all_gather | solution.py:579
  44.8 14.3 %all-to-all-start = ((bf16[16,2,1280]{2,1,0:T(2,128)(2,1)}), bf16[16,2,1280]{2,1,0:T(2,128)(2,1)S(1)}, u32[]{:S(2)}, u32[]{:S(2)}) async-start(bf16[16,2,1280]{2,1,0:T(2,128)(2,1)} %reshape.37), calls=%async_computation | async-start | bytes 163840 | tf_op jit(solution)/shard_map/all_to_all | solution.py:614
  53.7 9.2 %collective-permute-start = (bf16[32,312]{1,0:T(8,128)(2,1)S(1)}, bf16[32,312]{1,0:T(8,128)(2,1)S(1)}, u32[]{:S(2)}, u32[]{:S(2)}) collective-permute-start(bf16[32,312]{1,0:T(8,128)(2,1)S(1)} %get-tuple-element.15), channel_id=1, source_target_pairs={{0,32},{32,64},{64,96},{96,128},{128,160},{160,192},{192,224},{224... | collective-permute-start | bytes 59912 | tf_op jit(solution)/shard_map/ppermute | solution.py:550
  57.2 5.6 %collective-permute-start.1 = (bf16[16,312]{1,0:T(8,128)(2,1)S(1)}, bf16[16,312]{1,0:T(8,128)(2,1)S(1)}, u32[]{:S(2)}, u32[]{:S(2)}) collective-permute-start(bf16[16,312]{1,0:T(8,128)(2,1)S(1)} %get-tuple-element.16), channel_id=1, source_target_pairs={{32,0},{64,32},{96,64},{128,96},{160,128},{192,160},{224,192},{256... | collective-permute-start | bytes 29960 | tf_op jit(solution)/shard_map/ppermute | solution.py:550
  64.2 7.0 %collective-permute-start.2 = (bf16[80,768]{1,0:T(8,128)(2,1)S(1)}, bf16[80,768]{1,0:T(8,128)(2,1)S(1)}, u32[]{:S(2)}, u32[]{:S(2)}) collective-permute-start(bf16[80,768]{1,0:T(8,128)(2,1)S(1)} %get-tuple-element.22), channel_id=1, source_target_pairs={{0,1},{1,2},{2,3},{3,4},{4,5},{5,6},{6,7},{7,8},{8,9},{9,10},{10,1... | collective-permute-start | bytes 368648 | tf_op jit(solution)/shard_map/ppermute | solution.py:550
  67.8 6.0 %collective-permute-start.3 = (bf16[80,768]{1,0:T(8,128)(2,1)S(1)}, bf16[80,768]{1,0:T(8,128)(2,1)S(1)}, u32[]{:S(2)}, u32[]{:S(2)}) collective-permute-start(bf16[80,768]{1,0:T(8,128)(2,1)S(1)} %get-tuple-element.23), channel_id=1, source_target_pairs={{1,0},{2,1},{3,2},{4,3},{5,4},{6,5},{7,6},{8,7},{9,8},{10,9},{11,1... | collective-permute-start | bytes 368648 | tf_op jit(solution)/shard_map/ppermute | solution.py:550
Sparse Core Ops, SparseCore 0:
  10.1 80.7 all-gather.4

commit v11 on v10

--- a/solution.py
+++ b/solution.py
@@ -24,6 +24,8 @@
 HALF = HEAD_ROWS // 2
 SHARD_ROWS = 544
 SHARDS = 16
+GROUPS = 4
+PER_GROUP = SHARDS // GROUPS
 TILE = 56
 STRIP = 64
 QUERIES = 96
@@ -426,18 +428,29 @@
     sems,
 ):
     spans = (
-        (out_ref, 2 * BLOCK_ROWS, OUT_ROWS),
         (expand_ref, 0, BLOCK_ROWS),
         (shrink_ref, BLOCK_ROWS, BLOCK_ROWS),
         (taps_ref, 2 * BLOCK_ROWS + 32, TAP_ROWS),
     )
-    order = (0, 1, 3, 2)
-    copies = [
-        pltpu.make_async_copy(gathered_ref.at[:, pl.ds(first, count)], target, sems.at[part])
-        for part, (target, first, count) in enumerate(spans)
-    ]
-    for part in order:
-        copies[part].start()
+    out_copy = pltpu.make_async_copy(
+        gathered_ref.at[:, pl.ds(2 * BLOCK_ROWS, OUT_ROWS)], out_ref, sems.at[3, 0]
+    )
+    out_copy.start()
+    copies = []
+    for group in range(GROUPS):
+        shards = pl.ds(group * PER_GROUP, PER_GROUP)
+        copies.append(
+            [
+                pltpu.make_async_copy(
+                    gathered_ref.at[shards, pl.ds(first, count)],
+                    target.at[shards],
+                    sems.at[part, group],
+                )
+                for part, (target, first, count) in enumerate(spans)
+            ]
+        )
+        for copy in copies[-1]:
+            copy.start()
     for copy in small:
         copy.wait()
     width = own_ref.shape[1]
@@ -455,16 +468,17 @@
         (slice(first, first + 16), side[64:80, :], side[48:64, :width])
         for first, side in ((STRIP, left_ref), (STRIP + 16, right_ref))
     )
-    copies[0].wait()
+    out_copy.wait()
     out = out_ref[...].reshape(SHARDS * OUT_ROWS, width)
     for rows, attended, image in pieces:
         mixed_ref[rows, :] = image.astype(jnp.float32) + nn(attended, out)
     mixed = mixed_ref[...]
     middle = nn(square_ref[...], mixed.astype(jnp.bfloat16)).astype(jnp.bfloat16)
     normed_mid = norm_rows(middle.astype(jnp.float32))
-    copies[1].wait()
-    chunk = 512
-    expand = expand_ref[...].reshape(SHARDS * BLOCK_ROWS, width)
+    chunk = PER_GROUP * BLOCK_ROWS
+
+    def group_of(ref, group):
+        return ref[group * PER_GROUP : (group + 1) * PER_GROUP].reshape(chunk, width)
 
     def downsample(shard):
         samples = samples_ref[...]
@@ -479,15 +493,18 @@
         down_ref[first : first + HALF, :64] += ninth[8 : 8 + HALF, :64]
         down_ref[first + HALF : first + HEAD_ROWS, :64] += ninth[8 : 8 + HALF, 64:]
 
-    shares = {2: range(0, 6), 3: range(6, 11), 4: range(11, SHARDS)}
-    for first in range(0, SHARDS * BLOCK_ROWS, chunk):
-        if first == 2 * chunk:
-            copies[3].wait()
-        for shard in shares.get(first // chunk, ()):
-            downsample(shard)
-        span = pl.ds(first, chunk)
-        hidden = gelu(nt(normed_mid, expand[first : first + chunk])) * inside
-        hidden_ref[:, span] = hidden.astype(jnp.bfloat16).astype(jnp.float32)
+    copies[0][0].wait()
+    ahead = nt(normed_mid, group_of(expand_ref, 0))
+    update = jnp.zeros((64, width), jnp.float32)
+    for group in range(GROUPS):
+        raw = ahead
+        copies[group][1].wait()
+        copies[group][2].wait()
+        if group + 1 < GROUPS:
+            copies[group + 1][0].wait()
+            ahead = nt(normed_mid, group_of(expand_ref, group + 1))
+        span = pl.ds(group * chunk, chunk)
+        hidden_ref[:, span] = (gelu(raw) * inside).astype(jnp.bfloat16).astype(jnp.float32)
         for row in range(WIN):
             total = jnp.zeros((8, chunk), jnp.float32)
             for tap in range(9):
@@ -495,9 +512,9 @@
                 window = hidden_ref[pl.ds((row + down) * RING + side, 8), span]
                 total += depth_ref[tap : tap + 1, span] * window
             conv_ref[row * 8 : row * 8 + 8, span] = gelu(total)
-    copies[2].wait()
-    shrink = shrink_ref[...].reshape(SHARDS * BLOCK_ROWS, width)
-    update = nn(conv_ref[...].astype(jnp.bfloat16), shrink)
+        for shard in range(group * PER_GROUP, (group + 1) * PER_GROUP):
+            downsample(shard)
+        update += nn(conv_ref[:, span].astype(jnp.bfloat16), group_of(shrink_ref, group))
     result = (nn(centre_ref[...], middle) + update).astype(jnp.bfloat16)
     spread = nn(repeat_ref[...], result).astype(jnp.bfloat16)
     upsampled = nt(spread, to_fine_ref[...])
@@ -536,7 +553,7 @@
             pltpu.VMEM((64, SHARDS * BLOCK_ROWS), jnp.float32),
             pltpu.VMEM((SHARDS * HEAD_ROWS, 128), jnp.float32),
             pltpu.VMEM((QUERIES, width), jnp.float32),
-            pltpu.SemaphoreType.DMA((4,)),
+            pltpu.SemaphoreType.DMA((4, GROUPS)),
             *(pltpu.VMEM(operand.shape, operand.dtype) for operand in operands[6:]),
             pltpu.SemaphoreType.DMA((len(operands) - 6,)),
         ],

time: 110 us -> 111 us (level)
  transfers between devices with their start and end apart: 6 -> 6, of which waited for: 3 -> 3; matrix products, arithmetic and copies ran while one was open for 3% -> 3% of each run, Pallas kernels for 17% -> 16%
where the time goes in v11:
time: 111 us
  Pallas kernels  33.2 us (30%)
  blocking collectives  30.2 us (27%)
  waiting for transfers between devices  15.8 us (14%)
  between operations  14.2 us (13%)
  starting transfers between devices  13.9 us (13%)
  local copies, waits for them, and re-layouts  3.22 us (3%)
    all_gather x1, blocking collectives, local(): strip = lax.all_gather(coarse_in.reshape(coarse_ch, coarse_cells).T, 'rows')  30.2 us
    pallas_call x5, Pallas kernels, call(): pl.pallas_call(fetching, out_shape=tuple((jax.ShapeDtypeStruct(shape, jnp...  20.4 us
    pallas_call x1, Pallas kernels, coarse_stream(): pl.pallas_call(coarse_kernel, out_shape=(jax.ShapeDtypeStruct((fine_cells...  12.9 us
    ppermute x4, starting transfers between devices, exchange(): return (lax.ppermute(onward, axis, up), lax.ppermute(back, axis, down))  10.5 us
    all_gather x1, waiting for transfers between devices, local(): gathered = lax.all_gather(mine, 'rows')  9.79 us
    ppermute x4, waiting for transfers between devices, exchange(): return (lax.ppermute(onward, axis, up), lax.ppermute(back, axis, down))  5.96 us
    all_to_all x1, starting transfers between devices, local(): blocks = lax.all_to_all(blocks, 'rows', 0, 0, tiled=True)  3.45 us
  transfers between devices with their start and end apart: 6, of which 3 were waited for; matrix products, arithmetic and copies ran while one was open for 3% of the time, Pallas kernels for 16%

profile of v11, /device:TPU:1, one launch (start us, length us, event | category | flops | bytes accessed | tf_op | source)
XLA Modules:
  0.0 110.6 jit_solution(8493039985789332875)
XLA Ops:
  7.2 0.0 all-gather.5.cloned.1.call-start
  7.2 2.2 %shard_map.266 = bf16[544,624]{1,0:T(8,128)(2,1)} custom-call(bf16[39,624]{1,0:T(8,128)(2,1)} %bitcast.32, bf16[156,624]{1,0:T(8,128)(2,1)} %refs_1_.2, bf16[156,624]{1,0:T(8,128)(2,1)} %bitcast.29, bf16[9,39,312]{2,1,0:T(8,128)(2,1)} %refs_3_.3), custom_call_target="tpu_custom_call" | custom-call | tf_op jit(solution)/shard_map/pallas_call | solution.py:375
  9.5 0.0 all-gather.5.cloned.1.call-update
  9.5 0.1 add_convert_fusion.refs_0_.edge_ref
  9.6 30.2 %all-gather.2.refs_2_ = bf16[16,49,624]{2,1,0:T(8,128)(2,1)S(1)} all-gather(bf16[1,49,624]{2,1,0:T(8,128)(2,1)} %bitcast.31), channel_id=3, replica_groups=mesh['rows'=16,'cols'=32] {'rows'}, dimensions={0}, use_global_device_ids=true | all-gather | bytes 1039584 | tf_op jit(solution)/shard_map/all_gather | solution.py:597
  39.8 4.1 %shard_map.268 = (bf16[16,64,40]{2,1,0:T(8,128)(2,1)S(1)}, bf16[64,624]{1,0:T(8,128)(2,1)S(1)}, bf16[32,624]{1,0:T(8,128)(2,1)S(1)}) custom-call(s32[4]{0:T(128)S(1)} %add_convert_fusion.refs_0_.edge_ref, s32[1]{0:T(128)} %bitcast.9.refs_1_, bf16[16,49,624]{2,1,0:T(8,128)(2,1)S(1)} %all-gather.2.refs_2_, bf16[3,39,624]{2,1,0:T(8,128)(2,1)} %refs_3_.4, ...), custom_call_target="tpu_custom_call" | custom-call | tf_op jit(solution)/shard_map/pallas_call | solution.py:375
  43.9 0.2 copy.29
  44.0 0.8 reshape.37
  44.8 3.5 %all-to-all-start = ((bf16[16,2,1280]{2,1,0:T(2,128)(2,1)}), bf16[16,2,1280]{2,1,0:T(2,128)(2,1)S(1)}, u32[]{:S(2)}, u32[]{:S(2)}) async-start(bf16[16,2,1280]{2,1,0:T(2,128)(2,1)} %reshape.37), calls=%async_computation | async-start | bytes 163840 | tf_op jit(solution)/shard_map/all_to_all | solution.py:631
  48.3 5.4 %shard_map.267 = (bf16[196,312]{1,0:T(8,128)(2,1)S(1)}, bf16[32,312]{1,0:T(8,128)(2,1)S(1)}, bf16[16,312]{1,0:T(8,128)(2,1)S(1)}) custom-call(bf16[196,312]{1,0:T(8,128)(2,1)} %bitcast.30, bf16[3,312,312]{2,1,0:T(8,128)(2,1)} %refs_1_.3, bf16[312,312]{1,0:T(8,128)(2,1)} %refs_2_.1, f32[196,196]{1,0:T(8,128)} %constant.43.clone.refs_3_), custom_call_target="tpu_custom_call" | custom-call | tf_op jit(solution)/shard_map/pallas_call | solution.py:375
  53.7 3.5 %collective-permute-start = (bf16[32,312]{1,0:T(8,128)(2,1)S(1)}, bf16[32,312]{1,0:T(8,128)(2,1)S(1)}, u32[]{:S(2)}, u32[]{:S(2)}) collective-permute-start(bf16[32,312]{1,0:T(8,128)(2,1)S(1)} %get-tuple-element.15), channel_id=1, source_target_pairs={{0,32},{32,64},{64,96},{96,128},{128,160},{160,192},{192,224},{224... | collective-permute-start | bytes 59912 | tf_op jit(solution)/shard_map/ppermute | solution.py:567
  57.2 1.9 %collective-permute-start.1 = (bf16[16,312]{1,0:T(8,128)(2,1)S(1)}, bf16[16,312]{1,0:T(8,128)(2,1)S(1)}, u32[]{:S(2)}, u32[]{:S(2)}) collective-permute-start(bf16[16,312]{1,0:T(8,128)(2,1)S(1)} %get-tuple-element.16), channel_id=1, source_target_pairs={{32,0},{64,32},{96,64},{128,96},{160,128},{192,160},{224,192},{256... | collective-permute-start | bytes 29960 | tf_op jit(solution)/shard_map/ppermute | solution.py:567
  59.2 0.0 all-to-all-done
  59.2 0.2 reshape.38
  59.3 0.2 copy.30.refs_4_
  59.5 3.4 %collective-permute-done.1.refs_1_.refs_2_ = bf16[16,312]{1,0:T(8,128)(2,1)S(1)} collective-permute-done((bf16[16,312]{1,0:T(8,128)(2,1)S(1)}, bf16[16,312]{1,0:T(8,128)(2,1)S(1)}, u32[]{:S(2)}, u32[]{:S(2)}) %collective-permute-start.1) | collective-permute-done | bytes 10016 | tf_op jit(solution)/shard_map/ppermute | solution.py:567
  62.9 0.0 collective-permute-done.refs_0_.refs_1_
  62.9 1.3 %shard_map.269 = (bf16[80,768]{1,0:T(8,128)(2,1)S(1)}, bf16[80,768]{1,0:T(8,128)(2,1)S(1)}, bf16[64,768]{1,0:T(8,128)(2,1)S(1)}) custom-call(bf16[32,312]{1,0:T(8,128)(2,1)S(1)} %collective-permute-done.refs_0_.refs_1_, bf16[16,312]{1,0:T(8,128)(2,1)S(1)} %collective-permute-done.1.refs_1_.refs_2_, bf16[196,312]{1,0:T(8,128)(2,1)S(1)} %get-tuple-element.17.refs_2_.refs_5_, ...), custom_call_target="tpu_custom_call" | custom-call | tf_op jit(solution)/shard_map/pallas_call | solution.py:375
  64.2 3.6 %collective-permute-start.2 = (bf16[80,768]{1,0:T(8,128)(2,1)S(1)}, bf16[80,768]{1,0:T(8,128)(2,1)S(1)}, u32[]{:S(2)}, u32[]{:S(2)}) collective-permute-start(bf16[80,768]{1,0:T(8,128)(2,1)S(1)} %get-tuple-element.22), channel_id=1, source_target_pairs={{0,1},{1,2},{2,3},{3,4},{4,5},{5,6},{6,7},{7,8},{8,9},{9,10},{10,1... | collective-permute-start | bytes 368648 | tf_op jit(solution)/shard_map/ppermute | solution.py:567
  67.8 1.5 %collective-permute-start.3 = (bf16[80,768]{1,0:T(8,128)(2,1)S(1)}, bf16[80,768]{1,0:T(8,128)(2,1)S(1)}, u32[]{:S(2)}, u32[]{:S(2)}) collective-permute-start(bf16[80,768]{1,0:T(8,128)(2,1)S(1)} %get-tuple-element.23), channel_id=1, source_target_pairs={{1,0},{2,1},{3,2},{4,3},{5,4},{6,5},{7,6},{8,7},{9,8},{10,9},{11,1... | collective-permute-start | bytes 368648 | tf_op jit(solution)/shard_map/ppermute | solution.py:567
  69.3 1.1 %reshape.28 = f32[9,16,156]{2,1,0:T(8,128)S(1)} reshape(f32[9,2496]{1,0:T(8,128)} %param.37) | data formatting | bytes 179712 | tf_op jit(solution)/shard_map/reshape | solution.py:666
  70.4 0.8 reshape.29.refs_6_
  71.2 0.0 collective-permute-done.2.refs_3_.refs_2_
  71.2 2.6 %collective-permute-done.3.refs_4_.refs_3_ = bf16[80,768]{1,0:T(8,128)(2,1)S(1)} collective-permute-done((bf16[80,768]{1,0:T(8,128)(2,1)S(1)}, bf16[80,768]{1,0:T(8,128)(2,1)S(1)}, u32[]{:S(2)}, u32[]{:S(2)}) %collective-permute-start.3) | collective-permute-done | bytes 122912 | tf_op jit(solution)/shard_map/ppermute | solution.py:567
  73.8 7.3 %shard_map.270 = (bf16[196,312]{1,0:T(8,128)(2,1)S(1)}, bf16[384,624]{1,0:T(8,128)(2,1)S(1)}) custom-call(s32[4]{0:T(128)S(1)} %add_convert_fusion.refs_0_.edge_ref, bf16[32,312]{1,0:T(8,128)(2,1)S(1)} %collective-permute-done.refs_0_.refs_1_, bf16[16,312]{1,0:T(8,128)(2,1)S(1)} %collective-permute-done.1.refs_1_.refs_2_, ...), custom_call_target="tpu_custom_call" | custom-call | tf_op jit(solution)/shard_map/pallas_call | solution.py:375
  81.1 9.8 %all-gather.5.cloned.1.call-done = bf16[8704,624]{1,0:T(8,128)(2,1)} async-done(((bf16[544,624]{1,0:T(8,128)(2,1)}), bf16[8704,624]{1,0:T(8,128)(2,1)}) %all-gather.5.cloned.1.call-update) | async-done | bytes 10862608 | tf_op jit(solution)/shard_map/all_gather | solution.py:596
  90.9 12.9 %shard_map.271 = (bf16[196,312]{1,0:T(8,128)(2,1)}, bf16[49,624]{1,0:T(8,128)(2,1)}) custom-call(s32[4]{0:T(128)S(1)} %add_convert_fusion.refs_0_.edge_ref, bf16[16,544,624]{2,1,0:T(8,128)(2,1)} %bitcast.25, bf16[64,768]{1,0:T(8,128)(2,1)S(1)} %get-tuple-element.20.refs_0_, bf16[64,624]{1,0:T(8,128)(2,1)S(1)} %get-tuple-element.21.refs_1_, ...), custom_call_target="tpu_custom_call" | custom-call | tf_op jit(solution)/shard_map/pallas_call | solution.py:539
  (1 shorter events, 0.0 us)
Async XLA Ops:
  7.2 83.7 %all-gather.5.cloned.1.call-start = ((), (), s32[]{:S(2)}) async-start(), calls=%async_computation.1 | async-start | bytes 11837440 | tf_op jit(solution)/shard_map/all_gather | solution.py:596
  44.8 14.3 %all-to-all-start = ((bf16[16,2,1280]{2,1,0:T(2,128)(2,1)}), bf16[16,2,1280]{2,1,0:T(2,128)(2,1)S(1)}, u32[]{:S(2)}, u32[]{:S(2)}) async-start(bf16[16,2,1280]{2,1,0:T(2,128)(2,1)} %reshape.37), calls=%async_computation | async-start | bytes 163840 | tf_op jit(solution)/shard_map/all_to_all | solution.py:631
  53.7 9.2 %collective-permute-start = (bf16[32,312]{1,0:T(8,128)(2,1)S(1)}, bf16[32,312]{1,0:T(8,128)(2,1)S(1)}, u32[]{:S(2)}, u32[]{:S(2)}) collective-permute-start(bf16[32,312]{1,0:T(8,128)(2,1)S(1)} %get-tuple-element.15), channel_id=1, source_target_pairs={{0,32},{32,64},{64,96},{96,128},{128,160},{160,192},{192,224},{224... | collective-permute-start | bytes 59912 | tf_op jit(solution)/shard_map/ppermute | solution.py:567
  57.2 5.6 %collective-permute-start.1 = (bf16[16,312]{1,0:T(8,128)(2,1)S(1)}, bf16[16,312]{1,0:T(8,128)(2,1)S(1)}, u32[]{:S(2)}, u32[]{:S(2)}) collective-permute-start(bf16[16,312]{1,0:T(8,128)(2,1)S(1)} %get-tuple-element.16), channel_id=1, source_target_pairs={{32,0},{64,32},{96,64},{128,96},{160,128},{192,160},{224,192},{256... | collective-permute-start | bytes 29960 | tf_op jit(solution)/shard_map/ppermute | solution.py:567
  64.2 7.0 %collective-permute-start.2 = (bf16[80,768]{1,0:T(8,128)(2,1)S(1)}, bf16[80,768]{1,0:T(8,128)(2,1)S(1)}, u32[]{:S(2)}, u32[]{:S(2)}) collective-permute-start(bf16[80,768]{1,0:T(8,128)(2,1)S(1)} %get-tuple-element.22), channel_id=1, source_target_pairs={{0,1},{1,2},{2,3},{3,4},{4,5},{5,6},{6,7},{7,8},{8,9},{9,10},{10,1... | collective-permute-start | bytes 368648 | tf_op jit(solution)/shard_map/ppermute | solution.py:567
  67.8 6.0 %collective-permute-start.3 = (bf16[80,768]{1,0:T(8,128)(2,1)S(1)}, bf16[80,768]{1,0:T(8,128)(2,1)S(1)}, u32[]{:S(2)}, u32[]{:S(2)}) collective-permute-start(bf16[80,768]{1,0:T(8,128)(2,1)S(1)} %get-tuple-element.23), channel_id=1, source_target_pairs={{1,0},{2,1},{3,2},{4,3},{5,4},{6,5},{7,6},{8,7},{9,8},{10,9},{11,1... | collective-permute-start | bytes 368648 | tf_op jit(solution)/shard_map/ppermute | solution.py:567
Sparse Core Ops, SparseCore 0:
  10.1 80.7 all-gather.4

commit v12 on v10

--- a/solution.py
+++ b/solution.py
@@ -463,7 +463,7 @@
     middle = nn(square_ref[...], mixed.astype(jnp.bfloat16)).astype(jnp.bfloat16)
     normed_mid = norm_rows(middle.astype(jnp.float32))
     copies[1].wait()
-    chunk = 512
+    chunk = 256
     expand = expand_ref[...].reshape(SHARDS * BLOCK_ROWS, width)
 
     def downsample(shard):
@@ -479,22 +479,25 @@
         down_ref[first : first + HALF, :64] += ninth[8 : 8 + HALF, :64]
         down_ref[first + HALF : first + HEAD_ROWS, :64] += ninth[8 : 8 + HALF, 64:]
 
-    shares = {2: range(0, 6), 3: range(6, 11), 4: range(11, SHARDS)}
+    shares = {4 + i: range(3 * i, min(3 * i + 3, SHARDS)) for i in range(6)}
     for first in range(0, SHARDS * BLOCK_ROWS, chunk):
-        if first == 2 * chunk:
+        if first == 4 * chunk:
             copies[3].wait()
         for shard in shares.get(first // chunk, ()):
             downsample(shard)
         span = pl.ds(first, chunk)
         hidden = gelu(nt(normed_mid, expand[first : first + chunk])) * inside
         hidden_ref[:, span] = hidden.astype(jnp.bfloat16).astype(jnp.float32)
+        totals = [jnp.zeros((8, chunk), jnp.float32)] * WIN
+        for place in range(3 * RING):
+            source, side = divmod(place, 3)
+            window = hidden_ref[pl.ds(source * RING + side, 8), span]
+            for down in range(3):
+                if 0 <= source - down < WIN:
+                    tap = 3 * down + side
+                    totals[source - down] += depth_ref[tap : tap + 1, span] * window
         for row in range(WIN):
-            total = jnp.zeros((8, chunk), jnp.float32)
-            for tap in range(9):
-                down, side = divmod(tap, 3)
-                window = hidden_ref[pl.ds((row + down) * RING + side, 8), span]
-                total += depth_ref[tap : tap + 1, span] * window
-            conv_ref[row * 8 : row * 8 + 8, span] = gelu(total)
+            conv_ref[row * 8 : row * 8 + 8, span] = gelu(totals[row])
     copies[2].wait()
     shrink = shrink_ref[...].reshape(SHARDS * BLOCK_ROWS, width)
     update = nn(conv_ref[...].astype(jnp.bfloat16), shrink)

time: 110 us -> 110 us (level)
  no operation moved by 1% of the time
where the time goes in v12:
time: 110 us
  Pallas kernels  32.4 us (29%)
  blocking collectives  30.2 us (27%)
  waiting for transfers between devices  15.8 us (14%)
  between operations  14.2 us (13%)
  starting transfers between devices  13.9 us (13%)
  local copies, waits for them, and re-layouts  3.22 us (3%)
    all_gather x1, blocking collectives, local(): strip = lax.all_gather(coarse_in.reshape(coarse_ch, coarse_cells).T, 'rows')  30.2 us
    pallas_call x5, Pallas kernels, call(): pl.pallas_call(fetching, out_shape=tuple((jax.ShapeDtypeStruct(shape, jnp...  20.4 us
    pallas_call x1, Pallas kernels, coarse_stream(): pl.pallas_call(coarse_kernel, out_shape=(jax.ShapeDtypeStruct((fine_cells...  12 us
    ppermute x4, starting transfers between devices, exchange(): return (lax.ppermute(onward, axis, up), lax.ppermute(back, axis, down))  10.5 us
    all_gather x1, waiting for transfers between devices, local(): gathered = lax.all_gather(mine, 'rows')  9.79 us
    ppermute x4, waiting for transfers between devices, exchange(): return (lax.ppermute(onward, axis, up), lax.ppermute(back, axis, down))  5.96 us
    all_to_all x1, starting transfers between devices, local(): blocks = lax.all_to_all(blocks, 'rows', 0, 0, tiled=True)  3.45 us
  transfers between devices with their start and end apart: 6, of which 3 were waited for; matrix products, arithmetic and copies ran while one was open for 3% of the time, Pallas kernels for 17%

profile of v12, /device:TPU:1, one launch (start us, length us, event | category | flops | bytes accessed | tf_op | source)
XLA Modules:
  0.0 109.8 jit_solution(7401401047648577348)
XLA Ops:
  7.2 0.0 all-gather.5.cloned.1.call-start
  7.2 2.2 %shard_map.266 = bf16[544,624]{1,0:T(8,128)(2,1)} custom-call(bf16[39,624]{1,0:T(8,128)(2,1)} %bitcast.32, bf16[156,624]{1,0:T(8,128)(2,1)} %refs_1_.2, bf16[156,624]{1,0:T(8,128)(2,1)} %bitcast.29, bf16[9,39,312]{2,1,0:T(8,128)(2,1)} %refs_3_.3), custom_call_target="tpu_custom_call" | custom-call | tf_op jit(solution)/shard_map/pallas_call | solution.py:373
  9.5 0.0 all-gather.5.cloned.1.call-update
  9.5 0.1 add_convert_fusion.refs_0_.edge_ref
  9.6 30.2 %all-gather.2.refs_2_ = bf16[16,49,624]{2,1,0:T(8,128)(2,1)S(1)} all-gather(bf16[1,49,624]{2,1,0:T(8,128)(2,1)} %bitcast.31), channel_id=3, replica_groups=mesh['rows'=16,'cols'=32] {'rows'}, dimensions={0}, use_global_device_ids=true | all-gather | bytes 1039584 | tf_op jit(solution)/shard_map/all_gather | solution.py:583
  39.8 4.1 %shard_map.268 = (bf16[16,64,40]{2,1,0:T(8,128)(2,1)S(1)}, bf16[64,624]{1,0:T(8,128)(2,1)S(1)}, bf16[32,624]{1,0:T(8,128)(2,1)S(1)}) custom-call(s32[4]{0:T(128)S(1)} %add_convert_fusion.refs_0_.edge_ref, s32[1]{0:T(128)} %bitcast.9.refs_1_, bf16[16,49,624]{2,1,0:T(8,128)(2,1)S(1)} %all-gather.2.refs_2_, bf16[3,39,624]{2,1,0:T(8,128)(2,1)} %refs_3_.4, ...), custom_call_target="tpu_custom_call" | custom-call | tf_op jit(solution)/shard_map/pallas_call | solution.py:373
  43.9 0.2 copy.29
  44.0 0.8 reshape.37
  44.8 3.5 %all-to-all-start = ((bf16[16,2,1280]{2,1,0:T(2,128)(2,1)}), bf16[16,2,1280]{2,1,0:T(2,128)(2,1)S(1)}, u32[]{:S(2)}, u32[]{:S(2)}) async-start(bf16[16,2,1280]{2,1,0:T(2,128)(2,1)} %reshape.37), calls=%async_computation | async-start | bytes 163840 | tf_op jit(solution)/shard_map/all_to_all | solution.py:617
  48.3 5.4 %shard_map.267 = (bf16[196,312]{1,0:T(8,128)(2,1)S(1)}, bf16[32,312]{1,0:T(8,128)(2,1)S(1)}, bf16[16,312]{1,0:T(8,128)(2,1)S(1)}) custom-call(bf16[196,312]{1,0:T(8,128)(2,1)} %bitcast.30, bf16[3,312,312]{2,1,0:T(8,128)(2,1)} %refs_1_.3, bf16[312,312]{1,0:T(8,128)(2,1)} %refs_2_.1, f32[196,196]{1,0:T(8,128)} %constant.43.clone.refs_3_), custom_call_target="tpu_custom_call" | custom-call | tf_op jit(solution)/shard_map/pallas_call | solution.py:373
  53.7 3.5 %collective-permute-start = (bf16[32,312]{1,0:T(8,128)(2,1)S(1)}, bf16[32,312]{1,0:T(8,128)(2,1)S(1)}, u32[]{:S(2)}, u32[]{:S(2)}) collective-permute-start(bf16[32,312]{1,0:T(8,128)(2,1)S(1)} %get-tuple-element.15), channel_id=1, source_target_pairs={{0,32},{32,64},{64,96},{96,128},{128,160},{160,192},{192,224},{224... | collective-permute-start | bytes 59912 | tf_op jit(solution)/shard_map/ppermute | solution.py:553
  57.2 1.9 %collective-permute-start.1 = (bf16[16,312]{1,0:T(8,128)(2,1)S(1)}, bf16[16,312]{1,0:T(8,128)(2,1)S(1)}, u32[]{:S(2)}, u32[]{:S(2)}) collective-permute-start(bf16[16,312]{1,0:T(8,128)(2,1)S(1)} %get-tuple-element.16), channel_id=1, source_target_pairs={{32,0},{64,32},{96,64},{128,96},{160,128},{192,160},{224,192},{256... | collective-permute-start | bytes 29960 | tf_op jit(solution)/shard_map/ppermute | solution.py:553
  59.2 0.0 all-to-all-done
  59.2 0.2 reshape.38
  59.3 0.2 copy.30.refs_4_
  59.5 3.4 %collective-permute-done.1.refs_1_.refs_2_ = bf16[16,312]{1,0:T(8,128)(2,1)S(1)} collective-permute-done((bf16[16,312]{1,0:T(8,128)(2,1)S(1)}, bf16[16,312]{1,0:T(8,128)(2,1)S(1)}, u32[]{:S(2)}, u32[]{:S(2)}) %collective-permute-start.1) | collective-permute-done | bytes 10016 | tf_op jit(solution)/shard_map/ppermute | solution.py:553
  62.9 0.0 collective-permute-done.refs_0_.refs_1_
  62.9 1.3 %shard_map.269 = (bf16[80,768]{1,0:T(8,128)(2,1)S(1)}, bf16[80,768]{1,0:T(8,128)(2,1)S(1)}, bf16[64,768]{1,0:T(8,128)(2,1)S(1)}) custom-call(bf16[32,312]{1,0:T(8,128)(2,1)S(1)} %collective-permute-done.refs_0_.refs_1_, bf16[16,312]{1,0:T(8,128)(2,1)S(1)} %collective-permute-done.1.refs_1_.refs_2_, bf16[196,312]{1,0:T(8,128)(2,1)S(1)} %get-tuple-element.17.refs_2_.refs_5_, ...), custom_call_target="tpu_custom_call" | custom-call | tf_op jit(solution)/shard_map/pallas_call | solution.py:373
  64.2 3.6 %collective-permute-start.2 = (bf16[80,768]{1,0:T(8,128)(2,1)S(1)}, bf16[80,768]{1,0:T(8,128)(2,1)S(1)}, u32[]{:S(2)}, u32[]{:S(2)}) collective-permute-start(bf16[80,768]{1,0:T(8,128)(2,1)S(1)} %get-tuple-element.22), channel_id=1, source_target_pairs={{0,1},{1,2},{2,3},{3,4},{4,5},{5,6},{6,7},{7,8},{8,9},{9,10},{10,1... | collective-permute-start | bytes 368648 | tf_op jit(solution)/shard_map/ppermute | solution.py:553
  67.8 1.5 %collective-permute-start.3 = (bf16[80,768]{1,0:T(8,128)(2,1)S(1)}, bf16[80,768]{1,0:T(8,128)(2,1)S(1)}, u32[]{:S(2)}, u32[]{:S(2)}) collective-permute-start(bf16[80,768]{1,0:T(8,128)(2,1)S(1)} %get-tuple-element.23), channel_id=1, source_target_pairs={{1,0},{2,1},{3,2},{4,3},{5,4},{6,5},{7,6},{8,7},{9,8},{10,9},{11,1... | collective-permute-start | bytes 368648 | tf_op jit(solution)/shard_map/ppermute | solution.py:553
  69.3 1.1 %reshape.28 = f32[9,16,156]{2,1,0:T(8,128)S(1)} reshape(f32[9,2496]{1,0:T(8,128)} %param.37) | data formatting | bytes 179712 | tf_op jit(solution)/shard_map/reshape | solution.py:652
  70.4 0.8 reshape.29.refs_6_
  71.2 0.0 collective-permute-done.2.refs_3_.refs_2_
  71.2 2.6 %collective-permute-done.3.refs_4_.refs_3_ = bf16[80,768]{1,0:T(8,128)(2,1)S(1)} collective-permute-done((bf16[80,768]{1,0:T(8,128)(2,1)S(1)}, bf16[80,768]{1,0:T(8,128)(2,1)S(1)}, u32[]{:S(2)}, u32[]{:S(2)}) %collective-permute-start.3) | collective-permute-done | bytes 122912 | tf_op jit(solution)/shard_map/ppermute | solution.py:553
  73.8 7.3 %shard_map.270 = (bf16[196,312]{1,0:T(8,128)(2,1)S(1)}, bf16[384,624]{1,0:T(8,128)(2,1)S(1)}) custom-call(s32[4]{0:T(128)S(1)} %add_convert_fusion.refs_0_.edge_ref, bf16[32,312]{1,0:T(8,128)(2,1)S(1)} %collective-permute-done.refs_0_.refs_1_, bf16[16,312]{1,0:T(8,128)(2,1)S(1)} %collective-permute-done.1.refs_1_.refs_2_, ...), custom_call_target="tpu_custom_call" | custom-call | tf_op jit(solution)/shard_map/pallas_call | solution.py:373
  81.1 9.8 %all-gather.5.cloned.1.call-done = bf16[8704,624]{1,0:T(8,128)(2,1)} async-done(((bf16[544,624]{1,0:T(8,128)(2,1)}), bf16[8704,624]{1,0:T(8,128)(2,1)}) %all-gather.5.cloned.1.call-update) | async-done | bytes 10862608 | tf_op jit(solution)/shard_map/all_gather | solution.py:582
  90.9 12.0 %shard_map.271 = (bf16[196,312]{1,0:T(8,128)(2,1)}, bf16[49,624]{1,0:T(8,128)(2,1)}) custom-call(s32[4]{0:T(128)S(1)} %add_convert_fusion.refs_0_.edge_ref, bf16[16,544,624]{2,1,0:T(8,128)(2,1)} %bitcast.25, bf16[64,768]{1,0:T(8,128)(2,1)S(1)} %get-tuple-element.20.refs_0_, bf16[64,624]{1,0:T(8,128)(2,1)S(1)} %get-tuple-element.21.refs_1_, ...), custom_call_target="tpu_custom_call" | custom-call | tf_op jit(solution)/shard_map/pallas_call | solution.py:525
  (1 shorter events, 0.0 us)
Async XLA Ops:
  7.2 83.7 %all-gather.5.cloned.1.call-start = ((), (), s32[]{:S(2)}) async-start(), calls=%async_computation.1 | async-start | bytes 11837440 | tf_op jit(solution)/shard_map/all_gather | solution.py:582
  44.8 14.3 %all-to-all-start = ((bf16[16,2,1280]{2,1,0:T(2,128)(2,1)}), bf16[16,2,1280]{2,1,0:T(2,128)(2,1)S(1)}, u32[]{:S(2)}, u32[]{:S(2)}) async-start(bf16[16,2,1280]{2,1,0:T(2,128)(2,1)} %reshape.37), calls=%async_computation | async-start | bytes 163840 | tf_op jit(solution)/shard_map/all_to_all | solution.py:617
  53.7 9.2 %collective-permute-start = (bf16[32,312]{1,0:T(8,128)(2,1)S(1)}, bf16[32,312]{1,0:T(8,128)(2,1)S(1)}, u32[]{:S(2)}, u32[]{:S(2)}) collective-permute-start(bf16[32,312]{1,0:T(8,128)(2,1)S(1)} %get-tuple-element.15), channel_id=1, source_target_pairs={{0,32},{32,64},{64,96},{96,128},{128,160},{160,192},{192,224},{224... | collective-permute-start | bytes 59912 | tf_op jit(solution)/shard_map/ppermute | solution.py:553
  57.2 5.6 %collective-permute-start.1 = (bf16[16,312]{1,0:T(8,128)(2,1)S(1)}, bf16[16,312]{1,0:T(8,128)(2,1)S(1)}, u32[]{:S(2)}, u32[]{:S(2)}) collective-permute-start(bf16[16,312]{1,0:T(8,128)(2,1)S(1)} %get-tuple-element.16), channel_id=1, source_target_pairs={{32,0},{64,32},{96,64},{128,96},{160,128},{192,160},{224,192},{256... | collective-permute-start | bytes 29960 | tf_op jit(solution)/shard_map/ppermute | solution.py:553
  64.2 7.0 %collective-permute-start.2 = (bf16[80,768]{1,0:T(8,128)(2,1)S(1)}, bf16[80,768]{1,0:T(8,128)(2,1)S(1)}, u32[]{:S(2)}, u32[]{:S(2)}) collective-permute-start(bf16[80,768]{1,0:T(8,128)(2,1)S(1)} %get-tuple-element.22), channel_id=1, source_target_pairs={{0,1},{1,2},{2,3},{3,4},{4,5},{5,6},{6,7},{7,8},{8,9},{9,10},{10,1... | collective-permute-start | bytes 368648 | tf_op jit(solution)/shard_map/ppermute | solution.py:553
  67.8 6.0 %collective-permute-start.3 = (bf16[80,768]{1,0:T(8,128)(2,1)S(1)}, bf16[80,768]{1,0:T(8,128)(2,1)S(1)}, u32[]{:S(2)}, u32[]{:S(2)}) collective-permute-start(bf16[80,768]{1,0:T(8,128)(2,1)S(1)} %get-tuple-element.23), channel_id=1, source_target_pairs={{1,0},{2,1},{3,2},{4,3},{5,4},{6,5},{7,6},{8,7},{9,8},{10,9},{11,1... | collective-permute-start | bytes 368648 | tf_op jit(solution)/shard_map/ppermute | solution.py:553
Sparse Core Ops, SparseCore 0:
  10.1 80.7 all-gather.4
